TPU v7x, 512 devices: a whole 4x4x16 slice. The times are simulated.
512 devices in a mesh: chain: 4 (over y), tp: 32 (over z, core), dec: 4 (over x).
Axes of the slice: x: 4, y: 4, z: 16, core: 2. Of those that a mesh axis runs over, the one named last changes fastest.
Arguments:
- query_comp: bfloat16 [4, 2048, 1536], P('dec', ('chain', 'tp')), may hold values from -6 to 6
- latent_rows: bfloat16 [4, 16, 128, 512], P('dec', 'chain', 'tp'), may hold values from -6 to 6
- rope_keys: bfloat16 [4, 16, 128, 64], P('dec', 'chain', 'tp'), may hold values from -6 to 6
- latent_gain: float32 [512], replicated, may hold values from 0.1 to 1.9
- query_up: bfloat16 [1536, 12288], P(None, 'tp'), may hold values from -0.15625 to 0.15625
- absorb_key: bfloat16 [64, 128, 512], P('tp'), may hold values from -17 to 17
- absorb_value: bfloat16 [64, 512, 128], P('tp'), may hold values from -0.25 to 0.25
- out_proj: bfloat16 [8192, 3584], P('tp'), may hold values from -0.0625 to 0.0625
- page_owner: int32 [4, 16], P('dec', 'chain'), may hold values from 0 to 3, as said below
- page_slot: int32 [4, 16], P('dec', 'chain'), may hold values from 0 to 7
Outputs:
- layer_output: bfloat16 [4, 2048, 3584], P('dec', ('chain', 'tp'))
- cache_latent: bfloat16 [4, 4, 8, 128, 512], P('dec', 'chain', None, 'tp')
- cache_rope: bfloat16 [4, 4, 8, 128, 64], P('dec', 'chain', None, 'tp')
Inputs may be any that keep to these rules, and one draw needn't show every extreme that they name: `page_owner`: among the pages of one block index of all prompts, no two share an owner and a slot.
All inputs are finite; a program needn't handle non-finite values.
Results may differ from a plain program's by a relative error of at most 0.035.
Values may be sent and summed in bfloat16 or wider, within the bound.
No kernel may reach another device: no remote copies, remote signals or barrier semaphores. Data moves between devices by JAX's collectives and lax.ppermute only.
A program may use at most 64 MiB of HBM per device.

v0:
```python
import jax
import jax.numpy as jnp
from jax import lax
from jax.sharding import PartitionSpec as P


def rotate(values, where_at):
    full_width = values.shape[-1]
    half_width = full_width // 2
    frequency = 10000.0 ** (-(jnp.arange(half_width).astype(jnp.float32) * 2.0 / full_width))
    angles = where_at.astype(jnp.float32)[:, None] * frequency[None, :]
    angles = angles.reshape((where_at.shape[0],) + (1,) * (values.ndim - 2) + (half_width,))
    cosine = jnp.cos(angles)
    sine_part = jnp.sin(angles)
    first_half = values[..., :half_width]
    second_half = values[..., half_width:]
    return jnp.concatenate(
        [
            first_half * cosine - second_half * sine_part,
            second_half * cosine + first_half * sine_part,
        ],
        -1,
    )


def local(
    query_comp,
    latent_rows,
    rope_keys,
    latent_gain,
    query_up,
    absorb_key,
    absorb_value,
    out_proj,
    page_owner,
    page_slot,
):
    tp_count = lax.axis_size("tp")
    tp_index = lax.axis_index("tp")
    chain_index = lax.axis_index("chain")
    dec_count = lax.axis_size("dec")
    pages_here = latent_rows.shape[1]
    page_part = latent_rows.shape[2]
    page_length = page_part * tp_count
    block_len = pages_here * page_length
    heads_here = absorb_key.shape[0]
    nope_width = absorb_key.shape[1]
    latent_width = latent_rows.shape[3]
    rope_width = rope_keys.shape[3]
    value_width = absorb_value.shape[2]
    slot_count = 2 * pages_here
    key_where = (
        chain_index * block_len
        + jnp.arange(pages_here, dtype=jnp.int32)[:, None] * page_length
        + tp_index * page_part
        + jnp.arange(page_part, dtype=jnp.int32)[None, :]
    ).reshape(-1)
    latent = latent_rows[0].astype(jnp.float32)
    normed = (
        latent * lax.rsqrt(jnp.mean(latent * latent, -1, keepdims=True) + 1e-06) * latent_gain
    ).astype(jnp.bfloat16)
    key_rot = rotate(
        rope_keys[0].reshape(pages_here * page_part, rope_width).astype(jnp.float32), key_where
    )
    key_rot = key_rot.astype(jnp.bfloat16).reshape(pages_here, page_part, rope_width)
    owners = page_owner[0]
    slots = page_slot[0]
    peers = jnp.arange(dec_count, dtype=jnp.int32)
    picked = owners[None, :] == peers[:, None]
    send_latent = jnp.where(picked[:, :, None, None], normed[None], jnp.zeros((), jnp.bfloat16))
    send_rope = jnp.where(picked[:, :, None, None], key_rot[None], jnp.zeros((), jnp.bfloat16))
    send_slots = jnp.where(picked, slots[None, :], -1)
    got_latent, got_rope, got_slots = (
        lax.all_to_all(send_latent, "dec", split_axis=0, concat_axis=0, tiled=True),
        lax.all_to_all(send_rope, "dec", split_axis=0, concat_axis=0, tiled=True),
        lax.all_to_all(send_slots, "dec", split_axis=0, concat_axis=0, tiled=True),
    )
    arrivals = dec_count * pages_here
    placing = (
        got_slots.reshape(arrivals)[None, :] == jnp.arange(slot_count, dtype=jnp.int32)[:, None]
    ).astype(jnp.bfloat16)
    cache_latent = jnp.einsum(
        "sp,pjc->sjc",
        placing,
        got_latent.reshape(arrivals, page_part, latent_width),
        preferred_element_type=jnp.float32,
    )
    cache_latent = cache_latent.astype(jnp.bfloat16)[None, None]
    cache_rope = jnp.einsum(
        "sp,pjc->sjc",
        placing,
        got_rope.reshape(arrivals, page_part, rope_width),
        preferred_element_type=jnp.float32,
    )
    cache_rope = cache_rope.astype(jnp.bfloat16)[None, None]
    full_latent, full_rope = (
        lax.all_gather(normed[None], "tp", axis=2, tiled=True),
        lax.all_gather(key_rot[None], "tp", axis=2, tiled=True),
    )
    full_latent = full_latent.reshape(block_len, latent_width)
    full_rope = full_rope.reshape(block_len, rope_width)
    query = jnp.dot(
        lax.all_gather(query_comp, "tp", axis=1, tiled=True)[0],
        query_up,
        preferred_element_type=jnp.float32,
    ).astype(jnp.bfloat16)[None][0]
    query_where = chain_index * block_len + jnp.arange(block_len, dtype=jnp.int32)
    query = query.reshape(block_len, heads_here, nope_width + rope_width)
    query_lat = jnp.einsum(
        "thn,hnc->htc", query[..., :nope_width], absorb_key, preferred_element_type=jnp.float32
    ).astype(jnp.bfloat16)
    query_rot = jnp.transpose(
        rotate(query[..., nope_width:].astype(jnp.float32), query_where), (1, 0, 2)
    ).astype(jnp.bfloat16)
    scale = (nope_width + rope_width) ** (-0.5)
    highest = jnp.full((heads_here, block_len), -1e30, jnp.float32)
    keys_lat = lax.all_gather(full_latent, "chain", axis=0, tiled=True)
    keys_rope = lax.all_gather(full_rope, "chain", axis=0, tiled=True)
    key_pos = jnp.arange(keys_lat.shape[0], dtype=jnp.int32)
    scores = (
        jnp.einsum("hqc,kc->hqk", query_lat, keys_lat, preferred_element_type=jnp.float32)
        + jnp.einsum("hqr,kr->hqk", query_rot, keys_rope, preferred_element_type=jnp.float32)
    ) * scale
    allowed = key_pos[None, None, :] <= query_where[None, :, None]
    newest = jnp.maximum(highest, jnp.max(jnp.where(allowed, scores, -jnp.inf), -1))
    weights = jnp.where(allowed, jnp.exp(scores - newest[..., None]), 0.0)
    totals = jnp.sum(weights, -1)
    running = jnp.einsum(
        "hqk,kc->hqc", weights.astype(jnp.bfloat16), keys_lat, preferred_element_type=jnp.float32
    )
    highest, totals, running = (newest, totals, running)
    mixed = (running / totals[..., None]).astype(jnp.bfloat16)
    heads_out = jnp.einsum(
        "hqc,hcv->qhv", mixed, absorb_value, preferred_element_type=jnp.float32
    ).astype(jnp.bfloat16)
    heads_out = heads_out.reshape(block_len, heads_here * value_width)
    rows_here = block_len // tp_count
    partial_sum = jnp.dot(heads_out, out_proj, preferred_element_type=jnp.float32).astype(
        jnp.bfloat16
    )
    partial_sum = lax.optimization_barrier(partial_sum)
    summed = lax.psum(partial_sum.astype(jnp.float32).astype(jnp.bfloat16), "tp").astype(
        jnp.float32
    )
    mine = lax.dynamic_slice_in_dim(summed, tp_index * rows_here, rows_here, 0)
    layer_output = mine.astype(jnp.bfloat16)[None]
    return (layer_output, cache_latent, cache_rope)


def solution(mesh):
    return jax.shard_map(
        local,
        mesh=mesh,
        in_specs=(
            P("dec", ("chain", "tp"), None),
            P("dec", "chain", "tp", None),
            P("dec", "chain", "tp", None),
            P(),
            P(None, "tp"),
            P("tp", None, None),
            P("tp", None, None),
            P("tp", None),
            P("dec", "chain"),
            P("dec", "chain"),
        ),
        out_specs=(
            P("dec", ("chain", "tp"), None),
            P("dec", "chain", None, "tp", None),
            P("dec", "chain", None, "tp", None),
        ),
        check_vma=False,
    )
```

profile of v0, /device:TPU:24, one launch (start us, length us, event | category | flops | bytes accessed | tf_op | source)
XLA Modules:
  0.0 378.6 jit_solution(14204950047341312257)
XLA Ops:
  7.2 0.7 all-gather.3.cloned.1.call-update
  8.0 0.8 fusion.31
  8.8 0.8 fusion.33
  9.6 37.9 %all_gather.16 = bf16[1,4,128,512]{3,1,0,2:T(4,128)(2,1)S(1)} all-gather(bf16[1,4,4,512]{3,1,0,2:T(4,128)(2,1)S(1)} %fusion.33), channel_id=1, replica_groups=mesh['chain'=4,'tp'=32,'dec'=4] {'tp'}, dimensions={2}, use_global_device_ids=true | all-gather | bytes 540672 | tf_op jit(solution)/shard_map/all_gather | solution.py:97
  47.5 0.9 copy.29
  48.6 0.7 convert.23
  49.5 27.4 %all_gather.18 = bf16[1,4,128,64]{3,1,0,2:T(4,128)(2,1)S(1)} all-gather(bf16[1,4,4,64]{3,1,0,2:T(4,128)(2,1)S(1)} %copy.30), channel_id=1, replica_groups=mesh['chain'=4,'tp'=32,'dec'=4] {'tp'}, dimensions={2}, use_global_device_ids=true | all-gather | bytes 67584 | tf_op jit(solution)/shard_map/all_gather | solution.py:98
  77.1 12.3 %all_gather.19 = bf16[2048,64]{0,1:T(8,128)(2,1)S(1)} all-gather(bf16[512,64]{0,1:T(8,128)(2,1)S(1)} %bitcast.72), channel_id=1, replica_groups=mesh['chain'=4,'tp'=32,'dec'=4] {'chain'}, dimensions={0}, use_global_device_ids=true | all-gather | bytes 327680 | tf_op jit(solution)/shard_map/all_gather | solution.py:118
  89.7 0.7 iota_compare_fusion
  90.4 2.6 fusion.12
  93.0 0.7 copy-done.3
  93.8 27.9 %all-gather.5.cloned.1.call-done = bf16[2048,512]{1,0:T(8,128)(2,1)} async-done(((bf16[512,512]{1,0:T(8,128)(2,1)}), bf16[2048,512]{1,0:T(8,128)(2,1)}) %all-gather.5.cloned.1.call-update) | async-done | bytes 2097168 | tf_op jit(solution)/shard_map/all_gather | solution.py:117
  121.7 7.6 %fusion.8 = f32[2,512,2048]{2,1,0:T(8,128)} fusion(bf16[2048,512]{1,0:T(8,128)(2,1)} %all-gather.5.cloned.1.call-done, bf16[2,128,512]{2,1,0:T(8,128)(2,1)} %param.15, bf16[512,2,192]{0,2,1:T(8,128)(2,1)} %bitcast.76), kind=kOutput, calls=%fused_computation.12 | convolution fusion | flops 2282225664 | bytes 11010048 | tf_op jit(solution)/shard_map/hqc,kc->hqk/dot_general | solution.py:121
  129.3 4.7 %select_reduce_fusion = (f32[2,512]{1,0:T(2,128)S(1)}, f32[2,512,2048]{2,1,0:T(8,128)S(1)}) fusion(pred[512,2048]{1,0:T(8,128)(4,1)S(1)} %iota_compare_fusion, f32[2,512,2048]{2,1,0:T(8,128)} %fusion.8, bf16[2048,64]{0,1:T(8,128)(2,1)S(1)} %all_gather.19, bf16[512,2,32]{0,2,1:T(8,128)(2,1)S(1)} %get-tuple-element.13, ...), kind=kOutput, calls=%fused_computation.1 | convolution fusion | flops 277085184 | bytes 18223104 | tf_op jit(solution)/shard_map/hqr,kr->hqk/dot_general | solution.py:122
  134.1 3.2 copy-done.1
  137.3 2.4 fusion
  139.6 6.7 %convolution_convert_fusion.2 = bf16[2,512,128]{1,2,0:T(8,128)(2,1)S(1)} fusion(bf16[2,512,128]{2,1,0:T(8,128)(2,1)S(1)} %copy-done.7, f32[2,512]{1,0:T(2,128)S(1)} %fusion, f32[2,512,2048]{2,1,0:T(8,128)} %copy-done.1, f32[2,512]{1,0:T(2,128)S(1)} %broadcast_maximum_fusion, pred[512,2048]{1,0:T(8,128)(4,1)S(1)} %iota_compare_fusion, ...), kind=kOutput, calls=%fused_computation.19 | convolution fusion | flops 2289172480 | bytes 12066816 | tf_op jit(solution)/shard_map/hqc,hcv->qhv/dot_general | solution.py:133
  146.4 3.0 convolution_convert_fusion
  149.4 0.6 compare_select_fusion
  150.0 4.2 %all-to-all-start = ((s32[4,1,4]{2,1,0:T(1,128)}), s32[4,1,4]{2,1,0:T(1,128)S(1)}, u32[]{:S(2)}, u32[]{:S(2)}) async-start(s32[4,1,4]{2,1,0:T(1,128)} %compare_select_fusion), calls=%async_computation | async-start | bytes 4096 | tf_op jit(solution)/shard_map/all_to_all | solution.py:76
  154.5 0.7 reshape.290
  155.2 4.2 %all-to-all-done = s32[4,1,4]{2,1,0:T(1,128)S(1)} async-done(((s32[4,1,4]{2,1,0:T(1,128)}), s32[4,1,4]{2,1,0:T(1,128)S(1)}, u32[]{:S(2)}, u32[]{:S(2)}) %all-to-all-start) | async-done | bytes 96 | tf_op jit(solution)/shard_map/all_to_all | solution.py:76
  159.5 3.2 all-to-all-start.2
  162.7 0.7 broadcast_select_fusion
  164.0 0.7 reduce.4
  164.7 3.3 all-to-all-done.2
  168.0 3.3 all-to-all-start.1
  171.5 0.6 copy.37
  172.1 4.8 %all-to-all-done.1 = bf16[4,4,4,512]{3,1,2,0:T(4,128)(2,1)S(1)} async-done(((bf16[4,4,4,512]{3,1,2,0:T(4,128)(2,1)}), bf16[4,4,4,512]{3,1,2,0:T(4,128)(2,1)S(1)}, u32[]{:S(2)}, u32[]{:S(2)}) %all-to-all-start.1) | async-done | bytes 65568 | tf_op jit(solution)/shard_map/all_to_all | solution.py:74
  177.1 0.6 copy.36
  177.7 192.8 %all-reduce.2.cloned.1.call-done = bf16[512,3584]{1,0:T(8,128)(2,1)} async-done(((bf16[512,3584]{1,0:T(8,128)(2,1)}), bf16[512,3584]{1,0:T(8,128)(2,1)}) %all-reduce.2.cloned.1.call-update) | async-done | bytes 3670032 | tf_op jit(solution)/shard_map/psum | solution.py:142
  370.5 1.6 fusion.30
  (49 shorter events, 2.4 us)
Async XLA Ops:
  7.2 139.2 %copy-start = (bf16[256,3584]{1,0:T(8,128)(2,1)S(1)}, bf16[256,3584]{1,0:T(8,128)(2,1)}, u32[]{:S(2)}) copy-start(bf16[256,3584]{1,0:T(8,128)(2,1)} %param.17) | copy-start | bytes 5505028
  7.2 83.2 %all-gather.3.cloned.1.call-start = ((), (), s32[]{:S(2)}) async-start(), calls=%async_computation.3 | async-start | bytes 1622016 | tf_op jit(solution)/shard_map/all_gather | solution.py:103
  7.9 113.8 %all-gather.5.cloned.1.call-start = ((), (), s32[]{:S(2)}) async-start(), calls=%async_computation.4 | async-start | bytes 2621440 | tf_op jit(solution)/shard_map/all_gather | solution.py:117
  48.4 322.1 %all-reduce.2.cloned.1.call-start = ((), (), s32[]{:S(2)}) async-start(), calls=%async_computation.5 | async-start | bytes 7340032 | tf_op jit(solution)/shard_map/psum | solution.py:142
  93.0 0.8 copy-start.3
  134.0 3.2 copy-start.1
  137.3 2.4 copy-start.7
  146.4 3.1 copy-start.5
  146.4 3.1 copy-start.6
  146.4 8.8 %copy-start.2 = (bf16[1,4,4,512]{3,2,1,0:T(4,128)(2,1)S(1)}, bf16[1,4,4,512]{3,2,1,0:T(4,128)(2,1)}, u32[]{:S(2)}) copy-start(bf16[1,4,4,512]{3,2,1,0:T(4,128)(2,1)} %param.11) | copy-start | bytes 49156
  146.4 8.7 %copy-start.4 = (f32[512]{0:T(512)S(1)}, f32[512]{0:T(512)}, u32[]{:S(2)}) copy-start(f32[512]{0:T(512)} %param.13) | copy-start | bytes 6148
  150.0 9.4 %all-to-all-start = ((s32[4,1,4]{2,1,0:T(1,128)}), s32[4,1,4]{2,1,0:T(1,128)S(1)}, u32[]{:S(2)}, u32[]{:S(2)}) async-start(s32[4,1,4]{2,1,0:T(1,128)} %compare_select_fusion), calls=%async_computation | async-start | bytes 4096 | tf_op jit(solution)/shard_map/all_to_all | solution.py:76
  159.5 8.5 %all-to-all-start.2 = ((bf16[4,2,512]{2,1,0:T(2,128)(2,1)}), bf16[4,2,512]{2,1,0:T(2,128)(2,1)S(1)}, u32[]{:S(2)}, u32[]{:S(2)}) async-start(bf16[4,2,512]{2,1,0:T(2,128)(2,1)} %reshape.290), calls=%async_computation.2 | async-start | bytes 16384 | tf_op jit(solution)/shard_map/all_to_all | solution.py:75
  168.0 8.9 %all-to-all-start.1 = ((bf16[4,4,4,512]{3,1,2,0:T(4,128)(2,1)}), bf16[4,4,4,512]{3,1,2,0:T(4,128)(2,1)S(1)}, u32[]{:S(2)}, u32[]{:S(2)}) async-start(bf16[4,4,4,512]{3,1,2,0:T(4,128)(2,1)} %broadcast_select_fusion), calls=%async_computation.1 | async-start | bytes 131072 | tf_op jit(solution)/shard_map/all_to_all | solution.py:74
Sparse Core Ops, SparseCore 0:
  10.1 75.5 all-gather.2
  87.8 33.8 all-gather.4
  149.5 220.9 all-reduce.1
where the time goes:
time: 381 us; the launch traced here: 379 us
  waiting for transfers between devices  234 us (61%)
  blocking collectives  77.6 us (20%)
  matrix products  24.9 us (7%)
  between operations  14 us (4%)
  starting transfers between devices  10.9 us (3%)
  other arithmetic  9.78 us (3%)
  local copies, waits for them, and re-layouts  7.76 us (2%)
    psum x1, waiting for transfers between devices, local(): lax.psum(partial_sum.astype(jnp.float32).astype(jnp.bfloat16), 'tp')  193 us
    all_gather x1, blocking collectives, local(): lax.all_gather(normed[None], 'tp', axis=2, tiled=True)  37.9 us
    all_gather x1, waiting for transfers between devices, local(): keys_lat = lax.all_gather(full_latent, 'chain', axis=0, tiled=True)  27.9 us
    all_gather x1, blocking collectives, local(): lax.all_gather(key_rot[None], 'tp', axis=2, tiled=True)  27.4 us
    all_gather x1, blocking collectives, local(): keys_rope = lax.all_gather(full_rope, 'chain', axis=0, tiled=True)  12.3 us
    dot_general x1, matrix products, local(): jnp.einsum('hqc,kc->hqk', query_lat, keys_lat, preferred_element_type=jnp...  7.64 us
  transfers between devices with their start and end apart: 6, of which 5 were waited for; matrix products, arithmetic and copies ran while one was open for 3% of the time, Pallas kernels for 0%

commit v1 on v0

v1 whole, which is shorter than its diff:
```python
import functools

import jax
import jax.numpy as jnp
import numpy as np
from jax import lax
from jax.experimental import pallas as pl
from jax.experimental.pallas import tpu as pltpu
from jax.sharding import Mesh, PartitionSpec as P

BF = jnp.bfloat16
F32 = jnp.float32
LOG2E = 1.4426950408889634
Z = ("zh", "zl")
TP = ("zh", "zl", "core")
NEG = -1e30


def rope_tables(where_at, full_width):
    half = full_width // 2
    frequency = 10000.0 ** (-(jnp.arange(half).astype(F32) * 2.0 / full_width))
    angles = where_at.astype(F32)[:, None] * frequency[None, :]
    cosine, sine = jnp.cos(angles), jnp.sin(angles)
    return (
        jnp.concatenate([cosine, cosine], -1),
        jnp.concatenate([-sine, sine], -1),
    )


def swap_halves(v):
    half = v.shape[-1] // 2
    return jnp.concatenate([v[..., half:], v[..., :half]], -1)


def shift_z(x, step):
    n = lax.axis_size("zh") * lax.axis_size("zl")
    return lax.ppermute(x, Z, [(i, (i + step) % n) for i in range(n)])


def swap_core(x):
    return lax.ppermute(x, "core", [(0, 1), (1, 0)])


def spread(x, axis):
    n = lax.axis_size(axis)
    return lax.all_to_all(jnp.broadcast_to(x[None], (n,) + x.shape), axis, 0, 0, tiled=True)


def gather_classes(g):
    half = g.shape[0] // 2
    return (
        g,
        shift_z(g, -1),
        shift_z(g[:half], -2),
        shift_z(g[half:], 2),
        shift_z(g, 1),
    )


def query_kernel(g0, g1, g2a, g2b, g3, wq0, wq1, ak0, ak1, cos_ref, sin_ref, out_ref, x_ref, *, nope, rope):
    at = 0
    for g in (g0, g1, g2a, g2b, g3):
        n = g.shape[0]
        x_ref[at : at + n, :] = g[...]
        at += n
    x = x_ref[...]
    rows = x.shape[0]
    lat = ak0.shape[-1]
    head = 0
    for wq, ak in ((wq0, ak0), (wq1, ak1)):
        q = jnp.dot(x, wq[...], preferred_element_type=F32).astype(BF)
        for h in range(ak.shape[0]):
            base = h * (nope + rope)
            r0 = head * rows
            out_ref[r0 : r0 + rows, :lat] = jnp.dot(
                q[:, base : base + nope], ak[h], preferred_element_type=F32
            ).astype(BF)
            rot = q[:, base + nope : base + nope + rope].astype(F32)
            out_ref[r0 : r0 + rows, lat:] = (
                rot * cos_ref[...] + swap_halves(rot) * sin_ref[...]
            ).astype(BF)
            head += 1


def attend_kernel(
    where_ref, q_ref, kown, kown2, k1, k12, k2, k22, k3, k32, av0, av1, op0, op1, out_ref,
    m_ref, l_ref, acc_ref, ho_ref, *, rows, lat, scale, lay,
):
    chain, zl, core = where_ref[0], where_ref[1], where_ref[2]
    nzh, nzl, part, qrows, pages = lay
    s2 = scale * LOG2E
    vh = av0.shape[-1]
    heads = q_ref.shape[0] // rows
    half_keys = kown.shape[0]

    def key_pos(idx, kcore):
        d = idx // (nzh * pages * part)
        zh = (idx // (pages * part)) % nzh
        page = (idx // part) % pages
        r = idx % part
        z = zh * nzl + (zl + d) % nzl
        return page * (nzh * nzl * 2 * part) + z * (2 * part) + kcore * part + r

    def query_pos(idx):
        d = idx // (nzh * qrows)
        zh = (idx // qrows) % nzh
        j = idx % qrows
        z = zh * nzl + (zl + d) % nzl
        return z * (2 * qrows) + core * qrows + j

    qp = query_pos(lax.broadcasted_iota(jnp.int32, (rows, 1), 0))
    kidx = lax.broadcasted_iota(jnp.int32, (1, half_keys), 1)
    ok_a = key_pos(kidx, core) <= qp
    ok_b = key_pos(kidx, 1 - core) <= qp
    nt = (((1,), (1,)), ((), ()))

    def scores(q, ka, kb, masked):
        sa = lax.dot_general(q, ka, nt, preferred_element_type=F32)
        sb = lax.dot_general(q, kb, nt, preferred_element_type=F32)
        if masked:
            sa = jnp.where(ok_a, sa, NEG)
            sb = jnp.where(ok_b, sb, NEG)
        return sa, sb

    def step(q, kar, kbr, first):
        ka, kb = kar[...], kbr[...]
        sa, sb = scores(q, ka, kb, first)
        top = jnp.maximum(jnp.max(sa, -1, keepdims=True), jnp.max(sb, -1, keepdims=True))
        m = top if first else jnp.maximum(m_ref[...], top)
        pa = jnp.exp2((sa - m) * s2)
        pb = jnp.exp2((sb - m) * s2)
        total = jnp.sum(pa, -1, keepdims=True) + jnp.sum(pb, -1, keepdims=True)
        pv = jnp.dot(pa.astype(BF), ka[:, :lat], preferred_element_type=F32) + jnp.dot(
            pb.astype(BF), kb[:, :lat], preferred_element_type=F32
        )
        if first:
            l_ref[...] = total
            acc_ref[...] = pv
        else:
            fade = jnp.exp2((m_ref[...] - m) * s2)
            l_ref[...] = l_ref[...] * fade + total
            acc_ref[...] = acc_ref[...] * fade + pv
        m_ref[...] = m

    for h in range(heads):
        q = q_ref[h * rows : (h + 1) * rows, :]
        step(q, kown, kown2, True)
        for back, (ka, kb) in enumerate(((k1, k12), (k2, k22), (k3, k32)), 1):
            pl.when(chain >= back)(functools.partial(step, q, ka, kb, False))
        mixed = (acc_ref[...] / l_ref[...]).astype(BF)
        per = heads // 2
        av = (av0 if h < per else av1)[h % per]
        ho_ref[:, h * vh : (h + 1) * vh] = jnp.dot(mixed, av, preferred_element_type=F32).astype(BF)
    ho = ho_ref[...]
    k = op0.shape[0]
    width = out_ref.shape[1]
    cut = 512 if width % 512 == 0 else width
    for c in range(0, width, cut):
        out_ref[:, c : c + cut] = (
            jnp.dot(ho[:, :k], op0[:, c : c + cut], preferred_element_type=F32)
            + jnp.dot(ho[:, k:], op1[:, c : c + cut], preferred_element_type=F32)
        ).astype(BF)


def local(
    query_comp, latent_rows, rope_keys, latent_gain, query_up, absorb_key, absorb_value, out_proj,
    page_owner, page_slot,
):
    nzh, nzl, nch = lax.axis_size("zh"), lax.axis_size("zl"), lax.axis_size("chain")
    zh, zl, core = lax.axis_index("zh"), lax.axis_index("zl"), lax.axis_index("core")
    chain, dec = lax.axis_index("chain"), lax.axis_index("dec")
    pages, part, lat = latent_rows.shape[1:]
    rope = rope_keys.shape[3]
    heads_here, nope = absorb_key.shape[:2]
    vh = absorb_value.shape[2]
    qrows, ql = query_comp.shape[1:]
    width = out_proj.shape[1]
    tp_index = (zh * nzl + zl) * 2 + core
    tp_count = nzh * nzl * 2
    block_len = qrows * tp_count
    slots = 2 * pages

    key_where = (
        chain * block_len
        + jnp.arange(pages, dtype=jnp.int32)[:, None] * (part * tp_count)
        + tp_index * part
        + jnp.arange(part, dtype=jnp.int32)[None, :]
    ).reshape(-1)
    x = latent_rows[0].reshape(pages * part, lat).astype(F32)
    normed = (x * lax.rsqrt(jnp.mean(x * x, -1, keepdims=True) + 1e-06) * latent_gain).astype(BF)
    kcos, ksin = rope_tables(key_where, rope)
    kr = rope_keys[0].reshape(pages * part, rope).astype(F32)
    key_rot = (kr * kcos + swap_halves(kr) * ksin).astype(BF)
    keys = jnp.concatenate([normed, key_rot], -1)

    wq1 = swap_core(query_up)
    ak1 = swap_core(absorb_key)
    av1 = swap_core(absorb_value)
    op1 = swap_core(out_proj)

    kg = gather_classes(spread(keys, "zh"))
    qg = gather_classes(spread(query_comp[0], "zh"))
    own = jnp.concatenate([p.reshape(-1, lat + rope) for p in kg], 0)
    backs = [
        lax.ppermute(own, "chain", [(i, i + k) for i in range(nch - k)]) for k in range(1, nch)
    ]
    key_sets = []
    for a in [own] + backs:
        key_sets += [a, swap_core(a)]

    rows = qrows * nzh * nzl
    idx = jnp.arange(rows, dtype=jnp.int32)
    zq = (idx // qrows) % nzh * nzl + (zl + idx // (nzh * qrows)) % nzl
    query_where = chain * block_len + zq * (2 * qrows) + core * qrows + idx % qrows
    qcos, qsin = rope_tables(query_where, rope)
    heads = 2 * heads_here
    big = dict(vmem_limit_bytes=32 * 1024 * 1024)
    q = pl.pallas_call(
        functools.partial(query_kernel, nope=nope, rope=rope),
        out_shape=jax.ShapeDtypeStruct((heads * rows, lat + rope), BF),
        scratch_shapes=[pltpu.VMEM((rows, ql), BF)],
        compiler_params=pltpu.CompilerParams(**big),
        cost_estimate=pl.CostEstimate(
            flops=2 * rows * heads * (nope + rope) * ql + 2 * rows * heads * nope * lat,
            bytes_accessed=6000000, transcendentals=0,
        ),
        name="queries",
    )(*[p.reshape(-1, ql) for p in qg], query_up, wq1, absorb_key, ak1, qcos, qsin)

    vm = pl.BlockSpec(memory_space=pltpu.VMEM)
    partial = pl.pallas_call(
        functools.partial(
            attend_kernel, rows=rows, lat=lat, scale=(nope + rope) ** -0.5,
            lay=(nzh, nzl, part, qrows, pages),
        ),
        out_shape=jax.ShapeDtypeStruct((rows, width), BF),
        in_specs=[pl.BlockSpec(memory_space=pltpu.SMEM)] + [vm] * 13,
        out_specs=vm,
        scratch_shapes=[
            pltpu.VMEM((rows, 1), F32),
            pltpu.VMEM((rows, 1), F32),
            pltpu.VMEM((rows, lat), F32),
            pltpu.VMEM((rows, heads * vh), BF),
        ],
        compiler_params=pltpu.CompilerParams(**big),
        cost_estimate=pl.CostEstimate(
            flops=4 * rows * heads * nch * block_len * lat, bytes_accessed=9000000,
            transcendentals=rows * heads * nch * block_len,
        ),
        name="attend",
    )(
        jnp.stack([chain, zl, core]).astype(jnp.int32), q, *key_sets,
        absorb_value, av1, out_proj, op1,
    )

    sums = partial.reshape(nzl, nzh, qrows, width)
    half = nzh // 2
    up = shift_z(sums[1], 1)
    down = shift_z(sums[3], -1)
    up2 = shift_z(sums[2, :half], 2)
    down2 = shift_z(sums[2, half:], -2)
    near = (
        sums[0].astype(F32) + up.astype(F32) + down.astype(F32)
        + jnp.concatenate([up2, down2], 0).astype(F32)
    ).astype(BF)
    got = lax.all_to_all(near, "zh", 0, 0, tiled=True)
    layer_output = jnp.sum(got.astype(F32), 0).astype(BF)[None]

    code = (page_owner[0] * slots + page_slot[0]).astype(BF)
    tail = jnp.broadcast_to(code[:, None, None], (pages, part, 128 - rope))
    page = jnp.concatenate([keys.reshape(pages, part, lat + rope), tail], -1)
    page = spread(page, "dec")
    came = page[:, :, 0, lat + rope].reshape(-1).astype(jnp.int32)
    take = (came[None, :] == dec * slots + jnp.arange(slots, dtype=jnp.int32)[:, None]).astype(BF)
    placed = jnp.einsum(
        "sp,pjc->sjc", take, page.reshape(-1, part, page.shape[-1]), preferred_element_type=F32
    ).astype(BF)
    cache_latent = placed[..., :lat][None, None]
    cache_rope = placed[..., lat : lat + rope][None, None]
    return (layer_output, cache_latent, cache_rope)


def solution(mesh):
    shape = mesh.shape
    chips = shape["tp"] // 2
    nzl = 4
    fine = Mesh(
        np.asarray(mesh.devices).reshape(shape["chain"], chips // nzl, nzl, 2, shape["dec"]),
        ("chain", "zh", "zl", "core", "dec"),
    )
    row = ("chain",) + TP
    return jax.shard_map(
        local,
        mesh=fine,
        in_specs=(
            P("dec", row, None),
            P("dec", "chain", TP, None),
            P("dec", "chain", TP, None),
            P(),
            P(None, TP),
            P(TP, None, None),
            P(TP, None, None),
            P(TP, None),
            P("dec", "chain"),
            P("dec", "chain"),
        ),
        out_specs=(
            P("dec", row, None),
            P("dec", "chain", None, TP, None),
            P("dec", "chain", None, TP, None),
        ),
        check_vma=False,
    )
```

time: 381 us -> 206 us (0.54)
  waiting for transfers between devices: 234 us -> 58.3 us
  starting transfers between devices: 10.9 us -> 112 us
  blocking collectives: 77.6 us -> 0 us
  matrix products: 24.9 us -> 0.2 us
  Pallas kernels: 0 us -> 18.3 us
  between operations: 14 us -> 1.17 us
    psum x1 -> x0, waiting for transfers between devices: 193 us -> none  [local(): lax.psum(partial_sum.astype(jnp.float32).astype(jnp.bfloat16), 'tp')]
    all_gather x3 -> x0, blocking collectives: 77.6 us -> none  [the longest x1 37.9 us: local(): lax.all_gather(normed[None], 'tp', axis=2, tiled=True)]
    ppermute x0 -> x23, starting transfers between devices: none -> 73.7 us  [the longest x12 52.5 us: shift_z(): return lax.ppermute(x, Z, [(i, (i + step) % n) for i in range(n)])]
    ppermute x0 -> x23, waiting for transfers between devices: none -> 30 us  [the longest x12 24.9 us: shift_z(): return lax.ppermute(x, Z, [(i, (i + step) % n) for i in range(n)])]
    all_gather x2 -> x0, waiting for transfers between devices: 28 us -> none  [the longest x1 27.9 us: local(): keys_lat = lax.all_gather(full_latent, 'chain', axis=0, tiled=True)]
    all_to_all x3 -> x4, starting transfers between devices: 10.8 us -> 38 us  [the longest x3 27.7 us: spread(): lax.all_to_all(jnp.broadcast_to(x[None], (n,) + x.shape), axis, 0, 0, til...]
    dot_general x7 -> x1, matrix products: 24.9 us -> 0.2 us  [local(): jnp.einsum('sp,pjc->sjc', take, page.reshape(-1, part, page.shape[-1]), p...]
    pallas_call x0 -> x2, Pallas kernels: none -> 18.3 us  [the longest x1 16.8 us: local(): pl.pallas_call(functools.partial(attend_kernel, rows=rows, lat=lat, scale...]
  transfers between devices with their start and end apart: 6 -> 27, of which waited for: 5 -> 10; matrix products, arithmetic and copies ran while one was open for 3% -> 4% of each run, Pallas kernels for 0% -> 1%
where the time goes in v1:
time: 206 us; the launch traced here: 204 us
  starting transfers between devices  112 us (54%)
  waiting for transfers between devices  58.3 us (28%)
  Pallas kernels  18.3 us (9%)
  other arithmetic  9.29 us (5%)
  local copies, waits for them, and re-layouts  5.35 us (3%)
    ppermute x12, starting transfers between devices, shift_z(): return lax.ppermute(x, Z, [(i, (i + step) % n) for i in range(n)])  52.5 us
    all_to_all x3, starting transfers between devices, spread(): lax.all_to_all(jnp.broadcast_to(x[None], (n,) + x.shape), axis, 0, 0, til...  27.7 us
    ppermute x12, waiting for transfers between devices, shift_z(): return lax.ppermute(x, Z, [(i, (i + step) % n) for i in range(n)])  24.9 us
    all_to_all x1, waiting for transfers between devices, local(): got = lax.all_to_all(near, 'zh', 0, 0, tiled=True)  24.6 us
    ppermute x8, starting transfers between devices, swap_core(): return lax.ppermute(x, 'core', [(0, 1), (1, 0)])  17.3 us
    pallas_call x1, Pallas kernels, local(): pl.pallas_call(functools.partial(attend_kernel, rows=rows, lat=lat, scale...  16.8 us
    all_to_all x1, starting transfers between devices, local(): got = lax.all_to_all(near, 'zh', 0, 0, tiled=True)  10.3 us
    ppermute x3, waiting for transfers between devices, local(): lax.ppermute(own, 'chain', [(i, i + k) for i in range(nch - k)])  5.13 us
  transfers between devices with their start and end apart: 27, of which 10 were waited for; matrix products, arithmetic and copies ran while one was open for 4% of the time, Pallas kernels for 1%

profile of v1, /device:TPU:24, one launch (start us, length us, event | category | flops | bytes accessed | tf_op | source)
XLA Modules:
  0.0 204.3 jit_solution(12688856983445931460)
XLA Ops:
  5.7 15.1 %all-to-all-start.1 = ((bf16[4,16,576]{2,1,0:T(8,128)(2,1)}), bf16[4,16,576]{2,1,0:T(8,128)(2,1)S(1)}, u32[]{:S(2)}, u32[]{:S(2)}) async-start(bf16[4,16,576]{2,1,0:T(8,128)(2,1)} %broadcast_in_dim.18), calls=%async_computation.1 | async-start | bytes 163840 | tf_op jit(solution)/shard_map/all_to_all | solution.py:46
  22.7 2.4 %collective-permute-start.5 = (bf16[2,128,512]{2,1,0:T(8,128)(2,1)}, bf16[2,128,512]{2,1,0:T(8,128)(2,1)S(1)}, u32[]{:S(2)}, u32[]{:S(2)}) collective-permute-start(bf16[2,128,512]{2,1,0:T(8,128)(2,1)} %ak0.1), channel_id=1, source_target_pairs={{0,4},{4,0},{1,5},{5,1},{2,6},{6,2},{3,7},{7,3},{8,12},{12,8},{9,1... | collective-permute-start | bytes 786440 | tf_op jit(solution)/shard_map/ppermute | solution.py:41
  25.1 1.9 collective-permute-start.18
  27.0 2.4 %collective-permute-start.17 = (bf16[2,512,128]{2,1,0:T(8,128)(2,1)}, bf16[2,512,128]{2,1,0:T(8,128)(2,1)}, u32[]{:S(2)}, u32[]{:S(2)}) collective-permute-start(bf16[2,512,128]{2,1,0:T(8,128)(2,1)} %av0.1), channel_id=1, source_target_pairs={{0,4},{4,0},{1,5},{5,1},{2,6},{6,2},{3,7},{7,3},{8,12},{12,8},{9,1... | collective-permute-start | bytes 786440 | tf_op jit(solution)/shard_map/ppermute | solution.py:41
  30.9 3.7 %all-to-all-done.1 = bf16[4,16,576]{2,1,0:T(8,128)(2,1)S(1)} async-done(((bf16[4,16,576]{2,1,0:T(8,128)(2,1)}), bf16[4,16,576]{2,1,0:T(8,128)(2,1)S(1)}, u32[]{:S(2)}, u32[]{:S(2)}) %all-to-all-start.1) | async-done | bytes 73760 | tf_op jit(solution)/shard_map/all_to_all | solution.py:46
  36.1 8.3 %all-to-all-start = ((bf16[4,16,1536]{2,1,0:T(8,128)(2,1)}), bf16[4,16,1536]{2,1,0:T(8,128)(2,1)S(1)}, u32[]{:S(2)}, u32[]{:S(2)}) async-start(bf16[4,16,1536]{2,1,0:T(8,128)(2,1)} %broadcast_in_dim.17), calls=%async_computation | async-start | bytes 393216 | tf_op jit(solution)/shard_map/all_to_all | solution.py:46
  44.4 6.5 %collective-permute-start.6 = (bf16[4,16,576]{2,1,0:T(8,128)(2,1)S(1)}, bf16[4,16,576]{2,1,0:T(8,128)(2,1)S(1)}, u32[]{:S(2)}, u32[]{:S(2)}) collective-permute-start(bf16[4,16,576]{2,1,0:T(8,128)(2,1)S(1)} %all-to-all-done.1), channel_id=1, source_target_pairs={{0,120},{8,0},{16,8},{24,16},{32,24},{40,32},{48,40},{56,48},{64,5... | collective-permute-start | bytes 221192 | tf_op jit(solution)/shard_map/ppermute | solution.py:37
  50.9 4.1 %collective-permute-done.6 = bf16[4,16,576]{2,1,0:T(8,128)(2,1)S(1)} collective-permute-done((bf16[4,16,576]{2,1,0:T(8,128)(2,1)S(1)}, bf16[4,16,576]{2,1,0:T(8,128)(2,1)S(1)}, u32[]{:S(2)}, u32[]{:S(2)}) %collective-permute-start.6) | collective-permute-done | bytes 73760 | tf_op jit(solution)/shard_map/ppermute | solution.py:37
  55.0 5.5 %collective-permute-start.7 = (bf16[2,16,576]{2,1,0:T(8,128)(2,1)S(1)}, bf16[2,16,576]{2,1,0:T(8,128)(2,1)S(1)}, u32[]{:S(2)}, u32[]{:S(2)}) collective-permute-start(bf16[2,16,576]{2,1,0:T(8,128)(2,1)S(1)} %get-tuple-element.23), channel_id=1, source_target_pairs={{0,112},{8,120},{16,0},{24,8},{32,16},{40,24},{48,32},{56,40},{64,... | collective-permute-start | bytes 110600 | tf_op jit(solution)/shard_map/ppermute | solution.py:37
  60.5 1.9 collective-permute-done.7
  62.4 4.4 %collective-permute-start.8 = (bf16[2,16,576]{2,1,0:T(8,128)(2,1)S(1)}, bf16[2,16,576]{2,1,0:T(8,128)(2,1)S(1)}, u32[]{:S(2)}, u32[]{:S(2)}) collective-permute-start(bf16[2,16,576]{2,1,0:T(8,128)(2,1)S(1)} %get-tuple-element.22), channel_id=1, source_target_pairs={{0,16},{8,24},{16,32},{24,40},{32,48},{40,56},{48,64},{56,72},{64,... | collective-permute-start | bytes 110600 | tf_op jit(solution)/shard_map/ppermute | solution.py:37
  66.9 4.0 %collective-permute-done.8 = bf16[2,16,576]{2,1,0:T(8,128)(2,1)S(1)} collective-permute-done((bf16[2,16,576]{2,1,0:T(8,128)(2,1)S(1)}, bf16[2,16,576]{2,1,0:T(8,128)(2,1)S(1)}, u32[]{:S(2)}, u32[]{:S(2)}) %collective-permute-start.8) | collective-permute-done | bytes 36896 | tf_op jit(solution)/shard_map/ppermute | solution.py:37
  70.9 4.3 %collective-permute-start.9 = (bf16[4,16,576]{2,1,0:T(8,128)(2,1)S(1)}, bf16[4,16,576]{2,1,0:T(8,128)(2,1)S(1)}, u32[]{:S(2)}, u32[]{:S(2)}) collective-permute-start(bf16[4,16,576]{2,1,0:T(8,128)(2,1)S(1)} %all-to-all-done.1), channel_id=1, source_target_pairs={{0,8},{8,16},{16,24},{24,32},{32,40},{40,48},{48,56},{56,64},{64,7... | collective-permute-start | bytes 221192 | tf_op jit(solution)/shard_map/ppermute | solution.py:37
  75.2 3.2 %collective-permute-done.9 = bf16[4,16,576]{2,1,0:T(8,128)(2,1)S(1)} collective-permute-done((bf16[4,16,576]{2,1,0:T(8,128)(2,1)S(1)}, bf16[4,16,576]{2,1,0:T(8,128)(2,1)S(1)}, u32[]{:S(2)}, u32[]{:S(2)}) %collective-permute-start.9) | collective-permute-done | bytes 73760 | tf_op jit(solution)/shard_map/ppermute | solution.py:37
  82.4 5.1 %collective-permute-done.11.k1 = bf16[256,576]{1,0:T(8,128)(2,1)} collective-permute-done((bf16[256,576]{1,0:T(8,128)(2,1)S(1)}, bf16[256,576]{1,0:T(8,128)(2,1)}, u32[]{:S(2)}, u32[]{:S(2)}) %collective-permute-start.11) | collective-permute-done | bytes 294944 | tf_op jit(solution)/shard_map/ppermute | solution.py:205
  87.5 4.5 %collective-permute-start.1 = (bf16[2,16,1536]{2,1,0:T(8,128)(2,1)S(1)}, bf16[2,16,1536]{2,1,0:T(8,128)(2,1)S(1)}, u32[]{:S(2)}, u32[]{:S(2)}) collective-permute-start(bf16[2,16,1536]{2,1,0:T(8,128)(2,1)S(1)} %get-tuple-element.21), channel_id=1, source_target_pairs={{0,112},{8,120},{16,0},{24,8},{32,16},{40,24},{48,32},{56,40},{64,... | collective-permute-start | bytes 294920 | tf_op jit(solution)/shard_map/ppermute | solution.py:37
  92.0 3.9 %collective-permute-start = (bf16[4,16,1536]{2,1,0:T(8,128)(2,1)S(1)}, bf16[4,16,1536]{2,1,0:T(8,128)(2,1)S(1)}, u32[]{:S(2)}, u32[]{:S(2)}) collective-permute-start(bf16[4,16,1536]{2,1,0:T(8,128)(2,1)S(1)} %all-to-all-done), channel_id=1, source_target_pairs={{0,120},{8,0},{16,8},{24,16},{32,24},{40,32},{48,40},{56,48},{64,5... | collective-permute-start | bytes 589832 | tf_op jit(solution)/shard_map/ppermute | solution.py:37
  95.9 3.6 %collective-permute-start.3 = (bf16[4,16,1536]{2,1,0:T(8,128)(2,1)S(1)}, bf16[4,16,1536]{2,1,0:T(8,128)(2,1)S(1)}, u32[]{:S(2)}, u32[]{:S(2)}) collective-permute-start(bf16[4,16,1536]{2,1,0:T(8,128)(2,1)S(1)} %all-to-all-done), channel_id=1, source_target_pairs={{0,8},{8,16},{16,24},{24,32},{32,40},{40,48},{48,56},{56,64},{64,7... | collective-permute-start | bytes 589832 | tf_op jit(solution)/shard_map/ppermute | solution.py:37
  99.6 4.8 %collective-permute-start.2 = (bf16[2,16,1536]{2,1,0:T(8,128)(2,1)S(1)}, bf16[2,16,1536]{2,1,0:T(8,128)(2,1)S(1)}, u32[]{:S(2)}, u32[]{:S(2)}) collective-permute-start(bf16[2,16,1536]{2,1,0:T(8,128)(2,1)S(1)} %get-tuple-element.20), channel_id=1, source_target_pairs={{0,16},{8,24},{16,32},{24,40},{32,48},{40,56},{48,64},{56,72},{64,... | collective-permute-start | bytes 294920 | tf_op jit(solution)/shard_map/ppermute | solution.py:37
  105.7 4.0 %collective-permute-done.2 = bf16[2,16,1536]{2,1,0:T(8,128)(2,1)S(1)} collective-permute-done((bf16[2,16,1536]{2,1,0:T(8,128)(2,1)S(1)}, bf16[2,16,1536]{2,1,0:T(8,128)(2,1)S(1)}, u32[]{:S(2)}, u32[]{:S(2)}) %collective-permute-start.2) | collective-permute-done | bytes 98336 | tf_op jit(solution)/shard_map/ppermute | solution.py:37
  111.5 2.4 %collective-permute-start.12 = (bf16[256,576]{1,0:T(8,128)(2,1)}, bf16[256,576]{1,0:T(8,128)(2,1)S(1)}, u32[]{:S(2)}, u32[]{:S(2)}) collective-permute-start(bf16[256,576]{1,0:T(8,128)(2,1)} %collective-permute-done.11.k1), channel_id=1, source_target_pairs={{0,4},{4,0},{1,5},{5,1},{2,6},{6,2},{3,7},{7,3},{8,12},{12,8},{9,1... | collective-permute-start | bytes 884744 | tf_op jit(solution)/shard_map/ppermute | solution.py:41
  115.9 2.4 %collective-permute-start.16 = (bf16[256,576]{1,0:T(8,128)(2,1)}, bf16[256,576]{1,0:T(8,128)(2,1)S(1)}, u32[]{:S(2)}, u32[]{:S(2)}) collective-permute-start(bf16[256,576]{1,0:T(8,128)(2,1)} %collective-permute-done.15.k3), channel_id=1, source_target_pairs={{0,4},{4,0},{1,5},{5,1},{2,6},{6,2},{3,7},{7,3},{8,12},{12,8},{9,1... | collective-permute-start | bytes 884744 | tf_op jit(solution)/shard_map/ppermute | solution.py:41
  120.8 16.8 %attend.1 = bf16[256,3584]{1,0:T(8,128)(2,1)S(1)} custom-call(s32[3]{0:T(128)S(1)} %pad_add_fusion.where_ref, bf16[1024,576]{1,0:T(8,128)(2,1)S(1)} %queries.1.q_ref, bf16[256,576]{1,0:T(8,128)(2,1)S(1)} %constant_dynamic-update-slice_fusion.kown, bf16[256,576]{1,0:T(8,128)(2,1)S(1)} %collective-permute-done.10.kown2, ...), custom_call_target="tpu_custom_call" | custom-call | flops 4294967296 | bytes 9000000 | tf_op jit(solution)/shard_map/attend/pallas_call | solution.py:231
  137.7 2.4 %collective-permute-start.19 = (bf16[4,16,3584]{2,1,0:T(8,128)(2,1)S(1)}, bf16[4,16,3584]{2,1,0:T(8,128)(2,1)S(1)}, u32[]{:S(2)}, u32[]{:S(2)}) collective-permute-start(bf16[4,16,3584]{2,1,0:T(8,128)(2,1)S(1)} %bitcast.55), channel_id=1, source_target_pairs={{0,8},{8,16},{16,24},{24,32},{32,40},{40,48},{48,56},{56,64},{64,7... | collective-permute-start | bytes 1376264 | tf_op jit(solution)/shard_map/ppermute | solution.py:37
  140.1 4.7 %collective-permute-start.20 = (bf16[4,16,3584]{2,1,0:T(8,128)(2,1)S(1)}, bf16[4,16,3584]{2,1,0:T(8,128)(2,1)S(1)}, u32[]{:S(2)}, u32[]{:S(2)}) collective-permute-start(bf16[4,16,3584]{2,1,0:T(8,128)(2,1)S(1)} %bitcast.54), channel_id=1, source_target_pairs={{0,120},{8,0},{16,8},{24,16},{32,24},{40,32},{48,40},{56,48},{64,5... | collective-permute-start | bytes 1376264 | tf_op jit(solution)/shard_map/ppermute | solution.py:37
  144.8 2.6 %collective-permute-start.21 = (bf16[2,16,3584]{2,1,0:T(8,128)(2,1)S(1)}, bf16[2,16,3584]{2,1,0:T(8,128)(2,1)S(1)}, u32[]{:S(2)}, u32[]{:S(2)}) collective-permute-start(bf16[2,16,3584]{2,1,0:T(8,128)(2,1)S(1)} %get-tuple-element.15), channel_id=1, source_target_pairs={{0,16},{8,24},{16,32},{24,40},{32,48},{40,56},{48,64},{56,72},{64,... | collective-permute-start | bytes 688136 | tf_op jit(solution)/shard_map/ppermute | solution.py:37
  147.4 5.4 %collective-permute-start.22 = (bf16[2,16,3584]{2,1,0:T(8,128)(2,1)S(1)}, bf16[2,16,3584]{2,1,0:T(8,128)(2,1)S(1)}, u32[]{:S(2)}, u32[]{:S(2)}) collective-permute-start(bf16[2,16,3584]{2,1,0:T(8,128)(2,1)S(1)} %get-tuple-element.16), channel_id=1, source_target_pairs={{0,112},{8,120},{16,0},{24,8},{32,16},{40,24},{48,32},{56,40},{64,... | collective-permute-start | bytes 688136 | tf_op jit(solution)/shard_map/ppermute | solution.py:37
  153.6 4.3 %all-to-all-start.3 = ((bf16[4,4,4,640]{3,2,1,0:T(4,128)(2,1)}), bf16[4,4,4,640]{3,2,1,0:T(4,128)(2,1)S(1)}, u32[]{:S(2)}, u32[]{:S(2)}) async-start(bf16[4,4,4,640]{3,2,1,0:T(4,128)(2,1)} %broadcast_in_dim.21), calls=%async_computation.3 | async-start | bytes 163840 | tf_op jit(solution)/shard_map/all_to_all | solution.py:46
  157.9 2.9 %collective-permute-done.21 = bf16[2,16,3584]{2,1,0:T(8,128)(2,1)S(1)} collective-permute-done((bf16[2,16,3584]{2,1,0:T(8,128)(2,1)S(1)}, bf16[2,16,3584]{2,1,0:T(8,128)(2,1)S(1)}, u32[]{:S(2)}, u32[]{:S(2)}) %collective-permute-start.21) | collective-permute-done | bytes 229408 | tf_op jit(solution)/shard_map/ppermute | solution.py:37
  160.9 4.8 %collective-permute-done.22 = bf16[2,16,3584]{2,1,0:T(8,128)(2,1)S(1)} collective-permute-done((bf16[2,16,3584]{2,1,0:T(8,128)(2,1)S(1)}, bf16[2,16,3584]{2,1,0:T(8,128)(2,1)S(1)}, u32[]{:S(2)}, u32[]{:S(2)}) %collective-permute-start.22) | collective-permute-done | bytes 229408 | tf_op jit(solution)/shard_map/ppermute | solution.py:37
  166.7 10.3 %all-to-all-start.2 = ((bf16[4,16,3584]{2,1,0:T(8,128)(2,1)}), bf16[4,16,3584]{2,1,0:T(8,128)(2,1)S(1)}, u32[]{:S(2)}, u32[]{:S(2)}) async-start(bf16[4,16,3584]{2,1,0:T(8,128)(2,1)} %fusion.2), calls=%async_computation.2 | async-start | bytes 917504 | tf_op jit(solution)/shard_map/all_to_all | solution.py:266
  179.0 24.6 %all-to-all-done.2 = bf16[4,16,3584]{2,1,0:T(8,128)(2,1)S(1)} async-done(((bf16[4,16,3584]{2,1,0:T(8,128)(2,1)}), bf16[4,16,3584]{2,1,0:T(8,128)(2,1)S(1)}, u32[]{:S(2)}, u32[]{:S(2)}) %all-to-all-start.2) | async-done | bytes 458784 | tf_op jit(solution)/shard_map/all_to_all | solution.py:266
  (84 shorter events, 26.0 us)
Async XLA Ops:
  0.6 117.8 %copy-start.5 = (bf16[1,4,4,512]{3,2,1,0:T(4,128)(2,1)S(1)}, bf16[1,4,4,512]{3,2,1,0:T(4,128)(2,1)}, u32[]{:S(2)}) copy-start(bf16[1,4,4,512]{3,2,1,0:T(4,128)(2,1)} %param.11) | copy-start | bytes 49156
  0.6 98.9 %copy-start.4 = (bf16[1,4,4,64]{3,2,1,0:T(4,128)(2,1)S(1)}, bf16[1,4,4,64]{3,2,1,0:T(4,128)(2,1)}, u32[]{:S(2)}) copy-start(bf16[1,4,4,64]{3,2,1,0:T(4,128)(2,1)} %param.12) | copy-start | bytes 6148
  0.7 118.5 %copy-start = (bf16[1536,384]{1,0:T(8,128)(2,1)S(1)}, bf16[1536,384]{1,0:T(8,128)(2,1)}, u32[]{:S(2)}) copy-start(bf16[1536,384]{1,0:T(8,128)(2,1)} %wq0.1) | copy-start | bytes 3538948
  0.7 118.5 %copy-start.1 = (bf16[2,128,512]{2,1,0:T(8,128)(2,1)S(1)}, bf16[2,128,512]{2,1,0:T(8,128)(2,1)}, u32[]{:S(2)}) copy-start(bf16[2,128,512]{2,1,0:T(8,128)(2,1)} %ak0.1) | copy-start | bytes 786436
  5.7 28.9 %all-to-all-start.1 = ((bf16[4,16,576]{2,1,0:T(8,128)(2,1)}), bf16[4,16,576]{2,1,0:T(8,128)(2,1)S(1)}, u32[]{:S(2)}, u32[]{:S(2)}) async-start(bf16[4,16,576]{2,1,0:T(8,128)(2,1)} %broadcast_in_dim.18), calls=%async_computation.1 | async-start | bytes 163840 | tf_op jit(solution)/shard_map/all_to_all | solution.py:46
  20.8 95.2 %collective-permute-start.4 = (bf16[1536,384]{1,0:T(8,128)(2,1)}, bf16[1536,384]{1,0:T(8,128)(2,1)S(1)}, u32[]{:S(2)}, u32[]{:S(2)}) collective-permute-start(bf16[1536,384]{1,0:T(8,128)(2,1)} %wq0.1), channel_id=1, source_target_pairs={{0,4},{4,0},{1,5},{5,1},{2,6},{6,2},{3,7},{7,3},{8,12},{12,8},{9,1... | collective-permute-start | bytes 3538952 | tf_op jit(solution)/shard_map/ppermute | solution.py:41
  22.7 57.1 %collective-permute-start.5 = (bf16[2,128,512]{2,1,0:T(8,128)(2,1)}, bf16[2,128,512]{2,1,0:T(8,128)(2,1)S(1)}, u32[]{:S(2)}, u32[]{:S(2)}) collective-permute-start(bf16[2,128,512]{2,1,0:T(8,128)(2,1)} %ak0.1), channel_id=1, source_target_pairs={{0,4},{4,0},{1,5},{5,1},{2,6},{6,2},{3,7},{7,3},{8,12},{12,8},{9,1... | collective-permute-start | bytes 786440 | tf_op jit(solution)/shard_map/ppermute | solution.py:41
  25.1 95.7 %collective-permute-start.18 = (bf16[256,3584]{1,0:T(8,128)(2,1)}, bf16[256,3584]{1,0:T(8,128)(2,1)}, u32[]{:S(2)}, u32[]{:S(2)}) collective-permute-start(bf16[256,3584]{1,0:T(8,128)(2,1)} %op0.1), channel_id=1, source_target_pairs={{0,4},{4,0},{1,5},{5,1},{2,6},{6,2},{3,7},{7,3},{8,12},{12,8},{9,1... | collective-permute-start | bytes 5505032 | tf_op jit(solution)/shard_map/ppermute | solution.py:41
  27.0 54.0 %collective-permute-start.17 = (bf16[2,512,128]{2,1,0:T(8,128)(2,1)}, bf16[2,512,128]{2,1,0:T(8,128)(2,1)}, u32[]{:S(2)}, u32[]{:S(2)}) collective-permute-start(bf16[2,512,128]{2,1,0:T(8,128)(2,1)} %av0.1), channel_id=1, source_target_pairs={{0,4},{4,0},{1,5},{5,1},{2,6},{6,2},{3,7},{7,3},{8,12},{12,8},{9,1... | collective-permute-start | bytes 786440 | tf_op jit(solution)/shard_map/ppermute | solution.py:41
  36.1 46.3 %all-to-all-start = ((bf16[4,16,1536]{2,1,0:T(8,128)(2,1)}), bf16[4,16,1536]{2,1,0:T(8,128)(2,1)S(1)}, u32[]{:S(2)}, u32[]{:S(2)}) async-start(bf16[4,16,1536]{2,1,0:T(8,128)(2,1)} %broadcast_in_dim.17), calls=%async_computation | async-start | bytes 393216 | tf_op jit(solution)/shard_map/all_to_all | solution.py:46
  44.4 10.6 %collective-permute-start.6 = (bf16[4,16,576]{2,1,0:T(8,128)(2,1)S(1)}, bf16[4,16,576]{2,1,0:T(8,128)(2,1)S(1)}, u32[]{:S(2)}, u32[]{:S(2)}) collective-permute-start(bf16[4,16,576]{2,1,0:T(8,128)(2,1)S(1)} %all-to-all-done.1), channel_id=1, source_target_pairs={{0,120},{8,0},{16,8},{24,16},{32,24},{40,32},{48,40},{56,48},{64,5... | collective-permute-start | bytes 221192 | tf_op jit(solution)/shard_map/ppermute | solution.py:37
  55.0 7.5 %collective-permute-start.7 = (bf16[2,16,576]{2,1,0:T(8,128)(2,1)S(1)}, bf16[2,16,576]{2,1,0:T(8,128)(2,1)S(1)}, u32[]{:S(2)}, u32[]{:S(2)}) collective-permute-start(bf16[2,16,576]{2,1,0:T(8,128)(2,1)S(1)} %get-tuple-element.23), channel_id=1, source_target_pairs={{0,112},{8,120},{16,0},{24,8},{32,16},{40,24},{48,32},{56,40},{64,... | collective-permute-start | bytes 110600 | tf_op jit(solution)/shard_map/ppermute | solution.py:37
  62.4 8.4 %collective-permute-start.8 = (bf16[2,16,576]{2,1,0:T(8,128)(2,1)S(1)}, bf16[2,16,576]{2,1,0:T(8,128)(2,1)S(1)}, u32[]{:S(2)}, u32[]{:S(2)}) collective-permute-start(bf16[2,16,576]{2,1,0:T(8,128)(2,1)S(1)} %get-tuple-element.22), channel_id=1, source_target_pairs={{0,16},{8,24},{16,32},{24,40},{32,48},{40,56},{48,64},{56,72},{64,... | collective-permute-start | bytes 110600 | tf_op jit(solution)/shard_map/ppermute | solution.py:37
  70.9 7.5 %collective-permute-start.9 = (bf16[4,16,576]{2,1,0:T(8,128)(2,1)S(1)}, bf16[4,16,576]{2,1,0:T(8,128)(2,1)S(1)}, u32[]{:S(2)}, u32[]{:S(2)}) collective-permute-start(bf16[4,16,576]{2,1,0:T(8,128)(2,1)S(1)} %all-to-all-done.1), channel_id=1, source_target_pairs={{0,8},{8,16},{16,24},{24,32},{32,40},{40,48},{48,56},{56,64},{64,7... | collective-permute-start | bytes 221192 | tf_op jit(solution)/shard_map/ppermute | solution.py:37
  78.4 9.1 %collective-permute-start.11 = (bf16[256,576]{1,0:T(8,128)(2,1)S(1)}, bf16[256,576]{1,0:T(8,128)(2,1)}, u32[]{:S(2)}, u32[]{:S(2)}) collective-permute-start(bf16[256,576]{1,0:T(8,128)(2,1)S(1)} %constant_dynamic-update-slice_fusion.kown), channel_id=1, source_target_pairs={{0,128},{128,256},{256,384},{1,129},{129,257},{257,385},{2,130},{1... | collective-permute-start | bytes 884744 | tf_op jit(solution)/shard_map/ppermute | solution.py:205
  79.7 12.3 %collective-permute-start.13 = (bf16[256,576]{1,0:T(8,128)(2,1)S(1)}, bf16[256,576]{1,0:T(8,128)(2,1)}, u32[]{:S(2)}, u32[]{:S(2)}) collective-permute-start(bf16[256,576]{1,0:T(8,128)(2,1)S(1)} %constant_dynamic-update-slice_fusion.kown), channel_id=1, source_target_pairs={{0,256},{128,384},{1,257},{129,385},{2,258},{130,386},{3,259},{131... | collective-permute-start | bytes 884744 | tf_op jit(solution)/shard_map/ppermute | solution.py:205
  81.0 14.9 %collective-permute-start.15 = (bf16[256,576]{1,0:T(8,128)(2,1)S(1)}, bf16[256,576]{1,0:T(8,128)(2,1)}, u32[]{:S(2)}, u32[]{:S(2)}) collective-permute-start(bf16[256,576]{1,0:T(8,128)(2,1)S(1)} %constant_dynamic-update-slice_fusion.kown), channel_id=1, source_target_pairs={{0,384},{1,385},{2,386},{3,387},{4,388},{5,389},{6,390},{7,391},{8... | collective-permute-start | bytes 884744 | tf_op jit(solution)/shard_map/ppermute | solution.py:205
  87.5 12.1 %collective-permute-start.1 = (bf16[2,16,1536]{2,1,0:T(8,128)(2,1)S(1)}, bf16[2,16,1536]{2,1,0:T(8,128)(2,1)S(1)}, u32[]{:S(2)}, u32[]{:S(2)}) collective-permute-start(bf16[2,16,1536]{2,1,0:T(8,128)(2,1)S(1)} %get-tuple-element.21), channel_id=1, source_target_pairs={{0,112},{8,120},{16,0},{24,8},{32,16},{40,24},{48,32},{56,40},{64,... | collective-permute-start | bytes 294920 | tf_op jit(solution)/shard_map/ppermute | solution.py:37
  92.0 19.5 %collective-permute-start = (bf16[4,16,1536]{2,1,0:T(8,128)(2,1)S(1)}, bf16[4,16,1536]{2,1,0:T(8,128)(2,1)S(1)}, u32[]{:S(2)}, u32[]{:S(2)}) collective-permute-start(bf16[4,16,1536]{2,1,0:T(8,128)(2,1)S(1)} %all-to-all-done), channel_id=1, source_target_pairs={{0,120},{8,0},{16,8},{24,16},{32,24},{40,32},{48,40},{56,48},{64,5... | collective-permute-start | bytes 589832 | tf_op jit(solution)/shard_map/ppermute | solution.py:37
  95.9 18.0 %collective-permute-start.3 = (bf16[4,16,1536]{2,1,0:T(8,128)(2,1)S(1)}, bf16[4,16,1536]{2,1,0:T(8,128)(2,1)S(1)}, u32[]{:S(2)}, u32[]{:S(2)}) collective-permute-start(bf16[4,16,1536]{2,1,0:T(8,128)(2,1)S(1)} %all-to-all-done), channel_id=1, source_target_pairs={{0,8},{8,16},{16,24},{24,32},{32,40},{40,48},{48,56},{56,64},{64,7... | collective-permute-start | bytes 589832 | tf_op jit(solution)/shard_map/ppermute | solution.py:37
  99.6 10.0 %collective-permute-start.2 = (bf16[2,16,1536]{2,1,0:T(8,128)(2,1)S(1)}, bf16[2,16,1536]{2,1,0:T(8,128)(2,1)S(1)}, u32[]{:S(2)}, u32[]{:S(2)}) collective-permute-start(bf16[2,16,1536]{2,1,0:T(8,128)(2,1)S(1)} %get-tuple-element.20), channel_id=1, source_target_pairs={{0,16},{8,24},{16,32},{24,40},{32,48},{40,56},{48,64},{56,72},{64,... | collective-permute-start | bytes 294920 | tf_op jit(solution)/shard_map/ppermute | solution.py:37
  109.6 11.1 %collective-permute-start.10 = (bf16[256,576]{1,0:T(8,128)(2,1)S(1)}, bf16[256,576]{1,0:T(8,128)(2,1)S(1)}, u32[]{:S(2)}, u32[]{:S(2)}) collective-permute-start(bf16[256,576]{1,0:T(8,128)(2,1)S(1)} %constant_dynamic-update-slice_fusion.kown), channel_id=1, source_target_pairs={{0,4},{4,0},{1,5},{5,1},{2,6},{6,2},{3,7},{7,3},{8,12},{12,8},{9,1... | collective-permute-start | bytes 884744 | tf_op jit(solution)/shard_map/ppermute | solution.py:41
  111.5 9.2 %collective-permute-start.12 = (bf16[256,576]{1,0:T(8,128)(2,1)}, bf16[256,576]{1,0:T(8,128)(2,1)S(1)}, u32[]{:S(2)}, u32[]{:S(2)}) collective-permute-start(bf16[256,576]{1,0:T(8,128)(2,1)} %collective-permute-done.11.k1), channel_id=1, source_target_pairs={{0,4},{4,0},{1,5},{5,1},{2,6},{6,2},{3,7},{7,3},{8,12},{12,8},{9,1... | collective-permute-start | bytes 884744 | tf_op jit(solution)/shard_map/ppermute | solution.py:41
  114.0 6.8 %collective-permute-start.14 = (bf16[256,576]{1,0:T(8,128)(2,1)}, bf16[256,576]{1,0:T(8,128)(2,1)S(1)}, u32[]{:S(2)}, u32[]{:S(2)}) collective-permute-start(bf16[256,576]{1,0:T(8,128)(2,1)} %collective-permute-done.13.k2), channel_id=1, source_target_pairs={{0,4},{4,0},{1,5},{5,1},{2,6},{6,2},{3,7},{7,3},{8,12},{12,8},{9,1... | collective-permute-start | bytes 884744 | tf_op jit(solution)/shard_map/ppermute | solution.py:41
  115.9 4.8 %collective-permute-start.16 = (bf16[256,576]{1,0:T(8,128)(2,1)}, bf16[256,576]{1,0:T(8,128)(2,1)S(1)}, u32[]{:S(2)}, u32[]{:S(2)}) collective-permute-start(bf16[256,576]{1,0:T(8,128)(2,1)} %collective-permute-done.15.k3), channel_id=1, source_target_pairs={{0,4},{4,0},{1,5},{5,1},{2,6},{6,2},{3,7},{7,3},{8,12},{12,8},{9,1... | collective-permute-start | bytes 884744 | tf_op jit(solution)/shard_map/ppermute | solution.py:41
  137.6 15.2 %copy-start.6 = (s32[1,4]{1,0:T(1,128)S(1)}, s32[1,4]{1,0:T(1,128)}, u32[]{:S(2)}) copy-start(s32[1,4]{1,0:T(1,128)} %param.19) | copy-start | bytes 52
  137.7 28.0 %collective-permute-start.19 = (bf16[4,16,3584]{2,1,0:T(8,128)(2,1)S(1)}, bf16[4,16,3584]{2,1,0:T(8,128)(2,1)S(1)}, u32[]{:S(2)}, u32[]{:S(2)}) collective-permute-start(bf16[4,16,3584]{2,1,0:T(8,128)(2,1)S(1)} %bitcast.55), channel_id=1, source_target_pairs={{0,8},{8,16},{16,24},{24,32},{32,40},{40,48},{48,56},{56,64},{64,7... | collective-permute-start | bytes 1376264 | tf_op jit(solution)/shard_map/ppermute | solution.py:37
  140.1 25.6 %collective-permute-start.20 = (bf16[4,16,3584]{2,1,0:T(8,128)(2,1)S(1)}, bf16[4,16,3584]{2,1,0:T(8,128)(2,1)S(1)}, u32[]{:S(2)}, u32[]{:S(2)}) collective-permute-start(bf16[4,16,3584]{2,1,0:T(8,128)(2,1)S(1)} %bitcast.54), channel_id=1, source_target_pairs={{0,120},{8,0},{16,8},{24,16},{32,24},{40,32},{48,40},{56,48},{64,5... | collective-permute-start | bytes 1376264 | tf_op jit(solution)/shard_map/ppermute | solution.py:37
  144.8 16.1 %collective-permute-start.21 = (bf16[2,16,3584]{2,1,0:T(8,128)(2,1)S(1)}, bf16[2,16,3584]{2,1,0:T(8,128)(2,1)S(1)}, u32[]{:S(2)}, u32[]{:S(2)}) collective-permute-start(bf16[2,16,3584]{2,1,0:T(8,128)(2,1)S(1)} %get-tuple-element.15), channel_id=1, source_target_pairs={{0,16},{8,24},{16,32},{24,40},{32,48},{40,56},{48,64},{56,72},{64,... | collective-permute-start | bytes 688136 | tf_op jit(solution)/shard_map/ppermute | solution.py:37
  147.4 18.3 %collective-permute-start.22 = (bf16[2,16,3584]{2,1,0:T(8,128)(2,1)S(1)}, bf16[2,16,3584]{2,1,0:T(8,128)(2,1)S(1)}, u32[]{:S(2)}, u32[]{:S(2)}) collective-permute-start(bf16[2,16,3584]{2,1,0:T(8,128)(2,1)S(1)} %get-tuple-element.16), channel_id=1, source_target_pairs={{0,112},{8,120},{16,0},{24,8},{32,16},{40,24},{48,32},{56,40},{64,... | collective-permute-start | bytes 688136 | tf_op jit(solution)/shard_map/ppermute | solution.py:37
  153.6 13.0 %all-to-all-start.3 = ((bf16[4,4,4,640]{3,2,1,0:T(4,128)(2,1)}), bf16[4,4,4,640]{3,2,1,0:T(4,128)(2,1)S(1)}, u32[]{:S(2)}, u32[]{:S(2)}) async-start(bf16[4,4,4,640]{3,2,1,0:T(4,128)(2,1)} %broadcast_in_dim.21), calls=%async_computation.3 | async-start | bytes 163840 | tf_op jit(solution)/shard_map/all_to_all | solution.py:46
  166.7 36.9 %all-to-all-start.2 = ((bf16[4,16,3584]{2,1,0:T(8,128)(2,1)}), bf16[4,16,3584]{2,1,0:T(8,128)(2,1)S(1)}, u32[]{:S(2)}, u32[]{:S(2)}) async-start(bf16[4,16,3584]{2,1,0:T(8,128)(2,1)} %fusion.2), calls=%async_computation.2 | async-start | bytes 917504 | tf_op jit(solution)/shard_map/all_to_all | solution.py:266
  (3 other events, 18.4 us)

commit v2 on v1

v2 whole, which is shorter than its diff:
```python
import functools

import jax
import jax.numpy as jnp
import numpy as np
from jax import lax
from jax.experimental import pallas as pl
from jax.experimental.pallas import tpu as pltpu
from jax.sharding import Mesh, PartitionSpec as P

BF = jnp.bfloat16
F32 = jnp.float32
LOG2E = 1.4426950408889634
Z = ("zh", "zl")
TP = ("zh", "zl", "core")
NEG = -1e30


def rope_tables(where_at, full_width):
    half = full_width // 2
    frequency = 10000.0 ** (-(jnp.arange(half).astype(F32) * 2.0 / full_width))
    angles = where_at.astype(F32)[:, None] * frequency[None, :]
    cosine, sine = jnp.cos(angles), jnp.sin(angles)
    return (
        jnp.concatenate([cosine, cosine], -1),
        jnp.concatenate([-sine, sine], -1),
    )


def swap_halves(v):
    half = v.shape[-1] // 2
    return jnp.concatenate([v[..., half:], v[..., :half]], -1)


def shift_z(x, step):
    n = lax.axis_size("zh") * lax.axis_size("zl")
    return lax.ppermute(x, Z, [(i, (i + step) % n) for i in range(n)])


def swap_core(x):
    return lax.ppermute(x, "core", [(0, 1), (1, 0)])


def spread(x, axis):
    n = lax.axis_size(axis)
    return lax.all_to_all(jnp.broadcast_to(x[None], (n,) + x.shape), axis, 0, 0, tiled=True)


def frequencies(width):
    half = width // 2
    f = 10000.0 ** (-(np.arange(half) * 2.0 / width))
    return jnp.asarray(np.concatenate([f, f]).astype(np.float32))[None]


def key_kernel(base_ref, x_ref, gain_ref, freq_ref, out_ref, *, lat, part, page_len):
    x = x_ref[...].astype(F32)
    n = x.shape[0]
    latent, rot = x[:, :lat], x[:, lat:]
    norm = lax.rsqrt(jnp.mean(latent * latent, -1, keepdims=True) + 1e-06)
    out_ref[:, :lat] = (latent * norm * gain_ref[...]).astype(BF)
    row = lax.broadcasted_iota(jnp.int32, rot.shape, 0)
    lane = lax.broadcasted_iota(jnp.int32, rot.shape, 1)
    where_at = base_ref[0] + row // part * page_len + row % part
    angle = where_at.astype(F32) * freq_ref[...]
    sine = jnp.sin(angle)
    sine = jnp.where(lane < rot.shape[1] // 2, -sine, sine)
    out_ref[:, lat:] = (rot * jnp.cos(angle) + swap_halves(rot) * sine).astype(BF)


def query_kernel(where_ref, g, wq0, wq1, ak0, ak1, cos_ref, sin_ref, out_ref, x_ref, *, nope, rope, qrows, nzh, nzl):
    zl = where_ref[1]
    for d in range(nzl):
        for zh in range(nzh):
            z = zh * nzl + lax.rem(zl + d, nzl)
            at = (d * nzh + zh) * qrows
            x_ref[at : at + qrows, :] = g[pl.ds(pl.multiple_of(z * qrows, qrows), qrows), :]
    x = x_ref[...]
    rows = x.shape[0]
    lat = ak0.shape[-1]
    head = 0
    for wq, ak in ((wq0, ak0), (wq1, ak1)):
        q = jnp.dot(x, wq[...], preferred_element_type=F32).astype(BF)
        for h in range(ak.shape[0]):
            base = h * (nope + rope)
            r0 = head * rows
            out_ref[r0 : r0 + rows, :lat] = jnp.dot(
                q[:, base : base + nope], ak[h], preferred_element_type=F32
            ).astype(BF)
            rot = q[:, base + nope : base + nope + rope].astype(F32)
            out_ref[r0 : r0 + rows, lat:] = (
                rot * cos_ref[...] + swap_halves(rot) * sin_ref[...]
            ).astype(BF)
            head += 1


def attend_kernel(
    where_ref, q_ref, ka_ref, kb_ref, av0, av1, op0, op1, out_ref,
    s_ref, top_ref, l_ref, acc_ref, ho_ref, *, rows, lat, scale, lay,
):
    chain, zl, core = where_ref[0], where_ref[1], where_ref[2]
    nch, nzh, nzl, part, qrows, pages = lay
    s2 = scale * LOG2E
    vh = av0.shape[-1]
    heads = q_ref.shape[0] // rows
    n = ka_ref.shape[0] // nch
    nt = (((1,), (1,)), ((), ()))

    def key_pos(idx, kcore):
        z = idx // (pages * part)
        page = (idx // part) % pages
        return page * (nzh * nzl * 2 * part) + z * (2 * part) + kcore * part + idx % part

    def query_pos(idx):
        d = idx // (nzh * qrows)
        z = (idx // qrows) % nzh * nzl + (zl + d) % nzl
        return z * (2 * qrows) + core * qrows + idx % qrows

    def lanes(x, op):
        out = x[:, :128]
        for c in range(128, x.shape[1], 128):
            out = op(out, x[:, c : c + 128])
        return out

    def score(back):
        if back == 0:
            qp = query_pos(lax.broadcasted_iota(jnp.int32, (rows, 1), 0))
            kidx = lax.broadcasted_iota(jnp.int32, (1, n), 1)
            ok = (key_pos(kidx, core) <= qp, key_pos(kidx, 1 - core) <= qp)
        for h in range(heads):
            q = q_ref[h * rows : (h + 1) * rows, :]
            for i, k_ref in enumerate((ka_ref, kb_ref)):
                s = lax.dot_general(q, k_ref[back * n : (back + 1) * n, :], nt, preferred_element_type=F32)
                if back == 0:
                    s = jnp.where(ok[i], s, NEG)
                at = (2 * back + i) * n
                s_ref[h, :, at : at + n] = s
                top = lanes(s, jnp.maximum)
                if back or i:
                    top = jnp.maximum(top, top_ref[h])
                top_ref[h] = top

    def mix(back):
        for h in range(heads):
            m = top_ref[h][:, :1]
            pv = None
            for i, k_ref in enumerate((ka_ref, kb_ref)):
                at = (2 * back + i) * n
                p = jnp.exp2(s_ref[h, :, at : at + n] * s2 - m)
                total = lanes(p, jnp.add)
                if back or i:
                    total += l_ref[h]
                l_ref[h] = total
                part_pv = jnp.dot(
                    p.astype(BF), k_ref[back * n : (back + 1) * n, :lat], preferred_element_type=F32
                )
                pv = part_pv if pv is None else pv + part_pv
            acc_ref[h] = acc_ref[h] + pv if back else pv

    score(0)
    for back in range(1, nch):
        pl.when(chain >= back)(functools.partial(score, back))
    for h in range(heads):
        m = jnp.max(top_ref[h], -1, keepdims=True) * s2
        top_ref[h] = jnp.broadcast_to(m, top_ref.shape[1:])
    mix(0)
    for back in range(1, nch):
        pl.when(chain >= back)(functools.partial(mix, back))
    per = heads // 2
    for h in range(heads):
        total = jnp.sum(l_ref[h], -1, keepdims=True)
        mixed = (acc_ref[h] / total).astype(BF)
        av = (av0 if h < per else av1)[h % per]
        ho_ref[:, h * vh : (h + 1) * vh] = jnp.dot(mixed, av, preferred_element_type=F32).astype(BF)
    ho = ho_ref[...]
    k = op0.shape[0]
    width = out_ref.shape[1]
    cut = 512 if width % 512 == 0 else width
    for c in range(0, width, cut):
        out_ref[:, c : c + cut] = (
            jnp.dot(ho[:, :k], op0[:, c : c + cut], preferred_element_type=F32)
            + jnp.dot(ho[:, k:], op1[:, c : c + cut], preferred_element_type=F32)
        ).astype(BF)


def local(
    query_comp, latent_rows, rope_keys, latent_gain, query_up, absorb_key, absorb_value, out_proj,
    page_owner, page_slot,
):
    nzh, nzl, nch = lax.axis_size("zh"), lax.axis_size("zl"), lax.axis_size("chain")
    zh, zl, core = lax.axis_index("zh"), lax.axis_index("zl"), lax.axis_index("core")
    chain, dec = lax.axis_index("chain"), lax.axis_index("dec")
    pages, part, lat = latent_rows.shape[1:]
    rope = rope_keys.shape[3]
    heads_here, nope = absorb_key.shape[:2]
    vh = absorb_value.shape[2]
    qrows, ql = query_comp.shape[1:]
    width = out_proj.shape[1]
    tp_index = (zh * nzl + zl) * 2 + core
    tp_count = nzh * nzl * 2
    block_len = qrows * tp_count
    slots = 2 * pages
    smem = pl.BlockSpec(memory_space=pltpu.SMEM)
    vm = pl.BlockSpec(memory_space=pltpu.VMEM)
    big = pltpu.CompilerParams(vmem_limit_bytes=40 * 1024 * 1024)

    raw = jnp.concatenate(
        [latent_rows[0].reshape(pages * part, lat), rope_keys[0].reshape(pages * part, rope)], -1
    )
    keys = pl.pallas_call(
        functools.partial(key_kernel, lat=lat, part=part, page_len=part * tp_count),
        out_shape=jax.ShapeDtypeStruct(raw.shape, BF),
        in_specs=[smem, vm, vm, vm],
        out_specs=vm,
        compiler_params=big,
        name="keys",
    )((chain * block_len + tp_index * part).astype(jnp.int32)[None], raw, latent_gain[None], frequencies(rope))

    own = lax.all_gather(keys, Z, axis=0, tiled=True)
    qg = lax.all_gather(query_comp[0], Z, axis=0, tiled=True)
    backs = [
        lax.ppermute(own, "chain", [(i, i + k) for i in range(nch - k)]) for k in range(1, nch)
    ]
    mine = jnp.concatenate([own] + backs, 0)
    other = swap_core(mine)

    wq1 = swap_core(query_up)
    ak1 = swap_core(absorb_key)
    av1 = swap_core(absorb_value)
    op1 = swap_core(out_proj)

    rows = qrows * nzh * nzl
    idx = jnp.arange(rows, dtype=jnp.int32)
    zq = (idx // qrows) % nzh * nzl + (zl + idx // (nzh * qrows)) % nzl
    query_where = chain * block_len + zq * (2 * qrows) + core * qrows + idx % qrows
    qcos, qsin = rope_tables(query_where, rope)
    heads = 2 * heads_here
    where = jnp.stack([chain, zl, core]).astype(jnp.int32)
    q = pl.pallas_call(
        functools.partial(query_kernel, nope=nope, rope=rope, qrows=qrows, nzh=nzh, nzl=nzl),
        out_shape=jax.ShapeDtypeStruct((heads * rows, lat + rope), BF),
        in_specs=[smem] + [vm] * 7,
        out_specs=vm,
        scratch_shapes=[pltpu.VMEM((rows, ql), BF)],
        compiler_params=big,
        cost_estimate=pl.CostEstimate(
            flops=2 * rows * heads * (nope + rope) * ql + 2 * rows * heads * nope * lat,
            bytes_accessed=6000000, transcendentals=0,
        ),
        name="queries",
    )(where, qg, query_up, wq1, absorb_key, ak1, qcos, qsin)

    partial = pl.pallas_call(
        functools.partial(
            attend_kernel, rows=rows, lat=lat, scale=(nope + rope) ** -0.5,
            lay=(nch, nzh, nzl, part, qrows, pages),
        ),
        out_shape=jax.ShapeDtypeStruct((rows, width), BF),
        in_specs=[smem] + [vm] * 7,
        out_specs=vm,
        scratch_shapes=[
            pltpu.VMEM((heads, rows, nch * block_len), F32),
            pltpu.VMEM((heads, rows, 128), F32),
            pltpu.VMEM((heads, rows, 128), F32),
            pltpu.VMEM((heads, rows, lat), F32),
            pltpu.VMEM((rows, heads * vh), BF),
        ],
        compiler_params=big,
        cost_estimate=pl.CostEstimate(
            flops=4 * rows * heads * nch * block_len * lat, bytes_accessed=9000000,
            transcendentals=rows * heads * nch * block_len,
        ),
        name="attend",
    )(where, q, mine, other, absorb_value, av1, out_proj, op1)

    sums = partial.reshape(nzl, nzh, qrows, width)
    half = nzh // 2
    up2 = shift_z(sums[2, :half], 2)
    down2 = shift_z(sums[2, half:], -2)
    up = shift_z(sums[1], 1)
    down = shift_z(sums[3], -1)
    near = (
        sums[0].astype(F32) + up.astype(F32) + down.astype(F32)
        + jnp.concatenate([up2, down2], 0).astype(F32)
    ).astype(BF)
    cut = width // 2

    def chunk(steps):
        return lax.dynamic_index_in_dim(near, lax.rem(zh + steps, nzh), 0, keepdims=False)

    far = chunk(2)
    around = shift_z(far[:, cut:], -nzl)
    direct = shift_z(far[:, :cut], 2 * nzl)
    ahead = shift_z(chunk(1), nzl)
    behind = chunk(3).astype(F32)
    behind = jnp.concatenate([behind[:, :cut], behind[:, cut:] + around.astype(F32)], -1).astype(BF)
    behind = shift_z(behind, -nzl)
    total = chunk(0).astype(F32) + ahead.astype(F32) + behind.astype(F32)
    total = jnp.concatenate([total[:, :cut] + direct.astype(F32), total[:, cut:]], -1)
    layer_output = total.astype(BF)[None]

    code = (page_owner[0] * slots + page_slot[0]).astype(BF)
    tail = jnp.broadcast_to(code[:, None, None], (pages, part, 128 - rope))
    page = jnp.concatenate([keys.reshape(pages, part, lat + rope), tail], -1)
    page = spread(page, "dec")
    came = page[:, :, 0, lat + rope].reshape(-1).astype(jnp.int32)
    take = (came[None, :] == dec * slots + jnp.arange(slots, dtype=jnp.int32)[:, None]).astype(BF)
    placed = jnp.einsum(
        "sp,pjc->sjc", take, page.reshape(-1, part, page.shape[-1]), preferred_element_type=F32
    ).astype(BF)
    cache_latent = placed[..., :lat][None, None]
    cache_rope = placed[..., lat : lat + rope][None, None]
    return (layer_output, cache_latent, cache_rope)


def solution(mesh):
    shape = mesh.shape
    chips = shape["tp"] // 2
    nzl = 4
    fine = Mesh(
        np.asarray(mesh.devices).reshape(shape["chain"], chips // nzl, nzl, 2, shape["dec"]),
        ("chain", "zh", "zl", "core", "dec"),
    )
    row = ("chain",) + TP
    return jax.shard_map(
        local,
        mesh=fine,
        in_specs=(
            P("dec", row, None),
            P("dec", "chain", TP, None),
            P("dec", "chain", TP, None),
            P(),
            P(None, TP),
            P(TP, None, None),
            P(TP, None, None),
            P(TP, None),
            P("dec", "chain"),
            P("dec", "chain"),
        ),
        out_specs=(
            P("dec", row, None),
            P("dec", "chain", None, TP, None),
            P("dec", "chain", None, TP, None),
        ),
        check_vma=False,
    )
```

time: 206 us -> 175 us (0.85)
  the two profiles are of different devices: /device:TPU:24 before, /device:TPU:122 now
where the time goes in v2:
time: 175 us; the launch traced here: 174 us
  blocking collectives  65.2 us (37%)
  starting transfers between devices  56.6 us (32%)
  waiting for transfers between devices  18.5 us (11%)
  Pallas kernels  14.3 us (8%)
  local copies, waits for them, and re-layouts  11.5 us (7%)
  other arithmetic  6.22 us (4%)
    ppermute x8, starting transfers between devices, shift_z(): return lax.ppermute(x, Z, [(i, (i + step) % n) for i in range(n)])  37.2 us
    all_gather x1, blocking collectives, local(): qg = lax.all_gather(query_comp[0], Z, axis=0, tiled=True)  33 us
    all_gather x1, blocking collectives, local(): own = lax.all_gather(keys, Z, axis=0, tiled=True)  32.2 us
    ppermute x8, waiting for transfers between devices, shift_z(): return lax.ppermute(x, Z, [(i, (i + step) % n) for i in range(n)])  18.5 us
    pallas_call x1, Pallas kernels, local(): pl.pallas_call(functools.partial(attend_kernel, rows=rows, lat=lat, scale...  11.3 us
    ppermute x5, starting transfers between devices, swap_core(): return lax.ppermute(x, 'core', [(0, 1), (1, 0)])  10.7 us
    unnamed x19, local copies, waits for them, and re-layouts  6.56 us
    all_to_all x1, starting transfers between devices, spread(): lax.all_to_all(jnp.broadcast_to(x[None], (n,) + x.shape), axis, 0, 0, til...  4.82 us
  transfers between devices with their start and end apart: 17, of which 5 were waited for; matrix products, arithmetic and copies ran while one was open for 6% of the time, Pallas kernels for 8%

profile of v2, /device:TPU:122, one launch (start us, length us, event | category | flops | bytes accessed | tf_op | source)
XLA Modules:
  0.0 174.4 jit_solution(11344347877784130674)
XLA Ops:
  3.5 32.2 %all_gather.7 = bf16[256,576]{1,0:T(8,128)(2,1)S(1)} all-gather(bf16[16,576]{1,0:T(8,128)(2,1)S(1)} %keys.1), channel_id=1, replica_groups=mesh['chain'=4,'zh'=4,'zl'=4,'core'=2,'dec'=4] {'zh','zl'}, dimensions={0}, use_global_device_ids=true | all-gather | bytes 313344 | tf_op jit(solution)/shard_map/all_gather | solution.py:218
  35.7 1.3 collective-permute-start.2
  37.0 1.3 collective-permute-start.3
  38.3 1.3 collective-permute-start.4
  39.6 1.9 %collective-permute-start = (bf16[1536,384]{1,0:T(8,128)(2,1)}, bf16[1536,384]{1,0:T(8,128)(2,1)}, u32[]{:S(2)}, u32[]{:S(2)}) collective-permute-start(bf16[1536,384]{1,0:T(8,128)(2,1)} %wq0.1), channel_id=1, source_target_pairs={{0,4},{4,0},{1,5},{5,1},{2,6},{6,2},{3,7},{7,3},{8,12},{12,8},{9,1... | collective-permute-start | bytes 3538952 | tf_op jit(solution)/shard_map/ppermute | solution.py:41
  41.5 2.4 %collective-permute-start.7 = (bf16[256,3584]{1,0:T(8,128)(2,1)}, bf16[256,3584]{1,0:T(8,128)(2,1)}, u32[]{:S(2)}, u32[]{:S(2)}) collective-permute-start(bf16[256,3584]{1,0:T(8,128)(2,1)} %op0.1), channel_id=1, source_target_pairs={{0,4},{4,0},{1,5},{5,1},{2,6},{6,2},{3,7},{7,3},{8,12},{12,8},{9,1... | collective-permute-start | bytes 5505032 | tf_op jit(solution)/shard_map/ppermute | solution.py:41
  45.4 4.8 %all-to-all-start = ((bf16[4,4,4,640]{3,2,1,0:T(4,128)(2,1)}), bf16[4,4,4,640]{3,2,1,0:T(4,128)(2,1)}, u32[]{:S(2)}, u32[]{:S(2)}) async-start(bf16[4,4,4,640]{3,2,1,0:T(4,128)(2,1)} %broadcast_in_dim.36), calls=%async_computation | async-start | bytes 163840 | tf_op jit(solution)/shard_map/all_to_all | solution.py:46
  50.3 1.9 %collective-permute-start.1 = (bf16[2,128,512]{2,1,0:T(8,128)(2,1)S(1)}, bf16[2,128,512]{2,1,0:T(8,128)(2,1)}, u32[]{:S(2)}, u32[]{:S(2)}) collective-permute-start(bf16[2,128,512]{2,1,0:T(8,128)(2,1)S(1)} %copy-done.3), channel_id=1, source_target_pairs={{0,4},{4,0},{1,5},{5,1},{2,6},{6,2},{3,7},{7,3},{8,12},{12,8},{9,1... | collective-permute-start | bytes 786440 | tf_op jit(solution)/shard_map/ppermute | solution.py:41
  52.3 2.4 %collective-permute-start.6 = (bf16[2,512,128]{2,1,0:T(8,128)(2,1)}, bf16[2,512,128]{2,1,0:T(8,128)(2,1)}, u32[]{:S(2)}, u32[]{:S(2)}) collective-permute-start(bf16[2,512,128]{2,1,0:T(8,128)(2,1)} %av0.1), channel_id=1, source_target_pairs={{0,4},{4,0},{1,5},{5,1},{2,6},{6,2},{3,7},{7,3},{8,12},{12,8},{9,1... | collective-permute-start | bytes 786440 | tf_op jit(solution)/shard_map/ppermute | solution.py:41
  54.8 1.5 copy.29
  56.3 2.0 %collective-permute-start.5 = (bf16[1024,576]{0,1:T(8,128)(2,1)}, bf16[1024,576]{0,1:T(8,128)(2,1)}, u32[]{:S(2)}, u32[]{:S(2)}) collective-permute-start(bf16[1024,576]{0,1:T(8,128)(2,1)} %copy.29), channel_id=1, source_target_pairs={{0,4},{4,0},{1,5},{5,1},{2,6},{6,2},{3,7},{7,3},{8,12},{12,8},{9,1... | collective-permute-start | bytes 3538952 | tf_op jit(solution)/shard_map/ppermute | solution.py:41
  58.4 1.3 fusion.8
  59.7 33.0 %all-gather = bf16[1,256,1536]{2,1,0:T(8,128)(2,1)S(1)} all-gather(bf16[1,16,1536]{2,1,0:T(8,128)(2,1)} %param.11), channel_id=2, replica_groups=mesh['chain'=4,'zh'=4,'zl'=4,'core'=2,'dec'=4] {'zh','zl'}, dimensions={1}, use_global_device_ids=true | all-gather | bytes 835584 | tf_op jit(solution)/shard_map/all_gather | solution.py:219
  92.8 1.2 pad_maximum_fusion
  94.1 2.8 %queries.1.q_ref = bf16[1024,576]{1,0:T(8,128)(2,1)S(1)} custom-call(s32[3]{0:T(128)S(1)} %pad_add_fusion.where_ref, bf16[256,1536]{1,0:T(8,128)(2,1)S(1)} %bitcast.39, bf16[1536,384]{1,0:T(8,128)(2,1)S(1)} %copy-done.2, bf16[1536,384]{1,0:T(8,128)(2,1)} %collective-permute-done.wq1, bf16[2,128,512]{2,1,0:T(8,128)(2,1)S(1)} %copy-done.3, ...), custom_call_target="tpu_custom_call" | custom-call | flops 738197504 | bytes 6000000 | tf_op jit(solution)/shard_map/queries/pallas_call | solution.py:238
  98.0 1.7 copy.30.kb_ref
  99.7 1.3 copy-done.1
  101.0 1.5 copy-done.6
  102.5 11.3 %attend.1 = bf16[256,3584]{1,0:T(8,128)(2,1)S(1)} custom-call(s32[3]{0:T(128)S(1)} %pad_add_fusion.where_ref, bf16[1024,576]{1,0:T(8,128)(2,1)S(1)} %copy-done.1, bf16[1024,576]{1,0:T(8,128)(2,1)S(1)} %constant_dynamic-update-slice_fusion.ka_ref, bf16[1024,576]{1,0:T(8,128)(2,1)S(1)} %copy.30.kb_ref, bf16[2,512,128]{2,1,0:T(8,128)(2,1)} %av0.1, ...), custom_call_target="tpu_custom_call" | custom-call | flops 4294967296 | bytes 9000000 | tf_op jit(solution)/shard_map/attend/pallas_call | solution.py:252
  113.9 3.0 %collective-permute-start.8 = (bf16[4,16,3584]{2,1,0:T(8,128)(2,1)S(1)}, bf16[4,16,3584]{2,1,0:T(8,128)(2,1)S(1)}, u32[]{:S(2)}, u32[]{:S(2)}) collective-permute-start(bf16[4,16,3584]{2,1,0:T(8,128)(2,1)S(1)} %bitcast.44), channel_id=1, source_target_pairs={{0,8},{8,16},{16,24},{24,32},{32,40},{40,48},{48,56},{56,64},{64,7... | collective-permute-start | bytes 1376264 | tf_op jit(solution)/shard_map/ppermute | solution.py:37
  117.0 2.8 %collective-permute-start.9 = (bf16[4,16,3584]{2,1,0:T(8,128)(2,1)S(1)}, bf16[4,16,3584]{2,1,0:T(8,128)(2,1)S(1)}, u32[]{:S(2)}, u32[]{:S(2)}) collective-permute-start(bf16[4,16,3584]{2,1,0:T(8,128)(2,1)S(1)} %bitcast.43), channel_id=1, source_target_pairs={{0,120},{8,0},{16,8},{24,16},{32,24},{40,32},{48,40},{56,48},{64,5... | collective-permute-start | bytes 1376264 | tf_op jit(solution)/shard_map/ppermute | solution.py:37
  119.8 3.4 %collective-permute-start.10 = (bf16[2,16,3584]{2,1,0:T(8,128)(2,1)S(1)}, bf16[2,16,3584]{2,1,0:T(8,128)(2,1)S(1)}, u32[]{:S(2)}, u32[]{:S(2)}) collective-permute-start(bf16[2,16,3584]{2,1,0:T(8,128)(2,1)S(1)} %get-tuple-element.15), channel_id=1, source_target_pairs={{0,16},{8,24},{16,32},{24,40},{32,48},{40,56},{48,64},{56,72},{64,... | collective-permute-start | bytes 688136 | tf_op jit(solution)/shard_map/ppermute | solution.py:37
  123.2 3.4 %collective-permute-start.11 = (bf16[2,16,3584]{2,1,0:T(8,128)(2,1)S(1)}, bf16[2,16,3584]{2,1,0:T(8,128)(2,1)S(1)}, u32[]{:S(2)}, u32[]{:S(2)}) collective-permute-start(bf16[2,16,3584]{2,1,0:T(8,128)(2,1)S(1)} %get-tuple-element.16), channel_id=1, source_target_pairs={{0,112},{8,120},{16,0},{24,8},{32,16},{40,24},{48,32},{56,40},{64,... | collective-permute-start | bytes 688136 | tf_op jit(solution)/shard_map/ppermute | solution.py:37
  126.6 1.2 fusion.9
  129.0 3.7 %collective-permute-done.10 = bf16[2,16,3584]{2,1,0:T(8,128)(2,1)S(1)} collective-permute-done((bf16[2,16,3584]{2,1,0:T(8,128)(2,1)S(1)}, bf16[2,16,3584]{2,1,0:T(8,128)(2,1)S(1)}, u32[]{:S(2)}, u32[]{:S(2)}) %collective-permute-start.10) | collective-permute-done | bytes 229408 | tf_op jit(solution)/shard_map/ppermute | solution.py:37
  132.7 2.9 %collective-permute-done.11 = bf16[2,16,3584]{2,1,0:T(8,128)(2,1)S(1)} collective-permute-done((bf16[2,16,3584]{2,1,0:T(8,128)(2,1)S(1)}, bf16[2,16,3584]{2,1,0:T(8,128)(2,1)S(1)}, u32[]{:S(2)}, u32[]{:S(2)}) %collective-permute-start.11) | collective-permute-done | bytes 229408 | tf_op jit(solution)/shard_map/ppermute | solution.py:37
  135.9 9.2 %collective-permute-start.13 = (bf16[16,1792]{1,0:T(8,128)(2,1)S(1)}, bf16[16,1792]{1,0:T(8,128)(2,1)S(1)}, u32[]{:S(2)}, u32[]{:S(2)}) collective-permute-start(bf16[16,1792]{1,0:T(8,128)(2,1)S(1)} %get-tuple-element.24), channel_id=1, source_target_pairs={{0,96},{8,104},{16,112},{24,120},{32,0},{40,8},{48,16},{56,24},{64... | collective-permute-start | bytes 172040 | tf_op jit(solution)/shard_map/ppermute | solution.py:37
  145.8 1.9 %collective-permute-start.12 = (bf16[16,3584]{1,0:T(8,128)(2,1)S(1)}, bf16[16,3584]{1,0:T(8,128)(2,1)S(1)}, u32[]{:S(2)}, u32[]{:S(2)}) collective-permute-start(bf16[16,3584]{1,0:T(8,128)(2,1)S(1)} %get-tuple-element.20), channel_id=1, source_target_pairs={{0,32},{8,40},{16,48},{24,56},{32,64},{40,72},{48,80},{56,88},{64,... | collective-permute-start | bytes 344072 | tf_op jit(solution)/shard_map/ppermute | solution.py:37
  147.7 2.0 %collective-permute-done.13 = bf16[16,1792]{1,0:T(8,128)(2,1)S(1)} collective-permute-done((bf16[16,1792]{1,0:T(8,128)(2,1)S(1)}, bf16[16,1792]{1,0:T(8,128)(2,1)S(1)}, u32[]{:S(2)}, u32[]{:S(2)}) %collective-permute-start.13) | collective-permute-done | bytes 57376 | tf_op jit(solution)/shard_map/ppermute | solution.py:37
  149.7 8.4 %collective-permute-start.14 = (bf16[16,3584]{1,0:T(8,128)(2,1)S(1)}, bf16[16,3584]{1,0:T(8,128)(2,1)S(1)}, u32[]{:S(2)}, u32[]{:S(2)}) collective-permute-start(bf16[16,3584]{1,0:T(8,128)(2,1)S(1)} %pad_maximum_fusion.2), channel_id=1, source_target_pairs={{0,96},{8,104},{16,112},{24,120},{32,0},{40,8},{48,16},{56,24},{64... | collective-permute-start | bytes 344072 | tf_op jit(solution)/shard_map/ppermute | solution.py:37
  158.8 5.1 %collective-permute-start.15 = (bf16[16,1792]{1,0:T(8,128)(2,1)S(1)}, bf16[16,1792]{1,0:T(8,128)(2,1)S(1)}, u32[]{:S(2)}, u32[]{:S(2)}) collective-permute-start(bf16[16,1792]{1,0:T(8,128)(2,1)S(1)} %get-tuple-element.23), channel_id=1, source_target_pairs={{0,64},{8,72},{16,80},{24,88},{32,96},{40,104},{48,112},{56,120},{... | collective-permute-start | bytes 172040 | tf_op jit(solution)/shard_map/ppermute | solution.py:37
  164.5 9.3 %collective-permute-done.15 = bf16[16,1792]{1,0:T(8,128)(2,1)S(1)} collective-permute-done((bf16[16,1792]{1,0:T(8,128)(2,1)S(1)}, bf16[16,1792]{1,0:T(8,128)(2,1)S(1)}, u32[]{:S(2)}, u32[]{:S(2)}) %collective-permute-start.15) | collective-permute-done | bytes 57376 | tf_op jit(solution)/shard_map/ppermute | solution.py:37
  (59 shorter events, 9.9 us)
Async XLA Ops:
  0.6 49.7 %copy-start.3 = (bf16[2,128,512]{2,1,0:T(8,128)(2,1)S(1)}, bf16[2,128,512]{2,1,0:T(8,128)(2,1)}, u32[]{:S(2)}) copy-start(bf16[2,128,512]{2,1,0:T(8,128)(2,1)} %ak0.1) | copy-start | bytes 786436
  2.1 0.7 copy-start.4
  2.8 0.7 copy-start.5
  35.7 14.6 %collective-permute-start.2 = (bf16[256,576]{1,0:T(8,128)(2,1)S(1)}, bf16[256,576]{1,0:T(8,128)(2,1)S(1)}, u32[]{:S(2)}, u32[]{:S(2)}) collective-permute-start(bf16[256,576]{1,0:T(8,128)(2,1)S(1)} %all_gather.7), channel_id=1, source_target_pairs={{0,128},{128,256},{256,384},{1,129},{129,257},{257,385},{2,130},{1... | collective-permute-start | bytes 884744 | tf_op jit(solution)/shard_map/ppermute | solution.py:221
  37.0 15.3 %collective-permute-start.3 = (bf16[256,576]{1,0:T(8,128)(2,1)S(1)}, bf16[256,576]{1,0:T(8,128)(2,1)S(1)}, u32[]{:S(2)}, u32[]{:S(2)}) collective-permute-start(bf16[256,576]{1,0:T(8,128)(2,1)S(1)} %all_gather.7), channel_id=1, source_target_pairs={{0,256},{128,384},{1,257},{129,385},{2,258},{130,386},{3,259},{131... | collective-permute-start | bytes 884744 | tf_op jit(solution)/shard_map/ppermute | solution.py:221
  38.3 16.5 %collective-permute-start.4 = (bf16[256,576]{1,0:T(8,128)(2,1)S(1)}, bf16[256,576]{1,0:T(8,128)(2,1)S(1)}, u32[]{:S(2)}, u32[]{:S(2)}) collective-permute-start(bf16[256,576]{1,0:T(8,128)(2,1)S(1)} %all_gather.7), channel_id=1, source_target_pairs={{0,384},{1,385},{2,386},{3,387},{4,388},{5,389},{6,390},{7,391},{8... | collective-permute-start | bytes 884744 | tf_op jit(solution)/shard_map/ppermute | solution.py:221
  39.6 54.4 %collective-permute-start = (bf16[1536,384]{1,0:T(8,128)(2,1)}, bf16[1536,384]{1,0:T(8,128)(2,1)}, u32[]{:S(2)}, u32[]{:S(2)}) collective-permute-start(bf16[1536,384]{1,0:T(8,128)(2,1)} %wq0.1), channel_id=1, source_target_pairs={{0,4},{4,0},{1,5},{5,1},{2,6},{6,2},{3,7},{7,3},{8,12},{12,8},{9,1... | collective-permute-start | bytes 3538952 | tf_op jit(solution)/shard_map/ppermute | solution.py:41
  41.5 58.1 %collective-permute-start.7 = (bf16[256,3584]{1,0:T(8,128)(2,1)}, bf16[256,3584]{1,0:T(8,128)(2,1)}, u32[]{:S(2)}, u32[]{:S(2)}) collective-permute-start(bf16[256,3584]{1,0:T(8,128)(2,1)} %op0.1), channel_id=1, source_target_pairs={{0,4},{4,0},{1,5},{5,1},{2,6},{6,2},{3,7},{7,3},{8,12},{12,8},{9,1... | collective-permute-start | bytes 5505032 | tf_op jit(solution)/shard_map/ppermute | solution.py:41
  45.4 81.2 %all-to-all-start = ((bf16[4,4,4,640]{3,2,1,0:T(4,128)(2,1)}), bf16[4,4,4,640]{3,2,1,0:T(4,128)(2,1)}, u32[]{:S(2)}, u32[]{:S(2)}) async-start(bf16[4,4,4,640]{3,2,1,0:T(4,128)(2,1)} %broadcast_in_dim.36), calls=%async_computation | async-start | bytes 163840 | tf_op jit(solution)/shard_map/all_to_all | solution.py:46
  50.3 43.7 %collective-permute-start.1 = (bf16[2,128,512]{2,1,0:T(8,128)(2,1)S(1)}, bf16[2,128,512]{2,1,0:T(8,128)(2,1)}, u32[]{:S(2)}, u32[]{:S(2)}) collective-permute-start(bf16[2,128,512]{2,1,0:T(8,128)(2,1)S(1)} %copy-done.3), channel_id=1, source_target_pairs={{0,4},{4,0},{1,5},{5,1},{2,6},{6,2},{3,7},{7,3},{8,12},{12,8},{9,1... | collective-permute-start | bytes 786440 | tf_op jit(solution)/shard_map/ppermute | solution.py:41
  52.3 47.3 %collective-permute-start.6 = (bf16[2,512,128]{2,1,0:T(8,128)(2,1)}, bf16[2,512,128]{2,1,0:T(8,128)(2,1)}, u32[]{:S(2)}, u32[]{:S(2)}) collective-permute-start(bf16[2,512,128]{2,1,0:T(8,128)(2,1)} %av0.1), channel_id=1, source_target_pairs={{0,4},{4,0},{1,5},{5,1},{2,6},{6,2},{3,7},{7,3},{8,12},{12,8},{9,1... | collective-permute-start | bytes 786440 | tf_op jit(solution)/shard_map/ppermute | solution.py:41
  56.3 37.8 %copy-start.2 = (bf16[1536,384]{1,0:T(8,128)(2,1)S(1)}, bf16[1536,384]{1,0:T(8,128)(2,1)}, u32[]{:S(2)}) copy-start(bf16[1536,384]{1,0:T(8,128)(2,1)} %wq0.1) | copy-start | bytes 3538948
  56.3 41.7 %collective-permute-start.5 = (bf16[1024,576]{0,1:T(8,128)(2,1)}, bf16[1024,576]{0,1:T(8,128)(2,1)}, u32[]{:S(2)}, u32[]{:S(2)}) collective-permute-start(bf16[1024,576]{0,1:T(8,128)(2,1)} %copy.29), channel_id=1, source_target_pairs={{0,4},{4,0},{1,5},{5,1},{2,6},{6,2},{3,7},{7,3},{8,12},{12,8},{9,1... | collective-permute-start | bytes 3538952 | tf_op jit(solution)/shard_map/ppermute | solution.py:41
  96.9 1.1 copy-start
  99.7 1.3 copy-start.1
  101.0 1.5 copy-start.6
  113.9 21.7 %collective-permute-start.8 = (bf16[4,16,3584]{2,1,0:T(8,128)(2,1)S(1)}, bf16[4,16,3584]{2,1,0:T(8,128)(2,1)S(1)}, u32[]{:S(2)}, u32[]{:S(2)}) collective-permute-start(bf16[4,16,3584]{2,1,0:T(8,128)(2,1)S(1)} %bitcast.44), channel_id=1, source_target_pairs={{0,8},{8,16},{16,24},{24,32},{32,40},{40,48},{48,56},{56,64},{64,7... | collective-permute-start | bytes 1376264 | tf_op jit(solution)/shard_map/ppermute | solution.py:37
  117.0 18.7 %collective-permute-start.9 = (bf16[4,16,3584]{2,1,0:T(8,128)(2,1)S(1)}, bf16[4,16,3584]{2,1,0:T(8,128)(2,1)S(1)}, u32[]{:S(2)}, u32[]{:S(2)}) collective-permute-start(bf16[4,16,3584]{2,1,0:T(8,128)(2,1)S(1)} %bitcast.43), channel_id=1, source_target_pairs={{0,120},{8,0},{16,8},{24,16},{32,24},{40,32},{48,40},{56,48},{64,5... | collective-permute-start | bytes 1376264 | tf_op jit(solution)/shard_map/ppermute | solution.py:37
  119.8 12.9 %collective-permute-start.10 = (bf16[2,16,3584]{2,1,0:T(8,128)(2,1)S(1)}, bf16[2,16,3584]{2,1,0:T(8,128)(2,1)S(1)}, u32[]{:S(2)}, u32[]{:S(2)}) collective-permute-start(bf16[2,16,3584]{2,1,0:T(8,128)(2,1)S(1)} %get-tuple-element.15), channel_id=1, source_target_pairs={{0,16},{8,24},{16,32},{24,40},{32,48},{40,56},{48,64},{56,72},{64,... | collective-permute-start | bytes 688136 | tf_op jit(solution)/shard_map/ppermute | solution.py:37
  123.2 12.4 %collective-permute-start.11 = (bf16[2,16,3584]{2,1,0:T(8,128)(2,1)S(1)}, bf16[2,16,3584]{2,1,0:T(8,128)(2,1)S(1)}, u32[]{:S(2)}, u32[]{:S(2)}) collective-permute-start(bf16[2,16,3584]{2,1,0:T(8,128)(2,1)S(1)} %get-tuple-element.16), channel_id=1, source_target_pairs={{0,112},{8,120},{16,0},{24,8},{32,16},{40,24},{48,32},{56,40},{64,... | collective-permute-start | bytes 688136 | tf_op jit(solution)/shard_map/ppermute | solution.py:37
  135.9 13.8 %collective-permute-start.13 = (bf16[16,1792]{1,0:T(8,128)(2,1)S(1)}, bf16[16,1792]{1,0:T(8,128)(2,1)S(1)}, u32[]{:S(2)}, u32[]{:S(2)}) collective-permute-start(bf16[16,1792]{1,0:T(8,128)(2,1)S(1)} %get-tuple-element.24), channel_id=1, source_target_pairs={{0,96},{8,104},{16,112},{24,120},{32,0},{40,8},{48,16},{56,24},{64... | collective-permute-start | bytes 172040 | tf_op jit(solution)/shard_map/ppermute | solution.py:37
  145.8 18.1 %collective-permute-start.12 = (bf16[16,3584]{1,0:T(8,128)(2,1)S(1)}, bf16[16,3584]{1,0:T(8,128)(2,1)S(1)}, u32[]{:S(2)}, u32[]{:S(2)}) collective-permute-start(bf16[16,3584]{1,0:T(8,128)(2,1)S(1)} %get-tuple-element.20), channel_id=1, source_target_pairs={{0,32},{8,40},{16,48},{24,56},{32,64},{40,72},{48,80},{56,88},{64,... | collective-permute-start | bytes 344072 | tf_op jit(solution)/shard_map/ppermute | solution.py:37
  149.7 14.7 %collective-permute-start.14 = (bf16[16,3584]{1,0:T(8,128)(2,1)S(1)}, bf16[16,3584]{1,0:T(8,128)(2,1)S(1)}, u32[]{:S(2)}, u32[]{:S(2)}) collective-permute-start(bf16[16,3584]{1,0:T(8,128)(2,1)S(1)} %pad_maximum_fusion.2), channel_id=1, source_target_pairs={{0,96},{8,104},{16,112},{24,120},{32,0},{40,8},{48,16},{56,24},{64... | collective-permute-start | bytes 344072 | tf_op jit(solution)/shard_map/ppermute | solution.py:37
  158.8 15.0 %collective-permute-start.15 = (bf16[16,1792]{1,0:T(8,128)(2,1)S(1)}, bf16[16,1792]{1,0:T(8,128)(2,1)S(1)}, u32[]{:S(2)}, u32[]{:S(2)}) collective-permute-start(bf16[16,1792]{1,0:T(8,128)(2,1)S(1)} %get-tuple-element.23), channel_id=1, source_target_pairs={{0,64},{8,72},{16,80},{24,88},{32,96},{40,104},{48,112},{56,120},{... | collective-permute-start | bytes 172040 | tf_op jit(solution)/shard_map/ppermute | solution.py:37

commit v3 on v2

--- a/solution.py
+++ b/solution.py
@@ -52,7 +52,7 @@
     return jnp.asarray(np.concatenate([f, f]).astype(np.float32))[None]
 
 
-def key_kernel(base_ref, x_ref, gain_ref, freq_ref, out_ref, *, lat, part, page_len):
+def key_kernel(base_ref, owner_ref, slot_ref, q_ref, x_ref, gain_ref, freq_ref, all_ref, out_ref, *, lat, part, page_len, slots):
     x = x_ref[...].astype(F32)
     n = x.shape[0]
     latent, rot = x[:, :lat], x[:, lat:]
@@ -64,17 +64,19 @@
     angle = where_at.astype(F32) * freq_ref[...]
     sine = jnp.sin(angle)
     sine = jnp.where(lane < rot.shape[1] // 2, -sine, sine)
-    out_ref[:, lat:] = (rot * jnp.cos(angle) + swap_halves(rot) * sine).astype(BF)
-
-
-def query_kernel(where_ref, g, wq0, wq1, ak0, ak1, cos_ref, sin_ref, out_ref, x_ref, *, nope, rope, qrows, nzh, nzl):
-    zl = where_ref[1]
-    for d in range(nzl):
-        for zh in range(nzh):
-            z = zh * nzl + lax.rem(zl + d, nzl)
-            at = (d * nzh + zh) * qrows
-            x_ref[at : at + qrows, :] = g[pl.ds(pl.multiple_of(z * qrows, qrows), qrows), :]
-    x = x_ref[...]
+    code = jnp.zeros(rot.shape, F32)
+    for p in range(n // part):
+        here = (owner_ref[0, p] * slots + slot_ref[0, p]).astype(F32)
+        code = jnp.where(row // part == p, here, code)
+    turned = rot * jnp.cos(angle) + swap_halves(rot) * sine
+    out_ref[:, lat:] = jnp.concatenate([turned, code], -1).astype(BF)
+    ql = q_ref.shape[1]
+    all_ref[:, :ql] = q_ref[...]
+    all_ref[:, ql:] = out_ref[...]
+
+
+def query_kernel(g, wq0, wq1, ak0, ak1, cos_ref, sin_ref, out_ref, *, nope, rope):
+    x = g[:, : wq0.shape[0]]
     rows = x.shape[0]
     lat = ak0.shape[-1]
     head = 0
@@ -87,8 +89,9 @@
                 q[:, base : base + nope], ak[h], preferred_element_type=F32
             ).astype(BF)
             rot = q[:, base + nope : base + nope + rope].astype(F32)
-            out_ref[r0 : r0 + rows, lat:] = (
-                rot * cos_ref[...] + swap_halves(rot) * sin_ref[...]
+            turned = rot * cos_ref[...] + swap_halves(rot) * sin_ref[...]
+            out_ref[r0 : r0 + rows, lat:] = jnp.concatenate(
+                [turned, jnp.zeros_like(turned)], -1
             ).astype(BF)
             head += 1
 
@@ -97,7 +100,7 @@
     where_ref, q_ref, ka_ref, kb_ref, av0, av1, op0, op1, out_ref,
     s_ref, top_ref, l_ref, acc_ref, ho_ref, *, rows, lat, scale, lay,
 ):
-    chain, zl, core = where_ref[0], where_ref[1], where_ref[2]
+    chain, core = where_ref[0], where_ref[1]
     nch, nzh, nzl, part, qrows, pages = lay
     s2 = scale * LOG2E
     vh = av0.shape[-1]
@@ -111,9 +114,7 @@
         return page * (nzh * nzl * 2 * part) + z * (2 * part) + kcore * part + idx % part
 
     def query_pos(idx):
-        d = idx // (nzh * qrows)
-        z = (idx // qrows) % nzh * nzl + (zl + d) % nzl
-        return z * (2 * qrows) + core * qrows + idx % qrows
+        return idx // qrows * (2 * qrows) + core * qrows + idx % qrows
 
     def lanes(x, op):
         out = x[:, :128]
@@ -201,22 +202,30 @@
     slots = 2 * pages
     smem = pl.BlockSpec(memory_space=pltpu.SMEM)
     vm = pl.BlockSpec(memory_space=pltpu.VMEM)
-    big = pltpu.CompilerParams(vmem_limit_bytes=40 * 1024 * 1024)
+
+    def room(mib):
+        return pltpu.CompilerParams(vmem_limit_bytes=mib * 1024 * 1024)
 
     raw = jnp.concatenate(
         [latent_rows[0].reshape(pages * part, lat), rope_keys[0].reshape(pages * part, rope)], -1
     )
-    keys = pl.pallas_call(
-        functools.partial(key_kernel, lat=lat, part=part, page_len=part * tp_count),
-        out_shape=jax.ShapeDtypeStruct(raw.shape, BF),
-        in_specs=[smem, vm, vm, vm],
-        out_specs=vm,
-        compiler_params=big,
+    merged, keys = pl.pallas_call(
+        functools.partial(key_kernel, lat=lat, part=part, page_len=part * tp_count, slots=slots),
+        out_shape=(
+            jax.ShapeDtypeStruct((qrows, ql + lat + 2 * rope), BF),
+            jax.ShapeDtypeStruct((pages * part, lat + 2 * rope), BF),
+        ),
+        in_specs=[smem] * 3 + [vm] * 4,
+        out_specs=(vm, vm),
+        compiler_params=room(4),
         name="keys",
-    )((chain * block_len + tp_index * part).astype(jnp.int32)[None], raw, latent_gain[None], frequencies(rope))
-
-    own = lax.all_gather(keys, Z, axis=0, tiled=True)
-    qg = lax.all_gather(query_comp[0], Z, axis=0, tiled=True)
+    )(
+        (chain * block_len + tp_index * part).astype(jnp.int32)[None],
+        page_owner, page_slot, query_comp[0], raw, latent_gain[None], frequencies(rope),
+    )
+
+    whole = lax.all_gather(merged, Z, axis=0, tiled=True)
+    own = whole[:, ql:]
     backs = [
         lax.ppermute(own, "chain", [(i, i + k) for i in range(nch - k)]) for k in range(1, nch)
     ]
@@ -230,24 +239,22 @@
 
     rows = qrows * nzh * nzl
     idx = jnp.arange(rows, dtype=jnp.int32)
-    zq = (idx // qrows) % nzh * nzl + (zl + idx // (nzh * qrows)) % nzl
-    query_where = chain * block_len + zq * (2 * qrows) + core * qrows + idx % qrows
+    query_where = chain * block_len + idx // qrows * (2 * qrows) + core * qrows + idx % qrows
     qcos, qsin = rope_tables(query_where, rope)
     heads = 2 * heads_here
-    where = jnp.stack([chain, zl, core]).astype(jnp.int32)
+    where = jnp.stack([chain, core]).astype(jnp.int32)
     q = pl.pallas_call(
-        functools.partial(query_kernel, nope=nope, rope=rope, qrows=qrows, nzh=nzh, nzl=nzl),
-        out_shape=jax.ShapeDtypeStruct((heads * rows, lat + rope), BF),
-        in_specs=[smem] + [vm] * 7,
+        functools.partial(query_kernel, nope=nope, rope=rope),
+        out_shape=jax.ShapeDtypeStruct((heads * rows, lat + 2 * rope), BF),
+        in_specs=[vm] * 7,
         out_specs=vm,
-        scratch_shapes=[pltpu.VMEM((rows, ql), BF)],
-        compiler_params=big,
+        compiler_params=room(12),
         cost_estimate=pl.CostEstimate(
             flops=2 * rows * heads * (nope + rope) * ql + 2 * rows * heads * nope * lat,
             bytes_accessed=6000000, transcendentals=0,
         ),
         name="queries",
-    )(where, qg, query_up, wq1, absorb_key, ak1, qcos, qsin)
+    )(whole, query_up, wq1, absorb_key, ak1, qcos, qsin)
 
     partial = pl.pallas_call(
         functools.partial(
@@ -264,7 +271,7 @@
             pltpu.VMEM((heads, rows, lat), F32),
             pltpu.VMEM((rows, heads * vh), BF),
         ],
-        compiler_params=big,
+        compiler_params=room(24),
         cost_estimate=pl.CostEstimate(
             flops=4 * rows * heads * nch * block_len * lat, bytes_accessed=9000000,
             transcendentals=rows * heads * nch * block_len,
@@ -272,36 +279,9 @@
         name="attend",
     )(where, q, mine, other, absorb_value, av1, out_proj, op1)
 
-    sums = partial.reshape(nzl, nzh, qrows, width)
-    half = nzh // 2
-    up2 = shift_z(sums[2, :half], 2)
-    down2 = shift_z(sums[2, half:], -2)
-    up = shift_z(sums[1], 1)
-    down = shift_z(sums[3], -1)
-    near = (
-        sums[0].astype(F32) + up.astype(F32) + down.astype(F32)
-        + jnp.concatenate([up2, down2], 0).astype(F32)
-    ).astype(BF)
-    cut = width // 2
-
-    def chunk(steps):
-        return lax.dynamic_index_in_dim(near, lax.rem(zh + steps, nzh), 0, keepdims=False)
-
-    far = chunk(2)
-    around = shift_z(far[:, cut:], -nzl)
-    direct = shift_z(far[:, :cut], 2 * nzl)
-    ahead = shift_z(chunk(1), nzl)
-    behind = chunk(3).astype(F32)
-    behind = jnp.concatenate([behind[:, :cut], behind[:, cut:] + around.astype(F32)], -1).astype(BF)
-    behind = shift_z(behind, -nzl)
-    total = chunk(0).astype(F32) + ahead.astype(F32) + behind.astype(F32)
-    total = jnp.concatenate([total[:, :cut] + direct.astype(F32), total[:, cut:]], -1)
-    layer_output = total.astype(BF)[None]
-
-    code = (page_owner[0] * slots + page_slot[0]).astype(BF)
-    tail = jnp.broadcast_to(code[:, None, None], (pages, part, 128 - rope))
-    page = jnp.concatenate([keys.reshape(pages, part, lat + rope), tail], -1)
-    page = spread(page, "dec")
+    layer_output = lax.psum_scatter(partial, Z, scatter_dimension=0, tiled=True)[None]
+
+    page = spread(keys.reshape(pages, part, -1), "dec")
     came = page[:, :, 0, lat + rope].reshape(-1).astype(jnp.int32)
     take = (came[None, :] == dec * slots + jnp.arange(slots, dtype=jnp.int32)[:, None]).astype(BF)
     placed = jnp.einsum(

time: 175 us -> 208 us (1.19)
  the two profiles are of different devices: /device:TPU:122 before, /device:TPU:24 now
where the time goes in v3:
time: 208 us; the launch traced here: 207 us
  waiting for transfers between devices  147 us (71%)
  starting transfers between devices  18.9 us (9%)
  Pallas kernels  17.3 us (8%)
  between operations  14.3 us (7%)
  local copies, waits for them, and re-layouts  7.19 us (3%)
    all_gather x1, waiting for transfers between devices, local(): whole = lax.all_gather(merged, Z, axis=0, tiled=True)  73.8 us
    reduce_scatter x1, waiting for transfers between devices, local(): lax.psum_scatter(partial, Z, scatter_dimension=0, tiled=True)[None]  56.5 us
    pallas_call x1, Pallas kernels, local(): pl.pallas_call(functools.partial(attend_kernel, rows=rows, lat=lat, scale...  12.7 us
    ppermute x3, waiting for transfers between devices, local(): lax.ppermute(own, 'chain', [(i, i + k) for i in range(nch - k)])  11.4 us
    ppermute x5, starting transfers between devices, swap_core(): return lax.ppermute(x, 'core', [(0, 1), (1, 0)])  10.6 us
    all_to_all x1, waiting for transfers between devices, spread(): lax.all_to_all(jnp.broadcast_to(x[None], (n,) + x.shape), axis, 0, 0, til...  5.71 us
    unnamed x20, local copies, waits for them, and re-layouts  4.7 us
    all_to_all x1, starting transfers between devices, spread(): lax.all_to_all(jnp.broadcast_to(x[None], (n,) + x.shape), axis, 0, 0, til...  4.2 us
  transfers between devices with their start and end apart: 11, of which 6 were waited for; matrix products, arithmetic and copies ran while one was open for 2% of the time, Pallas kernels for 2%

profile of v3, /device:TPU:24, one launch (start us, length us, event | category | flops | bytes accessed | tf_op | source)
XLA Modules:
  0.0 207.3 jit_solution(668170942551599824)
XLA Ops:
  7.2 0.7 reshape_squeeze.7
  8.0 0.7 pad_maximum_fusion.3.x_ref
  8.6 0.8 copy-done.2
  9.4 0.7 copy-done.3
  10.1 0.7 copy-done.4
  10.8 0.7 copy-done.5
  11.4 0.7 copy-done.6
  12.1 1.3 keys.1
  13.4 1.9 collective-permute-start.7
  15.4 73.8 %all-gather.2.cloned.1.call-done.g = bf16[256,2176]{1,0:T(8,128)(2,1)} async-done(((bf16[16,2176]{1,0:T(8,128)(2,1)}), bf16[256,2176]{1,0:T(8,128)(2,1)}) %all-gather.2.cloned.1.call-update) | async-done | bytes 1114128 | tf_op jit(solution)/shard_map/all_gather | solution.py:227
  89.2 1.0 slice.16
  90.2 1.4 collective-permute-start.2
  91.6 1.3 collective-permute-start.3
  92.9 1.3 collective-permute-start.4
  94.2 5.1 %collective-permute-done.2 = bf16[256,640]{1,0:T(8,128)(2,1)S(1)} collective-permute-done((bf16[256,640]{1,0:T(8,128)(2,1)S(1)}, bf16[256,640]{1,0:T(8,128)(2,1)S(1)}, u32[]{:S(2)}, u32[]{:S(2)}) %collective-permute-start.2) | collective-permute-done | bytes 327712 | tf_op jit(solution)/shard_map/ppermute | solution.py:230
  99.3 2.8 %collective-permute-done.3 = bf16[256,640]{1,0:T(8,128)(2,1)S(1)} collective-permute-done((bf16[256,640]{1,0:T(8,128)(2,1)S(1)}, bf16[256,640]{1,0:T(8,128)(2,1)S(1)}, u32[]{:S(2)}, u32[]{:S(2)}) %collective-permute-start.3) | collective-permute-done | bytes 327712 | tf_op jit(solution)/shard_map/ppermute | solution.py:230
  102.2 3.5 %collective-permute-done.4 = bf16[256,640]{1,0:T(8,128)(2,1)S(1)} collective-permute-done((bf16[256,640]{1,0:T(8,128)(2,1)S(1)}, bf16[256,640]{1,0:T(8,128)(2,1)S(1)}, u32[]{:S(2)}, u32[]{:S(2)}) %collective-permute-start.4) | collective-permute-done | bytes 327712 | tf_op jit(solution)/shard_map/ppermute | solution.py:230
  105.7 1.9 collective-permute-start.5
  107.7 2.4 %collective-permute-start = (bf16[1536,384]{1,0:T(8,128)(2,1)}, bf16[1536,384]{1,0:T(8,128)(2,1)}, u32[]{:S(2)}, u32[]{:S(2)}) collective-permute-start(bf16[1536,384]{1,0:T(8,128)(2,1)} %wq0.1), channel_id=1, source_target_pairs={{0,4},{4,0},{1,5},{5,1},{2,6},{6,2},{3,7},{7,3},{8,12},{12,8},{9,1... | collective-permute-start | bytes 3538952 | tf_op jit(solution)/shard_map/ppermute | solution.py:41
  110.1 1.9 collective-permute-start.1
  112.0 2.4 %collective-permute-start.6 = (bf16[2,512,128]{2,1,0:T(8,128)(2,1)S(1)}, bf16[2,512,128]{2,1,0:T(8,128)(2,1)S(1)}, u32[]{:S(2)}, u32[]{:S(2)}) collective-permute-start(bf16[2,512,128]{2,1,0:T(8,128)(2,1)S(1)} %copy-done.8), channel_id=1, source_target_pairs={{0,4},{4,0},{1,5},{5,1},{2,6},{6,2},{3,7},{7,3},{8,12},{12,8},{9,1... | collective-permute-start | bytes 786440 | tf_op jit(solution)/shard_map/ppermute | solution.py:41
  114.5 0.5 fusion.1
  115.3 3.3 %queries.1.q_ref = bf16[1024,640]{1,0:T(8,128)(2,1)S(1)} custom-call(bf16[256,2176]{1,0:T(8,128)(2,1)S(1)} %copy-done, bf16[1536,384]{1,0:T(8,128)(2,1)} %wq0.1, bf16[1536,384]{1,0:T(8,128)(2,1)} %collective-permute-done.wq1, bf16[2,128,512]{2,1,0:T(8,128)(2,1)S(1)} %copy-done.1, bf16[2,128,512]{2,1,0:T(8,128)(2,1)S(1)} %collective-permute-done.1.ak1, ...), custom_call_target="tpu_custom_call" | custom-call | flops 738197504 | bytes 6000000 | tf_op jit(solution)/shard_map/queries/pallas_call | solution.py:246
  118.6 12.7 %attend.1 = bf16[256,3584]{1,0:T(8,128)(2,1)} custom-call(s32[2]{0:T(128)S(1)} %pad_add_fusion.where_ref, bf16[1024,640]{1,0:T(8,128)(2,1)S(1)} %queries.1.q_ref, bf16[1024,640]{1,0:T(8,128)(2,1)S(1)} %pad_maximum_fusion.ka_ref, bf16[1024,640]{1,0:T(8,128)(2,1)} %collective-permute-done.5.kb_ref, bf16[2,512,128]{2,1,0:T(8,128)(2,1)S(1)} %copy-done.8, ...), custom_call_target="tpu_custom_call" | custom-call | flops 4294967296 | bytes 9000000 | tf_op jit(solution)/shard_map/attend/pallas_call | solution.py:259
  131.4 0.6 broadcast_in_dim.34
  132.0 4.2 %all-to-all-start = ((bf16[4,4,4,640]{3,2,1,0:T(4,128)(2,1)}), bf16[4,4,4,640]{3,2,1,0:T(4,128)(2,1)S(1)}, u32[]{:S(2)}, u32[]{:S(2)}) async-start(bf16[4,4,4,640]{3,2,1,0:T(4,128)(2,1)} %broadcast_in_dim.34), calls=%async_computation.1 | async-start | bytes 163840 | tf_op jit(solution)/shard_map/all_to_all | solution.py:46
  136.2 5.7 %all-to-all-done = bf16[4,4,4,640]{3,2,1,0:T(4,128)(2,1)S(1)} async-done(((bf16[4,4,4,640]{3,2,1,0:T(4,128)(2,1)}), bf16[4,4,4,640]{3,2,1,0:T(4,128)(2,1)S(1)}, u32[]{:S(2)}, u32[]{:S(2)}) %all-to-all-start) | async-done | bytes 81952 | tf_op jit(solution)/shard_map/all_to_all | solution.py:46
  141.9 0.4 fusion.2
  142.5 0.2 convolution_convert_fusion
  142.7 0.6 copy.26
  143.3 0.6 copy.27
  143.9 56.5 %reduce-scatter.2.cloned.1.call-done = bf16[16,3584]{1,0:T(8,128)(2,1)} async-done(((bf16[256,3584]{1,0:T(8,128)(2,1)}), bf16[16,3584]{1,0:T(8,128)(2,1)}) %reduce-scatter.2.cloned.1.call-update) | async-done | bytes 114704 | tf_op jit(solution)/shard_map/reduce_scatter | solution.py:282
  (32 shorter events, 0.6 us)
Async XLA Ops:
  7.2 82.0 %all-gather.2.cloned.1.call-start = ((), (), s32[]{:S(2)}) async-start(), calls=%async_computation.2 | async-start | bytes 1183744 | tf_op jit(solution)/shard_map/all_gather | solution.py:227
  8.6 0.8 copy-start.2
  9.4 0.7 copy-start.3
  10.1 0.7 copy-start.4
  10.8 0.7 copy-start.5
  11.4 0.7 copy-start.6
  13.4 187.1 %reduce-scatter.2.cloned.1.call-start = ((), (), s32[]{:S(2)}) async-start(), calls=%async_computation.3 | async-start | bytes 1949696 | tf_op jit(solution)/shard_map/reduce_scatter | solution.py:282
  13.4 105.1 %collective-permute-start.7 = (bf16[256,3584]{1,0:T(8,128)(2,1)}, bf16[256,3584]{1,0:T(8,128)(2,1)}, u32[]{:S(2)}, u32[]{:S(2)}) collective-permute-start(bf16[256,3584]{1,0:T(8,128)(2,1)} %op0.1), channel_id=1, source_target_pairs={{0,4},{4,0},{1,5},{5,1},{2,6},{6,2},{3,7},{7,3},{8,12},{12,8},{9,1... | collective-permute-start | bytes 5505032 | tf_op jit(solution)/shard_map/ppermute | solution.py:41
  90.2 19.9 %copy-start.1 = (bf16[2,128,512]{2,1,0:T(8,128)(2,1)S(1)}, bf16[2,128,512]{2,1,0:T(8,128)(2,1)}, u32[]{:S(2)}) copy-start(bf16[2,128,512]{2,1,0:T(8,128)(2,1)} %ak0.1) | copy-start | bytes 786436
  90.2 21.8 %copy-start.8 = (bf16[2,512,128]{2,1,0:T(8,128)(2,1)S(1)}, bf16[2,512,128]{2,1,0:T(8,128)(2,1)}, u32[]{:S(2)}) copy-start(bf16[2,512,128]{2,1,0:T(8,128)(2,1)} %av0.1) | copy-start | bytes 786436
  90.2 25.1 %copy-start = (bf16[256,2176]{1,0:T(8,128)(2,1)S(1)}, bf16[256,2176]{1,0:T(8,128)(2,1)}, u32[]{:S(2)}) copy-start(bf16[256,2176]{1,0:T(8,128)(2,1)} %all-gather.2.cloned.1.call-done.g) | copy-start | bytes 3342340
  90.2 9.1 %collective-permute-start.2 = (bf16[256,640]{1,0:T(8,128)(2,1)S(1)}, bf16[256,640]{1,0:T(8,128)(2,1)S(1)}, u32[]{:S(2)}, u32[]{:S(2)}) collective-permute-start(bf16[256,640]{1,0:T(8,128)(2,1)S(1)} %slice.16), channel_id=1, source_target_pairs={{0,128},{128,256},{256,384},{1,129},{129,257},{257,385},{2,130},{1... | collective-permute-start | bytes 983048 | tf_op jit(solution)/shard_map/ppermute | solution.py:230
  91.6 10.5 %collective-permute-start.3 = (bf16[256,640]{1,0:T(8,128)(2,1)S(1)}, bf16[256,640]{1,0:T(8,128)(2,1)S(1)}, u32[]{:S(2)}, u32[]{:S(2)}) collective-permute-start(bf16[256,640]{1,0:T(8,128)(2,1)S(1)} %slice.16), channel_id=1, source_target_pairs={{0,256},{128,384},{1,257},{129,385},{2,258},{130,386},{3,259},{131... | collective-permute-start | bytes 983048 | tf_op jit(solution)/shard_map/ppermute | solution.py:230
  92.9 12.7 %collective-permute-start.4 = (bf16[256,640]{1,0:T(8,128)(2,1)S(1)}, bf16[256,640]{1,0:T(8,128)(2,1)S(1)}, u32[]{:S(2)}, u32[]{:S(2)}) collective-permute-start(bf16[256,640]{1,0:T(8,128)(2,1)S(1)} %slice.16), channel_id=1, source_target_pairs={{0,384},{1,385},{2,386},{3,387},{4,388},{5,389},{6,390},{7,391},{8... | collective-permute-start | bytes 983048 | tf_op jit(solution)/shard_map/ppermute | solution.py:230
  105.7 12.8 %collective-permute-start.5 = (bf16[1024,640]{1,0:T(8,128)(2,1)S(1)}, bf16[1024,640]{1,0:T(8,128)(2,1)}, u32[]{:S(2)}, u32[]{:S(2)}) collective-permute-start(bf16[1024,640]{1,0:T(8,128)(2,1)S(1)} %pad_maximum_fusion.ka_ref), channel_id=1, source_target_pairs={{0,4},{4,0},{1,5},{5,1},{2,6},{6,2},{3,7},{7,3},{8,12},{12,8},{9,1... | collective-permute-start | bytes 3932168 | tf_op jit(solution)/shard_map/ppermute | solution.py:41
  107.7 7.6 %collective-permute-start = (bf16[1536,384]{1,0:T(8,128)(2,1)}, bf16[1536,384]{1,0:T(8,128)(2,1)}, u32[]{:S(2)}, u32[]{:S(2)}) collective-permute-start(bf16[1536,384]{1,0:T(8,128)(2,1)} %wq0.1), channel_id=1, source_target_pairs={{0,4},{4,0},{1,5},{5,1},{2,6},{6,2},{3,7},{7,3},{8,12},{12,8},{9,1... | collective-permute-start | bytes 3538952 | tf_op jit(solution)/shard_map/ppermute | solution.py:41
  110.1 5.1 %collective-permute-start.1 = (bf16[2,128,512]{2,1,0:T(8,128)(2,1)S(1)}, bf16[2,128,512]{2,1,0:T(8,128)(2,1)S(1)}, u32[]{:S(2)}, u32[]{:S(2)}) collective-permute-start(bf16[2,128,512]{2,1,0:T(8,128)(2,1)S(1)} %copy-done.1), channel_id=1, source_target_pairs={{0,4},{4,0},{1,5},{5,1},{2,6},{6,2},{3,7},{7,3},{8,12},{12,8},{9,1... | collective-permute-start | bytes 786440 | tf_op jit(solution)/shard_map/ppermute | solution.py:41
  112.0 6.5 %collective-permute-start.6 = (bf16[2,512,128]{2,1,0:T(8,128)(2,1)S(1)}, bf16[2,512,128]{2,1,0:T(8,128)(2,1)S(1)}, u32[]{:S(2)}, u32[]{:S(2)}) collective-permute-start(bf16[2,512,128]{2,1,0:T(8,128)(2,1)S(1)} %copy-done.8), channel_id=1, source_target_pairs={{0,4},{4,0},{1,5},{5,1},{2,6},{6,2},{3,7},{7,3},{8,12},{12,8},{9,1... | collective-permute-start | bytes 786440 | tf_op jit(solution)/shard_map/ppermute | solution.py:41
  115.3 3.3 %copy-start.7 = (bf16[256,3584]{1,0:T(8,128)(2,1)S(1)}, bf16[256,3584]{1,0:T(8,128)(2,1)}, u32[]{:S(2)}) copy-start(bf16[256,3584]{1,0:T(8,128)(2,1)} %op0.1) | copy-start | bytes 5505028
  132.0 9.9 %all-to-all-start = ((bf16[4,4,4,640]{3,2,1,0:T(4,128)(2,1)}), bf16[4,4,4,640]{3,2,1,0:T(4,128)(2,1)S(1)}, u32[]{:S(2)}, u32[]{:S(2)}) async-start(bf16[4,4,4,640]{3,2,1,0:T(4,128)(2,1)} %broadcast_in_dim.34), calls=%async_computation.1 | async-start | bytes 163840 | tf_op jit(solution)/shard_map/all_to_all | solution.py:46
Sparse Core Ops, SparseCore 0:
  13.5 75.6 all-gather.1
  131.5 68.9 reduce-scatter.1

commit v4 on v3

--- a/solution.py
+++ b/solution.py
@@ -75,8 +75,21 @@
     all_ref[:, ql:] = out_ref[...]
 
 
-def query_kernel(g, wq0, wq1, ak0, ak1, cos_ref, sin_ref, out_ref, *, nope, rope):
-    x = g[:, : wq0.shape[0]]
+def own_kernel(g0, g1, g2, g3, g4, own_ref, *, ql):
+    at = 0
+    for g in (g0, g1, g2, g3, g4):
+        n = g.shape[0]
+        own_ref[at : at + n, :] = g[:, ql:]
+        at += n
+
+
+def query_kernel(g0, g1, g2, g3, g4, wq0, wq1, ak0, ak1, cos_ref, sin_ref, out_ref, x_ref, *, nope, rope):
+    at = 0
+    for g in (g0, g1, g2, g3, g4):
+        n = g.shape[0]
+        x_ref[at : at + n, :] = g[:, : wq0.shape[0]]
+        at += n
+    x = x_ref[...]
     rows = x.shape[0]
     lat = ak0.shape[-1]
     head = 0
@@ -97,25 +110,16 @@
 
 
 def attend_kernel(
-    where_ref, q_ref, ka_ref, kb_ref, av0, av1, op0, op1, out_ref,
-    s_ref, top_ref, l_ref, acc_ref, ho_ref, *, rows, lat, scale, lay,
+    where_ref, qpos_ref, kpos_ref, q_ref, ka_ref, kb_ref, av0, av1, op0, op1, out_ref,
+    s_ref, top_ref, l_ref, acc_ref, ho_ref, *, rows, lat, scale, nch,
 ):
-    chain, core = where_ref[0], where_ref[1]
-    nch, nzh, nzl, part, qrows, pages = lay
+    chain = where_ref[0]
     s2 = scale * LOG2E
     vh = av0.shape[-1]
     heads = q_ref.shape[0] // rows
     n = ka_ref.shape[0] // nch
     nt = (((1,), (1,)), ((), ()))
 
-    def key_pos(idx, kcore):
-        z = idx // (pages * part)
-        page = (idx // part) % pages
-        return page * (nzh * nzl * 2 * part) + z * (2 * part) + kcore * part + idx % part
-
-    def query_pos(idx):
-        return idx // qrows * (2 * qrows) + core * qrows + idx % qrows
-
     def lanes(x, op):
         out = x[:, :128]
         for c in range(128, x.shape[1], 128):
@@ -124,9 +128,7 @@
 
     def score(back):
         if back == 0:
-            qp = query_pos(lax.broadcasted_iota(jnp.int32, (rows, 1), 0))
-            kidx = lax.broadcasted_iota(jnp.int32, (1, n), 1)
-            ok = (key_pos(kidx, core) <= qp, key_pos(kidx, 1 - core) <= qp)
+            ok = [kpos_ref[i : i + 1, :] <= qpos_ref[...] for i in range(2)]
         for h in range(heads):
             q = q_ref[h * rows : (h + 1) * rows, :]
             for i, k_ref in enumerate((ka_ref, kb_ref)):
@@ -224,12 +226,33 @@
         page_owner, page_slot, query_comp[0], raw, latent_gain[None], frequencies(rope),
     )
 
-    whole = lax.all_gather(merged, Z, axis=0, tiled=True)
-    own = whole[:, ql:]
-    backs = [
-        lax.ppermute(own, "chain", [(i, i + k) for i in range(nch - k)]) for k in range(1, nch)
+    group = jnp.concatenate(
+        [shift_z(merged, nzl), merged, shift_z(merged, -nzl), shift_z(merged, -2 * nzl)], 0
+    )
+    parts = [
+        group,
+        shift_z(group, -1),
+        shift_z(group, 1),
+        shift_z(group[qrows : 3 * qrows], -2),
+        shift_z(group[: 2 * qrows], 2),
     ]
-    mine = jnp.concatenate([own] + backs, 0)
+    rows = qrows * nzh * nzl
+    kw = lat + 2 * rope
+    own = pl.pallas_call(
+        functools.partial(own_kernel, ql=ql),
+        out_shape=jax.ShapeDtypeStruct((rows, kw), BF),
+        in_specs=[vm] * 5,
+        out_specs=vm,
+        compiler_params=room(4),
+        name="own",
+    )(*parts)
+
+    half = rows // 2
+    before = lax.ppermute(own, "chain", [(0, 1), (1, 2), (2, 3)])
+    across = lax.ppermute(own, "chain", [(0, 3), (1, 0)])
+    second = lax.ppermute(before[:half], "chain", [(1, 2), (2, 3)])
+    second2 = lax.ppermute(across[half:], "chain", [(3, 2), (0, 3)])
+    mine = jnp.concatenate([own, before, second, second2, across], 0)
     other = swap_core(mine)
 
     wq1 = swap_core(query_up)
@@ -237,32 +260,38 @@
     av1 = swap_core(absorb_value)
     op1 = swap_core(out_proj)
 
-    rows = qrows * nzh * nzl
-    idx = jnp.arange(rows, dtype=jnp.int32)
-    query_where = chain * block_len + idx // qrows * (2 * qrows) + core * qrows + idx % qrows
+    steps = [4 * e + d for d in (0, 1, -1) for e in (-1, 0, 1, 2)] + [2, 6, -6, -2]
+    z = (zh * nzl + zl + jnp.asarray(np.array(steps, np.int32))) % (nzh * nzl)
+    lane = jnp.arange(qrows, dtype=jnp.int32)
+    qpos = (z[:, None] * (2 * qrows) + core * qrows + lane[None]).reshape(rows)
+    lane = lane // part * (part * tp_count) + lane % part
+    kpos = (z[:, None] * (2 * part) + lane[None]).reshape(1, rows)
+    kpos = kpos + jnp.stack([core, 1 - core])[:, None] * part
+    query_where = chain * block_len + qpos
     qcos, qsin = rope_tables(query_where, rope)
     heads = 2 * heads_here
-    where = jnp.stack([chain, core]).astype(jnp.int32)
+    where = chain.astype(jnp.int32)[None]
     q = pl.pallas_call(
         functools.partial(query_kernel, nope=nope, rope=rope),
-        out_shape=jax.ShapeDtypeStruct((heads * rows, lat + 2 * rope), BF),
-        in_specs=[vm] * 7,
+        out_shape=jax.ShapeDtypeStruct((heads * rows, kw), BF),
+        in_specs=[vm] * 11,
         out_specs=vm,
+        scratch_shapes=[pltpu.VMEM((rows, ql), BF)],
         compiler_params=room(12),
         cost_estimate=pl.CostEstimate(
             flops=2 * rows * heads * (nope + rope) * ql + 2 * rows * heads * nope * lat,
             bytes_accessed=6000000, transcendentals=0,
         ),
         name="queries",
-    )(whole, query_up, wq1, absorb_key, ak1, qcos, qsin)
+    )(*parts, query_up, wq1, absorb_key, ak1, qcos, qsin)
 
     partial = pl.pallas_call(
         functools.partial(
             attend_kernel, rows=rows, lat=lat, scale=(nope + rope) ** -0.5,
-            lay=(nch, nzh, nzl, part, qrows, pages),
+            nch=nch,
         ),
         out_shape=jax.ShapeDtypeStruct((rows, width), BF),
-        in_specs=[smem] + [vm] * 7,
+        in_specs=[smem] + [vm] * 9,
         out_specs=vm,
         scratch_shapes=[
             pltpu.VMEM((heads, rows, nch * block_len), F32),
@@ -277,9 +306,30 @@
             transcendentals=rows * heads * nch * block_len,
         ),
         name="attend",
-    )(where, q, mine, other, absorb_value, av1, out_proj, op1)
-
-    layer_output = lax.psum_scatter(partial, Z, scatter_dimension=0, tiled=True)[None]
+    )(where, qpos[:, None], kpos, q, mine, other, absorb_value, av1, out_proj, op1)
+
+    n = nzh * qrows
+    up = shift_z(partial[n : 2 * n], 1)
+    down = shift_z(partial[2 * n : 3 * n], -1)
+    up2 = shift_z(partial[3 * n : 3 * n + n // 2], 2)
+    down2 = shift_z(partial[3 * n + n // 2 :], -2)
+
+    def near(e):
+        at = slice((e + 1) * qrows, (e + 2) * qrows)
+        return partial[at].astype(F32) + up[at].astype(F32) + down[at].astype(F32)
+
+    cut = width // 2
+    far = near(2).astype(BF)
+    around = shift_z(far[:, cut:], -nzl)
+    direct = shift_z(far[:, :cut], 2 * nzl)
+    ahead = shift_z((near(1) + up2[qrows:].astype(F32)).astype(BF), nzl)
+    behind = near(-1) + down2[:qrows].astype(F32)
+    behind = jnp.concatenate([behind[:, :cut], behind[:, cut:] + around.astype(F32)], -1)
+    behind = shift_z(behind.astype(BF), -nzl)
+    total = near(0) + up2[:qrows].astype(F32) + down2[qrows:].astype(F32)
+    total = total + ahead.astype(F32) + behind.astype(F32)
+    total = jnp.concatenate([total[:, :cut] + direct.astype(F32), total[:, cut:]], -1)
+    layer_output = total.astype(BF)[None]
 
     page = spread(keys.reshape(pages, part, -1), "dec")
     came = page[:, :, 0, lat + rope].reshape(-1).astype(jnp.int32)

time: 208 us -> 186 us (0.89)
  the two profiles are of different devices: /device:TPU:24 before, /device:TPU:57 now
where the time goes in v4:
time: 186 us; the launch traced here: 185 us
  starting transfers between devices  99.3 us (53%)
  waiting for transfers between devices  40 us (22%)
  local copies, waits for them, and re-layouts  16.7 us (9%)
  Pallas kernels  15.4 us (8%)
  other arithmetic  11.9 us (6%)
    ppermute x15, starting transfers between devices, shift_z(): return lax.ppermute(x, Z, [(i, (i + step) % n) for i in range(n)])  68.8 us
    ppermute x15, waiting for transfers between devices, shift_z(): return lax.ppermute(x, Z, [(i, (i + step) % n) for i in range(n)])  31.6 us
    ppermute x5, starting transfers between devices, swap_core(): return lax.ppermute(x, 'core', [(0, 1), (1, 0)])  19 us
    pallas_call x1, Pallas kernels, local(): pl.pallas_call(functools.partial(attend_kernel, rows=rows, lat=lat, scale...  12.1 us
    unnamed x33, local copies, waits for them, and re-layouts  9.44 us
    ppermute x1, waiting for transfers between devices, local(): before = lax.ppermute(own, 'chain', [(0, 1), (1, 2), (2, 3)])  7.93 us
    all_to_all x1, starting transfers between devices, spread(): lax.all_to_all(jnp.broadcast_to(x[None], (n,) + x.shape), axis, 0, 0, til...  4.01 us
  transfers between devices with their start and end apart: 25, of which 6 were waited for; matrix products, arithmetic and copies ran while one was open for 11% of the time, Pallas kernels for 8%

profile of v4, /device:TPU:57, one launch (start us, length us, event | category | flops | bytes accessed | tf_op | source)
XLA Modules:
  0.0 184.6 jit_solution(2794324801205826712)
XLA Ops:
  6.2 8.8 %collective-permute-start = (bf16[16,2176]{1,0:T(8,128)(2,1)S(1)}, bf16[16,2176]{1,0:T(8,128)(2,1)S(1)}, u32[]{:S(2)}, u32[]{:S(2)}) collective-permute-start(bf16[16,2176]{1,0:T(8,128)(2,1)S(1)} %get-tuple-element.5), channel_id=1, source_target_pairs={{0,32},{8,40},{16,48},{24,56},{32,64},{40,72},{48,80},{56,88},{64,... | collective-permute-start | bytes 208904 | tf_op jit(solution)/shard_map/ppermute | solution.py:37
  15.0 4.7 %collective-permute-start.1 = (bf16[16,2176]{1,0:T(8,128)(2,1)S(1)}, bf16[16,2176]{1,0:T(8,128)(2,1)S(1)}, u32[]{:S(2)}, u32[]{:S(2)}) collective-permute-start(bf16[16,2176]{1,0:T(8,128)(2,1)S(1)} %get-tuple-element.5), channel_id=1, source_target_pairs={{0,96},{8,104},{16,112},{24,120},{32,0},{40,8},{48,16},{56,24},{64... | collective-permute-start | bytes 208904 | tf_op jit(solution)/shard_map/ppermute | solution.py:37
  19.7 10.3 %collective-permute-start.2 = (bf16[16,2176]{1,0:T(8,128)(2,1)S(1)}, bf16[16,2176]{1,0:T(8,128)(2,1)S(1)}, u32[]{:S(2)}, u32[]{:S(2)}) collective-permute-start(bf16[16,2176]{1,0:T(8,128)(2,1)S(1)} %get-tuple-element.5), channel_id=1, source_target_pairs={{0,64},{8,72},{16,80},{24,88},{32,96},{40,104},{48,112},{56,120},{... | collective-permute-start | bytes 208904 | tf_op jit(solution)/shard_map/ppermute | solution.py:37
  29.9 3.4 %collective-permute-start.7 = (bf16[1536,384]{1,0:T(8,128)(2,1)}, bf16[1536,384]{1,0:T(8,128)(2,1)S(1)}, u32[]{:S(2)}, u32[]{:S(2)}) collective-permute-start(bf16[1536,384]{1,0:T(8,128)(2,1)} %wq0.1), channel_id=1, source_target_pairs={{0,4},{4,0},{1,5},{5,1},{2,6},{6,2},{3,7},{7,3},{8,12},{12,8},{9,1... | collective-permute-start | bytes 3538952 | tf_op jit(solution)/shard_map/ppermute | solution.py:41
  34.0 4.0 %all-to-all-start = ((bf16[4,4,4,640]{3,2,1,0:T(4,128)(2,1)}), bf16[4,4,4,640]{3,2,1,0:T(4,128)(2,1)S(1)}, u32[]{:S(2)}, u32[]{:S(2)}) async-start(bf16[4,4,4,640]{3,2,1,0:T(4,128)(2,1)} %broadcast_in_dim.40), calls=%async_computation | async-start | bytes 163840 | tf_op jit(solution)/shard_map/all_to_all | solution.py:46
  38.1 2.8 %collective-permute-done.2 = bf16[16,2176]{1,0:T(8,128)(2,1)S(1)} collective-permute-done((bf16[16,2176]{1,0:T(8,128)(2,1)S(1)}, bf16[16,2176]{1,0:T(8,128)(2,1)S(1)}, u32[]{:S(2)}, u32[]{:S(2)}) %collective-permute-start.2) | collective-permute-done | bytes 69664 | tf_op jit(solution)/shard_map/ppermute | solution.py:37
  40.9 1.9 %collective-permute-start.3 = (bf16[64,2176]{1,0:T(8,128)(2,1)S(1)}, bf16[64,2176]{1,0:T(8,128)(2,1)S(1)}, u32[]{:S(2)}, u32[]{:S(2)}) collective-permute-start(bf16[64,2176]{1,0:T(8,128)(2,1)S(1)} %constant_dynamic-update-slice_fusion.g0), channel_id=1, source_target_pairs={{0,120},{8,0},{16,8},{24,16},{32,24},{40,32},{48,40},{56,48},{64,5... | collective-permute-start | bytes 835592 | tf_op jit(solution)/shard_map/ppermute | solution.py:37
  42.8 3.4 %collective-permute-start.4 = (bf16[64,2176]{1,0:T(8,128)(2,1)S(1)}, bf16[64,2176]{1,0:T(8,128)(2,1)S(1)}, u32[]{:S(2)}, u32[]{:S(2)}) collective-permute-start(bf16[64,2176]{1,0:T(8,128)(2,1)S(1)} %constant_dynamic-update-slice_fusion.g0), channel_id=1, source_target_pairs={{0,8},{8,16},{16,24},{24,32},{32,40},{40,48},{48,56},{56,64},{64,7... | collective-permute-start | bytes 835592 | tf_op jit(solution)/shard_map/ppermute | solution.py:37
  46.2 4.6 %collective-permute-start.5 = (bf16[32,2176]{1,0:T(8,128)(2,1)S(1)}, bf16[32,2176]{1,0:T(8,128)(2,1)S(1)}, u32[]{:S(2)}, u32[]{:S(2)}) collective-permute-start(bf16[32,2176]{1,0:T(8,128)(2,1)S(1)} %get-tuple-element.34), channel_id=1, source_target_pairs={{0,112},{8,120},{16,0},{24,8},{32,16},{40,24},{48,32},{56,40},{64,... | collective-permute-start | bytes 417800 | tf_op jit(solution)/shard_map/ppermute | solution.py:37
  50.8 1.9 %collective-permute-start.6 = (bf16[32,2176]{1,0:T(8,128)(2,1)S(1)}, bf16[32,2176]{1,0:T(8,128)(2,1)S(1)}, u32[]{:S(2)}, u32[]{:S(2)}) collective-permute-start(bf16[32,2176]{1,0:T(8,128)(2,1)S(1)} %get-tuple-element.33), channel_id=1, source_target_pairs={{0,16},{8,24},{16,32},{24,40},{32,48},{40,56},{48,64},{56,72},{64,... | collective-permute-start | bytes 417800 | tf_op jit(solution)/shard_map/ppermute | solution.py:37
  53.3 2.6 %collective-permute-done.5.g3 = bf16[32,2176]{1,0:T(8,128)(2,1)S(1)} collective-permute-done((bf16[32,2176]{1,0:T(8,128)(2,1)S(1)}, bf16[32,2176]{1,0:T(8,128)(2,1)S(1)}, u32[]{:S(2)}, u32[]{:S(2)}) %collective-permute-start.5) | collective-permute-done | bytes 139296 | tf_op jit(solution)/shard_map/ppermute | solution.py:37
  55.9 4.1 %collective-permute-start.8 = (bf16[2,128,512]{2,1,0:T(8,128)(2,1)}, bf16[2,128,512]{2,1,0:T(8,128)(2,1)}, u32[]{:S(2)}, u32[]{:S(2)}) collective-permute-start(bf16[2,128,512]{2,1,0:T(8,128)(2,1)} %ak0.1), channel_id=1, source_target_pairs={{0,4},{4,0},{1,5},{5,1},{2,6},{6,2},{3,7},{7,3},{8,12},{12,8},{9,1... | collective-permute-start | bytes 786440 | tf_op jit(solution)/shard_map/ppermute | solution.py:41
  60.0 4.9 %collective-permute-start.15 = (bf16[256,3584]{1,0:T(8,128)(2,1)}, bf16[256,3584]{1,0:T(8,128)(2,1)}, u32[]{:S(2)}, u32[]{:S(2)}) collective-permute-start(bf16[256,3584]{1,0:T(8,128)(2,1)} %op0.1), channel_id=1, source_target_pairs={{0,4},{4,0},{1,5},{5,1},{2,6},{6,2},{3,7},{7,3},{8,12},{12,8},{9,1... | collective-permute-start | bytes 5505032 | tf_op jit(solution)/shard_map/ppermute | solution.py:41
  68.3 7.9 %collective-permute-done.9 = bf16[256,640]{1,0:T(8,128)(2,1)S(1)} collective-permute-done((bf16[256,640]{1,0:T(8,128)(2,1)S(1)}, bf16[256,640]{1,0:T(8,128)(2,1)S(1)}, u32[]{:S(2)}, u32[]{:S(2)}) %collective-permute-start.9) | collective-permute-done | bytes 327712 | tf_op jit(solution)/shard_map/ppermute | solution.py:251
  78.8 3.6 %collective-permute-start.12 = (bf16[128,640]{1,0:T(8,128)(2,1)S(1)}, bf16[128,640]{1,0:T(8,128)(2,1)S(1)}, u32[]{:S(2)}, u32[]{:S(2)}) collective-permute-start(bf16[128,640]{1,0:T(8,128)(2,1)S(1)} %slice.131), channel_id=1, source_target_pairs={{384,256},{0,384},{385,257},{1,385},{386,258},{2,386},{387,259},{3... | collective-permute-start | bytes 491528 | tf_op jit(solution)/shard_map/ppermute | solution.py:254
  83.1 3.7 %collective-permute-start.14 = (bf16[2,512,128]{2,1,0:T(8,128)(2,1)}, bf16[2,512,128]{2,1,0:T(8,128)(2,1)}, u32[]{:S(2)}, u32[]{:S(2)}) collective-permute-start(bf16[2,512,128]{2,1,0:T(8,128)(2,1)} %av0.1), channel_id=1, source_target_pairs={{0,4},{4,0},{1,5},{5,1},{2,6},{6,2},{3,7},{7,3},{8,12},{12,8},{9,1... | collective-permute-start | bytes 786440 | tf_op jit(solution)/shard_map/ppermute | solution.py:41
  89.0 2.9 %collective-permute-start.13 = (bf16[1024,640]{1,0:T(8,128)(2,1)}, bf16[1024,640]{1,0:T(8,128)(2,1)}, u32[]{:S(2)}, u32[]{:S(2)}) collective-permute-start(bf16[1024,640]{1,0:T(8,128)(2,1)} %constant_dynamic-update-slice_fusion.4.ka_ref), channel_id=1, source_target_pairs={{0,4},{4,0},{1,5},{5,1},{2,6},{6,2},{3,7},{7,3},{8,12},{12,8},{9,1... | collective-permute-start | bytes 3932168 | tf_op jit(solution)/shard_map/ppermute | solution.py:41
  92.4 1.4 convert_element_type.107
  98.9 1.3 add.195
  100.3 1.4 add.221.qpos_ref
  104.3 2.7 %queries.1.q_ref = bf16[1024,640]{1,0:T(8,128)(2,1)S(1)} custom-call(bf16[64,2176]{1,0:T(8,128)(2,1)S(1)} %constant_dynamic-update-slice_fusion.g0, bf16[64,2176]{1,0:T(8,128)(2,1)S(1)} %collective-permute-done.3.g1, bf16[64,2176]{1,0:T(8,128)(2,1)S(1)} %collective-permute-done.4.g2, bf16[32,2176]{1,0:T(8,128)(2,1)S(1)} %collective-permute-done.5.g3, ...), custom_call_target="tpu_custom_call" | custom-call | flops 738197504 | bytes 6000000 | tf_op jit(solution)/shard_map/queries/pallas_call | solution.py:274
  107.0 12.1 %attend.1 = bf16[256,3584]{1,0:T(8,128)(2,1)S(1)} custom-call(s32[1]{0:T(128)} %bitcast.where_ref, s32[256,1]{1,0:T(8,128)S(1)} %copy-done.3, s32[2,256]{1,0:T(2,128)S(1)} %broadcast_add_fusion.1.kpos_ref, bf16[1024,640]{1,0:T(8,128)(2,1)S(1)} %queries.1.q_ref, bf16[1024,640]{1,0:T(8,128)(2,1)} %constant_dynamic-update-slice_fusion.4.ka_ref, ...), custom_call_target="tpu_custom_call" | custom-call | flops 4294967296 | bytes 9000000 | tf_op jit(solution)/shard_map/attend/pallas_call | solution.py:288
  119.1 1.9 %collective-permute-start.16 = (bf16[64,3584]{1,0:T(8,128)(2,1)S(1)}, bf16[64,3584]{1,0:T(8,128)(2,1)S(1)}, u32[]{:S(2)}, u32[]{:S(2)}) collective-permute-start(bf16[64,3584]{1,0:T(8,128)(2,1)S(1)} %get-tuple-element.29), channel_id=1, source_target_pairs={{0,8},{8,16},{16,24},{24,32},{32,40},{40,48},{48,56},{56,64},{64,7... | collective-permute-start | bytes 1376264 | tf_op jit(solution)/shard_map/ppermute | solution.py:37
  121.1 3.4 %collective-permute-start.17 = (bf16[64,3584]{1,0:T(8,128)(2,1)S(1)}, bf16[64,3584]{1,0:T(8,128)(2,1)}, u32[]{:S(2)}, u32[]{:S(2)}) collective-permute-start(bf16[64,3584]{1,0:T(8,128)(2,1)S(1)} %get-tuple-element.30), channel_id=1, source_target_pairs={{0,120},{8,0},{16,8},{24,16},{32,24},{40,32},{48,40},{56,48},{64,5... | collective-permute-start | bytes 1376264 | tf_op jit(solution)/shard_map/ppermute | solution.py:37
  125.2 1.9 %collective-permute-start.18 = (bf16[32,3584]{1,0:T(8,128)(2,1)}, bf16[32,3584]{1,0:T(8,128)(2,1)}, u32[]{:S(2)}, u32[]{:S(2)}) collective-permute-start(bf16[32,3584]{1,0:T(8,128)(2,1)} %get-tuple-element.27), channel_id=1, source_target_pairs={{0,16},{8,24},{16,32},{24,40},{32,48},{40,56},{48,64},{56,72},{64,... | collective-permute-start | bytes 688136 | tf_op jit(solution)/shard_map/ppermute | solution.py:37
  127.1 5.5 %collective-permute-start.19 = (bf16[32,3584]{1,0:T(8,128)(2,1)S(1)}, bf16[32,3584]{1,0:T(8,128)(2,1)}, u32[]{:S(2)}, u32[]{:S(2)}) collective-permute-start(bf16[32,3584]{1,0:T(8,128)(2,1)S(1)} %get-tuple-element.28), channel_id=1, source_target_pairs={{0,112},{8,120},{16,0},{24,8},{32,16},{40,24},{48,32},{56,40},{64,... | collective-permute-start | bytes 688136 | tf_op jit(solution)/shard_map/ppermute | solution.py:37
  133.3 10.4 %collective-permute-done.18 = bf16[32,3584]{1,0:T(8,128)(2,1)} collective-permute-done((bf16[32,3584]{1,0:T(8,128)(2,1)}, bf16[32,3584]{1,0:T(8,128)(2,1)}, u32[]{:S(2)}, u32[]{:S(2)}) %collective-permute-start.18) | collective-permute-done | bytes 229408 | tf_op jit(solution)/shard_map/ppermute | solution.py:37
  145.1 4.1 %collective-permute-start.21 = (bf16[16,1792]{1,0:T(8,128)(2,1)S(1)}, bf16[16,1792]{1,0:T(8,128)(2,1)S(1)}, u32[]{:S(2)}, u32[]{:S(2)}) collective-permute-start(bf16[16,1792]{1,0:T(8,128)(2,1)S(1)} %get-tuple-element.32), channel_id=1, source_target_pairs={{0,96},{8,104},{16,112},{24,120},{32,0},{40,8},{48,16},{56,24},{64... | collective-permute-start | bytes 172040 | tf_op jit(solution)/shard_map/ppermute | solution.py:37
  149.8 5.1 %collective-permute-start.20 = (bf16[16,3584]{1,0:T(8,128)(2,1)S(1)}, bf16[16,3584]{1,0:T(8,128)(2,1)S(1)}, u32[]{:S(2)}, u32[]{:S(2)}) collective-permute-start(bf16[16,3584]{1,0:T(8,128)(2,1)S(1)} %get-tuple-element.24), channel_id=1, source_target_pairs={{0,32},{8,40},{16,48},{24,56},{32,64},{40,72},{48,80},{56,88},{64,... | collective-permute-start | bytes 344072 | tf_op jit(solution)/shard_map/ppermute | solution.py:37
  155.0 4.1 %collective-permute-start.22 = (bf16[16,3584]{1,0:T(8,128)(2,1)S(1)}, bf16[16,3584]{1,0:T(8,128)(2,1)S(1)}, u32[]{:S(2)}, u32[]{:S(2)}) collective-permute-start(bf16[16,3584]{1,0:T(8,128)(2,1)S(1)} %pad_maximum_fusion.4), channel_id=1, source_target_pairs={{0,96},{8,104},{16,112},{24,120},{32,0},{40,8},{48,16},{56,24},{64... | collective-permute-start | bytes 344072 | tf_op jit(solution)/shard_map/ppermute | solution.py:37
  159.6 7.4 %collective-permute-start.23 = (bf16[16,1792]{1,0:T(8,128)(2,1)S(1)}, bf16[16,1792]{1,0:T(8,128)(2,1)S(1)}, u32[]{:S(2)}, u32[]{:S(2)}) collective-permute-start(bf16[16,1792]{1,0:T(8,128)(2,1)S(1)} %get-tuple-element.31), channel_id=1, source_target_pairs={{0,64},{8,72},{16,80},{24,88},{32,96},{40,104},{48,112},{56,120},{... | collective-permute-start | bytes 172040 | tf_op jit(solution)/shard_map/ppermute | solution.py:37
  168.2 15.8 %collective-permute-done.23 = bf16[16,1792]{1,0:T(8,128)(2,1)S(1)} collective-permute-done((bf16[16,1792]{1,0:T(8,128)(2,1)S(1)}, bf16[16,1792]{1,0:T(8,128)(2,1)S(1)}, u32[]{:S(2)}, u32[]{:S(2)}) %collective-permute-start.23) | collective-permute-done | bytes 57376 | tf_op jit(solution)/shard_map/ppermute | solution.py:37
  (94 shorter events, 29.7 us)
Async XLA Ops:
  0.6 52.1 %copy-start.11 = (s32[16]{0:T(128)S(1)}, s32[16]{0:T(128)}, u32[]{:S(2)}) copy-start(s32[16]{0:T(128)} %constant.86.clone) | copy-start | bytes 196
  6.2 31.9 %collective-permute-start = (bf16[16,2176]{1,0:T(8,128)(2,1)S(1)}, bf16[16,2176]{1,0:T(8,128)(2,1)S(1)}, u32[]{:S(2)}, u32[]{:S(2)}) collective-permute-start(bf16[16,2176]{1,0:T(8,128)(2,1)S(1)} %get-tuple-element.5), channel_id=1, source_target_pairs={{0,32},{8,40},{16,48},{24,56},{32,64},{40,72},{48,80},{56,88},{64,... | collective-permute-start | bytes 208904 | tf_op jit(solution)/shard_map/ppermute | solution.py:37
  15.0 23.1 %collective-permute-start.1 = (bf16[16,2176]{1,0:T(8,128)(2,1)S(1)}, bf16[16,2176]{1,0:T(8,128)(2,1)S(1)}, u32[]{:S(2)}, u32[]{:S(2)}) collective-permute-start(bf16[16,2176]{1,0:T(8,128)(2,1)S(1)} %get-tuple-element.5), channel_id=1, source_target_pairs={{0,96},{8,104},{16,112},{24,120},{32,0},{40,8},{48,16},{56,24},{64... | collective-permute-start | bytes 208904 | tf_op jit(solution)/shard_map/ppermute | solution.py:37
  19.7 21.2 %collective-permute-start.2 = (bf16[16,2176]{1,0:T(8,128)(2,1)S(1)}, bf16[16,2176]{1,0:T(8,128)(2,1)S(1)}, u32[]{:S(2)}, u32[]{:S(2)}) collective-permute-start(bf16[16,2176]{1,0:T(8,128)(2,1)S(1)} %get-tuple-element.5), channel_id=1, source_target_pairs={{0,64},{8,72},{16,80},{24,88},{32,96},{40,104},{48,112},{56,120},{... | collective-permute-start | bytes 208904 | tf_op jit(solution)/shard_map/ppermute | solution.py:37
  29.9 72.5 %collective-permute-start.7 = (bf16[1536,384]{1,0:T(8,128)(2,1)}, bf16[1536,384]{1,0:T(8,128)(2,1)S(1)}, u32[]{:S(2)}, u32[]{:S(2)}) collective-permute-start(bf16[1536,384]{1,0:T(8,128)(2,1)} %wq0.1), channel_id=1, source_target_pairs={{0,4},{4,0},{1,5},{5,1},{2,6},{6,2},{3,7},{7,3},{8,12},{12,8},{9,1... | collective-permute-start | bytes 3538952 | tf_op jit(solution)/shard_map/ppermute | solution.py:41
  34.0 98.5 %all-to-all-start = ((bf16[4,4,4,640]{3,2,1,0:T(4,128)(2,1)}), bf16[4,4,4,640]{3,2,1,0:T(4,128)(2,1)S(1)}, u32[]{:S(2)}, u32[]{:S(2)}) async-start(bf16[4,4,4,640]{3,2,1,0:T(4,128)(2,1)} %broadcast_in_dim.40), calls=%async_computation | async-start | bytes 163840 | tf_op jit(solution)/shard_map/all_to_all | solution.py:46
  40.9 24.1 %collective-permute-start.3 = (bf16[64,2176]{1,0:T(8,128)(2,1)S(1)}, bf16[64,2176]{1,0:T(8,128)(2,1)S(1)}, u32[]{:S(2)}, u32[]{:S(2)}) collective-permute-start(bf16[64,2176]{1,0:T(8,128)(2,1)S(1)} %constant_dynamic-update-slice_fusion.g0), channel_id=1, source_target_pairs={{0,120},{8,0},{16,8},{24,16},{32,24},{40,32},{48,40},{56,48},{64,5... | collective-permute-start | bytes 835592 | tf_op jit(solution)/shard_map/ppermute | solution.py:37
  42.8 22.1 %collective-permute-start.4 = (bf16[64,2176]{1,0:T(8,128)(2,1)S(1)}, bf16[64,2176]{1,0:T(8,128)(2,1)S(1)}, u32[]{:S(2)}, u32[]{:S(2)}) collective-permute-start(bf16[64,2176]{1,0:T(8,128)(2,1)S(1)} %constant_dynamic-update-slice_fusion.g0), channel_id=1, source_target_pairs={{0,8},{8,16},{16,24},{24,32},{32,40},{40,48},{48,56},{56,64},{64,7... | collective-permute-start | bytes 835592 | tf_op jit(solution)/shard_map/ppermute | solution.py:37
  46.2 9.7 %collective-permute-start.5 = (bf16[32,2176]{1,0:T(8,128)(2,1)S(1)}, bf16[32,2176]{1,0:T(8,128)(2,1)S(1)}, u32[]{:S(2)}, u32[]{:S(2)}) collective-permute-start(bf16[32,2176]{1,0:T(8,128)(2,1)S(1)} %get-tuple-element.34), channel_id=1, source_target_pairs={{0,112},{8,120},{16,0},{24,8},{32,16},{40,24},{48,32},{56,40},{64,... | collective-permute-start | bytes 417800 | tf_op jit(solution)/shard_map/ppermute | solution.py:37
  50.8 9.2 %collective-permute-start.6 = (bf16[32,2176]{1,0:T(8,128)(2,1)S(1)}, bf16[32,2176]{1,0:T(8,128)(2,1)S(1)}, u32[]{:S(2)}, u32[]{:S(2)}) collective-permute-start(bf16[32,2176]{1,0:T(8,128)(2,1)S(1)} %get-tuple-element.33), channel_id=1, source_target_pairs={{0,16},{8,24},{16,32},{24,40},{32,48},{40,56},{48,64},{56,72},{64,... | collective-permute-start | bytes 417800 | tf_op jit(solution)/shard_map/ppermute | solution.py:37
  55.9 46.5 %collective-permute-start.8 = (bf16[2,128,512]{2,1,0:T(8,128)(2,1)}, bf16[2,128,512]{2,1,0:T(8,128)(2,1)}, u32[]{:S(2)}, u32[]{:S(2)}) collective-permute-start(bf16[2,128,512]{2,1,0:T(8,128)(2,1)} %ak0.1), channel_id=1, source_target_pairs={{0,4},{4,0},{1,5},{5,1},{2,6},{6,2},{3,7},{7,3},{8,12},{12,8},{9,1... | collective-permute-start | bytes 786440 | tf_op jit(solution)/shard_map/ppermute | solution.py:41
  60.0 46.9 %collective-permute-start.15 = (bf16[256,3584]{1,0:T(8,128)(2,1)}, bf16[256,3584]{1,0:T(8,128)(2,1)}, u32[]{:S(2)}, u32[]{:S(2)}) collective-permute-start(bf16[256,3584]{1,0:T(8,128)(2,1)} %op0.1), channel_id=1, source_target_pairs={{0,4},{4,0},{1,5},{5,1},{2,6},{6,2},{3,7},{7,3},{8,12},{12,8},{9,1... | collective-permute-start | bytes 5505032 | tf_op jit(solution)/shard_map/ppermute | solution.py:41
  65.0 11.2 %collective-permute-start.9 = (bf16[256,640]{1,0:T(8,128)(2,1)S(1)}, bf16[256,640]{1,0:T(8,128)(2,1)S(1)}, u32[]{:S(2)}, u32[]{:S(2)}) collective-permute-start(bf16[256,640]{1,0:T(8,128)(2,1)S(1)} %own.1), channel_id=1, source_target_pairs={{0,128},{128,256},{256,384},{1,129},{129,257},{257,385},{2,130},{1... | collective-permute-start | bytes 983048 | tf_op jit(solution)/shard_map/ppermute | solution.py:251
  66.3 12.4 %collective-permute-start.11 = (bf16[256,640]{1,0:T(8,128)(2,1)S(1)}, bf16[256,640]{1,0:T(8,128)(2,1)S(1)}, u32[]{:S(2)}, u32[]{:S(2)}) collective-permute-start(bf16[256,640]{1,0:T(8,128)(2,1)S(1)} %own.1), channel_id=1, source_target_pairs={{0,384},{128,0},{1,385},{129,1},{2,386},{130,2},{3,387},{131,3},{4... | collective-permute-start | bytes 983048 | tf_op jit(solution)/shard_map/ppermute | solution.py:252
  76.3 6.9 %collective-permute-start.10 = (bf16[128,640]{1,0:T(8,128)(2,1)S(1)}, bf16[128,640]{1,0:T(8,128)(2,1)S(1)}, u32[]{:S(2)}, u32[]{:S(2)}) collective-permute-start(bf16[128,640]{1,0:T(8,128)(2,1)S(1)} %slice.130), channel_id=1, source_target_pairs={{128,256},{256,384},{129,257},{257,385},{130,258},{258,386},{131,2... | collective-permute-start | bytes 491528 | tf_op jit(solution)/shard_map/ppermute | solution.py:253
  78.8 8.7 %collective-permute-start.12 = (bf16[128,640]{1,0:T(8,128)(2,1)S(1)}, bf16[128,640]{1,0:T(8,128)(2,1)S(1)}, u32[]{:S(2)}, u32[]{:S(2)}) collective-permute-start(bf16[128,640]{1,0:T(8,128)(2,1)S(1)} %slice.131), channel_id=1, source_target_pairs={{384,256},{0,384},{385,257},{1,385},{386,258},{2,386},{387,259},{3... | collective-permute-start | bytes 491528 | tf_op jit(solution)/shard_map/ppermute | solution.py:254
  83.1 19.3 %copy-start = (bf16[1536,384]{1,0:T(8,128)(2,1)S(1)}, bf16[1536,384]{1,0:T(8,128)(2,1)}, u32[]{:S(2)}) copy-start(bf16[1536,384]{1,0:T(8,128)(2,1)} %wq0.1) | copy-start | bytes 3538948
  83.1 23.8 %collective-permute-start.14 = (bf16[2,512,128]{2,1,0:T(8,128)(2,1)}, bf16[2,512,128]{2,1,0:T(8,128)(2,1)}, u32[]{:S(2)}, u32[]{:S(2)}) collective-permute-start(bf16[2,512,128]{2,1,0:T(8,128)(2,1)} %av0.1), channel_id=1, source_target_pairs={{0,4},{4,0},{1,5},{5,1},{2,6},{6,2},{3,7},{7,3},{8,12},{12,8},{9,1... | collective-permute-start | bytes 786440 | tf_op jit(solution)/shard_map/ppermute | solution.py:41
  89.0 18.0 %collective-permute-start.13 = (bf16[1024,640]{1,0:T(8,128)(2,1)}, bf16[1024,640]{1,0:T(8,128)(2,1)}, u32[]{:S(2)}, u32[]{:S(2)}) collective-permute-start(bf16[1024,640]{1,0:T(8,128)(2,1)} %constant_dynamic-update-slice_fusion.4.ka_ref), channel_id=1, source_target_pairs={{0,4},{4,0},{1,5},{5,1},{2,6},{6,2},{3,7},{7,3},{8,12},{12,8},{9,1... | collective-permute-start | bytes 3932168 | tf_op jit(solution)/shard_map/ppermute | solution.py:41
  102.4 0.9 copy-start.1
  103.3 0.9 copy-start.2
  104.2 2.7 %copy-start.3 = (s32[256,1]{1,0:T(8,128)S(1)}, s32[256,1]{1,0:T(8,128)}, u32[]{:S(2)}) copy-start(s32[256,1]{1,0:T(8,128)} %add.221.qpos_ref) | copy-start | bytes 3076
  104.3 2.7 %copy-start.9 = (bf16[256,3584]{1,0:T(8,128)(2,1)S(1)}, bf16[256,3584]{1,0:T(8,128)(2,1)}, u32[]{:S(2)}) copy-start(bf16[256,3584]{1,0:T(8,128)(2,1)} %op0.1) | copy-start | bytes 5505028
  119.1 14.0 %copy-start.10 = (s32[8]{0:T(128)S(1)}, s32[8]{0:T(128)}, u32[]{:S(2)}) copy-start(s32[8]{0:T(128)} %iota_add_fusion.1) | copy-start | bytes 100
  119.1 24.6 %collective-permute-start.16 = (bf16[64,3584]{1,0:T(8,128)(2,1)S(1)}, bf16[64,3584]{1,0:T(8,128)(2,1)S(1)}, u32[]{:S(2)}, u32[]{:S(2)}) collective-permute-start(bf16[64,3584]{1,0:T(8,128)(2,1)S(1)} %get-tuple-element.29), channel_id=1, source_target_pairs={{0,8},{8,16},{16,24},{24,32},{32,40},{40,48},{48,56},{56,64},{64,7... | collective-permute-start | bytes 1376264 | tf_op jit(solution)/shard_map/ppermute | solution.py:37
  121.1 22.7 %collective-permute-start.17 = (bf16[64,3584]{1,0:T(8,128)(2,1)S(1)}, bf16[64,3584]{1,0:T(8,128)(2,1)}, u32[]{:S(2)}, u32[]{:S(2)}) collective-permute-start(bf16[64,3584]{1,0:T(8,128)(2,1)S(1)} %get-tuple-element.30), channel_id=1, source_target_pairs={{0,120},{8,0},{16,8},{24,16},{32,24},{40,32},{48,40},{56,48},{64,5... | collective-permute-start | bytes 1376264 | tf_op jit(solution)/shard_map/ppermute | solution.py:37
  125.2 18.6 %collective-permute-start.18 = (bf16[32,3584]{1,0:T(8,128)(2,1)}, bf16[32,3584]{1,0:T(8,128)(2,1)}, u32[]{:S(2)}, u32[]{:S(2)}) collective-permute-start(bf16[32,3584]{1,0:T(8,128)(2,1)} %get-tuple-element.27), channel_id=1, source_target_pairs={{0,16},{8,24},{16,32},{24,40},{32,48},{40,56},{48,64},{56,72},{64,... | collective-permute-start | bytes 688136 | tf_op jit(solution)/shard_map/ppermute | solution.py:37
  127.1 16.7 %collective-permute-start.19 = (bf16[32,3584]{1,0:T(8,128)(2,1)S(1)}, bf16[32,3584]{1,0:T(8,128)(2,1)}, u32[]{:S(2)}, u32[]{:S(2)}) collective-permute-start(bf16[32,3584]{1,0:T(8,128)(2,1)S(1)} %get-tuple-element.28), channel_id=1, source_target_pairs={{0,112},{8,120},{16,0},{24,8},{32,16},{40,24},{48,32},{56,40},{64,... | collective-permute-start | bytes 688136 | tf_op jit(solution)/shard_map/ppermute | solution.py:37
  145.1 9.9 %collective-permute-start.21 = (bf16[16,1792]{1,0:T(8,128)(2,1)S(1)}, bf16[16,1792]{1,0:T(8,128)(2,1)S(1)}, u32[]{:S(2)}, u32[]{:S(2)}) collective-permute-start(bf16[16,1792]{1,0:T(8,128)(2,1)S(1)} %get-tuple-element.32), channel_id=1, source_target_pairs={{0,96},{8,104},{16,112},{24,120},{32,0},{40,8},{48,16},{56,24},{64... | collective-permute-start | bytes 172040 | tf_op jit(solution)/shard_map/ppermute | solution.py:37
  149.8 17.3 %collective-permute-start.20 = (bf16[16,3584]{1,0:T(8,128)(2,1)S(1)}, bf16[16,3584]{1,0:T(8,128)(2,1)S(1)}, u32[]{:S(2)}, u32[]{:S(2)}) collective-permute-start(bf16[16,3584]{1,0:T(8,128)(2,1)S(1)} %get-tuple-element.24), channel_id=1, source_target_pairs={{0,32},{8,40},{16,48},{24,56},{32,64},{40,72},{48,80},{56,88},{64,... | collective-permute-start | bytes 344072 | tf_op jit(solution)/shard_map/ppermute | solution.py:37
  155.0 12.1 %collective-permute-start.22 = (bf16[16,3584]{1,0:T(8,128)(2,1)S(1)}, bf16[16,3584]{1,0:T(8,128)(2,1)S(1)}, u32[]{:S(2)}, u32[]{:S(2)}) collective-permute-start(bf16[16,3584]{1,0:T(8,128)(2,1)S(1)} %pad_maximum_fusion.4), channel_id=1, source_target_pairs={{0,96},{8,104},{16,112},{24,120},{32,0},{40,8},{48,16},{56,24},{64... | collective-permute-start | bytes 344072 | tf_op jit(solution)/shard_map/ppermute | solution.py:37
  159.6 24.3 %collective-permute-start.23 = (bf16[16,1792]{1,0:T(8,128)(2,1)S(1)}, bf16[16,1792]{1,0:T(8,128)(2,1)S(1)}, u32[]{:S(2)}, u32[]{:S(2)}) collective-permute-start(bf16[16,1792]{1,0:T(8,128)(2,1)S(1)} %get-tuple-element.31), channel_id=1, source_target_pairs={{0,64},{8,72},{16,80},{24,88},{32,96},{40,104},{48,112},{56,120},{... | collective-permute-start | bytes 172040 | tf_op jit(solution)/shard_map/ppermute | solution.py:37
  (5 other events, 3.4 us)

commit v5 on v3

--- a/solution.py
+++ b/solution.py
@@ -14,17 +14,7 @@
 Z = ("zh", "zl")
 TP = ("zh", "zl", "core")
 NEG = -1e30
-
-
-def rope_tables(where_at, full_width):
-    half = full_width // 2
-    frequency = 10000.0 ** (-(jnp.arange(half).astype(F32) * 2.0 / full_width))
-    angles = where_at.astype(F32)[:, None] * frequency[None, :]
-    cosine, sine = jnp.cos(angles), jnp.sin(angles)
-    return (
-        jnp.concatenate([cosine, cosine], -1),
-        jnp.concatenate([-sine, sine], -1),
-    )
+STEPS = [4 * e + d for d in (0, 1, -1) for e in (-1, 0, 1, 2)] + [2, 6, -6, -2]
 
 
 def swap_halves(v):
@@ -52,36 +42,66 @@
     return jnp.asarray(np.concatenate([f, f]).astype(np.float32))[None]
 
 
-def key_kernel(base_ref, owner_ref, slot_ref, q_ref, x_ref, gain_ref, freq_ref, all_ref, out_ref, *, lat, part, page_len, slots):
+def turn(v, where_at, freq):
+    angle = where_at.astype(F32) * freq
+    lane = lax.broadcasted_iota(jnp.int32, v.shape, 1)
+    sine = jnp.sin(angle)
+    sine = jnp.where(lane < v.shape[1] // 2, -sine, sine)
+    return v * jnp.cos(angle) + swap_halves(v) * sine
+
+
+def key_kernel(base_ref, owner_ref, slot_ref, x_ref, gain_ref, freq_ref, out_ref, *, lat, part, page_len, slots):
     x = x_ref[...].astype(F32)
     n = x.shape[0]
     latent, rot = x[:, :lat], x[:, lat:]
     norm = lax.rsqrt(jnp.mean(latent * latent, -1, keepdims=True) + 1e-06)
     out_ref[:, :lat] = (latent * norm * gain_ref[...]).astype(BF)
     row = lax.broadcasted_iota(jnp.int32, rot.shape, 0)
-    lane = lax.broadcasted_iota(jnp.int32, rot.shape, 1)
     where_at = base_ref[0] + row // part * page_len + row % part
-    angle = where_at.astype(F32) * freq_ref[...]
-    sine = jnp.sin(angle)
-    sine = jnp.where(lane < rot.shape[1] // 2, -sine, sine)
+    turned = turn(rot, where_at, freq_ref[...])
     code = jnp.zeros(rot.shape, F32)
     for p in range(n // part):
         here = (owner_ref[0, p] * slots + slot_ref[0, p]).astype(F32)
         code = jnp.where(row // part == p, here, code)
-    turned = rot * jnp.cos(angle) + swap_halves(rot) * sine
     out_ref[:, lat:] = jnp.concatenate([turned, code], -1).astype(BF)
-    ql = q_ref.shape[1]
-    all_ref[:, :ql] = q_ref[...]
-    all_ref[:, ql:] = out_ref[...]
-
-
-def query_kernel(g, wq0, wq1, ak0, ak1, cos_ref, sin_ref, out_ref, *, nope, rope):
-    x = g[:, : wq0.shape[0]]
+
+
+def query_where(idx, z, core, qrows, chips):
+    blk = idx // qrows
+    off = jnp.zeros_like(idx)
+    for i, step in enumerate(STEPS):
+        off = jnp.where(blk == i, step % chips, off)
+    return lax.rem(z + off, chips) * (2 * qrows) + core * qrows + idx % qrows
+
+
+def pack_kernel(*refs):
+    out_ref, at = refs[-1], 0
+    for r in refs[:-1]:
+        n = r.shape[0]
+        out_ref[at : at + n, :] = r[...]
+        at += n
+
+
+def query_kernel(
+    where_ref, g_ref, wq_ref, ak0, ak1, freq_ref, out_ref, x_ref, *, nope, rope, qrows, chips
+):
+    chain, z, core = where_ref[0], where_ref[1], where_ref[2]
+    for i, step in enumerate(STEPS):
+        at = lax.rem(z + step % chips, chips)
+        x_ref[i * qrows : (i + 1) * qrows, :] = g_ref[pl.ds(pl.multiple_of(at * qrows, qrows), qrows), :]
+    x = x_ref[...]
     rows = x.shape[0]
     lat = ak0.shape[-1]
+    idx = lax.broadcasted_iota(jnp.int32, (rows, rope), 0)
+    place = chain * (chips * 2 * qrows) + query_where(idx, z, core, qrows, chips)
+    angle = place.astype(F32) * freq_ref[...]
+    lane = lax.broadcasted_iota(jnp.int32, angle.shape, 1)
+    sine = jnp.sin(angle)
+    sine = jnp.where(lane < rope // 2, -sine, sine)
+    cosine = jnp.cos(angle)
     head = 0
-    for wq, ak in ((wq0, ak0), (wq1, ak1)):
-        q = jnp.dot(x, wq[...], preferred_element_type=F32).astype(BF)
+    for side, ak in ((core, ak0), (1 - core, ak1)):
+        q = jnp.dot(x, wq_ref[side], preferred_element_type=F32).astype(BF)
         for h in range(ak.shape[0]):
             base = h * (nope + rope)
             r0 = head * rows
@@ -89,7 +109,7 @@
                 q[:, base : base + nope], ak[h], preferred_element_type=F32
             ).astype(BF)
             rot = q[:, base + nope : base + nope + rope].astype(F32)
-            turned = rot * cos_ref[...] + swap_halves(rot) * sin_ref[...]
+            turned = rot * cosine + swap_halves(rot) * sine
             out_ref[r0 : r0 + rows, lat:] = jnp.concatenate(
                 [turned, jnp.zeros_like(turned)], -1
             ).astype(BF)
@@ -97,25 +117,16 @@
 
 
 def attend_kernel(
-    where_ref, q_ref, ka_ref, kb_ref, av0, av1, op0, op1, out_ref,
-    s_ref, top_ref, l_ref, acc_ref, ho_ref, *, rows, lat, scale, lay,
+    where_ref, q_ref, ka_ref, kb_ref, av0, av1, op_ref, out_ref,
+    s_ref, top_ref, l_ref, acc_ref, ho_ref, *, rows, lat, scale, nch, chips, qrows, part,
 ):
-    chain, core = where_ref[0], where_ref[1]
-    nch, nzh, nzl, part, qrows, pages = lay
+    chain, z, core = where_ref[0], where_ref[1], where_ref[2]
     s2 = scale * LOG2E
     vh = av0.shape[-1]
     heads = q_ref.shape[0] // rows
     n = ka_ref.shape[0] // nch
     nt = (((1,), (1,)), ((), ()))
 
-    def key_pos(idx, kcore):
-        z = idx // (pages * part)
-        page = (idx // part) % pages
-        return page * (nzh * nzl * 2 * part) + z * (2 * part) + kcore * part + idx % part
-
-    def query_pos(idx):
-        return idx // qrows * (2 * qrows) + core * qrows + idx % qrows
-
     def lanes(x, op):
         out = x[:, :128]
         for c in range(128, x.shape[1], 128):
@@ -124,9 +135,11 @@
 
     def score(back):
         if back == 0:
-            qp = query_pos(lax.broadcasted_iota(jnp.int32, (rows, 1), 0))
-            kidx = lax.broadcasted_iota(jnp.int32, (1, n), 1)
-            ok = (key_pos(kidx, core) <= qp, key_pos(kidx, 1 - core) <= qp)
+            idx = lax.broadcasted_iota(jnp.int32, (rows, 1), 0)
+            qpos = query_where(idx, z, core, qrows, chips)
+            idx = lax.broadcasted_iota(jnp.int32, (1, n), 1)
+            kpos = (idx % qrows) // part * (chips * 2 * part) + idx // qrows * (2 * part) + idx % part
+            ok = [kpos + i * part <= qpos for i in (core, 1 - core)]
         for h in range(heads):
             q = q_ref[h * rows : (h + 1) * rows, :]
             for i, k_ref in enumerate((ka_ref, kb_ref)):
@@ -173,13 +186,13 @@
         av = (av0 if h < per else av1)[h % per]
         ho_ref[:, h * vh : (h + 1) * vh] = jnp.dot(mixed, av, preferred_element_type=F32).astype(BF)
     ho = ho_ref[...]
-    k = op0.shape[0]
+    k = op_ref.shape[1]
     width = out_ref.shape[1]
     cut = 512 if width % 512 == 0 else width
     for c in range(0, width, cut):
         out_ref[:, c : c + cut] = (
-            jnp.dot(ho[:, :k], op0[:, c : c + cut], preferred_element_type=F32)
-            + jnp.dot(ho[:, k:], op1[:, c : c + cut], preferred_element_type=F32)
+            jnp.dot(ho[:, :k], op_ref[core, :, c : c + cut], preferred_element_type=F32)
+            + jnp.dot(ho[:, k:], op_ref[1 - core, :, c : c + cut], preferred_element_type=F32)
         ).astype(BF)
 
 
@@ -209,60 +222,66 @@
     raw = jnp.concatenate(
         [latent_rows[0].reshape(pages * part, lat), rope_keys[0].reshape(pages * part, rope)], -1
     )
-    merged, keys = pl.pallas_call(
+    rows = qrows * nzh * nzl
+    kw = lat + 2 * rope
+    heads = 2 * heads_here
+    z = zh * nzl + zl
+    where = jnp.stack([chain, z, core]).astype(jnp.int32)
+    keys = pl.pallas_call(
         functools.partial(key_kernel, lat=lat, part=part, page_len=part * tp_count, slots=slots),
-        out_shape=(
-            jax.ShapeDtypeStruct((qrows, ql + lat + 2 * rope), BF),
-            jax.ShapeDtypeStruct((pages * part, lat + 2 * rope), BF),
-        ),
-        in_specs=[smem] * 3 + [vm] * 4,
-        out_specs=(vm, vm),
+        out_shape=jax.ShapeDtypeStruct((pages * part, kw), BF),
+        in_specs=[smem] * 3 + [vm] * 3,
+        out_specs=vm,
         compiler_params=room(4),
         name="keys",
     )(
         (chain * block_len + tp_index * part).astype(jnp.int32)[None],
-        page_owner, page_slot, query_comp[0], raw, latent_gain[None], frequencies(rope),
+        page_owner, page_slot, raw, latent_gain[None], frequencies(rope),
     )
 
-    whole = lax.all_gather(merged, Z, axis=0, tiled=True)
-    own = whole[:, ql:]
+    wq = lax.all_gather(query_up, "core", axis=0, tiled=False)
+    op = lax.all_gather(out_proj, "core", axis=0, tiled=False)
+    ak1 = swap_core(absorb_key)
+    av1 = swap_core(absorb_value)
+
+    own = lax.all_gather(keys, Z, axis=0, tiled=True)
     backs = [
         lax.ppermute(own, "chain", [(i, i + k) for i in range(nch - k)]) for k in range(1, nch)
     ]
-    mine = jnp.concatenate([own] + backs, 0)
+    held = lax.optimization_barrier((query_comp[0], own))[0]
+    qg = lax.all_gather(held, Z, axis=0, tiled=True)
+    qg, *backs = lax.optimization_barrier((qg, *backs))
+    mine = pl.pallas_call(
+        pack_kernel,
+        out_shape=jax.ShapeDtypeStruct((nch * rows, kw), BF),
+        in_specs=[vm] * nch,
+        out_specs=vm,
+        compiler_params=room(4),
+        name="pack",
+    )(own, *backs)
     other = swap_core(mine)
 
-    wq1 = swap_core(query_up)
-    ak1 = swap_core(absorb_key)
-    av1 = swap_core(absorb_value)
-    op1 = swap_core(out_proj)
-
-    rows = qrows * nzh * nzl
-    idx = jnp.arange(rows, dtype=jnp.int32)
-    query_where = chain * block_len + idx // qrows * (2 * qrows) + core * qrows + idx % qrows
-    qcos, qsin = rope_tables(query_where, rope)
-    heads = 2 * heads_here
-    where = jnp.stack([chain, core]).astype(jnp.int32)
     q = pl.pallas_call(
-        functools.partial(query_kernel, nope=nope, rope=rope),
-        out_shape=jax.ShapeDtypeStruct((heads * rows, lat + 2 * rope), BF),
-        in_specs=[vm] * 7,
+        functools.partial(query_kernel, nope=nope, rope=rope, qrows=qrows, chips=nzh * nzl),
+        out_shape=jax.ShapeDtypeStruct((heads * rows, kw), BF),
+        in_specs=[smem] + [vm] * 5,
         out_specs=vm,
+        scratch_shapes=[pltpu.VMEM((rows, ql), BF)],
         compiler_params=room(12),
         cost_estimate=pl.CostEstimate(
             flops=2 * rows * heads * (nope + rope) * ql + 2 * rows * heads * nope * lat,
             bytes_accessed=6000000, transcendentals=0,
         ),
         name="queries",
-    )(whole, query_up, wq1, absorb_key, ak1, qcos, qsin)
+    )(where, qg, wq, absorb_key, ak1, frequencies(rope))
 
     partial = pl.pallas_call(
         functools.partial(
             attend_kernel, rows=rows, lat=lat, scale=(nope + rope) ** -0.5,
-            lay=(nch, nzh, nzl, part, qrows, pages),
+            nch=nch, chips=nzh * nzl, qrows=qrows, part=part,
         ),
         out_shape=jax.ShapeDtypeStruct((rows, width), BF),
-        in_specs=[smem] + [vm] * 7,
+        in_specs=[smem] + [vm] * 6,
         out_specs=vm,
         scratch_shapes=[
             pltpu.VMEM((heads, rows, nch * block_len), F32),
@@ -277,10 +296,32 @@
             transcendentals=rows * heads * nch * block_len,
         ),
         name="attend",
-    )(where, q, mine, other, absorb_value, av1, out_proj, op1)
-
-    layer_output = lax.psum_scatter(partial, Z, scatter_dimension=0, tiled=True)[None]
-
+    )(where, q, mine, other, absorb_value, av1, op)
+
+    n = nzh * qrows
+    up2 = shift_z(partial[3 * n : 3 * n + n // 2], 2)
+    down2 = shift_z(partial[3 * n + n // 2 :], -2)
+    up = shift_z(partial[n : 2 * n], 1)
+    down = shift_z(partial[2 * n : 3 * n], -1)
+
+    def near(e):
+        at = slice((e + 1) * qrows, (e + 2) * qrows)
+        return partial[at].astype(F32) + up[at].astype(F32) + down[at].astype(F32)
+
+    cut = width // 2
+    far = near(2).astype(BF)
+    around = shift_z(far[:, cut:], -nzl)
+    direct = shift_z(far[:, :cut], 2 * nzl)
+    ahead = shift_z((near(1) + up2[qrows:].astype(F32)).astype(BF), nzl)
+    behind = near(-1) + down2[:qrows].astype(F32)
+    behind = jnp.concatenate([behind[:, :cut], behind[:, cut:] + around.astype(F32)], -1)
+    behind = shift_z(behind.astype(BF), -nzl)
+    total = near(0) + up2[:qrows].astype(F32) + down2[qrows:].astype(F32)
+    total = total + ahead.astype(F32) + behind.astype(F32)
+    total = jnp.concatenate([total[:, :cut] + direct.astype(F32), total[:, cut:]], -1)
+    layer_output = total.astype(BF)[None]
+
+    keys = lax.optimization_barrier((keys, partial))[0]
     page = spread(keys.reshape(pages, part, -1), "dec")
     came = page[:, :, 0, lat + rope].reshape(-1).astype(jnp.int32)
     take = (came[None, :] == dec * slots + jnp.arange(slots, dtype=jnp.int32)[:, None]).astype(BF)

time: 208 us -> 185 us (0.89); the launches traced: 207 us -> 182 us
  waiting for transfers between devices: 147 us -> 20.9 us
  blocking collectives: 0 us -> 67.7 us
  starting transfers between devices: 18.9 us -> 50.5 us
  local copies, waits for them, and re-layouts: 7.19 us -> 10.6 us
  Pallas kernels: 17.3 us -> 14.1 us
    all_gather x1 -> x2, waiting for transfers between devices: 73.8 us -> 0.01 us  [the longest x1 0.01 us: local(): wq = lax.all_gather(query_up, 'core', axis=0, tiled=False)]
    all_gather x0 -> x2, blocking collectives: none -> 67.7 us  [the longest x1 37.4 us: local(): own = lax.all_gather(keys, Z, axis=0, tiled=True)]
    reduce_scatter x1 -> x0, waiting for transfers between devices: 56.5 us -> none  [local(): lax.psum_scatter(partial, Z, scatter_dimension=0, tiled=True)[None]]
    ppermute x0 -> x8, starting transfers between devices: none -> 36.1 us  [shift_z(): return lax.ppermute(x, Z, [(i, (i + step) % n) for i in range(n)])]
    ppermute x0 -> x8, waiting for transfers between devices: none -> 19.5 us  [shift_z(): return lax.ppermute(x, Z, [(i, (i + step) % n) for i in range(n)])]
    ppermute x3, waiting for transfers between devices: 11.4 us -> 0.01 us  [local(): lax.ppermute(own, 'chain', [(i, i + k) for i in range(nch - k)])]
    all_to_all x1, waiting for transfers between devices: 5.71 us -> 0.01 us  [spread(): lax.all_to_all(jnp.broadcast_to(x[None], (n,) + x.shape), axis, 0, 0, til...]
    ppermute x5 -> x3, starting transfers between devices: 10.6 us -> 6.25 us  [swap_core(): return lax.ppermute(x, 'core', [(0, 1), (1, 0)])]
  transfers between devices with their start and end apart: 11 -> 17, of which waited for: 6 -> 5; matrix products, arithmetic and copies ran while one was open for 2% -> 2% of each run, Pallas kernels for 2% -> 2%
where the time goes in v5:
time: 185 us; the launch traced here: 182 us
  blocking collectives  67.7 us (37%)
  starting transfers between devices  50.5 us (27%)
  waiting for transfers between devices  20.9 us (11%)
  between operations  14.5 us (8%)
  Pallas kernels  14.1 us (8%)
  local copies, waits for them, and re-layouts  10.6 us (6%)
  other arithmetic  3.62 us (2%)
    all_gather x1, blocking collectives, local(): own = lax.all_gather(keys, Z, axis=0, tiled=True)  37.4 us
    ppermute x8, starting transfers between devices, shift_z(): return lax.ppermute(x, Z, [(i, (i + step) % n) for i in range(n)])  36.1 us
    all_gather x1, blocking collectives, local(): qg = lax.all_gather(held, Z, axis=0, tiled=True)  30.3 us
    ppermute x8, waiting for transfers between devices, shift_z(): return lax.ppermute(x, Z, [(i, (i + step) % n) for i in range(n)])  19.5 us
    pallas_call x1, Pallas kernels, local(): pl.pallas_call(functools.partial(attend_kernel, rows=rows, lat=lat, scale...  11 us
    unnamed x32, local copies, waits for them, and re-layouts  9.02 us
    ppermute x3, starting transfers between devices, swap_core(): return lax.ppermute(x, 'core', [(0, 1), (1, 0)])  6.25 us
    all_to_all x1, starting transfers between devices, spread(): lax.all_to_all(jnp.broadcast_to(x[None], (n,) + x.shape), axis, 0, 0, til...  4.29 us
  transfers between devices with their start and end apart: 17, of which 5 were waited for; matrix products, arithmetic and copies ran while one was open for 2% of the time, Pallas kernels for 2%

profile of v5, /device:TPU:24, one launch (start us, length us, event | category | flops | bytes accessed | tf_op | source)
XLA Modules:
  0.0 182.1 jit_solution(14889019170524352141)
XLA Ops:
  9.5 37.4 %all_gather.18.refs_0_ = bf16[256,640]{1,0:T(8,128)(2,1)S(1)} all-gather(bf16[16,640]{1,0:T(8,128)(2,1)S(1)} %keys.1), channel_id=1, replica_groups=mesh['chain'=4,'zh'=4,'zl'=4,'core'=2,'dec'=4] {'zh','zl'}, dimensions={0}, use_global_device_ids=true | all-gather | bytes 348160 | tf_op jit(solution)/shard_map/all_gather | solution.py:247
  46.9 1.3 collective-permute-start
  48.2 1.3 collective-permute-start.1
  49.5 1.3 collective-permute-start.2
  50.8 30.3 %all_gather.19.g_ref = bf16[256,1536]{1,0:T(8,128)(2,1)S(1)} all-gather(bf16[16,1536]{1,0:T(8,128)(2,1)S(1)} %bitcast.25), channel_id=1, replica_groups=mesh['chain'=4,'zh'=4,'zl'=4,'core'=2,'dec'=4] {'zh','zl'}, dimensions={0}, use_global_device_ids=true | all-gather | bytes 835584 | tf_op jit(solution)/shard_map/all_gather | solution.py:252
  81.2 1.9 %collective-permute-start.4 = (bf16[1024,640]{1,0:T(8,128)(2,1)S(1)}, bf16[1024,640]{1,0:T(8,128)(2,1)}, u32[]{:S(2)}, u32[]{:S(2)}) collective-permute-start(bf16[1024,640]{1,0:T(8,128)(2,1)S(1)} %pack.1.ka_ref), channel_id=1, source_target_pairs={{0,4},{4,0},{1,5},{5,1},{2,6},{6,2},{3,7},{7,3},{8,12},{12,8},{9,1... | collective-permute-start | bytes 3932168 | tf_op jit(solution)/shard_map/ppermute | solution.py:31
  83.1 2.4 %collective-permute-start.3 = (bf16[2,128,512]{2,1,0:T(8,128)(2,1)S(1)}, bf16[2,128,512]{2,1,0:T(8,128)(2,1)S(1)}, u32[]{:S(2)}, u32[]{:S(2)}) collective-permute-start(bf16[2,128,512]{2,1,0:T(8,128)(2,1)S(1)} %copy-done.3), channel_id=1, source_target_pairs={{0,4},{4,0},{1,5},{5,1},{2,6},{6,2},{3,7},{7,3},{8,12},{12,8},{9,1... | collective-permute-start | bytes 786440 | tf_op jit(solution)/shard_map/ppermute | solution.py:31
  85.6 1.9 %collective-permute-start.5 = (bf16[2,512,128]{2,1,0:T(8,128)(2,1)S(1)}, bf16[2,512,128]{2,1,0:T(8,128)(2,1)S(1)}, u32[]{:S(2)}, u32[]{:S(2)}) collective-permute-start(bf16[2,512,128]{2,1,0:T(8,128)(2,1)S(1)} %copy-done.9), channel_id=1, source_target_pairs={{0,4},{4,0},{1,5},{5,1},{2,6},{6,2},{3,7},{7,3},{8,12},{12,8},{9,1... | collective-permute-start | bytes 786440 | tf_op jit(solution)/shard_map/ppermute | solution.py:31
  87.6 1.7 copy-done
  89.3 2.4 %queries.1.q_ref = bf16[1024,640]{1,0:T(8,128)(2,1)S(1)} custom-call(s32[3]{0:T(128)S(1)} %pad_add_fusion.where_ref, bf16[256,1536]{1,0:T(8,128)(2,1)S(1)} %all_gather.19.g_ref, bf16[2,1536,384]{2,1,0:T(8,128)(2,1)S(1)} %bitcast.21, bf16[2,128,512]{2,1,0:T(8,128)(2,1)S(1)} %copy-done.3, bf16[2,128,512]{2,1,0:T(8,128)(2,1)S(1)} %collective-permute-done.3.ak1, ...), custom_call_target="tpu_custom_call" | custom-call | flops 738197504 | bytes 6000000 | tf_op jit(solution)/shard_map/queries/pallas_call | solution.py:264
  91.7 1.1 copy-done.1
  92.7 0.7 copy-done.10
  93.5 1.3 copy-done.2
  94.8 2.0 %copy-done.8 = bf16[512,3584]{1,0:T(8,128)(2,1)S(1)} copy-done((bf16[512,3584]{1,0:T(8,128)(2,1)S(1)}, bf16[512,3584]{1,0:T(8,128)(2,1)}, u32[]{:S(2)}) %copy-start.8) | copy-done | bytes 3670040
  96.8 0.9 copy-done.11
  97.8 11.0 %attend.1 = bf16[256,3584]{1,0:T(8,128)(2,1)S(1)} custom-call(s32[3]{0:T(128)S(1)} %pad_add_fusion.where_ref, bf16[1024,640]{1,0:T(8,128)(2,1)S(1)} %copy-done.2, bf16[1024,640]{1,0:T(8,128)(2,1)S(1)} %pack.1.ka_ref, bf16[1024,640]{1,0:T(8,128)(2,1)} %collective-permute-done.4.kb_ref, bf16[2,512,128]{2,1,0:T(8,128)(2,1)S(1)} %copy-done.9, ...), custom_call_target="tpu_custom_call" | custom-call | flops 4294967296 | bytes 9000000 | tf_op jit(solution)/shard_map/attend/pallas_call | solution.py:278
  109.5 4.3 %all-to-all-start = ((bf16[4,4,4,640]{3,2,1,0:T(4,128)(2,1)}), bf16[4,4,4,640]{3,2,1,0:T(4,128)(2,1)S(1)}, u32[]{:S(2)}, u32[]{:S(2)}) async-start(bf16[4,4,4,640]{3,2,1,0:T(4,128)(2,1)} %broadcast_in_dim.33), calls=%async_computation | async-start | bytes 163840 | tf_op jit(solution)/shard_map/all_to_all | solution.py:36
  113.8 3.7 %collective-permute-start.6 = (bf16[64,3584]{1,0:T(8,128)(2,1)S(1)}, bf16[64,3584]{1,0:T(8,128)(2,1)S(1)}, u32[]{:S(2)}, u32[]{:S(2)}) collective-permute-start(bf16[64,3584]{1,0:T(8,128)(2,1)S(1)} %get-tuple-element.29), channel_id=1, source_target_pairs={{0,8},{8,16},{16,24},{24,32},{32,40},{40,48},{48,56},{56,64},{64,7... | collective-permute-start | bytes 1376264 | tf_op jit(solution)/shard_map/ppermute | solution.py:27
  117.5 3.3 %collective-permute-start.7 = (bf16[64,3584]{1,0:T(8,128)(2,1)S(1)}, bf16[64,3584]{1,0:T(8,128)(2,1)}, u32[]{:S(2)}, u32[]{:S(2)}) collective-permute-start(bf16[64,3584]{1,0:T(8,128)(2,1)S(1)} %get-tuple-element.30), channel_id=1, source_target_pairs={{0,120},{8,0},{16,8},{24,16},{32,24},{40,32},{48,40},{56,48},{64,5... | collective-permute-start | bytes 1376264 | tf_op jit(solution)/shard_map/ppermute | solution.py:27
  120.9 0.7 fusion.10
  121.6 2.0 %collective-permute-start.8 = (bf16[32,3584]{1,0:T(8,128)(2,1)}, bf16[32,3584]{1,0:T(8,128)(2,1)}, u32[]{:S(2)}, u32[]{:S(2)}) collective-permute-start(bf16[32,3584]{1,0:T(8,128)(2,1)} %get-tuple-element.27), channel_id=1, source_target_pairs={{0,16},{8,24},{16,32},{24,40},{32,48},{40,56},{48,64},{56,72},{64,... | collective-permute-start | bytes 688136 | tf_op jit(solution)/shard_map/ppermute | solution.py:27
  123.6 6.0 %collective-permute-start.9 = (bf16[32,3584]{1,0:T(8,128)(2,1)S(1)}, bf16[32,3584]{1,0:T(8,128)(2,1)}, u32[]{:S(2)}, u32[]{:S(2)}) collective-permute-start(bf16[32,3584]{1,0:T(8,128)(2,1)S(1)} %get-tuple-element.28), channel_id=1, source_target_pairs={{0,112},{8,120},{16,0},{24,8},{32,16},{40,24},{48,32},{56,40},{64,... | collective-permute-start | bytes 688136 | tf_op jit(solution)/shard_map/ppermute | solution.py:27
  130.3 6.6 %collective-permute-done.8 = bf16[32,3584]{1,0:T(8,128)(2,1)} collective-permute-done((bf16[32,3584]{1,0:T(8,128)(2,1)}, bf16[32,3584]{1,0:T(8,128)(2,1)}, u32[]{:S(2)}, u32[]{:S(2)}) %collective-permute-start.8) | collective-permute-done | bytes 229408 | tf_op jit(solution)/shard_map/ppermute | solution.py:27
  136.9 4.7 %collective-permute-done.9 = bf16[32,3584]{1,0:T(8,128)(2,1)} collective-permute-done((bf16[32,3584]{1,0:T(8,128)(2,1)S(1)}, bf16[32,3584]{1,0:T(8,128)(2,1)}, u32[]{:S(2)}, u32[]{:S(2)}) %collective-permute-start.9) | collective-permute-done | bytes 229408 | tf_op jit(solution)/shard_map/ppermute | solution.py:27
  141.6 1.3 add_convert_fusion.1
  142.9 5.5 %collective-permute-start.11 = (bf16[16,1792]{1,0:T(8,128)(2,1)S(1)}, bf16[16,1792]{1,0:T(8,128)(2,1)S(1)}, u32[]{:S(2)}, u32[]{:S(2)}) collective-permute-start(bf16[16,1792]{1,0:T(8,128)(2,1)S(1)} %get-tuple-element.32), channel_id=1, source_target_pairs={{0,96},{8,104},{16,112},{24,120},{32,0},{40,8},{48,16},{56,24},{64... | collective-permute-start | bytes 172040 | tf_op jit(solution)/shard_map/ppermute | solution.py:27
  149.0 4.3 %collective-permute-start.10 = (bf16[16,3584]{1,0:T(8,128)(2,1)S(1)}, bf16[16,3584]{1,0:T(8,128)(2,1)S(1)}, u32[]{:S(2)}, u32[]{:S(2)}) collective-permute-start(bf16[16,3584]{1,0:T(8,128)(2,1)S(1)} %get-tuple-element.24), channel_id=1, source_target_pairs={{0,32},{8,40},{16,48},{24,56},{32,64},{40,72},{48,80},{56,88},{64,... | collective-permute-start | bytes 344072 | tf_op jit(solution)/shard_map/ppermute | solution.py:27
  153.9 4.9 %collective-permute-start.12 = (bf16[16,3584]{1,0:T(8,128)(2,1)S(1)}, bf16[16,3584]{1,0:T(8,128)(2,1)S(1)}, u32[]{:S(2)}, u32[]{:S(2)}) collective-permute-start(bf16[16,3584]{1,0:T(8,128)(2,1)S(1)} %pad_maximum_fusion), channel_id=1, source_target_pairs={{0,96},{8,104},{16,112},{24,120},{32,0},{40,8},{48,16},{56,24},{64... | collective-permute-start | bytes 344072 | tf_op jit(solution)/shard_map/ppermute | solution.py:27
  159.4 6.5 %collective-permute-start.13 = (bf16[16,1792]{1,0:T(8,128)(2,1)S(1)}, bf16[16,1792]{1,0:T(8,128)(2,1)S(1)}, u32[]{:S(2)}, u32[]{:S(2)}) collective-permute-start(bf16[16,1792]{1,0:T(8,128)(2,1)S(1)} %get-tuple-element.31), channel_id=1, source_target_pairs={{0,64},{8,72},{16,80},{24,88},{32,96},{40,104},{48,112},{56,120},{... | collective-permute-start | bytes 172040 | tf_op jit(solution)/shard_map/ppermute | solution.py:27
  165.9 1.3 collective-permute-done.12
  167.2 1.1 convert_add_fusion
  168.3 6.3 %collective-permute-done.13 = bf16[16,1792]{1,0:T(8,128)(2,1)S(1)} collective-permute-done((bf16[16,1792]{1,0:T(8,128)(2,1)S(1)}, bf16[16,1792]{1,0:T(8,128)(2,1)S(1)}, u32[]{:S(2)}, u32[]{:S(2)}) %collective-permute-start.13) | collective-permute-done | bytes 57376 | tf_op jit(solution)/shard_map/ppermute | solution.py:27
  (64 shorter events, 6.4 us)
Async XLA Ops:
  7.2 1.6 copy-start.5
  7.2 1.6 copy-start.13
  7.2 1.6 copy-start.14
  7.2 1.6 copy-start.4
  7.2 1.6 copy-start.6
  7.2 1.6 copy-start.7
  7.2 43.5 %copy-start.12 = (bf16[1,16,1536]{2,1,0:T(8,128)(2,1)S(1)}, bf16[1,16,1536]{2,1,0:T(8,128)(2,1)}, u32[]{:S(2)}) copy-start(bf16[1,16,1536]{2,1,0:T(8,128)(2,1)} %param.12) | copy-start | bytes 147460
  7.2 80.4 %all-gather.5.cloned.1.call-start = ((), (), s32[]{:S(2)}) async-start(), calls=%async_computation.1 | async-start | bytes 3538944 | tf_op jit(solution)/shard_map/all_gather | solution.py:242
  8.0 85.5 %all-gather.7.cloned.1.call-start = ((), (), s32[]{:S(2)}) async-start(), calls=%async_computation.2 | async-start | bytes 5505024 | tf_op jit(solution)/shard_map/all_gather | solution.py:243
  9.5 73.7 %copy-start.3 = (bf16[2,128,512]{2,1,0:T(8,128)(2,1)S(1)}, bf16[2,128,512]{2,1,0:T(8,128)(2,1)}, u32[]{:S(2)}) copy-start(bf16[2,128,512]{2,1,0:T(8,128)(2,1)} %ak0.1) | copy-start | bytes 786436
  9.5 76.1 %copy-start.9 = (bf16[2,512,128]{2,1,0:T(8,128)(2,1)S(1)}, bf16[2,512,128]{2,1,0:T(8,128)(2,1)}, u32[]{:S(2)}) copy-start(bf16[2,512,128]{2,1,0:T(8,128)(2,1)} %av0.1) | copy-start | bytes 786436
  46.9 34.2 %collective-permute-start = (bf16[256,640]{1,0:T(8,128)(2,1)S(1)}, bf16[256,640]{1,0:T(8,128)(2,1)S(1)}, u32[]{:S(2)}, u32[]{:S(2)}) collective-permute-start(bf16[256,640]{1,0:T(8,128)(2,1)S(1)} %all_gather.18.refs_0_), channel_id=1, source_target_pairs={{0,128},{128,256},{256,384},{1,129},{129,257},{257,385},{2,130},{1... | collective-permute-start | bytes 983048 | tf_op jit(solution)/shard_map/ppermute | solution.py:249
  48.2 32.9 %collective-permute-start.1 = (bf16[256,640]{1,0:T(8,128)(2,1)S(1)}, bf16[256,640]{1,0:T(8,128)(2,1)S(1)}, u32[]{:S(2)}, u32[]{:S(2)}) collective-permute-start(bf16[256,640]{1,0:T(8,128)(2,1)S(1)} %all_gather.18.refs_0_), channel_id=1, source_target_pairs={{0,256},{128,384},{1,257},{129,385},{2,258},{130,386},{3,259},{131... | collective-permute-start | bytes 983048 | tf_op jit(solution)/shard_map/ppermute | solution.py:249
  49.5 31.6 %collective-permute-start.2 = (bf16[256,640]{1,0:T(8,128)(2,1)S(1)}, bf16[256,640]{1,0:T(8,128)(2,1)S(1)}, u32[]{:S(2)}, u32[]{:S(2)}) collective-permute-start(bf16[256,640]{1,0:T(8,128)(2,1)S(1)} %all_gather.18.refs_0_), channel_id=1, source_target_pairs={{0,384},{1,385},{2,386},{3,387},{4,388},{5,389},{6,390},{7,391},{8... | collective-permute-start | bytes 983048 | tf_op jit(solution)/shard_map/ppermute | solution.py:249
  81.2 12.2 %collective-permute-start.4 = (bf16[1024,640]{1,0:T(8,128)(2,1)S(1)}, bf16[1024,640]{1,0:T(8,128)(2,1)}, u32[]{:S(2)}, u32[]{:S(2)}) collective-permute-start(bf16[1024,640]{1,0:T(8,128)(2,1)S(1)} %pack.1.ka_ref), channel_id=1, source_target_pairs={{0,4},{4,0},{1,5},{5,1},{2,6},{6,2},{3,7},{7,3},{8,12},{12,8},{9,1... | collective-permute-start | bytes 3932168 | tf_op jit(solution)/shard_map/ppermute | solution.py:31
  83.1 4.4 %collective-permute-start.3 = (bf16[2,128,512]{2,1,0:T(8,128)(2,1)S(1)}, bf16[2,128,512]{2,1,0:T(8,128)(2,1)S(1)}, u32[]{:S(2)}, u32[]{:S(2)}) collective-permute-start(bf16[2,128,512]{2,1,0:T(8,128)(2,1)S(1)} %copy-done.3), channel_id=1, source_target_pairs={{0,4},{4,0},{1,5},{5,1},{2,6},{6,2},{3,7},{7,3},{8,12},{12,8},{9,1... | collective-permute-start | bytes 786440 | tf_op jit(solution)/shard_map/ppermute | solution.py:31
  85.6 7.2 %collective-permute-start.5 = (bf16[2,512,128]{2,1,0:T(8,128)(2,1)S(1)}, bf16[2,512,128]{2,1,0:T(8,128)(2,1)S(1)}, u32[]{:S(2)}, u32[]{:S(2)}) collective-permute-start(bf16[2,512,128]{2,1,0:T(8,128)(2,1)S(1)} %copy-done.9), channel_id=1, source_target_pairs={{0,4},{4,0},{1,5},{5,1},{2,6},{6,2},{3,7},{7,3},{8,12},{12,8},{9,1... | collective-permute-start | bytes 786440 | tf_op jit(solution)/shard_map/ppermute | solution.py:31
  87.6 1.7 copy-start
  91.7 1.1 copy-start.1
  92.7 0.7 copy-start.10
  93.5 1.3 copy-start.2
  94.8 2.0 %copy-start.8 = (bf16[512,3584]{1,0:T(8,128)(2,1)S(1)}, bf16[512,3584]{1,0:T(8,128)(2,1)}, u32[]{:S(2)}) copy-start(bf16[512,3584]{1,0:T(8,128)(2,1)} %all-gather.7.cloned.1.call-done) | copy-start | bytes 11010052
  96.8 0.9 copy-start.11
  109.5 20.0 %all-to-all-start = ((bf16[4,4,4,640]{3,2,1,0:T(4,128)(2,1)}), bf16[4,4,4,640]{3,2,1,0:T(4,128)(2,1)S(1)}, u32[]{:S(2)}, u32[]{:S(2)}) async-start(bf16[4,4,4,640]{3,2,1,0:T(4,128)(2,1)} %broadcast_in_dim.33), calls=%async_computation | async-start | bytes 163840 | tf_op jit(solution)/shard_map/all_to_all | solution.py:36
  113.8 27.8 %collective-permute-start.6 = (bf16[64,3584]{1,0:T(8,128)(2,1)S(1)}, bf16[64,3584]{1,0:T(8,128)(2,1)S(1)}, u32[]{:S(2)}, u32[]{:S(2)}) collective-permute-start(bf16[64,3584]{1,0:T(8,128)(2,1)S(1)} %get-tuple-element.29), channel_id=1, source_target_pairs={{0,8},{8,16},{16,24},{24,32},{32,40},{40,48},{48,56},{56,64},{64,7... | collective-permute-start | bytes 1376264 | tf_op jit(solution)/shard_map/ppermute | solution.py:27
  117.5 24.0 %collective-permute-start.7 = (bf16[64,3584]{1,0:T(8,128)(2,1)S(1)}, bf16[64,3584]{1,0:T(8,128)(2,1)}, u32[]{:S(2)}, u32[]{:S(2)}) collective-permute-start(bf16[64,3584]{1,0:T(8,128)(2,1)S(1)} %get-tuple-element.30), channel_id=1, source_target_pairs={{0,120},{8,0},{16,8},{24,16},{32,24},{40,32},{48,40},{56,48},{64,5... | collective-permute-start | bytes 1376264 | tf_op jit(solution)/shard_map/ppermute | solution.py:27
  121.6 15.3 %collective-permute-start.8 = (bf16[32,3584]{1,0:T(8,128)(2,1)}, bf16[32,3584]{1,0:T(8,128)(2,1)}, u32[]{:S(2)}, u32[]{:S(2)}) collective-permute-start(bf16[32,3584]{1,0:T(8,128)(2,1)} %get-tuple-element.27), channel_id=1, source_target_pairs={{0,16},{8,24},{16,32},{24,40},{32,48},{40,56},{48,64},{56,72},{64,... | collective-permute-start | bytes 688136 | tf_op jit(solution)/shard_map/ppermute | solution.py:27
  123.6 18.0 %collective-permute-start.9 = (bf16[32,3584]{1,0:T(8,128)(2,1)S(1)}, bf16[32,3584]{1,0:T(8,128)(2,1)}, u32[]{:S(2)}, u32[]{:S(2)}) collective-permute-start(bf16[32,3584]{1,0:T(8,128)(2,1)S(1)} %get-tuple-element.28), channel_id=1, source_target_pairs={{0,112},{8,120},{16,0},{24,8},{32,16},{40,24},{48,32},{56,40},{64,... | collective-permute-start | bytes 688136 | tf_op jit(solution)/shard_map/ppermute | solution.py:27
  142.9 11.0 %collective-permute-start.11 = (bf16[16,1792]{1,0:T(8,128)(2,1)S(1)}, bf16[16,1792]{1,0:T(8,128)(2,1)S(1)}, u32[]{:S(2)}, u32[]{:S(2)}) collective-permute-start(bf16[16,1792]{1,0:T(8,128)(2,1)S(1)} %get-tuple-element.32), channel_id=1, source_target_pairs={{0,96},{8,104},{16,112},{24,120},{32,0},{40,8},{48,16},{56,24},{64... | collective-permute-start | bytes 172040 | tf_op jit(solution)/shard_map/ppermute | solution.py:27
  149.0 16.9 %collective-permute-start.10 = (bf16[16,3584]{1,0:T(8,128)(2,1)S(1)}, bf16[16,3584]{1,0:T(8,128)(2,1)S(1)}, u32[]{:S(2)}, u32[]{:S(2)}) collective-permute-start(bf16[16,3584]{1,0:T(8,128)(2,1)S(1)} %get-tuple-element.24), channel_id=1, source_target_pairs={{0,32},{8,40},{16,48},{24,56},{32,64},{40,72},{48,80},{56,88},{64,... | collective-permute-start | bytes 344072 | tf_op jit(solution)/shard_map/ppermute | solution.py:27
  153.9 13.2 %collective-permute-start.12 = (bf16[16,3584]{1,0:T(8,128)(2,1)S(1)}, bf16[16,3584]{1,0:T(8,128)(2,1)S(1)}, u32[]{:S(2)}, u32[]{:S(2)}) collective-permute-start(bf16[16,3584]{1,0:T(8,128)(2,1)S(1)} %pad_maximum_fusion), channel_id=1, source_target_pairs={{0,96},{8,104},{16,112},{24,120},{32,0},{40,8},{48,16},{56,24},{64... | collective-permute-start | bytes 344072 | tf_op jit(solution)/shard_map/ppermute | solution.py:27
  159.4 15.2 %collective-permute-start.13 = (bf16[16,1792]{1,0:T(8,128)(2,1)S(1)}, bf16[16,1792]{1,0:T(8,128)(2,1)S(1)}, u32[]{:S(2)}, u32[]{:S(2)}) collective-permute-start(bf16[16,1792]{1,0:T(8,128)(2,1)S(1)} %get-tuple-element.31), channel_id=1, source_target_pairs={{0,64},{8,72},{16,80},{24,88},{32,96},{40,104},{48,112},{56,120},{... | collective-permute-start | bytes 172040 | tf_op jit(solution)/shard_map/ppermute | solution.py:27
Sparse Core Ops, SparseCore 0:
  10.2 25.6 all-gather.4
  37.9 24.6 all-gather.6

commit v6 on v5

--- a/solution.py
+++ b/solution.py
@@ -83,11 +83,12 @@
 
 
 def query_kernel(
-    where_ref, g_ref, wq_ref, ak0, ak1, freq_ref, out_ref, x_ref, *, nope, rope, qrows, chips
+    where_ref, g_ref, wq0, wq1, ak0, ak1, freq_ref, out_ref, x_ref, *, nope, rope, qrows, chips, nzl
 ):
     chain, z, core = where_ref[0], where_ref[1], where_ref[2]
     for i, step in enumerate(STEPS):
         at = lax.rem(z + step % chips, chips)
+        at = lax.rem(at, nzl) * (chips // nzl) + at // nzl
         x_ref[i * qrows : (i + 1) * qrows, :] = g_ref[pl.ds(pl.multiple_of(at * qrows, qrows), qrows), :]
     x = x_ref[...]
     rows = x.shape[0]
@@ -100,8 +101,8 @@
     sine = jnp.where(lane < rope // 2, -sine, sine)
     cosine = jnp.cos(angle)
     head = 0
-    for side, ak in ((core, ak0), (1 - core, ak1)):
-        q = jnp.dot(x, wq_ref[side], preferred_element_type=F32).astype(BF)
+    for wq, ak in ((wq0, ak0), (wq1, ak1)):
+        q = jnp.dot(x, wq[...], preferred_element_type=F32).astype(BF)
         for h in range(ak.shape[0]):
             base = h * (nope + rope)
             r0 = head * rows
@@ -117,7 +118,7 @@
 
 
 def attend_kernel(
-    where_ref, q_ref, ka_ref, kb_ref, av0, av1, op_ref, out_ref,
+    where_ref, q_ref, ka_ref, kb_ref, av0, av1, op0, op1, o0, o1, o2, o3, o4,
     s_ref, top_ref, l_ref, acc_ref, ho_ref, *, rows, lat, scale, nch, chips, qrows, part,
 ):
     chain, z, core = where_ref[0], where_ref[1], where_ref[2]
@@ -186,14 +187,18 @@
         av = (av0 if h < per else av1)[h % per]
         ho_ref[:, h * vh : (h + 1) * vh] = jnp.dot(mixed, av, preferred_element_type=F32).astype(BF)
     ho = ho_ref[...]
-    k = op_ref.shape[1]
-    width = out_ref.shape[1]
+    k = op0.shape[0]
+    width = op0.shape[1]
     cut = 512 if width % 512 == 0 else width
     for c in range(0, width, cut):
-        out_ref[:, c : c + cut] = (
-            jnp.dot(ho[:, :k], op_ref[core, :, c : c + cut], preferred_element_type=F32)
-            + jnp.dot(ho[:, k:], op_ref[1 - core, :, c : c + cut], preferred_element_type=F32)
+        part_out = (
+            jnp.dot(ho[:, :k], op0[:, c : c + cut], preferred_element_type=F32)
+            + jnp.dot(ho[:, k:], op1[:, c : c + cut], preferred_element_type=F32)
         ).astype(BF)
+        at = 0
+        for out_ref in (o0, o1, o2, o3, o4):
+            out_ref[:, c : c + cut] = part_out[at : at + out_ref.shape[0]]
+            at += out_ref.shape[0]
 
 
 def local(
@@ -239,18 +244,16 @@
         page_owner, page_slot, raw, latent_gain[None], frequencies(rope),
     )
 
-    wq = lax.all_gather(query_up, "core", axis=0, tiled=False)
-    op = lax.all_gather(out_proj, "core", axis=0, tiled=False)
-    ak1 = swap_core(absorb_key)
-    av1 = swap_core(absorb_value)
-
+    qz = spread(query_comp[0], "zh")
     own = lax.all_gather(keys, Z, axis=0, tiled=True)
     backs = [
         lax.ppermute(own, "chain", [(i, i + k) for i in range(nch - k)]) for k in range(1, nch)
     ]
-    held = lax.optimization_barrier((query_comp[0], own))[0]
-    qg = lax.all_gather(held, Z, axis=0, tiled=True)
-    qg, *backs = lax.optimization_barrier((qg, *backs))
+    qz, *weights, _ = lax.optimization_barrier(
+        (qz, query_up, absorb_key, absorb_value, out_proj, own)
+    )
+    qg = spread(qz, "zl").reshape(rows, ql)
+    wq1, ak1, av1, op1 = [swap_core(w) for w in weights]
     mine = pl.pallas_call(
         pack_kernel,
         out_shape=jax.ShapeDtypeStruct((nch * rows, kw), BF),
@@ -262,9 +265,9 @@
     other = swap_core(mine)
 
     q = pl.pallas_call(
-        functools.partial(query_kernel, nope=nope, rope=rope, qrows=qrows, chips=nzh * nzl),
+        functools.partial(query_kernel, nope=nope, rope=rope, qrows=qrows, chips=nzh * nzl, nzl=nzl),
         out_shape=jax.ShapeDtypeStruct((heads * rows, kw), BF),
-        in_specs=[smem] + [vm] * 5,
+        in_specs=[smem] + [vm] * 6,
         out_specs=vm,
         scratch_shapes=[pltpu.VMEM((rows, ql), BF)],
         compiler_params=room(12),
@@ -273,16 +276,17 @@
             bytes_accessed=6000000, transcendentals=0,
         ),
         name="queries",
-    )(where, qg, wq, absorb_key, ak1, frequencies(rope))
-
-    partial = pl.pallas_call(
+    )(where, qg, query_up, wq1, absorb_key, ak1, frequencies(rope))
+
+    n = nzh * qrows
+    sums = pl.pallas_call(
         functools.partial(
             attend_kernel, rows=rows, lat=lat, scale=(nope + rope) ** -0.5,
             nch=nch, chips=nzh * nzl, qrows=qrows, part=part,
         ),
-        out_shape=jax.ShapeDtypeStruct((rows, width), BF),
-        in_specs=[smem] + [vm] * 6,
-        out_specs=vm,
+        out_shape=[jax.ShapeDtypeStruct((r, width), BF) for r in (n, n, n, n // 2, n // 2)],
+        in_specs=[smem] + [vm] * 7,
+        out_specs=[vm] * 5,
         scratch_shapes=[
             pltpu.VMEM((heads, rows, nch * block_len), F32),
             pltpu.VMEM((heads, rows, 128), F32),
@@ -296,17 +300,16 @@
             transcendentals=rows * heads * nch * block_len,
         ),
         name="attend",
-    )(where, q, mine, other, absorb_value, av1, op)
-
-    n = nzh * qrows
-    up2 = shift_z(partial[3 * n : 3 * n + n // 2], 2)
-    down2 = shift_z(partial[3 * n + n // 2 :], -2)
-    up = shift_z(partial[n : 2 * n], 1)
-    down = shift_z(partial[2 * n : 3 * n], -1)
+    )(where, q, mine, other, absorb_value, av1, out_proj, op1)
+
+    up2 = shift_z(sums[3], 2)
+    down2 = shift_z(sums[4], -2)
+    up = shift_z(sums[1], 1)
+    down = shift_z(sums[2], -1)
 
     def near(e):
         at = slice((e + 1) * qrows, (e + 2) * qrows)
-        return partial[at].astype(F32) + up[at].astype(F32) + down[at].astype(F32)
+        return sums[0][at].astype(F32) + up[at].astype(F32) + down[at].astype(F32)
 
     cut = width // 2
     far = near(2).astype(BF)
@@ -321,7 +324,7 @@
     total = jnp.concatenate([total[:, :cut] + direct.astype(F32), total[:, cut:]], -1)
     layer_output = total.astype(BF)[None]
 
-    keys = lax.optimization_barrier((keys, partial))[0]
+    keys = lax.optimization_barrier((keys, up2))[0]
     page = spread(keys.reshape(pages, part, -1), "dec")
     came = page[:, :, 0, lat + rope].reshape(-1).astype(jnp.int32)
     take = (came[None, :] == dec * slots + jnp.arange(slots, dtype=jnp.int32)[:, None]).astype(BF)

time: 185 us -> 183 us (0.989)
  blocking collectives: 67.7 us -> 33.2 us
  starting transfers between devices: 50.5 us -> 79.3 us
  waiting for transfers between devices: 20.9 us -> 36.4 us
  between operations: 14.5 us -> 0.99 us
  local copies, waits for them, and re-layouts: 10.6 us -> 13.1 us
    all_gather x1 -> x0, blocking collectives: 30.3 us -> none  [local(): qg = lax.all_gather(held, Z, axis=0, tiled=True)]
    all_to_all x1 -> x3, starting transfers between devices: 4.29 us -> 22.9 us  [spread(): lax.all_to_all(jnp.broadcast_to(x[None], (n,) + x.shape), axis, 0, 0, til...]
    ppermute x3, waiting for transfers between devices: 0.01 us -> 16.3 us  [local(): lax.ppermute(own, 'chain', [(i, i + k) for i in range(nch - k)])]
    ppermute x8, starting transfers between devices: 36.1 us -> 41.9 us  [shift_z(): return lax.ppermute(x, Z, [(i, (i + step) % n) for i in range(n)])]
    ppermute x3 -> x5, starting transfers between devices: 6.25 us -> 10.7 us  [swap_core(): return lax.ppermute(x, 'core', [(0, 1), (1, 0)])]
    all_gather x1, blocking collectives: 37.4 us -> 33.2 us  [local(): own = lax.all_gather(keys, Z, axis=0, tiled=True)]
    broadcast_in_dim x2 -> x4, local copies, waits for them, and re-layouts: 0.67 us -> 3.13 us  [spread(): jnp.broadcast_to(x[None], (n,) + x.shape)]
  transfers between devices with their start and end apart: 17 -> 19, of which waited for: 5 -> 6; matrix products, arithmetic and copies ran while one was open for 2% -> 2% of each run, Pallas kernels for 2% -> 2%
where the time goes in v6:
time: 183 us; the launch traced here: 180 us
  starting transfers between devices  79.3 us (43%)
  waiting for transfers between devices  36.4 us (20%)
  blocking collectives  33.2 us (18%)
  Pallas kernels  14.8 us (8%)
  local copies, waits for them, and re-layouts  13.1 us (7%)
  other arithmetic  2.17 us (1%)
    ppermute x8, starting transfers between devices, shift_z(): return lax.ppermute(x, Z, [(i, (i + step) % n) for i in range(n)])  41.9 us
    all_gather x1, blocking collectives, local(): own = lax.all_gather(keys, Z, axis=0, tiled=True)  33.2 us
    all_to_all x3, starting transfers between devices, spread(): lax.all_to_all(jnp.broadcast_to(x[None], (n,) + x.shape), axis, 0, 0, til...  22.9 us
    ppermute x8, waiting for transfers between devices, shift_z(): return lax.ppermute(x, Z, [(i, (i + step) % n) for i in range(n)])  20 us
    ppermute x3, waiting for transfers between devices, local(): lax.ppermute(own, 'chain', [(i, i + k) for i in range(nch - k)])  16.3 us
    pallas_call x1, Pallas kernels, local(): pl.pallas_call(functools.partial(attend_kernel, rows=rows, lat=lat, scale...  11.6 us
    ppermute x5, starting transfers between devices, swap_core(): return lax.ppermute(x, 'core', [(0, 1), (1, 0)])  10.7 us
    unnamed x32, local copies, waits for them, and re-layouts  9.1 us
  transfers between devices with their start and end apart: 19, of which 6 were waited for; matrix products, arithmetic and copies ran while one was open for 2% of the time, Pallas kernels for 2%

profile of v6, /device:TPU:24, one launch (start us, length us, event | category | flops | bytes accessed | tf_op | source)
XLA Modules:
  0.0 180.1 jit_solution(12414139403822287388)
XLA Ops:
  0.6 1.5 broadcast_in_dim.42
  2.1 15.1 %all-to-all-start = ((bf16[4,16,1536]{2,1,0:T(8,128)(2,1)}), bf16[4,16,1536]{2,1,0:T(8,128)(2,1)S(1)}, u32[]{:S(2)}, u32[]{:S(2)}) async-start(bf16[4,16,1536]{2,1,0:T(8,128)(2,1)} %broadcast_in_dim.42), calls=%async_computation | async-start | bytes 393216 | tf_op jit(solution)/shard_map/all_to_all | solution.py:36
  21.9 33.2 %all_gather.3.refs_0_ = bf16[256,640]{1,0:T(8,128)(2,1)S(1)} all-gather(bf16[16,640]{1,0:T(8,128)(2,1)S(1)} %keys.1), channel_id=1, replica_groups=mesh['chain'=4,'zh'=4,'zl'=4,'core'=2,'dec'=4] {'zh','zl'}, dimensions={0}, use_global_device_ids=true | all-gather | bytes 348160 | tf_op jit(solution)/shard_map/all_gather | solution.py:248
  56.1 3.5 %all-to-all-start.1 = ((bf16[4,4,16,1536]{3,2,1,0:T(8,128)(2,1)}), bf16[4,4,16,1536]{3,2,1,0:T(8,128)(2,1)S(1)}, u32[]{:S(2)}, u32[]{:S(2)}) async-start(bf16[4,4,16,1536]{3,2,1,0:T(8,128)(2,1)} %broadcast_in_dim.46), calls=%async_computation.1 | async-start | bytes 1572864 | tf_op jit(solution)/shard_map/all_to_all | solution.py:36
  59.6 2.1 %collective-permute-start.7 = (bf16[256,3584]{1,0:T(8,128)(2,1)}, bf16[256,3584]{1,0:T(8,128)(2,1)}, u32[]{:S(2)}, u32[]{:S(2)}) collective-permute-start(bf16[256,3584]{1,0:T(8,128)(2,1)} %op0.1), channel_id=1, source_target_pairs={{0,4},{4,0},{1,5},{5,1},{2,6},{6,2},{3,7},{7,3},{8,12},{12,8},{9,1... | collective-permute-start | bytes 5505032 | tf_op jit(solution)/shard_map/ppermute | solution.py:31
  61.7 1.3 collective-permute-start.4
  63.0 1.3 collective-permute-start.3
  64.3 1.3 collective-permute-start.2
  65.6 16.3 %collective-permute-done.4.refs_3_ = bf16[256,640]{1,0:T(8,128)(2,1)S(1)} collective-permute-done((bf16[256,640]{1,0:T(8,128)(2,1)S(1)}, bf16[256,640]{1,0:T(8,128)(2,1)S(1)}, u32[]{:S(2)}, u32[]{:S(2)}) %collective-permute-start.4) | collective-permute-done | bytes 327712 | tf_op jit(solution)/shard_map/ppermute | solution.py:250
  82.1 1.9 %collective-permute-start.5 = (bf16[1024,640]{1,0:T(8,128)(2,1)S(1)}, bf16[1024,640]{1,0:T(8,128)(2,1)}, u32[]{:S(2)}, u32[]{:S(2)}) collective-permute-start(bf16[1024,640]{1,0:T(8,128)(2,1)S(1)} %pack.1.ka_ref), channel_id=1, source_target_pairs={{0,4},{4,0},{1,5},{5,1},{2,6},{6,2},{3,7},{7,3},{8,12},{12,8},{9,1... | collective-permute-start | bytes 3932168 | tf_op jit(solution)/shard_map/ppermute | solution.py:31
  84.0 2.4 %collective-permute-start = (bf16[1536,384]{1,0:T(8,128)(2,1)S(1)}, bf16[1536,384]{1,0:T(8,128)(2,1)S(1)}, u32[]{:S(2)}, u32[]{:S(2)}) collective-permute-start(bf16[1536,384]{1,0:T(8,128)(2,1)S(1)} %copy-done), channel_id=1, source_target_pairs={{0,4},{4,0},{1,5},{5,1},{2,6},{6,2},{3,7},{7,3},{8,12},{12,8},{9,1... | collective-permute-start | bytes 3538952 | tf_op jit(solution)/shard_map/ppermute | solution.py:31
  86.4 1.9 %collective-permute-start.1 = (bf16[2,128,512]{2,1,0:T(8,128)(2,1)S(1)}, bf16[2,128,512]{2,1,0:T(8,128)(2,1)S(1)}, u32[]{:S(2)}, u32[]{:S(2)}) collective-permute-start(bf16[2,128,512]{2,1,0:T(8,128)(2,1)S(1)} %copy-done.4), channel_id=1, source_target_pairs={{0,4},{4,0},{1,5},{5,1},{2,6},{6,2},{3,7},{7,3},{8,12},{12,8},{9,1... | collective-permute-start | bytes 786440 | tf_op jit(solution)/shard_map/ppermute | solution.py:31
  88.4 2.4 %collective-permute-start.6 = (bf16[2,512,128]{2,1,0:T(8,128)(2,1)S(1)}, bf16[2,512,128]{2,1,0:T(8,128)(2,1)S(1)}, u32[]{:S(2)}, u32[]{:S(2)}) collective-permute-start(bf16[2,512,128]{2,1,0:T(8,128)(2,1)S(1)} %copy-done.11), channel_id=1, source_target_pairs={{0,4},{4,0},{1,5},{5,1},{2,6},{6,2},{3,7},{7,3},{8,12},{12,8},{9,1... | collective-permute-start | bytes 786440 | tf_op jit(solution)/shard_map/ppermute | solution.py:31
  90.9 1.0 copy-done.2
  91.9 1.3 copy-done.1
  93.2 1.3 copy-done.3
  94.4 2.4 %queries.1.q_ref = bf16[1024,640]{1,0:T(8,128)(2,1)S(1)} custom-call(s32[3]{0:T(128)S(1)} %pad_add_fusion.where_ref, bf16[256,1536]{1,0:T(8,128)(2,1)S(1)} %bitcast.20, bf16[1536,384]{1,0:T(8,128)(2,1)S(1)} %copy-done.1, bf16[1536,384]{1,0:T(8,128)(2,1)S(1)} %copy-done.3, bf16[2,128,512]{2,1,0:T(8,128)(2,1)S(1)} %copy-done.4, ...), custom_call_target="tpu_custom_call" | custom-call | flops 738197504 | bytes 6000000 | tf_op jit(solution)/shard_map/queries/pallas_call | solution.py:267
  98.5 11.6 %attend.1 = (bf16[64,3584]{1,0:T(8,128)(2,1)S(1)}, bf16[64,3584]{1,0:T(8,128)(2,1)S(1)}, bf16[64,3584]{1,0:T(8,128)(2,1)S(1)}, bf16[32,3584]{1,0:T(8,128)(2,1)S(1)}, bf16[32,3584]{1,0:T(8,128)(2,1)S(1)}) custom-call(s32[3]{0:T(128)S(1)} %pad_add_fusion.where_ref, bf16[1024,640]{1,0:T(8,128)(2,1)S(1)} %queries.1.q_ref, bf16[1024,640]{1,0:T(8,128)(2,1)S(1)} %pack.1.ka_ref, ...), custom_call_target="tpu_custom_call" | custom-call | flops 4294967296 | bytes 9000000 | tf_op jit(solution)/shard_map/attend/pallas_call | solution.py:282
  110.2 4.8 %collective-permute-start.10 = (bf16[32,3584]{1,0:T(8,128)(2,1)S(1)}, bf16[32,3584]{1,0:T(8,128)(2,1)S(1)}, u32[]{:S(2)}, u32[]{:S(2)}) collective-permute-start(bf16[32,3584]{1,0:T(8,128)(2,1)S(1)} %get-tuple-element.22), channel_id=1, source_target_pairs={{0,16},{8,24},{16,32},{24,40},{32,48},{40,56},{48,64},{56,72},{64,... | collective-permute-start | bytes 688136 | tf_op jit(solution)/shard_map/ppermute | solution.py:27
  114.9 3.4 %collective-permute-start.8 = (bf16[64,3584]{1,0:T(8,128)(2,1)S(1)}, bf16[64,3584]{1,0:T(8,128)(2,1)S(1)}, u32[]{:S(2)}, u32[]{:S(2)}) collective-permute-start(bf16[64,3584]{1,0:T(8,128)(2,1)S(1)} %get-tuple-element.20), channel_id=1, source_target_pairs={{0,8},{8,16},{16,24},{24,32},{32,40},{40,48},{48,56},{56,64},{64,7... | collective-permute-start | bytes 1376264 | tf_op jit(solution)/shard_map/ppermute | solution.py:27
  118.3 3.7 %collective-permute-start.9 = (bf16[64,3584]{1,0:T(8,128)(2,1)S(1)}, bf16[64,3584]{1,0:T(8,128)(2,1)S(1)}, u32[]{:S(2)}, u32[]{:S(2)}) collective-permute-start(bf16[64,3584]{1,0:T(8,128)(2,1)S(1)} %get-tuple-element.21), channel_id=1, source_target_pairs={{0,120},{8,0},{16,8},{24,16},{32,24},{40,32},{48,40},{56,48},{64,5... | collective-permute-start | bytes 1376264 | tf_op jit(solution)/shard_map/ppermute | solution.py:27
  122.0 1.6 collective-permute-done.10
  124.3 4.3 %all-to-all-start.2 = ((bf16[4,4,4,640]{3,2,1,0:T(4,128)(2,1)}), bf16[4,4,4,640]{3,2,1,0:T(4,128)(2,1)S(1)}, u32[]{:S(2)}, u32[]{:S(2)}) async-start(bf16[4,4,4,640]{3,2,1,0:T(4,128)(2,1)} %broadcast_in_dim.49), calls=%async_computation.2 | async-start | bytes 163840 | tf_op jit(solution)/shard_map/all_to_all | solution.py:36
  128.6 9.6 %collective-permute-start.11 = (bf16[32,3584]{1,0:T(8,128)(2,1)S(1)}, bf16[32,3584]{1,0:T(8,128)(2,1)S(1)}, u32[]{:S(2)}, u32[]{:S(2)}) collective-permute-start(bf16[32,3584]{1,0:T(8,128)(2,1)S(1)} %get-tuple-element.23), channel_id=1, source_target_pairs={{0,112},{8,120},{16,0},{24,8},{32,16},{40,24},{48,32},{56,40},{64,... | collective-permute-start | bytes 688136 | tf_op jit(solution)/shard_map/ppermute | solution.py:27
  138.9 7.6 %collective-permute-done.11 = bf16[32,3584]{1,0:T(8,128)(2,1)S(1)} collective-permute-done((bf16[32,3584]{1,0:T(8,128)(2,1)S(1)}, bf16[32,3584]{1,0:T(8,128)(2,1)S(1)}, u32[]{:S(2)}, u32[]{:S(2)}) %collective-permute-start.11) | collective-permute-done | bytes 229408 | tf_op jit(solution)/shard_map/ppermute | solution.py:27
  146.7 6.0 %collective-permute-start.13 = (bf16[16,1792]{1,0:T(8,128)(2,1)S(1)}, bf16[16,1792]{1,0:T(8,128)(2,1)S(1)}, u32[]{:S(2)}, u32[]{:S(2)}) collective-permute-start(bf16[16,1792]{1,0:T(8,128)(2,1)S(1)} %get-tuple-element.38), channel_id=1, source_target_pairs={{0,96},{8,104},{16,112},{24,120},{32,0},{40,8},{48,16},{56,24},{64... | collective-permute-start | bytes 172040 | tf_op jit(solution)/shard_map/ppermute | solution.py:27
  153.3 3.8 %collective-permute-start.12 = (bf16[16,3584]{1,0:T(8,128)(2,1)S(1)}, bf16[16,3584]{1,0:T(8,128)(2,1)S(1)}, u32[]{:S(2)}, u32[]{:S(2)}) collective-permute-start(bf16[16,3584]{1,0:T(8,128)(2,1)S(1)} %get-tuple-element.34), channel_id=1, source_target_pairs={{0,32},{8,40},{16,48},{24,56},{32,64},{40,72},{48,80},{56,88},{64,... | collective-permute-start | bytes 344072 | tf_op jit(solution)/shard_map/ppermute | solution.py:27
  157.1 1.2 collective-permute-done.13
  158.4 5.6 %collective-permute-start.14 = (bf16[16,3584]{1,0:T(8,128)(2,1)S(1)}, bf16[16,3584]{1,0:T(8,128)(2,1)S(1)}, u32[]{:S(2)}, u32[]{:S(2)}) collective-permute-start(bf16[16,3584]{1,0:T(8,128)(2,1)S(1)} %pad_maximum_fusion), channel_id=1, source_target_pairs={{0,96},{8,104},{16,112},{24,120},{32,0},{40,8},{48,16},{56,24},{64... | collective-permute-start | bytes 344072 | tf_op jit(solution)/shard_map/ppermute | solution.py:27
  164.6 5.1 %collective-permute-start.15 = (bf16[16,1792]{1,0:T(8,128)(2,1)S(1)}, bf16[16,1792]{1,0:T(8,128)(2,1)S(1)}, u32[]{:S(2)}, u32[]{:S(2)}) collective-permute-start(bf16[16,1792]{1,0:T(8,128)(2,1)S(1)} %get-tuple-element.37), channel_id=1, source_target_pairs={{0,64},{8,72},{16,80},{24,88},{32,96},{40,104},{48,112},{56,120},{... | collective-permute-start | bytes 172040 | tf_op jit(solution)/shard_map/ppermute | solution.py:27
  169.7 2.1 %collective-permute-done.14 = bf16[16,3584]{1,0:T(8,128)(2,1)S(1)} collective-permute-done((bf16[16,3584]{1,0:T(8,128)(2,1)S(1)}, bf16[16,3584]{1,0:T(8,128)(2,1)S(1)}, u32[]{:S(2)}, u32[]{:S(2)}) %collective-permute-start.14) | collective-permute-done | bytes 114720 | tf_op jit(solution)/shard_map/ppermute | solution.py:27
  171.9 7.5 %collective-permute-done.15 = bf16[16,1792]{1,0:T(8,128)(2,1)S(1)} collective-permute-done((bf16[16,1792]{1,0:T(8,128)(2,1)S(1)}, bf16[16,1792]{1,0:T(8,128)(2,1)S(1)}, u32[]{:S(2)}, u32[]{:S(2)}) %collective-permute-start.15) | collective-permute-done | bytes 57376 | tf_op jit(solution)/shard_map/ppermute | solution.py:27
  (65 shorter events, 11.2 us)
Async XLA Ops:
  2.1 53.0 %all-to-all-start = ((bf16[4,16,1536]{2,1,0:T(8,128)(2,1)}), bf16[4,16,1536]{2,1,0:T(8,128)(2,1)S(1)}, u32[]{:S(2)}, u32[]{:S(2)}) async-start(bf16[4,16,1536]{2,1,0:T(8,128)(2,1)} %broadcast_in_dim.42), calls=%async_computation | async-start | bytes 393216 | tf_op jit(solution)/shard_map/all_to_all | solution.py:36
  18.6 0.7 copy-start.5
  19.3 0.7 copy-start.6
  56.1 35.8 %all-to-all-start.1 = ((bf16[4,4,16,1536]{3,2,1,0:T(8,128)(2,1)}), bf16[4,4,16,1536]{3,2,1,0:T(8,128)(2,1)S(1)}, u32[]{:S(2)}, u32[]{:S(2)}) async-start(bf16[4,4,16,1536]{3,2,1,0:T(8,128)(2,1)} %broadcast_in_dim.46), calls=%async_computation.1 | async-start | bytes 1572864 | tf_op jit(solution)/shard_map/all_to_all | solution.py:36
  59.6 24.4 %copy-start = (bf16[1536,384]{1,0:T(8,128)(2,1)S(1)}, bf16[1536,384]{1,0:T(8,128)(2,1)}, u32[]{:S(2)}) copy-start(bf16[1536,384]{1,0:T(8,128)(2,1)} %wq0.1) | copy-start | bytes 3538948
  59.6 26.8 %copy-start.4 = (bf16[2,128,512]{2,1,0:T(8,128)(2,1)S(1)}, bf16[2,128,512]{2,1,0:T(8,128)(2,1)}, u32[]{:S(2)}) copy-start(bf16[2,128,512]{2,1,0:T(8,128)(2,1)} %ak0.1) | copy-start | bytes 786436
  59.6 28.7 %copy-start.11 = (bf16[2,512,128]{2,1,0:T(8,128)(2,1)S(1)}, bf16[2,512,128]{2,1,0:T(8,128)(2,1)}, u32[]{:S(2)}) copy-start(bf16[2,512,128]{2,1,0:T(8,128)(2,1)} %av0.1) | copy-start | bytes 786436
  59.6 32.3 %copy-start.7 = (f32[1,64]{1,0:T(1,128)S(1)}, f32[1,64]{1,0:T(1,128)}, u32[]{:S(2)}) copy-start(f32[1,64]{1,0:T(1,128)} %constant.38.freq_ref) | copy-start | bytes 772
  59.6 37.9 %collective-permute-start.7 = (bf16[256,3584]{1,0:T(8,128)(2,1)}, bf16[256,3584]{1,0:T(8,128)(2,1)}, u32[]{:S(2)}, u32[]{:S(2)}) collective-permute-start(bf16[256,3584]{1,0:T(8,128)(2,1)} %op0.1), channel_id=1, source_target_pairs={{0,4},{4,0},{1,5},{5,1},{2,6},{6,2},{3,7},{7,3},{8,12},{12,8},{9,1... | collective-permute-start | bytes 5505032 | tf_op jit(solution)/shard_map/ppermute | solution.py:31
  61.7 20.2 %collective-permute-start.4 = (bf16[256,640]{1,0:T(8,128)(2,1)S(1)}, bf16[256,640]{1,0:T(8,128)(2,1)S(1)}, u32[]{:S(2)}, u32[]{:S(2)}) collective-permute-start(bf16[256,640]{1,0:T(8,128)(2,1)S(1)} %all_gather.3.refs_0_), channel_id=1, source_target_pairs={{0,384},{1,385},{2,386},{3,387},{4,388},{5,389},{6,390},{7,391},{8... | collective-permute-start | bytes 983048 | tf_op jit(solution)/shard_map/ppermute | solution.py:250
  63.0 18.9 %collective-permute-start.3 = (bf16[256,640]{1,0:T(8,128)(2,1)S(1)}, bf16[256,640]{1,0:T(8,128)(2,1)S(1)}, u32[]{:S(2)}, u32[]{:S(2)}) collective-permute-start(bf16[256,640]{1,0:T(8,128)(2,1)S(1)} %all_gather.3.refs_0_), channel_id=1, source_target_pairs={{0,256},{128,384},{1,257},{129,385},{2,258},{130,386},{3,259},{131... | collective-permute-start | bytes 983048 | tf_op jit(solution)/shard_map/ppermute | solution.py:250
  64.3 17.6 %collective-permute-start.2 = (bf16[256,640]{1,0:T(8,128)(2,1)S(1)}, bf16[256,640]{1,0:T(8,128)(2,1)S(1)}, u32[]{:S(2)}, u32[]{:S(2)}) collective-permute-start(bf16[256,640]{1,0:T(8,128)(2,1)S(1)} %all_gather.3.refs_0_), channel_id=1, source_target_pairs={{0,128},{128,256},{256,384},{1,129},{129,257},{257,385},{2,130},{1... | collective-permute-start | bytes 983048 | tf_op jit(solution)/shard_map/ppermute | solution.py:250
  82.1 15.5 %collective-permute-start.5 = (bf16[1024,640]{1,0:T(8,128)(2,1)S(1)}, bf16[1024,640]{1,0:T(8,128)(2,1)}, u32[]{:S(2)}, u32[]{:S(2)}) collective-permute-start(bf16[1024,640]{1,0:T(8,128)(2,1)S(1)} %pack.1.ka_ref), channel_id=1, source_target_pairs={{0,4},{4,0},{1,5},{5,1},{2,6},{6,2},{3,7},{7,3},{8,12},{12,8},{9,1... | collective-permute-start | bytes 3932168 | tf_op jit(solution)/shard_map/ppermute | solution.py:31
  84.0 6.9 %collective-permute-start = (bf16[1536,384]{1,0:T(8,128)(2,1)S(1)}, bf16[1536,384]{1,0:T(8,128)(2,1)S(1)}, u32[]{:S(2)}, u32[]{:S(2)}) collective-permute-start(bf16[1536,384]{1,0:T(8,128)(2,1)S(1)} %copy-done), channel_id=1, source_target_pairs={{0,4},{4,0},{1,5},{5,1},{2,6},{6,2},{3,7},{7,3},{8,12},{12,8},{9,1... | collective-permute-start | bytes 3538952 | tf_op jit(solution)/shard_map/ppermute | solution.py:31
  86.4 4.4 %collective-permute-start.1 = (bf16[2,128,512]{2,1,0:T(8,128)(2,1)S(1)}, bf16[2,128,512]{2,1,0:T(8,128)(2,1)S(1)}, u32[]{:S(2)}, u32[]{:S(2)}) collective-permute-start(bf16[2,128,512]{2,1,0:T(8,128)(2,1)S(1)} %copy-done.4), channel_id=1, source_target_pairs={{0,4},{4,0},{1,5},{5,1},{2,6},{6,2},{3,7},{7,3},{8,12},{12,8},{9,1... | collective-permute-start | bytes 786440 | tf_op jit(solution)/shard_map/ppermute | solution.py:31
  88.4 8.5 %collective-permute-start.6 = (bf16[2,512,128]{2,1,0:T(8,128)(2,1)S(1)}, bf16[2,512,128]{2,1,0:T(8,128)(2,1)S(1)}, u32[]{:S(2)}, u32[]{:S(2)}) collective-permute-start(bf16[2,512,128]{2,1,0:T(8,128)(2,1)S(1)} %copy-done.11), channel_id=1, source_target_pairs={{0,4},{4,0},{1,5},{5,1},{2,6},{6,2},{3,7},{7,3},{8,12},{12,8},{9,1... | collective-permute-start | bytes 786440 | tf_op jit(solution)/shard_map/ppermute | solution.py:31
  90.9 1.0 copy-start.2
  91.9 1.3 copy-start.1
  93.2 1.3 copy-start.3
  94.4 3.1 %copy-start.10 = (bf16[256,3584]{1,0:T(8,128)(2,1)S(1)}, bf16[256,3584]{1,0:T(8,128)(2,1)}, u32[]{:S(2)}) copy-start(bf16[256,3584]{1,0:T(8,128)(2,1)} %op0.1) | copy-start | bytes 5505028
  94.4 3.1 %copy-start.12 = (bf16[2,512,128]{2,1,0:T(8,128)(2,1)S(1)}, bf16[2,512,128]{2,1,0:T(8,128)(2,1)}, u32[]{:S(2)}) copy-start(bf16[2,512,128]{2,1,0:T(8,128)(2,1)} %av0.1) | copy-start | bytes 786436
  96.9 0.7 copy-start.13
  97.6 1.0 copy-start.14
  110.2 13.4 %collective-permute-start.10 = (bf16[32,3584]{1,0:T(8,128)(2,1)S(1)}, bf16[32,3584]{1,0:T(8,128)(2,1)S(1)}, u32[]{:S(2)}, u32[]{:S(2)}) collective-permute-start(bf16[32,3584]{1,0:T(8,128)(2,1)S(1)} %get-tuple-element.22), channel_id=1, source_target_pairs={{0,16},{8,24},{16,32},{24,40},{32,48},{40,56},{48,64},{56,72},{64,... | collective-permute-start | bytes 688136 | tf_op jit(solution)/shard_map/ppermute | solution.py:27
  114.9 31.6 %collective-permute-start.8 = (bf16[64,3584]{1,0:T(8,128)(2,1)S(1)}, bf16[64,3584]{1,0:T(8,128)(2,1)S(1)}, u32[]{:S(2)}, u32[]{:S(2)}) collective-permute-start(bf16[64,3584]{1,0:T(8,128)(2,1)S(1)} %get-tuple-element.20), channel_id=1, source_target_pairs={{0,8},{8,16},{16,24},{24,32},{32,40},{40,48},{48,56},{56,64},{64,7... | collective-permute-start | bytes 1376264 | tf_op jit(solution)/shard_map/ppermute | solution.py:27
  118.3 28.2 %collective-permute-start.9 = (bf16[64,3584]{1,0:T(8,128)(2,1)S(1)}, bf16[64,3584]{1,0:T(8,128)(2,1)S(1)}, u32[]{:S(2)}, u32[]{:S(2)}) collective-permute-start(bf16[64,3584]{1,0:T(8,128)(2,1)S(1)} %get-tuple-element.21), channel_id=1, source_target_pairs={{0,120},{8,0},{16,8},{24,16},{32,24},{40,32},{48,40},{56,48},{64,5... | collective-permute-start | bytes 1376264 | tf_op jit(solution)/shard_map/ppermute | solution.py:27
  124.3 13.9 %all-to-all-start.2 = ((bf16[4,4,4,640]{3,2,1,0:T(4,128)(2,1)}), bf16[4,4,4,640]{3,2,1,0:T(4,128)(2,1)S(1)}, u32[]{:S(2)}, u32[]{:S(2)}) async-start(bf16[4,4,4,640]{3,2,1,0:T(4,128)(2,1)} %broadcast_in_dim.49), calls=%async_computation.2 | async-start | bytes 163840 | tf_op jit(solution)/shard_map/all_to_all | solution.py:36
  128.6 18.0 %collective-permute-start.11 = (bf16[32,3584]{1,0:T(8,128)(2,1)S(1)}, bf16[32,3584]{1,0:T(8,128)(2,1)S(1)}, u32[]{:S(2)}, u32[]{:S(2)}) collective-permute-start(bf16[32,3584]{1,0:T(8,128)(2,1)S(1)} %get-tuple-element.23), channel_id=1, source_target_pairs={{0,112},{8,120},{16,0},{24,8},{32,16},{40,24},{48,32},{56,40},{64,... | collective-permute-start | bytes 688136 | tf_op jit(solution)/shard_map/ppermute | solution.py:27
  146.7 11.6 %collective-permute-start.13 = (bf16[16,1792]{1,0:T(8,128)(2,1)S(1)}, bf16[16,1792]{1,0:T(8,128)(2,1)S(1)}, u32[]{:S(2)}, u32[]{:S(2)}) collective-permute-start(bf16[16,1792]{1,0:T(8,128)(2,1)S(1)} %get-tuple-element.38), channel_id=1, source_target_pairs={{0,96},{8,104},{16,112},{24,120},{32,0},{40,8},{48,16},{56,24},{64... | collective-permute-start | bytes 172040 | tf_op jit(solution)/shard_map/ppermute | solution.py:27
  153.3 16.4 %collective-permute-start.12 = (bf16[16,3584]{1,0:T(8,128)(2,1)S(1)}, bf16[16,3584]{1,0:T(8,128)(2,1)S(1)}, u32[]{:S(2)}, u32[]{:S(2)}) collective-permute-start(bf16[16,3584]{1,0:T(8,128)(2,1)S(1)} %get-tuple-element.34), channel_id=1, source_target_pairs={{0,32},{8,40},{16,48},{24,56},{32,64},{40,72},{48,80},{56,88},{64,... | collective-permute-start | bytes 344072 | tf_op jit(solution)/shard_map/ppermute | solution.py:27
  158.4 13.4 %collective-permute-start.14 = (bf16[16,3584]{1,0:T(8,128)(2,1)S(1)}, bf16[16,3584]{1,0:T(8,128)(2,1)S(1)}, u32[]{:S(2)}, u32[]{:S(2)}) collective-permute-start(bf16[16,3584]{1,0:T(8,128)(2,1)S(1)} %pad_maximum_fusion), channel_id=1, source_target_pairs={{0,96},{8,104},{16,112},{24,120},{32,0},{40,8},{48,16},{56,24},{64... | collective-permute-start | bytes 344072 | tf_op jit(solution)/shard_map/ppermute | solution.py:27
  164.6 14.9 %collective-permute-start.15 = (bf16[16,1792]{1,0:T(8,128)(2,1)S(1)}, bf16[16,1792]{1,0:T(8,128)(2,1)S(1)}, u32[]{:S(2)}, u32[]{:S(2)}) collective-permute-start(bf16[16,1792]{1,0:T(8,128)(2,1)S(1)} %get-tuple-element.37), channel_id=1, source_target_pairs={{0,64},{8,72},{16,80},{24,88},{32,96},{40,104},{48,112},{56,120},{... | collective-permute-start | bytes 172040 | tf_op jit(solution)/shard_map/ppermute | solution.py:27
  (2 other events, 1.3 us)

commit v7 on v6

--- a/solution.py
+++ b/solution.py
@@ -83,8 +83,16 @@
 
 
 def query_kernel(
-    where_ref, g_ref, wq0, wq1, ak0, ak1, freq_ref, out_ref, x_ref, *, nope, rope, qrows, chips, nzl
+    where_ref, g_ref, freq_ref, wq0, wq1, ak0, ak1, out_ref, x_ref, wq_ref, ak_ref, sems,
+    *, nope, rope, qrows, chips, nzl,
 ):
+    loads = [
+        pltpu.make_async_copy(src, dst.at[i], sems.at[2 * j + i])
+        for j, (pair, dst) in enumerate((((wq0, wq1), wq_ref), ((ak0, ak1), ak_ref)))
+        for i, src in enumerate(pair)
+    ]
+    for load in loads:
+        load.start()
     chain, z, core = where_ref[0], where_ref[1], where_ref[2]
     for i, step in enumerate(STEPS):
         at = lax.rem(z + step % chips, chips)
@@ -92,7 +100,7 @@
         x_ref[i * qrows : (i + 1) * qrows, :] = g_ref[pl.ds(pl.multiple_of(at * qrows, qrows), qrows), :]
     x = x_ref[...]
     rows = x.shape[0]
-    lat = ak0.shape[-1]
+    lat = ak_ref.shape[-1]
     idx = lax.broadcasted_iota(jnp.int32, (rows, rope), 0)
     place = chain * (chips * 2 * qrows) + query_where(idx, z, core, qrows, chips)
     angle = place.astype(F32) * freq_ref[...]
@@ -101,8 +109,11 @@
     sine = jnp.where(lane < rope // 2, -sine, sine)
     cosine = jnp.cos(angle)
     head = 0
-    for wq, ak in ((wq0, ak0), (wq1, ak1)):
-        q = jnp.dot(x, wq[...], preferred_element_type=F32).astype(BF)
+    for load in loads:
+        load.wait()
+    for side in range(2):
+        ak = ak_ref.at[side]
+        q = jnp.dot(x, wq_ref[side], preferred_element_type=F32).astype(BF)
         for h in range(ak.shape[0]):
             base = h * (nope + rope)
             r0 = head * rows
@@ -119,11 +130,18 @@
 
 def attend_kernel(
     where_ref, q_ref, ka_ref, kb_ref, av0, av1, op0, op1, o0, o1, o2, o3, o4,
-    s_ref, top_ref, l_ref, acc_ref, ho_ref, *, rows, lat, scale, nch, chips, qrows, part,
+    s_ref, top_ref, l_ref, acc_ref, ho_ref, av_ref, op_ref, sems, *, rows, lat, scale, nch, chips, qrows, part,
 ):
     chain, z, core = where_ref[0], where_ref[1], where_ref[2]
     s2 = scale * LOG2E
-    vh = av0.shape[-1]
+    loads = [
+        pltpu.make_async_copy(src, dst.at[i], sems.at[2 * j + i])
+        for j, (pair, dst) in enumerate((((av0, av1), av_ref), ((op0, op1), op_ref)))
+        for i, src in enumerate(pair)
+    ]
+    for load in loads:
+        load.start()
+    vh = av_ref.shape[-1]
     heads = q_ref.shape[0] // rows
     n = ka_ref.shape[0] // nch
     nt = (((1,), (1,)), ((), ()))
@@ -180,20 +198,21 @@
     mix(0)
     for back in range(1, nch):
         pl.when(chain >= back)(functools.partial(mix, back))
+    for load in loads:
+        load.wait()
     per = heads // 2
     for h in range(heads):
         total = jnp.sum(l_ref[h], -1, keepdims=True)
         mixed = (acc_ref[h] / total).astype(BF)
-        av = (av0 if h < per else av1)[h % per]
+        av = av_ref[h // per, h % per]
         ho_ref[:, h * vh : (h + 1) * vh] = jnp.dot(mixed, av, preferred_element_type=F32).astype(BF)
     ho = ho_ref[...]
-    k = op0.shape[0]
-    width = op0.shape[1]
+    k, width = op_ref.shape[1:]
     cut = 512 if width % 512 == 0 else width
     for c in range(0, width, cut):
         part_out = (
-            jnp.dot(ho[:, :k], op0[:, c : c + cut], preferred_element_type=F32)
-            + jnp.dot(ho[:, k:], op1[:, c : c + cut], preferred_element_type=F32)
+            jnp.dot(ho[:, :k], op_ref[0, :, c : c + cut], preferred_element_type=F32)
+            + jnp.dot(ho[:, k:], op_ref[1, :, c : c + cut], preferred_element_type=F32)
         ).astype(BF)
         at = 0
         for out_ref in (o0, o1, o2, o3, o4):
@@ -220,6 +239,7 @@
     slots = 2 * pages
     smem = pl.BlockSpec(memory_space=pltpu.SMEM)
     vm = pl.BlockSpec(memory_space=pltpu.VMEM)
+    hbm = pl.BlockSpec(memory_space=pl.ANY)
 
     def room(mib):
         return pltpu.CompilerParams(vmem_limit_bytes=mib * 1024 * 1024)
@@ -249,8 +269,9 @@
     backs = [
         lax.ppermute(own, "chain", [(i, i + k) for i in range(nch - k)]) for k in range(1, nch)
     ]
-    qz, *weights, _ = lax.optimization_barrier(
-        (qz, query_up, absorb_key, absorb_value, out_proj, own)
+    qz, _ = lax.optimization_barrier((qz, own))
+    *weights, page, _ = lax.optimization_barrier(
+        (query_up, absorb_key, absorb_value, out_proj, keys, backs[0])
     )
     qg = spread(qz, "zl").reshape(rows, ql)
     wq1, ak1, av1, op1 = [swap_core(w) for w in weights]
@@ -267,16 +288,21 @@
     q = pl.pallas_call(
         functools.partial(query_kernel, nope=nope, rope=rope, qrows=qrows, chips=nzh * nzl, nzl=nzl),
         out_shape=jax.ShapeDtypeStruct((heads * rows, kw), BF),
-        in_specs=[smem] + [vm] * 6,
+        in_specs=[smem] + [vm] * 2 + [hbm] * 4,
         out_specs=vm,
-        scratch_shapes=[pltpu.VMEM((rows, ql), BF)],
+        scratch_shapes=[
+            pltpu.VMEM((rows, ql), BF),
+            pltpu.VMEM((2,) + query_up.shape, BF),
+            pltpu.VMEM((2,) + absorb_key.shape, BF),
+            pltpu.SemaphoreType.DMA((4,)),
+        ],
         compiler_params=room(12),
         cost_estimate=pl.CostEstimate(
             flops=2 * rows * heads * (nope + rope) * ql + 2 * rows * heads * nope * lat,
             bytes_accessed=6000000, transcendentals=0,
         ),
         name="queries",
-    )(where, qg, query_up, wq1, absorb_key, ak1, frequencies(rope))
+    )(where, qg, frequencies(rope), query_up, wq1, absorb_key, ak1)
 
     n = nzh * qrows
     sums = pl.pallas_call(
@@ -285,7 +311,7 @@
             nch=nch, chips=nzh * nzl, qrows=qrows, part=part,
         ),
         out_shape=[jax.ShapeDtypeStruct((r, width), BF) for r in (n, n, n, n // 2, n // 2)],
-        in_specs=[smem] + [vm] * 7,
+        in_specs=[smem] + [vm] * 3 + [hbm] * 4,
         out_specs=[vm] * 5,
         scratch_shapes=[
             pltpu.VMEM((heads, rows, nch * block_len), F32),
@@ -293,8 +319,11 @@
             pltpu.VMEM((heads, rows, 128), F32),
             pltpu.VMEM((heads, rows, lat), F32),
             pltpu.VMEM((rows, heads * vh), BF),
+            pltpu.VMEM((2,) + absorb_value.shape, BF),
+            pltpu.VMEM((2,) + out_proj.shape, BF),
+            pltpu.SemaphoreType.DMA((4,)),
         ],
-        compiler_params=room(24),
+        compiler_params=room(28),
         cost_estimate=pl.CostEstimate(
             flops=4 * rows * heads * nch * block_len * lat, bytes_accessed=9000000,
             transcendentals=rows * heads * nch * block_len,
@@ -302,30 +331,31 @@
         name="attend",
     )(where, q, mine, other, absorb_value, av1, out_proj, op1)
 
+    up = shift_z(sums[1], 1)
+    down = shift_z(sums[2], -1)
     up2 = shift_z(sums[3], 2)
     down2 = shift_z(sums[4], -2)
-    up = shift_z(sums[1], 1)
-    down = shift_z(sums[2], -1)
-
-    def near(e):
+    cut = width // 2
+
+    def near(e, up, down):
         at = slice((e + 1) * qrows, (e + 2) * qrows)
         return sums[0][at].astype(F32) + up[at].astype(F32) + down[at].astype(F32)
 
-    cut = width // 2
-    far = near(2).astype(BF)
-    around = shift_z(far[:, cut:], -nzl)
-    direct = shift_z(far[:, :cut], 2 * nzl)
-    ahead = shift_z((near(1) + up2[qrows:].astype(F32)).astype(BF), nzl)
-    behind = near(-1) + down2[:qrows].astype(F32)
-    behind = jnp.concatenate([behind[:, :cut], behind[:, cut:] + around.astype(F32)], -1)
+    far = near(2, up, down).astype(BF)
+    far, up, down = lax.optimization_barrier((far, up, down))
+    left = shift_z(far[:, :cut], nzl).astype(F32)
+    right = shift_z(far[:, cut:], -nzl).astype(F32)
+    ahead = near(1, up, down) + up2[qrows:].astype(F32)
+    ahead = jnp.concatenate([ahead[:, :cut] + left, ahead[:, cut:]], -1)
+    ahead = shift_z(ahead.astype(BF), nzl)
+    behind = near(-1, up, down) + down2[:qrows].astype(F32)
+    behind = jnp.concatenate([behind[:, :cut], behind[:, cut:] + right], -1)
     behind = shift_z(behind.astype(BF), -nzl)
-    total = near(0) + up2[:qrows].astype(F32) + down2[qrows:].astype(F32)
+    total = near(0, up, down) + up2[:qrows].astype(F32) + down2[qrows:].astype(F32)
     total = total + ahead.astype(F32) + behind.astype(F32)
-    total = jnp.concatenate([total[:, :cut] + direct.astype(F32), total[:, cut:]], -1)
     layer_output = total.astype(BF)[None]
 
-    keys = lax.optimization_barrier((keys, up2))[0]
-    page = spread(keys.reshape(pages, part, -1), "dec")
+    page = spread(page.reshape(pages, part, -1), "dec")
     came = page[:, :, 0, lat + rope].reshape(-1).astype(jnp.int32)
     take = (came[None, :] == dec * slots + jnp.arange(slots, dtype=jnp.int32)[:, None]).astype(BF)
     placed = jnp.einsum(

time: 183 us -> 179 us (0.978)
  starting transfers between devices: 79.3 us -> 71.4 us
  waiting for transfers between devices: 36.4 us -> 43 us
  local copies, waits for them, and re-layouts: 13.1 us -> 10.9 us
    ppermute x3, waiting for transfers between devices: 16.3 us -> 25.6 us  [local(): lax.ppermute(own, 'chain', [(i, i + k) for i in range(nch - k)])]
    ppermute x8, starting transfers between devices: 41.9 us -> 33.9 us  [shift_z(): return lax.ppermute(x, Z, [(i, (i + step) % n) for i in range(n)])]
    ppermute x8, waiting for transfers between devices: 20 us -> 17.3 us  [shift_z(): return lax.ppermute(x, Z, [(i, (i + step) % n) for i in range(n)])]
    unnamed x32 -> x26, local copies, waits for them, and re-layouts: 9.1 us -> 6.92 us
  transfers between devices with their start and end apart: 19 -> 19, of which waited for: 6 -> 8; matrix products, arithmetic and copies ran while one was open for 2% -> 2% of each run, Pallas kernels for 2% -> 9%
where the time goes in v7:
time: 179 us; the launch traced here: 178 us
  starting transfers between devices  71.4 us (40%)
  waiting for transfers between devices  43 us (24%)
  blocking collectives  33.2 us (19%)
  Pallas kernels  15.7 us (9%)
  local copies, waits for them, and re-layouts  10.9 us (6%)
  other arithmetic  2.18 us (1%)
    ppermute x8, starting transfers between devices, shift_z(): return lax.ppermute(x, Z, [(i, (i + step) % n) for i in range(n)])  33.9 us
    all_gather x1, blocking collectives, local(): own = lax.all_gather(keys, Z, axis=0, tiled=True)  33.2 us
    ppermute x3, waiting for transfers between devices, local(): lax.ppermute(own, 'chain', [(i, i + k) for i in range(nch - k)])  25.6 us
    all_to_all x3, starting transfers between devices, spread(): lax.all_to_all(jnp.broadcast_to(x[None], (n,) + x.shape), axis, 0, 0, til...  22.9 us
    ppermute x8, waiting for transfers between devices, shift_z(): return lax.ppermute(x, Z, [(i, (i + step) % n) for i in range(n)])  17.3 us
    pallas_call x1, Pallas kernels, local(): pl.pallas_call(functools.partial(attend_kernel, rows=rows, lat=lat, scale...  11.2 us
    ppermute x5, starting transfers between devices, swap_core(): return lax.ppermute(x, 'core', [(0, 1), (1, 0)])  10.6 us
    unnamed x26, local copies, waits for them, and re-layouts  6.92 us
  transfers between devices with their start and end apart: 19, of which 8 were waited for; matrix products, arithmetic and copies ran while one was open for 2% of the time, Pallas kernels for 9%

profile of v7, /device:TPU:24, one launch (start us, length us, event | category | flops | bytes accessed | tf_op | source)
XLA Modules:
  0.0 177.5 jit_solution(3707668898423618975)
XLA Ops:
  0.6 1.5 broadcast_in_dim.44
  2.1 15.1 %all-to-all-start = ((bf16[4,16,1536]{2,1,0:T(8,128)(2,1)}), bf16[4,16,1536]{2,1,0:T(8,128)(2,1)S(1)}, u32[]{:S(2)}, u32[]{:S(2)}) async-start(bf16[4,16,1536]{2,1,0:T(8,128)(2,1)} %broadcast_in_dim.44), calls=%async_computation | async-start | bytes 393216 | tf_op jit(solution)/shard_map/all_to_all | solution.py:36
  21.9 33.2 %all_gather.3.refs_0_ = bf16[256,640]{1,0:T(8,128)(2,1)S(1)} all-gather(bf16[16,640]{1,0:T(8,128)(2,1)S(1)} %keys.1), channel_id=1, replica_groups=mesh['chain'=4,'zh'=4,'zl'=4,'core'=2,'dec'=4] {'zh','zl'}, dimensions={0}, use_global_device_ids=true | all-gather | bytes 348160 | tf_op jit(solution)/shard_map/all_gather | solution.py:268
  55.1 1.0 broadcast_in_dim.48
  56.1 3.5 %all-to-all-start.1 = ((bf16[4,4,16,1536]{3,2,1,0:T(8,128)(2,1)}), bf16[4,4,16,1536]{3,2,1,0:T(8,128)(2,1)S(1)}, u32[]{:S(2)}, u32[]{:S(2)}) async-start(bf16[4,4,16,1536]{3,2,1,0:T(8,128)(2,1)} %broadcast_in_dim.48), calls=%async_computation.1 | async-start | bytes 1572864 | tf_op jit(solution)/shard_map/all_to_all | solution.py:36
  59.6 1.4 collective-permute-start
  61.1 7.7 %collective-permute-done.refs_1_ = bf16[256,640]{1,0:T(8,128)(2,1)S(1)} collective-permute-done((bf16[256,640]{1,0:T(8,128)(2,1)S(1)}, bf16[256,640]{1,0:T(8,128)(2,1)S(1)}, u32[]{:S(2)}, u32[]{:S(2)}) %collective-permute-start) | collective-permute-done | bytes 327712 | tf_op jit(solution)/shard_map/ppermute | solution.py:270
  68.7 1.9 %collective-permute-start.7 = (bf16[256,3584]{1,0:T(8,128)(2,1)}, bf16[256,3584]{1,0:T(8,128)(2,1)}, u32[]{:S(2)}, u32[]{:S(2)}) collective-permute-start(bf16[256,3584]{1,0:T(8,128)(2,1)} %op0.1), channel_id=1, source_target_pairs={{0,4},{4,0},{1,5},{5,1},{2,6},{6,2},{3,7},{7,3},{8,12},{12,8},{9,1... | collective-permute-start | bytes 5505032 | tf_op jit(solution)/shard_map/ppermute | solution.py:31
  70.7 1.3 collective-permute-start.3
  72.0 1.3 collective-permute-start.4
  73.3 11.0 %collective-permute-done.3.refs_2_ = bf16[256,640]{1,0:T(8,128)(2,1)S(1)} collective-permute-done((bf16[256,640]{1,0:T(8,128)(2,1)S(1)}, bf16[256,640]{1,0:T(8,128)(2,1)S(1)}, u32[]{:S(2)}, u32[]{:S(2)}) %collective-permute-start.3) | collective-permute-done | bytes 327712 | tf_op jit(solution)/shard_map/ppermute | solution.py:270
  84.3 6.9 %collective-permute-done.4.refs_3_ = bf16[256,640]{1,0:T(8,128)(2,1)S(1)} collective-permute-done((bf16[256,640]{1,0:T(8,128)(2,1)S(1)}, bf16[256,640]{1,0:T(8,128)(2,1)S(1)}, u32[]{:S(2)}, u32[]{:S(2)}) %collective-permute-start.4) | collective-permute-done | bytes 327712 | tf_op jit(solution)/shard_map/ppermute | solution.py:270
  91.3 2.0 %collective-permute-start.5 = (bf16[1024,640]{1,0:T(8,128)(2,1)S(1)}, bf16[1024,640]{1,0:T(8,128)(2,1)}, u32[]{:S(2)}, u32[]{:S(2)}) collective-permute-start(bf16[1024,640]{1,0:T(8,128)(2,1)S(1)} %pack.1.ka_ref), channel_id=1, source_target_pairs={{0,4},{4,0},{1,5},{5,1},{2,6},{6,2},{3,7},{7,3},{8,12},{12,8},{9,1... | collective-permute-start | bytes 3932168 | tf_op jit(solution)/shard_map/ppermute | solution.py:31
  93.3 2.4 %collective-permute-start.1 = (bf16[1536,384]{1,0:T(8,128)(2,1)}, bf16[1536,384]{1,0:T(8,128)(2,1)}, u32[]{:S(2)}, u32[]{:S(2)}) collective-permute-start(bf16[1536,384]{1,0:T(8,128)(2,1)} %wq0.1), channel_id=1, source_target_pairs={{0,4},{4,0},{1,5},{5,1},{2,6},{6,2},{3,7},{7,3},{8,12},{12,8},{9,1... | collective-permute-start | bytes 3538952 | tf_op jit(solution)/shard_map/ppermute | solution.py:31
  95.7 2.0 %collective-permute-start.2 = (bf16[2,128,512]{2,1,0:T(8,128)(2,1)S(1)}, bf16[2,128,512]{2,1,0:T(8,128)(2,1)S(1)}, u32[]{:S(2)}, u32[]{:S(2)}) collective-permute-start(bf16[2,128,512]{2,1,0:T(8,128)(2,1)S(1)} %copy-done), channel_id=1, source_target_pairs={{0,4},{4,0},{1,5},{5,1},{2,6},{6,2},{3,7},{7,3},{8,12},{12,8},{9,1... | collective-permute-start | bytes 786440 | tf_op jit(solution)/shard_map/ppermute | solution.py:31
  97.7 2.3 %collective-permute-start.6 = (bf16[2,512,128]{2,1,0:T(8,128)(2,1)S(1)}, bf16[2,512,128]{2,1,0:T(8,128)(2,1)S(1)}, u32[]{:S(2)}, u32[]{:S(2)}) collective-permute-start(bf16[2,512,128]{2,1,0:T(8,128)(2,1)S(1)} %copy-done.7), channel_id=1, source_target_pairs={{0,4},{4,0},{1,5},{5,1},{2,6},{6,2},{3,7},{7,3},{8,12},{12,8},{9,1... | collective-permute-start | bytes 786440 | tf_op jit(solution)/shard_map/ppermute | solution.py:31
  100.8 4.3 %all-to-all-start.2 = ((bf16[4,4,4,640]{3,2,1,0:T(4,128)(2,1)}), bf16[4,4,4,640]{3,2,1,0:T(4,128)(2,1)S(1)}, u32[]{:S(2)}, u32[]{:S(2)}) async-start(bf16[4,4,4,640]{3,2,1,0:T(4,128)(2,1)} %broadcast_in_dim.52), calls=%async_computation.2 | async-start | bytes 163840 | tf_op jit(solution)/shard_map/all_to_all | solution.py:36
  105.1 3.7 %queries.1.q_ref = bf16[1024,640]{1,0:T(8,128)(2,1)S(1)} custom-call(s32[3]{0:T(128)S(1)} %pad_add_fusion.where_ref, bf16[256,1536]{1,0:T(8,128)(2,1)S(1)} %bitcast.18, f32[1,64]{1,0:T(1,128)S(1)} %copy-done.3, bf16[1536,384]{1,0:T(8,128)(2,1)} %wq0.1, bf16[1536,384]{1,0:T(8,128)(2,1)} %collective-permute-done.1.wq1, bf16[2,128,512]{2,1,0:T(8,128)(2,1)S(1)} %copy-done, ...), custom_call_target="tpu_custom_call" | custom-call | flops 738197504 | bytes 6000000 | tf_op jit(solution)/shard_map/queries/pallas_call | solution.py:288
  109.6 0.9 copy-done.9
  110.5 11.2 %attend.1 = (bf16[64,3584]{1,0:T(8,128)(2,1)S(1)}, bf16[64,3584]{1,0:T(8,128)(2,1)S(1)}, bf16[64,3584]{1,0:T(8,128)(2,1)S(1)}, bf16[32,3584]{1,0:T(8,128)(2,1)S(1)}, bf16[32,3584]{1,0:T(8,128)(2,1)S(1)}) custom-call(s32[3]{0:T(128)S(1)} %pad_add_fusion.where_ref, bf16[1024,640]{1,0:T(8,128)(2,1)S(1)} %queries.1.q_ref, bf16[1024,640]{1,0:T(8,128)(2,1)S(1)} %pack.1.ka_ref, ...), custom_call_target="tpu_custom_call" | custom-call | flops 4294967296 | bytes 9000000 | tf_op jit(solution)/shard_map/attend/pallas_call | solution.py:308
  123.1 3.8 %collective-permute-start.8 = (bf16[64,3584]{1,0:T(8,128)(2,1)S(1)}, bf16[64,3584]{1,0:T(8,128)(2,1)S(1)}, u32[]{:S(2)}, u32[]{:S(2)}) collective-permute-start(bf16[64,3584]{1,0:T(8,128)(2,1)S(1)} %get-tuple-element.23), channel_id=1, source_target_pairs={{0,8},{8,16},{16,24},{24,32},{32,40},{40,48},{48,56},{56,64},{64,7... | collective-permute-start | bytes 1376264 | tf_op jit(solution)/shard_map/ppermute | solution.py:27
  127.0 4.9 %collective-permute-start.9 = (bf16[64,3584]{1,0:T(8,128)(2,1)S(1)}, bf16[64,3584]{1,0:T(8,128)(2,1)S(1)}, u32[]{:S(2)}, u32[]{:S(2)}) collective-permute-start(bf16[64,3584]{1,0:T(8,128)(2,1)S(1)} %get-tuple-element.24), channel_id=1, source_target_pairs={{0,120},{8,0},{16,8},{24,16},{32,24},{40,32},{48,40},{56,48},{64,5... | collective-permute-start | bytes 1376264 | tf_op jit(solution)/shard_map/ppermute | solution.py:27
  133.3 1.9 %collective-permute-start.10 = (bf16[32,3584]{1,0:T(8,128)(2,1)}, bf16[32,3584]{1,0:T(8,128)(2,1)S(1)}, u32[]{:S(2)}, u32[]{:S(2)}) collective-permute-start(bf16[32,3584]{1,0:T(8,128)(2,1)} %copy-done.11), channel_id=1, source_target_pairs={{0,16},{8,24},{16,32},{24,40},{32,48},{40,56},{48,64},{56,72},{64,... | collective-permute-start | bytes 688136 | tf_op jit(solution)/shard_map/ppermute | solution.py:27
  135.3 6.0 %collective-permute-start.11 = (bf16[32,3584]{1,0:T(8,128)(2,1)}, bf16[32,3584]{1,0:T(8,128)(2,1)S(1)}, u32[]{:S(2)}, u32[]{:S(2)}) collective-permute-start(bf16[32,3584]{1,0:T(8,128)(2,1)} %copy-done.10), channel_id=1, source_target_pairs={{0,112},{8,120},{16,0},{24,8},{32,16},{40,24},{48,32},{56,40},{64,... | collective-permute-start | bytes 688136 | tf_op jit(solution)/shard_map/ppermute | solution.py:27
  141.9 5.7 %collective-permute-done.9 = bf16[64,3584]{1,0:T(8,128)(2,1)S(1)} collective-permute-done((bf16[64,3584]{1,0:T(8,128)(2,1)S(1)}, bf16[64,3584]{1,0:T(8,128)(2,1)S(1)}, u32[]{:S(2)}, u32[]{:S(2)}) %collective-permute-start.9) | collective-permute-done | bytes 458784 | tf_op jit(solution)/shard_map/ppermute | solution.py:27
  147.7 1.9 %collective-permute-start.12 = (bf16[16,1792]{1,0:T(8,128)(2,1)S(1)}, bf16[16,1792]{1,0:T(8,128)(2,1)S(1)}, u32[]{:S(2)}, u32[]{:S(2)}) collective-permute-start(bf16[16,1792]{1,0:T(8,128)(2,1)S(1)} %get-tuple-element.42), channel_id=1, source_target_pairs={{0,32},{8,40},{16,48},{24,56},{32,64},{40,72},{48,80},{56,88},{64,... | collective-permute-start | bytes 172040 | tf_op jit(solution)/shard_map/ppermute | solution.py:27
  149.6 3.9 %collective-permute-done.10 = bf16[32,3584]{1,0:T(8,128)(2,1)S(1)} collective-permute-done((bf16[32,3584]{1,0:T(8,128)(2,1)}, bf16[32,3584]{1,0:T(8,128)(2,1)S(1)}, u32[]{:S(2)}, u32[]{:S(2)}) %collective-permute-start.10) | collective-permute-done | bytes 229408 | tf_op jit(solution)/shard_map/ppermute | solution.py:27
  153.7 4.4 %collective-permute-start.14 = (bf16[16,1792]{1,0:T(8,128)(2,1)S(1)}, bf16[16,1792]{1,0:T(8,128)(2,1)S(1)}, u32[]{:S(2)}, u32[]{:S(2)}) collective-permute-start(bf16[16,1792]{1,0:T(8,128)(2,1)S(1)} %get-tuple-element.43), channel_id=1, source_target_pairs={{0,96},{8,104},{16,112},{24,120},{32,0},{40,8},{48,16},{56,24},{64... | collective-permute-start | bytes 172040 | tf_op jit(solution)/shard_map/ppermute | solution.py:27
  158.1 5.3 %collective-permute-start.13 = (bf16[16,3584]{1,0:T(8,128)(2,1)S(1)}, bf16[16,3584]{1,0:T(8,128)(2,1)S(1)}, u32[]{:S(2)}, u32[]{:S(2)}) collective-permute-start(bf16[16,3584]{1,0:T(8,128)(2,1)S(1)} %pad_maximum_fusion), channel_id=1, source_target_pairs={{0,32},{8,40},{16,48},{24,56},{32,64},{40,72},{48,80},{56,88},{64,... | collective-permute-start | bytes 344072 | tf_op jit(solution)/shard_map/ppermute | solution.py:27
  163.5 1.3 collective-permute-done.14
  164.8 5.6 %collective-permute-start.15 = (bf16[16,3584]{1,0:T(8,128)(2,1)S(1)}, bf16[16,3584]{1,0:T(8,128)(2,1)S(1)}, u32[]{:S(2)}, u32[]{:S(2)}) collective-permute-start(bf16[16,3584]{1,0:T(8,128)(2,1)S(1)} %pad_maximum_fusion.1), channel_id=1, source_target_pairs={{0,96},{8,104},{16,112},{24,120},{32,0},{40,8},{48,16},{56,24},{64... | collective-permute-start | bytes 344072 | tf_op jit(solution)/shard_map/ppermute | solution.py:27
  171.0 5.8 %collective-permute-done.15 = bf16[16,3584]{1,0:T(8,128)(2,1)S(1)} collective-permute-done((bf16[16,3584]{1,0:T(8,128)(2,1)S(1)}, bf16[16,3584]{1,0:T(8,128)(2,1)S(1)}, u32[]{:S(2)}, u32[]{:S(2)}) %collective-permute-start.15) | collective-permute-done | bytes 114720 | tf_op jit(solution)/shard_map/ppermute | solution.py:27
  (60 shorter events, 11.2 us)
Async XLA Ops:
  2.1 53.0 %all-to-all-start = ((bf16[4,16,1536]{2,1,0:T(8,128)(2,1)}), bf16[4,16,1536]{2,1,0:T(8,128)(2,1)S(1)}, u32[]{:S(2)}, u32[]{:S(2)}) async-start(bf16[4,16,1536]{2,1,0:T(8,128)(2,1)} %broadcast_in_dim.44), calls=%async_computation | async-start | bytes 393216 | tf_op jit(solution)/shard_map/all_to_all | solution.py:36
  18.6 0.7 copy-start.1
  19.3 0.7 copy-start.2
  20.0 0.7 copy-start.4
  20.6 0.7 copy-start.5
  56.1 44.0 %all-to-all-start.1 = ((bf16[4,4,16,1536]{3,2,1,0:T(8,128)(2,1)}), bf16[4,4,16,1536]{3,2,1,0:T(8,128)(2,1)S(1)}, u32[]{:S(2)}, u32[]{:S(2)}) async-start(bf16[4,4,16,1536]{3,2,1,0:T(8,128)(2,1)} %broadcast_in_dim.48), calls=%async_computation.1 | async-start | bytes 1572864 | tf_op jit(solution)/shard_map/all_to_all | solution.py:36
  59.6 36.0 %copy-start = (bf16[2,128,512]{2,1,0:T(8,128)(2,1)S(1)}, bf16[2,128,512]{2,1,0:T(8,128)(2,1)}, u32[]{:S(2)}) copy-start(bf16[2,128,512]{2,1,0:T(8,128)(2,1)} %ak0.1) | copy-start | bytes 786436
  59.6 38.0 %copy-start.7 = (bf16[2,512,128]{2,1,0:T(8,128)(2,1)S(1)}, bf16[2,512,128]{2,1,0:T(8,128)(2,1)}, u32[]{:S(2)}) copy-start(bf16[2,512,128]{2,1,0:T(8,128)(2,1)} %av0.1) | copy-start | bytes 786436
  59.6 45.5 %copy-start.3 = (f32[1,64]{1,0:T(1,128)S(1)}, f32[1,64]{1,0:T(1,128)}, u32[]{:S(2)}) copy-start(f32[1,64]{1,0:T(1,128)} %constant.38.freq_ref) | copy-start | bytes 772
  59.6 9.1 %collective-permute-start = (bf16[256,640]{1,0:T(8,128)(2,1)S(1)}, bf16[256,640]{1,0:T(8,128)(2,1)S(1)}, u32[]{:S(2)}, u32[]{:S(2)}) collective-permute-start(bf16[256,640]{1,0:T(8,128)(2,1)S(1)} %all_gather.3.refs_0_), channel_id=1, source_target_pairs={{0,128},{128,256},{256,384},{1,129},{129,257},{257,385},{2,130},{1... | collective-permute-start | bytes 983048 | tf_op jit(solution)/shard_map/ppermute | solution.py:270
  68.7 40.8 %collective-permute-start.7 = (bf16[256,3584]{1,0:T(8,128)(2,1)}, bf16[256,3584]{1,0:T(8,128)(2,1)}, u32[]{:S(2)}, u32[]{:S(2)}) collective-permute-start(bf16[256,3584]{1,0:T(8,128)(2,1)} %op0.1), channel_id=1, source_target_pairs={{0,4},{4,0},{1,5},{5,1},{2,6},{6,2},{3,7},{7,3},{8,12},{12,8},{9,1... | collective-permute-start | bytes 5505032 | tf_op jit(solution)/shard_map/ppermute | solution.py:31
  70.7 13.6 %collective-permute-start.3 = (bf16[256,640]{1,0:T(8,128)(2,1)S(1)}, bf16[256,640]{1,0:T(8,128)(2,1)S(1)}, u32[]{:S(2)}, u32[]{:S(2)}) collective-permute-start(bf16[256,640]{1,0:T(8,128)(2,1)S(1)} %all_gather.3.refs_0_), channel_id=1, source_target_pairs={{0,256},{128,384},{1,257},{129,385},{2,258},{130,386},{3,259},{131... | collective-permute-start | bytes 983048 | tf_op jit(solution)/shard_map/ppermute | solution.py:270
  72.0 19.2 %collective-permute-start.4 = (bf16[256,640]{1,0:T(8,128)(2,1)S(1)}, bf16[256,640]{1,0:T(8,128)(2,1)S(1)}, u32[]{:S(2)}, u32[]{:S(2)}) collective-permute-start(bf16[256,640]{1,0:T(8,128)(2,1)S(1)} %all_gather.3.refs_0_), channel_id=1, source_target_pairs={{0,384},{1,385},{2,386},{3,387},{4,388},{5,389},{6,390},{7,391},{8... | collective-permute-start | bytes 983048 | tf_op jit(solution)/shard_map/ppermute | solution.py:270
  91.3 18.2 %collective-permute-start.5 = (bf16[1024,640]{1,0:T(8,128)(2,1)S(1)}, bf16[1024,640]{1,0:T(8,128)(2,1)}, u32[]{:S(2)}, u32[]{:S(2)}) collective-permute-start(bf16[1024,640]{1,0:T(8,128)(2,1)S(1)} %pack.1.ka_ref), channel_id=1, source_target_pairs={{0,4},{4,0},{1,5},{5,1},{2,6},{6,2},{3,7},{7,3},{8,12},{12,8},{9,1... | collective-permute-start | bytes 3932168 | tf_op jit(solution)/shard_map/ppermute | solution.py:31
  93.3 11.8 %collective-permute-start.1 = (bf16[1536,384]{1,0:T(8,128)(2,1)}, bf16[1536,384]{1,0:T(8,128)(2,1)}, u32[]{:S(2)}, u32[]{:S(2)}) collective-permute-start(bf16[1536,384]{1,0:T(8,128)(2,1)} %wq0.1), channel_id=1, source_target_pairs={{0,4},{4,0},{1,5},{5,1},{2,6},{6,2},{3,7},{7,3},{8,12},{12,8},{9,1... | collective-permute-start | bytes 3538952 | tf_op jit(solution)/shard_map/ppermute | solution.py:31
  95.7 9.4 %collective-permute-start.2 = (bf16[2,128,512]{2,1,0:T(8,128)(2,1)S(1)}, bf16[2,128,512]{2,1,0:T(8,128)(2,1)S(1)}, u32[]{:S(2)}, u32[]{:S(2)}) collective-permute-start(bf16[2,128,512]{2,1,0:T(8,128)(2,1)S(1)} %copy-done), channel_id=1, source_target_pairs={{0,4},{4,0},{1,5},{5,1},{2,6},{6,2},{3,7},{7,3},{8,12},{12,8},{9,1... | collective-permute-start | bytes 786440 | tf_op jit(solution)/shard_map/ppermute | solution.py:31
  97.7 11.2 %collective-permute-start.6 = (bf16[2,512,128]{2,1,0:T(8,128)(2,1)S(1)}, bf16[2,512,128]{2,1,0:T(8,128)(2,1)S(1)}, u32[]{:S(2)}, u32[]{:S(2)}) collective-permute-start(bf16[2,512,128]{2,1,0:T(8,128)(2,1)S(1)} %copy-done.7), channel_id=1, source_target_pairs={{0,4},{4,0},{1,5},{5,1},{2,6},{6,2},{3,7},{7,3},{8,12},{12,8},{9,1... | collective-permute-start | bytes 786440 | tf_op jit(solution)/shard_map/ppermute | solution.py:31
  100.8 31.2 %all-to-all-start.2 = ((bf16[4,4,4,640]{3,2,1,0:T(4,128)(2,1)}), bf16[4,4,4,640]{3,2,1,0:T(4,128)(2,1)S(1)}, u32[]{:S(2)}, u32[]{:S(2)}) async-start(bf16[4,4,4,640]{3,2,1,0:T(4,128)(2,1)} %broadcast_in_dim.52), calls=%async_computation.2 | async-start | bytes 163840 | tf_op jit(solution)/shard_map/all_to_all | solution.py:36
  105.1 4.4 %copy-start.6 = (bf16[256,3584]{1,0:T(8,128)(2,1)S(1)}, bf16[256,3584]{1,0:T(8,128)(2,1)}, u32[]{:S(2)}) copy-start(bf16[256,3584]{1,0:T(8,128)(2,1)} %op0.1) | copy-start | bytes 5505028
  108.8 0.7 copy-start.8
  109.5 1.0 copy-start.9
  121.8 0.7 copy-start.10
  122.4 0.7 copy-start.11
  123.1 18.7 %collective-permute-start.8 = (bf16[64,3584]{1,0:T(8,128)(2,1)S(1)}, bf16[64,3584]{1,0:T(8,128)(2,1)S(1)}, u32[]{:S(2)}, u32[]{:S(2)}) collective-permute-start(bf16[64,3584]{1,0:T(8,128)(2,1)S(1)} %get-tuple-element.23), channel_id=1, source_target_pairs={{0,8},{8,16},{16,24},{24,32},{32,40},{40,48},{48,56},{56,64},{64,7... | collective-permute-start | bytes 1376264 | tf_op jit(solution)/shard_map/ppermute | solution.py:27
  127.0 20.6 %collective-permute-start.9 = (bf16[64,3584]{1,0:T(8,128)(2,1)S(1)}, bf16[64,3584]{1,0:T(8,128)(2,1)S(1)}, u32[]{:S(2)}, u32[]{:S(2)}) collective-permute-start(bf16[64,3584]{1,0:T(8,128)(2,1)S(1)} %get-tuple-element.24), channel_id=1, source_target_pairs={{0,120},{8,0},{16,8},{24,16},{32,24},{40,32},{48,40},{56,48},{64,5... | collective-permute-start | bytes 1376264 | tf_op jit(solution)/shard_map/ppermute | solution.py:27
  133.3 20.2 %collective-permute-start.10 = (bf16[32,3584]{1,0:T(8,128)(2,1)}, bf16[32,3584]{1,0:T(8,128)(2,1)S(1)}, u32[]{:S(2)}, u32[]{:S(2)}) collective-permute-start(bf16[32,3584]{1,0:T(8,128)(2,1)} %copy-done.11), channel_id=1, source_target_pairs={{0,16},{8,24},{16,32},{24,40},{32,48},{40,56},{48,64},{56,72},{64,... | collective-permute-start | bytes 688136 | tf_op jit(solution)/shard_map/ppermute | solution.py:27
  135.3 18.3 %collective-permute-start.11 = (bf16[32,3584]{1,0:T(8,128)(2,1)}, bf16[32,3584]{1,0:T(8,128)(2,1)S(1)}, u32[]{:S(2)}, u32[]{:S(2)}) collective-permute-start(bf16[32,3584]{1,0:T(8,128)(2,1)} %copy-done.10), channel_id=1, source_target_pairs={{0,112},{8,120},{16,0},{24,8},{32,16},{40,24},{48,32},{56,40},{64,... | collective-permute-start | bytes 688136 | tf_op jit(solution)/shard_map/ppermute | solution.py:27
  147.7 10.4 %collective-permute-start.12 = (bf16[16,1792]{1,0:T(8,128)(2,1)S(1)}, bf16[16,1792]{1,0:T(8,128)(2,1)S(1)}, u32[]{:S(2)}, u32[]{:S(2)}) collective-permute-start(bf16[16,1792]{1,0:T(8,128)(2,1)S(1)} %get-tuple-element.42), channel_id=1, source_target_pairs={{0,32},{8,40},{16,48},{24,56},{32,64},{40,72},{48,80},{56,88},{64,... | collective-permute-start | bytes 172040 | tf_op jit(solution)/shard_map/ppermute | solution.py:27
  153.7 11.1 %collective-permute-start.14 = (bf16[16,1792]{1,0:T(8,128)(2,1)S(1)}, bf16[16,1792]{1,0:T(8,128)(2,1)S(1)}, u32[]{:S(2)}, u32[]{:S(2)}) collective-permute-start(bf16[16,1792]{1,0:T(8,128)(2,1)S(1)} %get-tuple-element.43), channel_id=1, source_target_pairs={{0,96},{8,104},{16,112},{24,120},{32,0},{40,8},{48,16},{56,24},{64... | collective-permute-start | bytes 172040 | tf_op jit(solution)/shard_map/ppermute | solution.py:27
  158.1 12.8 %collective-permute-start.13 = (bf16[16,3584]{1,0:T(8,128)(2,1)S(1)}, bf16[16,3584]{1,0:T(8,128)(2,1)S(1)}, u32[]{:S(2)}, u32[]{:S(2)}) collective-permute-start(bf16[16,3584]{1,0:T(8,128)(2,1)S(1)} %pad_maximum_fusion), channel_id=1, source_target_pairs={{0,32},{8,40},{16,48},{24,56},{32,64},{40,72},{48,80},{56,88},{64,... | collective-permute-start | bytes 344072 | tf_op jit(solution)/shard_map/ppermute | solution.py:27
  164.8 12.0 %collective-permute-start.15 = (bf16[16,3584]{1,0:T(8,128)(2,1)S(1)}, bf16[16,3584]{1,0:T(8,128)(2,1)S(1)}, u32[]{:S(2)}, u32[]{:S(2)}) collective-permute-start(bf16[16,3584]{1,0:T(8,128)(2,1)S(1)} %pad_maximum_fusion.1), channel_id=1, source_target_pairs={{0,96},{8,104},{16,112},{24,120},{32,0},{40,8},{48,16},{56,24},{64... | collective-permute-start | bytes 344072 | tf_op jit(solution)/shard_map/ppermute | solution.py:27

commit v8 on v7

--- a/solution.py
+++ b/solution.py
@@ -74,17 +74,9 @@
     return lax.rem(z + off, chips) * (2 * qrows) + core * qrows + idx % qrows
 
 
-def pack_kernel(*refs):
-    out_ref, at = refs[-1], 0
-    for r in refs[:-1]:
-        n = r.shape[0]
-        out_ref[at : at + n, :] = r[...]
-        at += n
-
-
 def query_kernel(
     where_ref, g_ref, freq_ref, wq0, wq1, ak0, ak1, out_ref, x_ref, wq_ref, ak_ref, sems,
-    *, nope, rope, qrows, chips, nzl,
+    *, nope, rope, qrows, chips,
 ):
     loads = [
         pltpu.make_async_copy(src, dst.at[i], sems.at[2 * j + i])
@@ -96,7 +88,6 @@
     chain, z, core = where_ref[0], where_ref[1], where_ref[2]
     for i, step in enumerate(STEPS):
         at = lax.rem(z + step % chips, chips)
-        at = lax.rem(at, nzl) * (chips // nzl) + at // nzl
         x_ref[i * qrows : (i + 1) * qrows, :] = g_ref[pl.ds(pl.multiple_of(at * qrows, qrows), qrows), :]
     x = x_ref[...]
     rows = x.shape[0]
@@ -152,6 +143,9 @@
             out = op(out, x[:, c : c + 128])
         return out
 
+    def block(back):
+        return pl.ds(pl.multiple_of(jnp.maximum(chain - back, 0) * n, n), n)
+
     def score(back):
         if back == 0:
             idx = lax.broadcasted_iota(jnp.int32, (rows, 1), 0)
@@ -162,7 +156,7 @@
         for h in range(heads):
             q = q_ref[h * rows : (h + 1) * rows, :]
             for i, k_ref in enumerate((ka_ref, kb_ref)):
-                s = lax.dot_general(q, k_ref[back * n : (back + 1) * n, :], nt, preferred_element_type=F32)
+                s = lax.dot_general(q, k_ref[block(back), :], nt, preferred_element_type=F32)
                 if back == 0:
                     s = jnp.where(ok[i], s, NEG)
                 at = (2 * back + i) * n
@@ -184,7 +178,7 @@
                     total += l_ref[h]
                 l_ref[h] = total
                 part_pv = jnp.dot(
-                    p.astype(BF), k_ref[back * n : (back + 1) * n, :lat], preferred_element_type=F32
+                    p.astype(BF), k_ref[block(back), :lat], preferred_element_type=F32
                 )
                 pv = part_pv if pv is None else pv + part_pv
             acc_ref[h] = acc_ref[h] + pv if back else pv
@@ -239,7 +233,7 @@
     slots = 2 * pages
     smem = pl.BlockSpec(memory_space=pltpu.SMEM)
     vm = pl.BlockSpec(memory_space=pltpu.VMEM)
-    hbm = pl.BlockSpec(memory_space=pl.ANY)
+    hbm = pl.BlockSpec(memory_space=pltpu.HBM)
 
     def room(mib):
         return pltpu.CompilerParams(vmem_limit_bytes=mib * 1024 * 1024)
@@ -264,29 +258,16 @@
         page_owner, page_slot, raw, latent_gain[None], frequencies(rope),
     )
 
-    qz = spread(query_comp[0], "zh")
     own = lax.all_gather(keys, Z, axis=0, tiled=True)
-    backs = [
-        lax.ppermute(own, "chain", [(i, i + k) for i in range(nch - k)]) for k in range(1, nch)
-    ]
-    qz, _ = lax.optimization_barrier((qz, own))
-    *weights, page, _ = lax.optimization_barrier(
-        (query_up, absorb_key, absorb_value, out_proj, keys, backs[0])
-    )
-    qg = spread(qz, "zl").reshape(rows, ql)
-    wq1, ak1, av1, op1 = [swap_core(w) for w in weights]
-    mine = pl.pallas_call(
-        pack_kernel,
-        out_shape=jax.ShapeDtypeStruct((nch * rows, kw), BF),
-        in_specs=[vm] * nch,
-        out_specs=vm,
-        compiler_params=room(4),
-        name="pack",
-    )(own, *backs)
+    mine = spread(own, "chain").reshape(nch * rows, kw)
+    held = lax.optimization_barrier((query_comp[0], own))[0]
+    qg = lax.all_gather(held, Z, axis=0, tiled=True)
+    wq1, ak1, av1, op1 = [swap_core(w) for w in (query_up, absorb_key, absorb_value, out_proj)]
+    qg, mine = lax.optimization_barrier((qg, mine))
     other = swap_core(mine)
 
     q = pl.pallas_call(
-        functools.partial(query_kernel, nope=nope, rope=rope, qrows=qrows, chips=nzh * nzl, nzl=nzl),
+        functools.partial(query_kernel, nope=nope, rope=rope, qrows=qrows, chips=nzh * nzl),
         out_shape=jax.ShapeDtypeStruct((heads * rows, kw), BF),
         in_specs=[smem] + [vm] * 2 + [hbm] * 4,
         out_specs=vm,
@@ -355,6 +336,7 @@
     total = total + ahead.astype(F32) + behind.astype(F32)
     layer_output = total.astype(BF)[None]
 
+    page = lax.optimization_barrier((keys, far))[0]
     page = spread(page.reshape(pages, part, -1), "dec")
     came = page[:, :, 0, lat + rope].reshape(-1).astype(jnp.int32)
     take = (came[None, :] == dec * slots + jnp.arange(slots, dtype=jnp.int32)[:, None]).astype(BF)

time: 179 us -> 165 us (0.922)
  blocking collectives: 33.2 us -> 68.2 us
  waiting for transfers between devices: 43 us -> 15.1 us
  starting transfers between devices: 71.4 us -> 54.1 us
  local copies, waits for them, and re-layouts: 10.9 us -> 7.2 us
    all_gather x0 -> x1, blocking collectives: none -> 30.9 us  [local(): qg = lax.all_gather(held, Z, axis=0, tiled=True)]
    ppermute x3 -> x0, waiting for transfers between devices: 25.6 us -> none  [local(): lax.ppermute(own, 'chain', [(i, i + k) for i in range(nch - k)])]
    all_to_all x3 -> x2, starting transfers between devices: 22.9 us -> 9.08 us  [spread(): lax.all_to_all(jnp.broadcast_to(x[None], (n,) + x.shape), axis, 0, 0, til...]
    all_gather x1, blocking collectives: 33.2 us -> 37.2 us  [local(): own = lax.all_gather(keys, Z, axis=0, tiled=True)]
    ppermute x3 -> x0, starting transfers between devices: 4.01 us -> none  [local(): lax.ppermute(own, 'chain', [(i, i + k) for i in range(nch - k)])]
    unnamed x26 -> x24, local copies, waits for them, and re-layouts: 6.92 us -> 4.51 us
    ppermute x8, waiting for transfers between devices: 17.3 us -> 15 us  [shift_z(): return lax.ppermute(x, Z, [(i, (i + step) % n) for i in range(n)])]
  transfers between devices with their start and end apart: 19 -> 15, of which waited for: 8 -> 5; matrix products, arithmetic and copies ran while one was open for 2% -> 2% of each run, Pallas kernels for 9% -> 2%
where the time goes in v8:
time: 165 us; the launch traced here: 162 us
  blocking collectives  68.2 us (41%)
  starting transfers between devices  54.1 us (33%)
  waiting for transfers between devices  15.1 us (9%)
  Pallas kernels  14.4 us (9%)
  local copies, waits for them, and re-layouts  7.2 us (4%)
  other arithmetic  2.18 us (1%)
    all_gather x1, blocking collectives, local(): own = lax.all_gather(keys, Z, axis=0, tiled=True)  37.2 us
    ppermute x8, starting transfers between devices, shift_z(): return lax.ppermute(x, Z, [(i, (i + step) % n) for i in range(n)])  34.5 us
    all_gather x1, blocking collectives, local(): qg = lax.all_gather(held, Z, axis=0, tiled=True)  30.9 us
    ppermute x8, waiting for transfers between devices, shift_z(): return lax.ppermute(x, Z, [(i, (i + step) % n) for i in range(n)])  15 us
    ppermute x5, starting transfers between devices, swap_core(): return lax.ppermute(x, 'core', [(0, 1), (1, 0)])  10.6 us
    pallas_call x1, Pallas kernels, local(): pl.pallas_call(functools.partial(attend_kernel, rows=rows, lat=lat, scale...  10.5 us
    all_to_all x2, starting transfers between devices, spread(): lax.all_to_all(jnp.broadcast_to(x[None], (n,) + x.shape), axis, 0, 0, til...  9.08 us
    unnamed x24, local copies, waits for them, and re-layouts  4.51 us
  transfers between devices with their start and end apart: 15, of which 5 were waited for; matrix products, arithmetic and copies ran while one was open for 2% of the time, Pallas kernels for 2%

profile of v8, /device:TPU:24, one launch (start us, length us, event | category | flops | bytes accessed | tf_op | source)
XLA Modules:
  0.0 162.3 jit_solution(15294345074431960469)
XLA Ops:
  0.6 0.7 reshape_squeeze.7
  1.4 0.7 pad_maximum_fusion.2.x_ref
  2.1 0.7 copy-done.4
  2.8 0.7 copy-done.5
  3.4 0.7 copy-done.7
  6.0 37.2 %all_gather.6 = bf16[256,640]{1,0:T(8,128)(2,1)S(1)} all-gather(bf16[16,640]{1,0:T(8,128)(2,1)S(1)} %keys.1), channel_id=1, replica_groups=mesh['chain'=4,'zh'=4,'zl'=4,'core'=2,'dec'=4] {'zh','zl'}, dimensions={0}, use_global_device_ids=true | all-gather | bytes 348160 | tf_op jit(solution)/shard_map/all_gather | solution.py:261
  43.2 1.2 broadcast_in_dim.39
  44.4 4.8 %all-to-all-start = ((bf16[4,256,640]{2,1,0:T(8,128)(2,1)}), bf16[4,256,640]{2,1,0:T(8,128)(2,1)S(1)}, u32[]{:S(2)}, u32[]{:S(2)}) async-start(bf16[4,256,640]{2,1,0:T(8,128)(2,1)} %broadcast_in_dim.39), calls=%async_computation | async-start | bytes 2621440 | tf_op jit(solution)/shard_map/all_to_all | solution.py:36
  49.2 1.9 %collective-permute-start.4 = (bf16[256,3584]{1,0:T(8,128)(2,1)}, bf16[256,3584]{1,0:T(8,128)(2,1)}, u32[]{:S(2)}, u32[]{:S(2)}) collective-permute-start(bf16[256,3584]{1,0:T(8,128)(2,1)} %op0.1), channel_id=1, source_target_pairs={{0,4},{4,0},{1,5},{5,1},{2,6},{6,2},{3,7},{7,3},{8,12},{12,8},{9,1... | collective-permute-start | bytes 5505032 | tf_op jit(solution)/shard_map/ppermute | solution.py:31
  51.1 30.9 %all_gather.7.g_ref = bf16[256,1536]{1,0:T(8,128)(2,1)S(1)} all-gather(bf16[16,1536]{1,0:T(8,128)(2,1)} %bitcast.22), channel_id=1, replica_groups=mesh['chain'=4,'zh'=4,'zl'=4,'core'=2,'dec'=4] {'zh','zl'}, dimensions={0}, use_global_device_ids=true | all-gather | bytes 835584 | tf_op jit(solution)/shard_map/all_gather | solution.py:264
  82.1 1.9 %collective-permute-start.2 = (bf16[1024,640]{1,0:T(8,128)(2,1)S(1)}, bf16[1024,640]{1,0:T(8,128)(2,1)S(1)}, u32[]{:S(2)}, u32[]{:S(2)}) collective-permute-start(bf16[1024,640]{1,0:T(8,128)(2,1)S(1)} %bitcast.18), channel_id=1, source_target_pairs={{0,4},{4,0},{1,5},{5,1},{2,6},{6,2},{3,7},{7,3},{8,12},{12,8},{9,1... | collective-permute-start | bytes 3932168 | tf_op jit(solution)/shard_map/ppermute | solution.py:31
  84.0 2.4 %collective-permute-start = (bf16[1536,384]{1,0:T(8,128)(2,1)S(1)}, bf16[1536,384]{1,0:T(8,128)(2,1)S(1)}, u32[]{:S(2)}, u32[]{:S(2)}) collective-permute-start(bf16[1536,384]{1,0:T(8,128)(2,1)S(1)} %copy-done), channel_id=1, source_target_pairs={{0,4},{4,0},{1,5},{5,1},{2,6},{6,2},{3,7},{7,3},{8,12},{12,8},{9,1... | collective-permute-start | bytes 3538952 | tf_op jit(solution)/shard_map/ppermute | solution.py:31
  86.4 1.9 %collective-permute-start.1 = (bf16[2,128,512]{2,1,0:T(8,128)(2,1)S(1)}, bf16[2,128,512]{2,1,0:T(8,128)(2,1)S(1)}, u32[]{:S(2)}, u32[]{:S(2)}) collective-permute-start(bf16[2,128,512]{2,1,0:T(8,128)(2,1)S(1)} %copy-done.1), channel_id=1, source_target_pairs={{0,4},{4,0},{1,5},{5,1},{2,6},{6,2},{3,7},{7,3},{8,12},{12,8},{9,1... | collective-permute-start | bytes 786440 | tf_op jit(solution)/shard_map/ppermute | solution.py:31
  88.3 2.4 %collective-permute-start.3 = (bf16[2,512,128]{2,1,0:T(8,128)(2,1)}, bf16[2,512,128]{2,1,0:T(8,128)(2,1)S(1)}, u32[]{:S(2)}, u32[]{:S(2)}) collective-permute-start(bf16[2,512,128]{2,1,0:T(8,128)(2,1)} %av0.1), channel_id=1, source_target_pairs={{0,4},{4,0},{1,5},{5,1},{2,6},{6,2},{3,7},{7,3},{8,12},{12,8},{9,1... | collective-permute-start | bytes 786440 | tf_op jit(solution)/shard_map/ppermute | solution.py:31
  90.9 3.2 %queries.1.q_ref = bf16[1024,640]{1,0:T(8,128)(2,1)S(1)} custom-call(s32[3]{0:T(128)S(1)} %pad_add_fusion.where_ref, bf16[256,1536]{1,0:T(8,128)(2,1)S(1)} %all_gather.7.g_ref, f32[1,64]{1,0:T(1,128)S(1)} %copy-done.6, bf16[1536,384]{1,0:T(8,128)(2,1)S(1)} %copy-done, bf16[1536,384]{1,0:T(8,128)(2,1)S(1)} %collective-permute-done.wq1, ...), custom_call_target="tpu_custom_call" | custom-call | flops 738197504 | bytes 6000000 | tf_op jit(solution)/shard_map/queries/pallas_call | solution.py:269
  94.1 10.5 %attend.1 = (bf16[64,3584]{1,0:T(8,128)(2,1)S(1)}, bf16[64,3584]{1,0:T(8,128)(2,1)S(1)}, bf16[64,3584]{1,0:T(8,128)(2,1)S(1)}, bf16[32,3584]{1,0:T(8,128)(2,1)S(1)}, bf16[32,3584]{1,0:T(8,128)(2,1)S(1)}) custom-call(s32[3]{0:T(128)S(1)} %pad_add_fusion.where_ref, bf16[1024,640]{1,0:T(8,128)(2,1)S(1)} %queries.1.q_ref, bf16[1024,640]{1,0:T(8,128)(2,1)S(1)} %bitcast.19, ...), custom_call_target="tpu_custom_call" | custom-call | flops 4294967296 | bytes 9000000 | tf_op jit(solution)/shard_map/attend/pallas_call | solution.py:289
  104.7 3.6 %collective-permute-start.5 = (bf16[64,3584]{1,0:T(8,128)(2,1)S(1)}, bf16[64,3584]{1,0:T(8,128)(2,1)S(1)}, u32[]{:S(2)}, u32[]{:S(2)}) collective-permute-start(bf16[64,3584]{1,0:T(8,128)(2,1)S(1)} %get-tuple-element.19), channel_id=1, source_target_pairs={{0,8},{8,16},{16,24},{24,32},{32,40},{40,48},{48,56},{56,64},{64,7... | collective-permute-start | bytes 1376264 | tf_op jit(solution)/shard_map/ppermute | solution.py:27
  108.3 3.4 %collective-permute-start.6 = (bf16[64,3584]{1,0:T(8,128)(2,1)S(1)}, bf16[64,3584]{1,0:T(8,128)(2,1)S(1)}, u32[]{:S(2)}, u32[]{:S(2)}) collective-permute-start(bf16[64,3584]{1,0:T(8,128)(2,1)S(1)} %get-tuple-element.20), channel_id=1, source_target_pairs={{0,120},{8,0},{16,8},{24,16},{32,24},{40,32},{48,40},{56,48},{64,5... | collective-permute-start | bytes 1376264 | tf_op jit(solution)/shard_map/ppermute | solution.py:27
  111.8 1.9 %collective-permute-start.7 = (bf16[32,3584]{1,0:T(8,128)(2,1)S(1)}, bf16[32,3584]{1,0:T(8,128)(2,1)S(1)}, u32[]{:S(2)}, u32[]{:S(2)}) collective-permute-start(bf16[32,3584]{1,0:T(8,128)(2,1)S(1)} %get-tuple-element.23), channel_id=1, source_target_pairs={{0,16},{8,24},{16,32},{24,40},{32,48},{40,56},{48,64},{56,72},{64,... | collective-permute-start | bytes 688136 | tf_op jit(solution)/shard_map/ppermute | solution.py:27
  113.7 6.0 %collective-permute-start.8 = (bf16[32,3584]{1,0:T(8,128)(2,1)S(1)}, bf16[32,3584]{1,0:T(8,128)(2,1)S(1)}, u32[]{:S(2)}, u32[]{:S(2)}) collective-permute-start(bf16[32,3584]{1,0:T(8,128)(2,1)S(1)} %get-tuple-element.24), channel_id=1, source_target_pairs={{0,112},{8,120},{16,0},{24,8},{32,16},{40,24},{48,32},{56,40},{64,... | collective-permute-start | bytes 688136 | tf_op jit(solution)/shard_map/ppermute | solution.py:27
  119.7 3.0 %collective-permute-done.5 = bf16[64,3584]{1,0:T(8,128)(2,1)S(1)} collective-permute-done((bf16[64,3584]{1,0:T(8,128)(2,1)S(1)}, bf16[64,3584]{1,0:T(8,128)(2,1)S(1)}, u32[]{:S(2)}, u32[]{:S(2)}) %collective-permute-start.5) | collective-permute-done | bytes 458784 | tf_op jit(solution)/shard_map/ppermute | solution.py:27
  122.7 3.0 %collective-permute-done.6 = bf16[64,3584]{1,0:T(8,128)(2,1)S(1)} collective-permute-done((bf16[64,3584]{1,0:T(8,128)(2,1)S(1)}, bf16[64,3584]{1,0:T(8,128)(2,1)S(1)}, u32[]{:S(2)}, u32[]{:S(2)}) %collective-permute-start.6) | collective-permute-done | bytes 458784 | tf_op jit(solution)/shard_map/ppermute | solution.py:27
  125.8 0.7 broadcast_in_dim.43
  126.5 4.3 %all-to-all-start.1 = ((bf16[4,4,4,640]{3,2,1,0:T(4,128)(2,1)}), bf16[4,4,4,640]{3,2,1,0:T(4,128)(2,1)S(1)}, u32[]{:S(2)}, u32[]{:S(2)}) async-start(bf16[4,4,4,640]{3,2,1,0:T(4,128)(2,1)} %broadcast_in_dim.43), calls=%async_computation.1 | async-start | bytes 163840 | tf_op jit(solution)/shard_map/all_to_all | solution.py:36
  130.7 3.5 %collective-permute-start.9 = (bf16[16,1792]{1,0:T(8,128)(2,1)S(1)}, bf16[16,1792]{1,0:T(8,128)(2,1)S(1)}, u32[]{:S(2)}, u32[]{:S(2)}) collective-permute-start(bf16[16,1792]{1,0:T(8,128)(2,1)S(1)} %get-tuple-element.38), channel_id=1, source_target_pairs={{0,32},{8,40},{16,48},{24,56},{32,64},{40,72},{48,80},{56,88},{64,... | collective-permute-start | bytes 172040 | tf_op jit(solution)/shard_map/ppermute | solution.py:27
  134.2 6.2 %collective-permute-start.11 = (bf16[16,1792]{1,0:T(8,128)(2,1)S(1)}, bf16[16,1792]{1,0:T(8,128)(2,1)S(1)}, u32[]{:S(2)}, u32[]{:S(2)}) collective-permute-start(bf16[16,1792]{1,0:T(8,128)(2,1)S(1)} %get-tuple-element.39), channel_id=1, source_target_pairs={{0,96},{8,104},{16,112},{24,120},{32,0},{40,8},{48,16},{56,24},{64... | collective-permute-start | bytes 172040 | tf_op jit(solution)/shard_map/ppermute | solution.py:27
  140.7 4.9 %collective-permute-done.11 = bf16[16,1792]{1,0:T(8,128)(2,1)S(1)} collective-permute-done((bf16[16,1792]{1,0:T(8,128)(2,1)S(1)}, bf16[16,1792]{1,0:T(8,128)(2,1)S(1)}, u32[]{:S(2)}, u32[]{:S(2)}) %collective-permute-start.11) | collective-permute-done | bytes 57376 | tf_op jit(solution)/shard_map/ppermute | solution.py:27
  145.6 4.9 %collective-permute-start.12 = (bf16[16,3584]{1,0:T(8,128)(2,1)S(1)}, bf16[16,3584]{1,0:T(8,128)(2,1)S(1)}, u32[]{:S(2)}, u32[]{:S(2)}) collective-permute-start(bf16[16,3584]{1,0:T(8,128)(2,1)S(1)} %pad_maximum_fusion.1), channel_id=1, source_target_pairs={{0,96},{8,104},{16,112},{24,120},{32,0},{40,8},{48,16},{56,24},{64... | collective-permute-start | bytes 344072 | tf_op jit(solution)/shard_map/ppermute | solution.py:27
  150.6 4.9 %collective-permute-start.10 = (bf16[16,3584]{1,0:T(8,128)(2,1)S(1)}, bf16[16,3584]{1,0:T(8,128)(2,1)S(1)}, u32[]{:S(2)}, u32[]{:S(2)}) collective-permute-start(bf16[16,3584]{1,0:T(8,128)(2,1)S(1)} %pad_maximum_fusion), channel_id=1, source_target_pairs={{0,32},{8,40},{16,48},{24,56},{32,64},{40,72},{48,80},{56,88},{64,... | collective-permute-start | bytes 344072 | tf_op jit(solution)/shard_map/ppermute | solution.py:27
  157.5 1.8 %collective-permute-done.12 = bf16[16,3584]{1,0:T(8,128)(2,1)S(1)} collective-permute-done((bf16[16,3584]{1,0:T(8,128)(2,1)S(1)}, bf16[16,3584]{1,0:T(8,128)(2,1)S(1)}, u32[]{:S(2)}, u32[]{:S(2)}) %collective-permute-start.12) | collective-permute-done | bytes 114720 | tf_op jit(solution)/shard_map/ppermute | solution.py:27
  159.3 2.3 %collective-permute-done.10 = bf16[16,3584]{1,0:T(8,128)(2,1)S(1)} collective-permute-done((bf16[16,3584]{1,0:T(8,128)(2,1)S(1)}, bf16[16,3584]{1,0:T(8,128)(2,1)S(1)}, u32[]{:S(2)}, u32[]{:S(2)}) %collective-permute-start.10) | collective-permute-done | bytes 114720 | tf_op jit(solution)/shard_map/ppermute | solution.py:27
  161.6 0.8 fusion
  (49 shorter events, 4.2 us)
Async XLA Ops:
  2.1 0.7 copy-start.4
  2.7 0.7 copy-start.5
  3.4 0.7 copy-start.7
  4.1 0.7 copy-start.8
  5.4 0.6 copy-start.2
  44.4 39.6 %copy-start = (bf16[1536,384]{1,0:T(8,128)(2,1)S(1)}, bf16[1536,384]{1,0:T(8,128)(2,1)}, u32[]{:S(2)}) copy-start(bf16[1536,384]{1,0:T(8,128)(2,1)} %wq0.1) | copy-start | bytes 3538948
  44.4 42.0 %copy-start.1 = (bf16[2,128,512]{2,1,0:T(8,128)(2,1)S(1)}, bf16[2,128,512]{2,1,0:T(8,128)(2,1)}, u32[]{:S(2)}) copy-start(bf16[2,128,512]{2,1,0:T(8,128)(2,1)} %ak0.1) | copy-start | bytes 786436
  44.4 46.5 %copy-start.6 = (f32[1,64]{1,0:T(1,128)S(1)}, f32[1,64]{1,0:T(1,128)}, u32[]{:S(2)}) copy-start(f32[1,64]{1,0:T(1,128)} %constant.38.freq_ref) | copy-start | bytes 772
  44.4 37.7 %all-to-all-start = ((bf16[4,256,640]{2,1,0:T(8,128)(2,1)}), bf16[4,256,640]{2,1,0:T(8,128)(2,1)S(1)}, u32[]{:S(2)}, u32[]{:S(2)}) async-start(bf16[4,256,640]{2,1,0:T(8,128)(2,1)} %broadcast_in_dim.39), calls=%async_computation | async-start | bytes 2621440 | tf_op jit(solution)/shard_map/all_to_all | solution.py:36
  49.2 44.9 %collective-permute-start.4 = (bf16[256,3584]{1,0:T(8,128)(2,1)}, bf16[256,3584]{1,0:T(8,128)(2,1)}, u32[]{:S(2)}, u32[]{:S(2)}) collective-permute-start(bf16[256,3584]{1,0:T(8,128)(2,1)} %op0.1), channel_id=1, source_target_pairs={{0,4},{4,0},{1,5},{5,1},{2,6},{6,2},{3,7},{7,3},{8,12},{12,8},{9,1... | collective-permute-start | bytes 5505032 | tf_op jit(solution)/shard_map/ppermute | solution.py:31
  82.1 12.0 %collective-permute-start.2 = (bf16[1024,640]{1,0:T(8,128)(2,1)S(1)}, bf16[1024,640]{1,0:T(8,128)(2,1)S(1)}, u32[]{:S(2)}, u32[]{:S(2)}) collective-permute-start(bf16[1024,640]{1,0:T(8,128)(2,1)S(1)} %bitcast.18), channel_id=1, source_target_pairs={{0,4},{4,0},{1,5},{5,1},{2,6},{6,2},{3,7},{7,3},{8,12},{12,8},{9,1... | collective-permute-start | bytes 3932168 | tf_op jit(solution)/shard_map/ppermute | solution.py:31
  84.0 6.9 %collective-permute-start = (bf16[1536,384]{1,0:T(8,128)(2,1)S(1)}, bf16[1536,384]{1,0:T(8,128)(2,1)S(1)}, u32[]{:S(2)}, u32[]{:S(2)}) collective-permute-start(bf16[1536,384]{1,0:T(8,128)(2,1)S(1)} %copy-done), channel_id=1, source_target_pairs={{0,4},{4,0},{1,5},{5,1},{2,6},{6,2},{3,7},{7,3},{8,12},{12,8},{9,1... | collective-permute-start | bytes 3538952 | tf_op jit(solution)/shard_map/ppermute | solution.py:31
  86.4 4.4 %collective-permute-start.1 = (bf16[2,128,512]{2,1,0:T(8,128)(2,1)S(1)}, bf16[2,128,512]{2,1,0:T(8,128)(2,1)S(1)}, u32[]{:S(2)}, u32[]{:S(2)}) collective-permute-start(bf16[2,128,512]{2,1,0:T(8,128)(2,1)S(1)} %copy-done.1), channel_id=1, source_target_pairs={{0,4},{4,0},{1,5},{5,1},{2,6},{6,2},{3,7},{7,3},{8,12},{12,8},{9,1... | collective-permute-start | bytes 786440 | tf_op jit(solution)/shard_map/ppermute | solution.py:31
  88.3 5.7 %collective-permute-start.3 = (bf16[2,512,128]{2,1,0:T(8,128)(2,1)}, bf16[2,512,128]{2,1,0:T(8,128)(2,1)S(1)}, u32[]{:S(2)}, u32[]{:S(2)}) collective-permute-start(bf16[2,512,128]{2,1,0:T(8,128)(2,1)} %av0.1), channel_id=1, source_target_pairs={{0,4},{4,0},{1,5},{5,1},{2,6},{6,2},{3,7},{7,3},{8,12},{12,8},{9,1... | collective-permute-start | bytes 786440 | tf_op jit(solution)/shard_map/ppermute | solution.py:31
  90.8 3.3 %copy-start.9 = (bf16[256,3584]{1,0:T(8,128)(2,1)S(1)}, bf16[256,3584]{1,0:T(8,128)(2,1)}, u32[]{:S(2)}) copy-start(bf16[256,3584]{1,0:T(8,128)(2,1)} %op0.1) | copy-start | bytes 5505028
  90.8 3.3 %copy-start.10 = (bf16[2,512,128]{2,1,0:T(8,128)(2,1)S(1)}, bf16[2,512,128]{2,1,0:T(8,128)(2,1)}, u32[]{:S(2)}) copy-start(bf16[2,512,128]{2,1,0:T(8,128)(2,1)} %av0.1) | copy-start | bytes 786436
  94.1 31.7 %copy-start.3 = (bf16[16,640]{1,0:T(8,128)(2,1)S(1)}, bf16[16,640]{1,0:T(8,128)(2,1)}, u32[]{:S(2)}) copy-start(bf16[16,640]{1,0:T(8,128)(2,1)} %copy-done.2) | copy-start | bytes 61444
  104.7 18.0 %collective-permute-start.5 = (bf16[64,3584]{1,0:T(8,128)(2,1)S(1)}, bf16[64,3584]{1,0:T(8,128)(2,1)S(1)}, u32[]{:S(2)}, u32[]{:S(2)}) collective-permute-start(bf16[64,3584]{1,0:T(8,128)(2,1)S(1)} %get-tuple-element.19), channel_id=1, source_target_pairs={{0,8},{8,16},{16,24},{24,32},{32,40},{40,48},{48,56},{56,64},{64,7... | collective-permute-start | bytes 1376264 | tf_op jit(solution)/shard_map/ppermute | solution.py:27
  108.3 17.4 %collective-permute-start.6 = (bf16[64,3584]{1,0:T(8,128)(2,1)S(1)}, bf16[64,3584]{1,0:T(8,128)(2,1)S(1)}, u32[]{:S(2)}, u32[]{:S(2)}) collective-permute-start(bf16[64,3584]{1,0:T(8,128)(2,1)S(1)} %get-tuple-element.20), channel_id=1, source_target_pairs={{0,120},{8,0},{16,8},{24,16},{32,24},{40,32},{48,40},{56,48},{64,5... | collective-permute-start | bytes 1376264 | tf_op jit(solution)/shard_map/ppermute | solution.py:27
  111.8 28.7 %collective-permute-start.7 = (bf16[32,3584]{1,0:T(8,128)(2,1)S(1)}, bf16[32,3584]{1,0:T(8,128)(2,1)S(1)}, u32[]{:S(2)}, u32[]{:S(2)}) collective-permute-start(bf16[32,3584]{1,0:T(8,128)(2,1)S(1)} %get-tuple-element.23), channel_id=1, source_target_pairs={{0,16},{8,24},{16,32},{24,40},{32,48},{40,56},{48,64},{56,72},{64,... | collective-permute-start | bytes 688136 | tf_op jit(solution)/shard_map/ppermute | solution.py:27
  113.7 26.8 %collective-permute-start.8 = (bf16[32,3584]{1,0:T(8,128)(2,1)S(1)}, bf16[32,3584]{1,0:T(8,128)(2,1)S(1)}, u32[]{:S(2)}, u32[]{:S(2)}) collective-permute-start(bf16[32,3584]{1,0:T(8,128)(2,1)S(1)} %get-tuple-element.24), channel_id=1, source_target_pairs={{0,112},{8,120},{16,0},{24,8},{32,16},{40,24},{48,32},{56,40},{64,... | collective-permute-start | bytes 688136 | tf_op jit(solution)/shard_map/ppermute | solution.py:27
  126.5 29.0 %all-to-all-start.1 = ((bf16[4,4,4,640]{3,2,1,0:T(4,128)(2,1)}), bf16[4,4,4,640]{3,2,1,0:T(4,128)(2,1)S(1)}, u32[]{:S(2)}, u32[]{:S(2)}) async-start(bf16[4,4,4,640]{3,2,1,0:T(4,128)(2,1)} %broadcast_in_dim.43), calls=%async_computation.1 | async-start | bytes 163840 | tf_op jit(solution)/shard_map/all_to_all | solution.py:36
  130.7 19.8 %collective-permute-start.9 = (bf16[16,1792]{1,0:T(8,128)(2,1)S(1)}, bf16[16,1792]{1,0:T(8,128)(2,1)S(1)}, u32[]{:S(2)}, u32[]{:S(2)}) collective-permute-start(bf16[16,1792]{1,0:T(8,128)(2,1)S(1)} %get-tuple-element.38), channel_id=1, source_target_pairs={{0,32},{8,40},{16,48},{24,56},{32,64},{40,72},{48,80},{56,88},{64,... | collective-permute-start | bytes 172040 | tf_op jit(solution)/shard_map/ppermute | solution.py:27
  134.2 11.4 %collective-permute-start.11 = (bf16[16,1792]{1,0:T(8,128)(2,1)S(1)}, bf16[16,1792]{1,0:T(8,128)(2,1)S(1)}, u32[]{:S(2)}, u32[]{:S(2)}) collective-permute-start(bf16[16,1792]{1,0:T(8,128)(2,1)S(1)} %get-tuple-element.39), channel_id=1, source_target_pairs={{0,96},{8,104},{16,112},{24,120},{32,0},{40,8},{48,16},{56,24},{64... | collective-permute-start | bytes 172040 | tf_op jit(solution)/shard_map/ppermute | solution.py:27
  145.6 13.6 %collective-permute-start.12 = (bf16[16,3584]{1,0:T(8,128)(2,1)S(1)}, bf16[16,3584]{1,0:T(8,128)(2,1)S(1)}, u32[]{:S(2)}, u32[]{:S(2)}) collective-permute-start(bf16[16,3584]{1,0:T(8,128)(2,1)S(1)} %pad_maximum_fusion.1), channel_id=1, source_target_pairs={{0,96},{8,104},{16,112},{24,120},{32,0},{40,8},{48,16},{56,24},{64... | collective-permute-start | bytes 344072 | tf_op jit(solution)/shard_map/ppermute | solution.py:27
  150.6 11.0 %collective-permute-start.10 = (bf16[16,3584]{1,0:T(8,128)(2,1)S(1)}, bf16[16,3584]{1,0:T(8,128)(2,1)S(1)}, u32[]{:S(2)}, u32[]{:S(2)}) collective-permute-start(bf16[16,3584]{1,0:T(8,128)(2,1)S(1)} %pad_maximum_fusion), channel_id=1, source_target_pairs={{0,32},{8,40},{16,48},{24,56},{32,64},{40,72},{48,80},{56,88},{64,... | collective-permute-start | bytes 344072 | tf_op jit(solution)/shard_map/ppermute | solution.py:27

commit v9 on v8

--- a/solution.py
+++ b/solution.py
@@ -38,32 +38,88 @@
 
 def frequencies(width):
     half = width // 2
-    f = 10000.0 ** (-(np.arange(half) * 2.0 / width))
-    return jnp.asarray(np.concatenate([f, f]).astype(np.float32))[None]
-
-
-def turn(v, where_at, freq):
-    angle = where_at.astype(F32) * freq
-    lane = lax.broadcasted_iota(jnp.int32, v.shape, 1)
+    lane = lax.broadcasted_iota(jnp.int32, (1, width), 1)
+    out = jnp.ones((1, width), F32)
+    for i in range(1, half):
+        out = jnp.where(lane % half == i, np.float32(10000.0 ** (-2.0 * i / width)), out)
+    return out
+
+
+def rope_factors(where_at):
+    width = where_at.shape[1]
+    angle = where_at.astype(F32) * frequencies(width)
+    lane = lax.broadcasted_iota(jnp.int32, where_at.shape, 1)
     sine = jnp.sin(angle)
-    sine = jnp.where(lane < v.shape[1] // 2, -sine, sine)
-    return v * jnp.cos(angle) + swap_halves(v) * sine
-
-
-def key_kernel(base_ref, owner_ref, slot_ref, x_ref, gain_ref, freq_ref, out_ref, *, lat, part, page_len, slots):
+    return jnp.cos(angle), jnp.where(lane < width // 2, -sine, sine)
+
+
+def key_kernel(base_ref, x_ref, gain_ref, out_ref, *, lat, part, page_len):
     x = x_ref[...].astype(F32)
-    n = x.shape[0]
     latent, rot = x[:, :lat], x[:, lat:]
     norm = lax.rsqrt(jnp.mean(latent * latent, -1, keepdims=True) + 1e-06)
     out_ref[:, :lat] = (latent * norm * gain_ref[...]).astype(BF)
     row = lax.broadcasted_iota(jnp.int32, rot.shape, 0)
-    where_at = base_ref[0] + row // part * page_len + row % part
-    turned = turn(rot, where_at, freq_ref[...])
-    code = jnp.zeros(rot.shape, F32)
-    for p in range(n // part):
+    cosine, sine = rope_factors(base_ref[0] + row // part * page_len + row % part)
+    turned = rot * cosine + swap_halves(rot) * sine
+    out_ref[:, lat:] = jnp.concatenate([turned, jnp.zeros_like(turned)], -1).astype(BF)
+
+
+def page_kernel(owner_ref, slot_ref, key_ref, out_ref, *, lat, part, slots):
+    tail = key_ref[:, lat:].astype(F32)
+    row = lax.broadcasted_iota(jnp.int32, tail.shape, 0)
+    lane = lax.broadcasted_iota(jnp.int32, tail.shape, 1)
+    code = jnp.zeros(tail.shape, F32)
+    for p in range(tail.shape[0] // part):
         here = (owner_ref[0, p] * slots + slot_ref[0, p]).astype(F32)
         code = jnp.where(row // part == p, here, code)
-    out_ref[:, lat:] = jnp.concatenate([turned, code], -1).astype(BF)
+    tail = jnp.where(lane < tail.shape[1] // 2, tail, code).astype(BF)
+    for i in range(out_ref.shape[0]):
+        out_ref[i, :, :lat] = key_ref[:, :lat]
+        out_ref[i, :, lat:] = tail
+
+
+def blocks(shapes):
+    at = 0
+    for w, shape in enumerate(shapes):
+        for lead in range(int(np.prod(shape[:-2]))):
+            for c in range(0, shape[-1], 128):
+                yield at, w, lead, c, shape[-2]
+                at += shape[-2]
+
+
+def packed_rows(shapes):
+    return sum(int(np.prod(shape)) for shape in shapes) // 128
+
+
+def block_of(ref, lead, c):
+    if len(ref.shape) == 3:
+        return ref.at[lead, :, pl.ds(c, 128)]
+    return ref.at[:, pl.ds(c, 128)]
+
+
+def pack_kernel(*refs, shapes):
+    ins, out_ref, sems = refs[: len(shapes)], refs[-2], refs[-1]
+    loads = [
+        pltpu.make_async_copy(block_of(ins[w], lead, c), out_ref.at[pl.ds(at, n), :], sems.at[i])
+        for i, (at, w, lead, c, n) in enumerate(blocks(shapes))
+    ]
+    for load in loads:
+        load.start()
+    for load in loads:
+        load.wait()
+
+
+def weight_loads(own, packed, dst, which, shapes, sems):
+    loads = [(src, d.at[0]) for src, d in zip(own, dst)]
+    for at, w, lead, c, n in blocks(shapes):
+        if w in which:
+            to = block_of(dst[which.index(w)].at[1], lead, c)
+            loads.append((packed.at[pl.ds(at, n), :], to))
+    return [pltpu.make_async_copy(src, to, sems.at[i]) for i, (src, to) in enumerate(loads)]
+
+
+def load_count(which, shapes):
+    return len(which) + sum(1 for b in blocks(shapes) if b[1] in which)
 
 
 def query_where(idx, z, core, qrows, chips):
@@ -75,14 +131,10 @@
 
 
 def query_kernel(
-    where_ref, g_ref, freq_ref, wq0, wq1, ak0, ak1, out_ref, x_ref, wq_ref, ak_ref, sems,
-    *, nope, rope, qrows, chips,
+    where_ref, g_ref, wq0, ak0, packed, out_ref, x_ref, wq_ref, ak_ref, sems,
+    *, nope, rope, qrows, chips, shapes,
 ):
-    loads = [
-        pltpu.make_async_copy(src, dst.at[i], sems.at[2 * j + i])
-        for j, (pair, dst) in enumerate((((wq0, wq1), wq_ref), ((ak0, ak1), ak_ref)))
-        for i, src in enumerate(pair)
-    ]
+    loads = weight_loads((wq0, ak0), packed, (wq_ref, ak_ref), (0, 1), shapes, sems)
     for load in loads:
         load.start()
     chain, z, core = where_ref[0], where_ref[1], where_ref[2]
@@ -94,11 +146,7 @@
     lat = ak_ref.shape[-1]
     idx = lax.broadcasted_iota(jnp.int32, (rows, rope), 0)
     place = chain * (chips * 2 * qrows) + query_where(idx, z, core, qrows, chips)
-    angle = place.astype(F32) * freq_ref[...]
-    lane = lax.broadcasted_iota(jnp.int32, angle.shape, 1)
-    sine = jnp.sin(angle)
-    sine = jnp.where(lane < rope // 2, -sine, sine)
-    cosine = jnp.cos(angle)
+    cosine, sine = rope_factors(place)
     head = 0
     for load in loads:
         load.wait()
@@ -120,16 +168,12 @@
 
 
 def attend_kernel(
-    where_ref, q_ref, ka_ref, kb_ref, av0, av1, op0, op1, o0, o1, o2, o3, o4,
-    s_ref, top_ref, l_ref, acc_ref, ho_ref, av_ref, op_ref, sems, *, rows, lat, scale, nch, chips, qrows, part,
+    where_ref, q_ref, ka_ref, kb_ref, av0, op0, packed, o0, o1, o2, o3, o4,
+    s_ref, top_ref, l_ref, acc_ref, ho_ref, av_ref, op_ref, sems, *, rows, lat, scale, nch, chips, qrows, part, shapes,
 ):
     chain, z, core = where_ref[0], where_ref[1], where_ref[2]
     s2 = scale * LOG2E
-    loads = [
-        pltpu.make_async_copy(src, dst.at[i], sems.at[2 * j + i])
-        for j, (pair, dst) in enumerate((((av0, av1), av_ref), ((op0, op1), op_ref)))
-        for i, src in enumerate(pair)
-    ]
+    loads = weight_loads((av0, op0), packed, (av_ref, op_ref), (2, 3), shapes, sems)
     for load in loads:
         load.start()
     vh = av_ref.shape[-1]
@@ -247,35 +291,45 @@
     z = zh * nzl + zl
     where = jnp.stack([chain, z, core]).astype(jnp.int32)
     keys = pl.pallas_call(
-        functools.partial(key_kernel, lat=lat, part=part, page_len=part * tp_count, slots=slots),
+        functools.partial(key_kernel, lat=lat, part=part, page_len=part * tp_count),
         out_shape=jax.ShapeDtypeStruct((pages * part, kw), BF),
-        in_specs=[smem] * 3 + [vm] * 3,
+        in_specs=[smem, vm, vm],
         out_specs=vm,
         compiler_params=room(4),
         name="keys",
-    )(
-        (chain * block_len + tp_index * part).astype(jnp.int32)[None],
-        page_owner, page_slot, raw, latent_gain[None], frequencies(rope),
-    )
+    )((chain * block_len + tp_index * part).astype(jnp.int32)[None], raw, latent_gain[None])
+
+    weights = (query_up, absorb_key, absorb_value, out_proj)
+    shapes = tuple(w.shape for w in weights)
+    count = len(list(blocks(shapes)))
+    packed = pl.pallas_call(
+        functools.partial(pack_kernel, shapes=shapes),
+        out_shape=jax.ShapeDtypeStruct((packed_rows(shapes), 128), BF),
+        in_specs=[hbm] * 4,
+        out_specs=vm,
+        scratch_shapes=[pltpu.SemaphoreType.DMA((count,))],
+        compiler_params=room(8),
+        name="pack",
+    )(*weights)
+    packed = swap_core(packed)
 
     own = lax.all_gather(keys, Z, axis=0, tiled=True)
     mine = spread(own, "chain").reshape(nch * rows, kw)
     held = lax.optimization_barrier((query_comp[0], own))[0]
     qg = lax.all_gather(held, Z, axis=0, tiled=True)
-    wq1, ak1, av1, op1 = [swap_core(w) for w in (query_up, absorb_key, absorb_value, out_proj)]
     qg, mine = lax.optimization_barrier((qg, mine))
     other = swap_core(mine)
 
     q = pl.pallas_call(
-        functools.partial(query_kernel, nope=nope, rope=rope, qrows=qrows, chips=nzh * nzl),
+        functools.partial(query_kernel, nope=nope, rope=rope, qrows=qrows, chips=nzh * nzl, shapes=shapes),
         out_shape=jax.ShapeDtypeStruct((heads * rows, kw), BF),
-        in_specs=[smem] + [vm] * 2 + [hbm] * 4,
+        in_specs=[smem, vm] + [hbm] * 3,
         out_specs=vm,
         scratch_shapes=[
             pltpu.VMEM((rows, ql), BF),
             pltpu.VMEM((2,) + query_up.shape, BF),
             pltpu.VMEM((2,) + absorb_key.shape, BF),
-            pltpu.SemaphoreType.DMA((4,)),
+            pltpu.SemaphoreType.DMA((load_count((0, 1), shapes),)),
         ],
         compiler_params=room(12),
         cost_estimate=pl.CostEstimate(
@@ -283,16 +337,16 @@
             bytes_accessed=6000000, transcendentals=0,
         ),
         name="queries",
-    )(where, qg, frequencies(rope), query_up, wq1, absorb_key, ak1)
+    )(where, qg, query_up, absorb_key, packed)
 
     n = nzh * qrows
     sums = pl.pallas_call(
         functools.partial(
             attend_kernel, rows=rows, lat=lat, scale=(nope + rope) ** -0.5,
-            nch=nch, chips=nzh * nzl, qrows=qrows, part=part,
+            nch=nch, chips=nzh * nzl, qrows=qrows, part=part, shapes=shapes,
         ),
         out_shape=[jax.ShapeDtypeStruct((r, width), BF) for r in (n, n, n, n // 2, n // 2)],
-        in_specs=[smem] + [vm] * 3 + [hbm] * 4,
+        in_specs=[smem] + [vm] * 3 + [hbm] * 3,
         out_specs=[vm] * 5,
         scratch_shapes=[
             pltpu.VMEM((heads, rows, nch * block_len), F32),
@@ -302,7 +356,7 @@
             pltpu.VMEM((rows, heads * vh), BF),
             pltpu.VMEM((2,) + absorb_value.shape, BF),
             pltpu.VMEM((2,) + out_proj.shape, BF),
-            pltpu.SemaphoreType.DMA((4,)),
+            pltpu.SemaphoreType.DMA((load_count((2, 3), shapes),)),
         ],
         compiler_params=room(28),
         cost_estimate=pl.CostEstimate(
@@ -310,7 +364,7 @@
             transcendentals=rows * heads * nch * block_len,
         ),
         name="attend",
-    )(where, q, mine, other, absorb_value, av1, out_proj, op1)
+    )(where, q, mine, other, absorb_value, out_proj, packed)
 
     up = shift_z(sums[1], 1)
     down = shift_z(sums[2], -1)
@@ -336,8 +390,16 @@
     total = total + ahead.astype(F32) + behind.astype(F32)
     layer_output = total.astype(BF)[None]
 
-    page = lax.optimization_barrier((keys, far))[0]
-    page = spread(page.reshape(pages, part, -1), "dec")
+    page = lax.optimization_barrier((keys, up))[0]
+    page = pl.pallas_call(
+        functools.partial(page_kernel, lat=lat, part=part, slots=slots),
+        out_shape=jax.ShapeDtypeStruct((lax.axis_size("dec"),) + keys.shape, BF),
+        in_specs=[smem, smem, vm],
+        out_specs=vm,
+        compiler_params=room(4),
+        name="pages",
+    )(page_owner, page_slot, page)
+    page = lax.all_to_all(page, "dec", 0, 0, tiled=True).reshape(-1, pages, part, kw)
     came = page[:, :, 0, lat + rope].reshape(-1).astype(jnp.int32)
     take = (came[None, :] == dec * slots + jnp.arange(slots, dtype=jnp.int32)[:, None]).astype(BF)
     placed = jnp.einsum(

time: 165 us -> 160 us (0.970)
  the two profiles are of different devices: /device:TPU:24 before, /device:TPU:122 now
where the time goes in v9:
time: 160 us; the launch traced here: 159 us
  blocking collectives  64.7 us (40%)
  starting transfers between devices  45 us (28%)
  waiting for transfers between devices  20.4 us (13%)
  Pallas kernels  18.9 us (12%)
  local copies, waits for them, and re-layouts  8.19 us (5%)
    all_gather x1, blocking collectives, local(): own = lax.all_gather(keys, Z, axis=0, tiled=True)  32.4 us
    all_gather x1, blocking collectives, local(): qg = lax.all_gather(held, Z, axis=0, tiled=True)  32.4 us
    ppermute x8, starting transfers between devices, shift_z(): return lax.ppermute(x, Z, [(i, (i + step) % n) for i in range(n)])  31.5 us
    ppermute x8, waiting for transfers between devices, shift_z(): return lax.ppermute(x, Z, [(i, (i + step) % n) for i in range(n)])  20.4 us
    pallas_call x1, Pallas kernels, local(): pl.pallas_call(functools.partial(attend_kernel, rows=rows, lat=lat, scale...  10.8 us
    unnamed x33, local copies, waits for them, and re-layouts  6.67 us
    all_to_all x1, starting transfers between devices, local(): lax.all_to_all(page, 'dec', 0, 0, tiled=True).reshape(-1, pages, part, kw)  4.84 us
    all_to_all x1, starting transfers between devices, spread(): lax.all_to_all(jnp.broadcast_to(x[None], (n,) + x.shape), axis, 0, 0, til...  4.82 us
  transfers between devices with their start and end apart: 12, of which 5 were waited for; matrix products, arithmetic and copies ran while one was open for 2% of the time, Pallas kernels for 3%

profile of v9, /device:TPU:122, one launch (start us, length us, event | category | flops | bytes accessed | tf_op | source)
XLA Modules:
  0.0 159.5 jit_solution(15732753475173399938)
XLA Ops:
  0.6 1.3 copy-done
  1.9 1.5 copy-done.2
  3.4 0.9 copy-done.4
  4.4 0.9 copy-done.6
  5.3 3.1 %pack.1 = bf16[13824,128]{1,0:T(8,128)(2,1)} custom-call(bf16[1536,384]{1,0:T(8,128)(2,1)S(1)} %copy-done, bf16[2,128,512]{2,1,0:T(8,128)(2,1)S(1)} %copy-done.4, bf16[2,512,128]{2,1,0:T(8,128)(2,1)S(1)} %copy-done.6, bf16[256,3584]{1,0:T(8,128)(2,1)S(1)} %copy-done.2), custom_call_target="tpu_custom_call" | custom-call | tf_op jit(solution)/shard_map/pack/pallas_call | solution.py:305
  8.4 1.9 %collective-permute-start = (bf16[13824,128]{1,0:T(8,128)(2,1)}, bf16[13824,128]{1,0:T(8,128)(2,1)}, u32[]{:S(2)}, u32[]{:S(2)}) collective-permute-start(bf16[13824,128]{1,0:T(8,128)(2,1)} %pack.1), channel_id=1, source_target_pairs={{0,4},{4,0},{1,5},{5,1},{2,6},{6,2},{3,7},{7,3},{8,12},{12,8},{9,1... | collective-permute-start | bytes 10616840 | tf_op jit(solution)/shard_map/ppermute | solution.py:31
  10.5 32.4 %all_gather.6 = bf16[256,640]{1,0:T(8,128)(2,1)S(1)} all-gather(bf16[16,640]{1,0:T(8,128)(2,1)S(1)} %keys.1.key_ref), channel_id=1, replica_groups=mesh['chain'=4,'zh'=4,'zl'=4,'core'=2,'dec'=4] {'zh','zl'}, dimensions={0}, use_global_device_ids=true | all-gather | bytes 348160 | tf_op jit(solution)/shard_map/all_gather | solution.py:316
  42.9 0.6 copy-done.8
  43.5 1.3 broadcast_in_dim.25
  44.8 4.8 %all-to-all-start = ((bf16[4,256,640]{2,1,0:T(8,128)(2,1)}), bf16[4,256,640]{2,1,0:T(8,128)(2,1)S(1)}, u32[]{:S(2)}, u32[]{:S(2)}) async-start(bf16[4,256,640]{2,1,0:T(8,128)(2,1)} %broadcast_in_dim.25), calls=%async_computation | async-start | bytes 2621440 | tf_op jit(solution)/shard_map/all_to_all | solution.py:36
  49.6 32.4 %all_gather.7.g_ref = bf16[256,1536]{1,0:T(8,128)(2,1)S(1)} all-gather(bf16[16,1536]{1,0:T(8,128)(2,1)} %bitcast.22), channel_id=1, replica_groups=mesh['chain'=4,'zh'=4,'zl'=4,'core'=2,'dec'=4] {'zh','zl'}, dimensions={0}, use_global_device_ids=true | all-gather | bytes 835584 | tf_op jit(solution)/shard_map/all_gather | solution.py:319
  82.0 1.9 %collective-permute-start.1 = (bf16[1024,640]{1,0:T(8,128)(2,1)S(1)}, bf16[1024,640]{1,0:T(8,128)(2,1)S(1)}, u32[]{:S(2)}, u32[]{:S(2)}) collective-permute-start(bf16[1024,640]{1,0:T(8,128)(2,1)S(1)} %bitcast.19), channel_id=1, source_target_pairs={{0,4},{4,0},{1,5},{5,1},{2,6},{6,2},{3,7},{7,3},{8,12},{12,8},{9,1... | collective-permute-start | bytes 3932168 | tf_op jit(solution)/shard_map/ppermute | solution.py:31
  84.0 3.7 %queries.1.q_ref = bf16[1024,640]{1,0:T(8,128)(2,1)S(1)} custom-call(s32[3]{0:T(128)S(1)} %pad_add_fusion.where_ref, bf16[256,1536]{1,0:T(8,128)(2,1)S(1)} %all_gather.7.g_ref, bf16[1536,384]{1,0:T(8,128)(2,1)S(1)} %copy-done.1, bf16[2,128,512]{2,1,0:T(8,128)(2,1)S(1)} %copy-done.5, bf16[13824,128]{1,0:T(8,128)(2,1)} %collective-permute-done.packed), custom_call_target="tpu_custom_call" | custom-call | flops 738197504 | bytes 6000000 | tf_op jit(solution)/shard_map/queries/pallas_call | solution.py:323
  87.7 10.8 %attend.1 = (bf16[64,3584]{1,0:T(8,128)(2,1)S(1)}, bf16[64,3584]{1,0:T(8,128)(2,1)S(1)}, bf16[64,3584]{1,0:T(8,128)(2,1)S(1)}, bf16[32,3584]{1,0:T(8,128)(2,1)S(1)}, bf16[32,3584]{1,0:T(8,128)(2,1)S(1)}) custom-call(s32[3]{0:T(128)S(1)} %pad_add_fusion.where_ref, bf16[1024,640]{1,0:T(8,128)(2,1)S(1)} %queries.1.q_ref, bf16[1024,640]{1,0:T(8,128)(2,1)S(1)} %bitcast.20, ...), custom_call_target="tpu_custom_call" | custom-call | flops 4294967296 | bytes 9000000 | tf_op jit(solution)/shard_map/attend/pallas_call | solution.py:343
  98.5 3.5 %collective-permute-start.2 = (bf16[64,3584]{1,0:T(8,128)(2,1)S(1)}, bf16[64,3584]{1,0:T(8,128)(2,1)S(1)}, u32[]{:S(2)}, u32[]{:S(2)}) collective-permute-start(bf16[64,3584]{1,0:T(8,128)(2,1)S(1)} %get-tuple-element.19), channel_id=1, source_target_pairs={{0,8},{8,16},{16,24},{24,32},{32,40},{40,48},{48,56},{56,64},{64,7... | collective-permute-start | bytes 1376264 | tf_op jit(solution)/shard_map/ppermute | solution.py:27
  102.0 2.4 %collective-permute-start.3 = (bf16[64,3584]{1,0:T(8,128)(2,1)S(1)}, bf16[64,3584]{1,0:T(8,128)(2,1)S(1)}, u32[]{:S(2)}, u32[]{:S(2)}) collective-permute-start(bf16[64,3584]{1,0:T(8,128)(2,1)S(1)} %get-tuple-element.20), channel_id=1, source_target_pairs={{0,120},{8,0},{16,8},{24,16},{32,24},{40,32},{48,40},{56,48},{64,5... | collective-permute-start | bytes 1376264 | tf_op jit(solution)/shard_map/ppermute | solution.py:27
  104.4 4.1 %collective-permute-start.4 = (bf16[32,3584]{1,0:T(8,128)(2,1)S(1)}, bf16[32,3584]{1,0:T(8,128)(2,1)S(1)}, u32[]{:S(2)}, u32[]{:S(2)}) collective-permute-start(bf16[32,3584]{1,0:T(8,128)(2,1)S(1)} %get-tuple-element.23), channel_id=1, source_target_pairs={{0,16},{8,24},{16,32},{24,40},{32,48},{40,56},{48,64},{56,72},{64,... | collective-permute-start | bytes 688136 | tf_op jit(solution)/shard_map/ppermute | solution.py:27
  108.5 2.7 %collective-permute-start.5 = (bf16[32,3584]{1,0:T(8,128)(2,1)S(1)}, bf16[32,3584]{1,0:T(8,128)(2,1)S(1)}, u32[]{:S(2)}, u32[]{:S(2)}) collective-permute-start(bf16[32,3584]{1,0:T(8,128)(2,1)S(1)} %get-tuple-element.24), channel_id=1, source_target_pairs={{0,112},{8,120},{16,0},{24,8},{32,16},{40,24},{48,32},{56,40},{64,... | collective-permute-start | bytes 688136 | tf_op jit(solution)/shard_map/ppermute | solution.py:27
  111.2 2.6 %collective-permute-done.2 = bf16[64,3584]{1,0:T(8,128)(2,1)S(1)} collective-permute-done((bf16[64,3584]{1,0:T(8,128)(2,1)S(1)}, bf16[64,3584]{1,0:T(8,128)(2,1)S(1)}, u32[]{:S(2)}, u32[]{:S(2)}) %collective-permute-start.2) | collective-permute-done | bytes 458784 | tf_op jit(solution)/shard_map/ppermute | solution.py:27
  113.8 5.9 %collective-permute-done.3 = bf16[64,3584]{1,0:T(8,128)(2,1)S(1)} collective-permute-done((bf16[64,3584]{1,0:T(8,128)(2,1)S(1)}, bf16[64,3584]{1,0:T(8,128)(2,1)S(1)}, u32[]{:S(2)}, u32[]{:S(2)}) %collective-permute-start.3) | collective-permute-done | bytes 458784 | tf_op jit(solution)/shard_map/ppermute | solution.py:27
  119.7 1.2 pages.1
  120.9 4.8 %all-to-all-start.1 = ((bf16[4,16,640]{2,1,0:T(8,128)(2,1)}), bf16[4,16,640]{2,1,0:T(8,128)(2,1)S(1)}, u32[]{:S(2)}, u32[]{:S(2)}) async-start(bf16[4,16,640]{2,1,0:T(8,128)(2,1)} %pages.1), calls=%async_computation.1 | async-start | bytes 163840 | tf_op jit(solution)/shard_map/all_to_all | solution.py:402
  125.8 6.9 %collective-permute-start.6 = (bf16[16,1792]{1,0:T(8,128)(2,1)S(1)}, bf16[16,1792]{1,0:T(8,128)(2,1)S(1)}, u32[]{:S(2)}, u32[]{:S(2)}) collective-permute-start(bf16[16,1792]{1,0:T(8,128)(2,1)S(1)} %get-tuple-element.32), channel_id=1, source_target_pairs={{0,32},{8,40},{16,48},{24,56},{32,64},{40,72},{48,80},{56,88},{64,... | collective-permute-start | bytes 172040 | tf_op jit(solution)/shard_map/ppermute | solution.py:27
  132.8 2.9 %collective-permute-start.8 = (bf16[16,1792]{1,0:T(8,128)(2,1)S(1)}, bf16[16,1792]{1,0:T(8,128)(2,1)S(1)}, u32[]{:S(2)}, u32[]{:S(2)}) collective-permute-start(bf16[16,1792]{1,0:T(8,128)(2,1)S(1)} %get-tuple-element.33), channel_id=1, source_target_pairs={{0,96},{8,104},{16,112},{24,120},{32,0},{40,8},{48,16},{56,24},{64... | collective-permute-start | bytes 172040 | tf_op jit(solution)/shard_map/ppermute | solution.py:27
  135.8 6.9 %collective-permute-start.7 = (bf16[16,3584]{1,0:T(8,128)(2,1)S(1)}, bf16[16,3584]{1,0:T(8,128)(2,1)S(1)}, u32[]{:S(2)}, u32[]{:S(2)}) collective-permute-start(bf16[16,3584]{1,0:T(8,128)(2,1)S(1)} %pad_maximum_fusion), channel_id=1, source_target_pairs={{0,32},{8,40},{16,48},{24,56},{32,64},{40,72},{48,80},{56,88},{64,... | collective-permute-start | bytes 344072 | tf_op jit(solution)/shard_map/ppermute | solution.py:27
  142.7 0.8 collective-permute-done.8
  143.5 2.3 %collective-permute-start.9 = (bf16[16,3584]{1,0:T(8,128)(2,1)S(1)}, bf16[16,3584]{1,0:T(8,128)(2,1)S(1)}, u32[]{:S(2)}, u32[]{:S(2)}) collective-permute-start(bf16[16,3584]{1,0:T(8,128)(2,1)S(1)} %pad_maximum_fusion.1), channel_id=1, source_target_pairs={{0,96},{8,104},{16,112},{24,120},{32,0},{40,8},{48,16},{56,24},{64... | collective-permute-start | bytes 344072 | tf_op jit(solution)/shard_map/ppermute | solution.py:27
  146.3 0.6 copy.15
  147.0 0.6 copy.16
  147.6 0.8 collective-permute-done.7
  148.4 10.4 %collective-permute-done.9 = bf16[16,3584]{1,0:T(8,128)(2,1)S(1)} collective-permute-done((bf16[16,3584]{1,0:T(8,128)(2,1)S(1)}, bf16[16,3584]{1,0:T(8,128)(2,1)S(1)}, u32[]{:S(2)}, u32[]{:S(2)}) %collective-permute-start.9) | collective-permute-done | bytes 114720 | tf_op jit(solution)/shard_map/ppermute | solution.py:27
  158.7 0.8 fusion
  (55 shorter events, 1.1 us)
Async XLA Ops:
  0.6 1.3 copy-start
  1.9 1.5 copy-start.2
  3.4 0.9 copy-start.4
  4.4 0.9 copy-start.6
  5.3 5.1 %copy-start.13 = (bf16[1,4,4,512]{3,2,1,0:T(4,128)(2,1)S(1)}, bf16[1,4,4,512]{3,2,1,0:T(4,128)(2,1)}, u32[]{:S(2)}) copy-start(bf16[1,4,4,512]{3,2,1,0:T(4,128)(2,1)} %param.11) | copy-start | bytes 49156
  5.3 5.1 %copy-start.14 = (bf16[1,4,4,64]{3,2,1,0:T(4,128)(2,1)S(1)}, bf16[1,4,4,64]{3,2,1,0:T(4,128)(2,1)}, u32[]{:S(2)}) copy-start(bf16[1,4,4,64]{3,2,1,0:T(4,128)(2,1)} %param.12) | copy-start | bytes 6148
  5.3 5.1 %copy-start.10 = (f32[512]{0:T(512)S(1)}, f32[512]{0:T(512)}, u32[]{:S(2)}) copy-start(f32[512]{0:T(512)} %param.13) | copy-start | bytes 6148
  8.4 75.5 %collective-permute-start = (bf16[13824,128]{1,0:T(8,128)(2,1)}, bf16[13824,128]{1,0:T(8,128)(2,1)}, u32[]{:S(2)}, u32[]{:S(2)}) collective-permute-start(bf16[13824,128]{1,0:T(8,128)(2,1)} %pack.1), channel_id=1, source_target_pairs={{0,4},{4,0},{1,5},{5,1},{2,6},{6,2},{3,7},{7,3},{8,12},{12,8},{9,1... | collective-permute-start | bytes 10616840 | tf_op jit(solution)/shard_map/ppermute | solution.py:31
  42.9 0.6 copy-start.8
  44.8 39.2 %copy-start.1 = (bf16[1536,384]{1,0:T(8,128)(2,1)S(1)}, bf16[1536,384]{1,0:T(8,128)(2,1)}, u32[]{:S(2)}) copy-start(bf16[1536,384]{1,0:T(8,128)(2,1)} %wq0.1) | copy-start | bytes 3538948
  44.8 39.2 %copy-start.5 = (bf16[2,128,512]{2,1,0:T(8,128)(2,1)S(1)}, bf16[2,128,512]{2,1,0:T(8,128)(2,1)}, u32[]{:S(2)}) copy-start(bf16[2,128,512]{2,1,0:T(8,128)(2,1)} %ak0.1) | copy-start | bytes 786436
  44.8 37.2 %all-to-all-start = ((bf16[4,256,640]{2,1,0:T(8,128)(2,1)}), bf16[4,256,640]{2,1,0:T(8,128)(2,1)S(1)}, u32[]{:S(2)}, u32[]{:S(2)}) async-start(bf16[4,256,640]{2,1,0:T(8,128)(2,1)} %broadcast_in_dim.25), calls=%async_computation | async-start | bytes 2621440 | tf_op jit(solution)/shard_map/all_to_all | solution.py:36
  82.0 5.7 %collective-permute-start.1 = (bf16[1024,640]{1,0:T(8,128)(2,1)S(1)}, bf16[1024,640]{1,0:T(8,128)(2,1)S(1)}, u32[]{:S(2)}, u32[]{:S(2)}) collective-permute-start(bf16[1024,640]{1,0:T(8,128)(2,1)S(1)} %bitcast.19), channel_id=1, source_target_pairs={{0,4},{4,0},{1,5},{5,1},{2,6},{6,2},{3,7},{7,3},{8,12},{12,8},{9,1... | collective-permute-start | bytes 3932168 | tf_op jit(solution)/shard_map/ppermute | solution.py:31
  83.9 3.7 %copy-start.3 = (bf16[256,3584]{1,0:T(8,128)(2,1)S(1)}, bf16[256,3584]{1,0:T(8,128)(2,1)}, u32[]{:S(2)}) copy-start(bf16[256,3584]{1,0:T(8,128)(2,1)} %op0.1) | copy-start | bytes 5505028
  83.9 3.8 %copy-start.7 = (bf16[2,512,128]{2,1,0:T(8,128)(2,1)S(1)}, bf16[2,512,128]{2,1,0:T(8,128)(2,1)}, u32[]{:S(2)}) copy-start(bf16[2,512,128]{2,1,0:T(8,128)(2,1)} %av0.1) | copy-start | bytes 786436
  87.6 32.0 %copy-start.9 = (bf16[16,640]{1,0:T(8,128)(2,1)S(1)}, bf16[16,640]{1,0:T(8,128)(2,1)}, u32[]{:S(2)}) copy-start(bf16[16,640]{1,0:T(8,128)(2,1)} %copy-done.8) | copy-start | bytes 61444
  87.7 32.0 %copy-start.11 = (s32[1,4]{1,0:T(1,128)S(1)}, s32[1,4]{1,0:T(1,128)}, u32[]{:S(2)}) copy-start(s32[1,4]{1,0:T(1,128)} %owner_ref.1) | copy-start | bytes 52
  87.7 32.0 %copy-start.12 = (s32[1,4]{1,0:T(1,128)S(1)}, s32[1,4]{1,0:T(1,128)}, u32[]{:S(2)}) copy-start(s32[1,4]{1,0:T(1,128)} %slot_ref.1) | copy-start | bytes 52
  98.5 15.2 %collective-permute-start.2 = (bf16[64,3584]{1,0:T(8,128)(2,1)S(1)}, bf16[64,3584]{1,0:T(8,128)(2,1)S(1)}, u32[]{:S(2)}, u32[]{:S(2)}) collective-permute-start(bf16[64,3584]{1,0:T(8,128)(2,1)S(1)} %get-tuple-element.19), channel_id=1, source_target_pairs={{0,8},{8,16},{16,24},{24,32},{32,40},{40,48},{48,56},{56,64},{64,7... | collective-permute-start | bytes 1376264 | tf_op jit(solution)/shard_map/ppermute | solution.py:27
  102.0 17.6 %collective-permute-start.3 = (bf16[64,3584]{1,0:T(8,128)(2,1)S(1)}, bf16[64,3584]{1,0:T(8,128)(2,1)S(1)}, u32[]{:S(2)}, u32[]{:S(2)}) collective-permute-start(bf16[64,3584]{1,0:T(8,128)(2,1)S(1)} %get-tuple-element.20), channel_id=1, source_target_pairs={{0,120},{8,0},{16,8},{24,16},{32,24},{40,32},{48,40},{56,48},{64,5... | collective-permute-start | bytes 1376264 | tf_op jit(solution)/shard_map/ppermute | solution.py:27
  104.4 28.3 %collective-permute-start.4 = (bf16[32,3584]{1,0:T(8,128)(2,1)S(1)}, bf16[32,3584]{1,0:T(8,128)(2,1)S(1)}, u32[]{:S(2)}, u32[]{:S(2)}) collective-permute-start(bf16[32,3584]{1,0:T(8,128)(2,1)S(1)} %get-tuple-element.23), channel_id=1, source_target_pairs={{0,16},{8,24},{16,32},{24,40},{32,48},{40,56},{48,64},{56,72},{64,... | collective-permute-start | bytes 688136 | tf_op jit(solution)/shard_map/ppermute | solution.py:27
  108.5 24.2 %collective-permute-start.5 = (bf16[32,3584]{1,0:T(8,128)(2,1)S(1)}, bf16[32,3584]{1,0:T(8,128)(2,1)S(1)}, u32[]{:S(2)}, u32[]{:S(2)}) collective-permute-start(bf16[32,3584]{1,0:T(8,128)(2,1)S(1)} %get-tuple-element.24), channel_id=1, source_target_pairs={{0,112},{8,120},{16,0},{24,8},{32,16},{40,24},{48,32},{56,40},{64,... | collective-permute-start | bytes 688136 | tf_op jit(solution)/shard_map/ppermute | solution.py:27
  120.9 24.9 %all-to-all-start.1 = ((bf16[4,16,640]{2,1,0:T(8,128)(2,1)}), bf16[4,16,640]{2,1,0:T(8,128)(2,1)S(1)}, u32[]{:S(2)}, u32[]{:S(2)}) async-start(bf16[4,16,640]{2,1,0:T(8,128)(2,1)} %pages.1), calls=%async_computation.1 | async-start | bytes 163840 | tf_op jit(solution)/shard_map/all_to_all | solution.py:402
  125.8 10.0 %collective-permute-start.6 = (bf16[16,1792]{1,0:T(8,128)(2,1)S(1)}, bf16[16,1792]{1,0:T(8,128)(2,1)S(1)}, u32[]{:S(2)}, u32[]{:S(2)}) collective-permute-start(bf16[16,1792]{1,0:T(8,128)(2,1)S(1)} %get-tuple-element.32), channel_id=1, source_target_pairs={{0,32},{8,40},{16,48},{24,56},{32,64},{40,72},{48,80},{56,88},{64,... | collective-permute-start | bytes 172040 | tf_op jit(solution)/shard_map/ppermute | solution.py:27
  132.8 10.6 %collective-permute-start.8 = (bf16[16,1792]{1,0:T(8,128)(2,1)S(1)}, bf16[16,1792]{1,0:T(8,128)(2,1)S(1)}, u32[]{:S(2)}, u32[]{:S(2)}) collective-permute-start(bf16[16,1792]{1,0:T(8,128)(2,1)S(1)} %get-tuple-element.33), channel_id=1, source_target_pairs={{0,96},{8,104},{16,112},{24,120},{32,0},{40,8},{48,16},{56,24},{64... | collective-permute-start | bytes 172040 | tf_op jit(solution)/shard_map/ppermute | solution.py:27
  135.8 12.6 %collective-permute-start.7 = (bf16[16,3584]{1,0:T(8,128)(2,1)S(1)}, bf16[16,3584]{1,0:T(8,128)(2,1)S(1)}, u32[]{:S(2)}, u32[]{:S(2)}) collective-permute-start(bf16[16,3584]{1,0:T(8,128)(2,1)S(1)} %pad_maximum_fusion), channel_id=1, source_target_pairs={{0,32},{8,40},{16,48},{24,56},{32,64},{40,72},{48,80},{56,88},{64,... | collective-permute-start | bytes 344072 | tf_op jit(solution)/shard_map/ppermute | solution.py:27
  143.5 15.3 %collective-permute-start.9 = (bf16[16,3584]{1,0:T(8,128)(2,1)S(1)}, bf16[16,3584]{1,0:T(8,128)(2,1)S(1)}, u32[]{:S(2)}, u32[]{:S(2)}) collective-permute-start(bf16[16,3584]{1,0:T(8,128)(2,1)S(1)} %pad_maximum_fusion.1), channel_id=1, source_target_pairs={{0,96},{8,104},{16,112},{24,120},{32,0},{40,8},{48,16},{56,24},{64... | collective-permute-start | bytes 344072 | tf_op jit(solution)/shard_map/ppermute | solution.py:27

commit v10 on v9

--- a/solution.py
+++ b/solution.py
@@ -51,17 +51,6 @@
     lane = lax.broadcasted_iota(jnp.int32, where_at.shape, 1)
     sine = jnp.sin(angle)
     return jnp.cos(angle), jnp.where(lane < width // 2, -sine, sine)
-
-
-def key_kernel(base_ref, x_ref, gain_ref, out_ref, *, lat, part, page_len):
-    x = x_ref[...].astype(F32)
-    latent, rot = x[:, :lat], x[:, lat:]
-    norm = lax.rsqrt(jnp.mean(latent * latent, -1, keepdims=True) + 1e-06)
-    out_ref[:, :lat] = (latent * norm * gain_ref[...]).astype(BF)
-    row = lax.broadcasted_iota(jnp.int32, rot.shape, 0)
-    cosine, sine = rope_factors(base_ref[0] + row // part * page_len + row % part)
-    turned = rot * cosine + swap_halves(rot) * sine
-    out_ref[:, lat:] = jnp.concatenate([turned, jnp.zeros_like(turned)], -1).astype(BF)
 
 
 def page_kernel(owner_ref, slot_ref, key_ref, out_ref, *, lat, part, slots):
@@ -97,14 +86,22 @@
     return ref.at[:, pl.ds(c, 128)]
 
 
-def pack_kernel(*refs, shapes):
-    ins, out_ref, sems = refs[: len(shapes)], refs[-2], refs[-1]
+def key_kernel(base_ref, x_ref, gain_ref, *refs, lat, part, page_len, shapes):
+    ins, out_ref, packed, sems = refs[: len(shapes)], refs[-3], refs[-2], refs[-1]
     loads = [
-        pltpu.make_async_copy(block_of(ins[w], lead, c), out_ref.at[pl.ds(at, n), :], sems.at[i])
+        pltpu.make_async_copy(block_of(ins[w], lead, c), packed.at[pl.ds(at, n), :], sems.at[i])
         for i, (at, w, lead, c, n) in enumerate(blocks(shapes))
     ]
     for load in loads:
         load.start()
+    x = x_ref[...].astype(F32)
+    latent, rot = x[:, :lat], x[:, lat:]
+    norm = lax.rsqrt(jnp.mean(latent * latent, -1, keepdims=True) + 1e-06)
+    out_ref[:, :lat] = (latent * norm * gain_ref[...]).astype(BF)
+    row = lax.broadcasted_iota(jnp.int32, rot.shape, 0)
+    cosine, sine = rope_factors(base_ref[0] + row // part * page_len + row % part)
+    turned = rot * cosine + swap_halves(rot) * sine
+    out_ref[:, lat:] = jnp.concatenate([turned, jnp.zeros_like(turned)], -1).astype(BF)
     for load in loads:
         load.wait()
 
@@ -290,34 +287,43 @@
     heads = 2 * heads_here
     z = zh * nzl + zl
     where = jnp.stack([chain, z, core]).astype(jnp.int32)
-    keys = pl.pallas_call(
-        functools.partial(key_kernel, lat=lat, part=part, page_len=part * tp_count),
-        out_shape=jax.ShapeDtypeStruct((pages * part, kw), BF),
-        in_specs=[smem, vm, vm],
-        out_specs=vm,
-        compiler_params=room(4),
-        name="keys",
-    )((chain * block_len + tp_index * part).astype(jnp.int32)[None], raw, latent_gain[None])
-
     weights = (query_up, absorb_key, absorb_value, out_proj)
     shapes = tuple(w.shape for w in weights)
     count = len(list(blocks(shapes)))
-    packed = pl.pallas_call(
-        functools.partial(pack_kernel, shapes=shapes),
-        out_shape=jax.ShapeDtypeStruct((packed_rows(shapes), 128), BF),
-        in_specs=[hbm] * 4,
-        out_specs=vm,
+    keys, packed = pl.pallas_call(
+        functools.partial(
+            key_kernel, lat=lat, part=part, page_len=part * tp_count, shapes=shapes
+        ),
+        out_shape=(
+            jax.ShapeDtypeStruct((pages * part, kw), BF),
+            jax.ShapeDtypeStruct((packed_rows(shapes), 128), BF),
+        ),
+        in_specs=[smem, vm, vm] + [hbm] * 4,
+        out_specs=(vm, hbm),
         scratch_shapes=[pltpu.SemaphoreType.DMA((count,))],
-        compiler_params=room(8),
-        name="pack",
-    )(*weights)
+        compiler_params=room(56),
+        name="keys",
+    )(
+        (chain * block_len + tp_index * part).astype(jnp.int32)[None], raw, latent_gain[None],
+        *weights,
+    )
     packed = swap_core(packed)
 
     own = lax.all_gather(keys, Z, axis=0, tiled=True)
     mine = spread(own, "chain").reshape(nch * rows, kw)
     held = lax.optimization_barrier((query_comp[0], own))[0]
     qg = lax.all_gather(held, Z, axis=0, tiled=True)
-    qg, mine = lax.optimization_barrier((qg, mine))
+    page = lax.optimization_barrier((keys, own))[0]
+    page = pl.pallas_call(
+        functools.partial(page_kernel, lat=lat, part=part, slots=slots),
+        out_shape=jax.ShapeDtypeStruct((lax.axis_size("dec"),) + keys.shape, BF),
+        in_specs=[smem, smem, vm],
+        out_specs=vm,
+        compiler_params=room(4),
+        name="pages",
+    )(page_owner, page_slot, page)
+    page = lax.all_to_all(page, "dec", 0, 0, tiled=True).reshape(-1, pages, part, kw)
+    qg, mine, page = lax.optimization_barrier((qg, mine, page))
     other = swap_core(mine)
 
     q = pl.pallas_call(
@@ -390,16 +396,6 @@
     total = total + ahead.astype(F32) + behind.astype(F32)
     layer_output = total.astype(BF)[None]
 
-    page = lax.optimization_barrier((keys, up))[0]
-    page = pl.pallas_call(
-        functools.partial(page_kernel, lat=lat, part=part, slots=slots),
-        out_shape=jax.ShapeDtypeStruct((lax.axis_size("dec"),) + keys.shape, BF),
-        in_specs=[smem, smem, vm],
-        out_specs=vm,
-        compiler_params=room(4),
-        name="pages",
-    )(page_owner, page_slot, page)
-    page = lax.all_to_all(page, "dec", 0, 0, tiled=True).reshape(-1, pages, part, kw)
     came = page[:, :, 0, lat + rope].reshape(-1).astype(jnp.int32)
     take = (came[None, :] == dec * slots + jnp.arange(slots, dtype=jnp.int32)[:, None]).astype(BF)
     placed = jnp.einsum(

time: 160 us -> 279 us (1.74)
  the two profiles are of different devices: /device:TPU:122 before, /device:TPU:24 now
where the time goes in v10:
time: 279 us; the launch traced here: 277 us
  Pallas kernels  126 us (45%)
  blocking collectives  78.9 us (28%)
  starting transfers between devices  41.1 us (15%)
  waiting for transfers between devices  17.1 us (6%)
  local copies, waits for them, and re-layouts  9.65 us (3%)
  other arithmetic  3 us (1%)
    pallas_call x1, Pallas kernels, local(): pl.pallas_call(functools.partial(key_kernel, lat=lat, part=part, page_len...  110 us
    all_gather x1, blocking collectives, local(): own = lax.all_gather(keys, Z, axis=0, tiled=True)  37.4 us
    ppermute x8, starting transfers between devices, shift_z(): return lax.ppermute(x, Z, [(i, (i + step) % n) for i in range(n)])  32.5 us
    all_gather x1, blocking collectives, local(): qg = lax.all_gather(held, Z, axis=0, tiled=True)  31.6 us
    ppermute x8, waiting for transfers between devices, shift_z(): return lax.ppermute(x, Z, [(i, (i + step) % n) for i in range(n)])  17.1 us
    pallas_call x1, Pallas kernels, local(): pl.pallas_call(functools.partial(attend_kernel, rows=rows, lat=lat, scale...  11.5 us
    all_to_all x1, blocking collectives, local(): lax.all_to_all(page, 'dec', 0, 0, tiled=True).reshape(-1, pages, part, kw)  9.91 us
  transfers between devices with their start and end apart: 11, of which 7 were waited for; matrix products, arithmetic and copies ran while one was open for 3% of the time, Pallas kernels for 2%

profile of v10, /device:TPU:24, one launch (start us, length us, event | category | flops | bytes accessed | tf_op | source)
XLA Modules:
  0.0 276.5 jit_solution(15395324216412345364)
XLA Ops:
  0.6 0.7 reshape_squeeze.7
  1.4 1.3 pad_maximum_fusion.2.x_ref
  2.7 110.0 %keys.1 = (bf16[16,640]{1,0:T(8,128)(2,1)}, bf16[13824,128]{1,0:T(8,128)(2,1)}) custom-call(s32[1]{0:T(128)} %bitcast.4.base_ref, bf16[16,576]{1,0:T(8,128)(2,1)} %pad_maximum_fusion.2.x_ref, f32[1,512]{1,0:T(1,128)} %bitcast.25, bf16[1536,384]{1,0:T(8,128)(2,1)} %wq0.1, bf16[2,128,512]{2,1,0:T(8,128)(2,1)} %ak0.1, bf16[2,512,128]{2,1,0:T(8,128)(2,1)} %av0.1, ...), custom_call_target="tpu_custom_call" | custom-call | tf_op jit(solution)/shard_map/keys/pallas_call | solution.py:293
  112.7 1.9 collective-permute-start
  114.6 37.4 %all_gather.6 = bf16[256,640]{1,0:T(8,128)(2,1)S(1)} all-gather(bf16[16,640]{1,0:T(8,128)(2,1)} %get-tuple-element.20.key_ref), channel_id=1, replica_groups=mesh['chain'=4,'zh'=4,'zl'=4,'core'=2,'dec'=4] {'zh','zl'}, dimensions={0}, use_global_device_ids=true | all-gather | bytes 348160 | tf_op jit(solution)/shard_map/all_gather | solution.py:312
  152.0 0.7 copy-done.4
  153.3 9.9 %all_to_all.10 = bf16[4,16,640]{2,1,0:T(8,128)(2,1)} all-to-all(bf16[4,16,640]{2,1,0:T(8,128)(2,1)S(1)} %pages.1), channel_id=1, replica_groups=mesh['chain'=4,'zh'=4,'zl'=4,'core'=2,'dec'=4] {'dec'}, dimensions={0} | all-to-all | bytes 163840 | tf_op jit(solution)/shard_map/all_to_all | solution.py:325
  163.2 1.2 broadcast_in_dim.25
  164.5 4.7 %all-to-all-start = ((bf16[4,256,640]{2,1,0:T(8,128)(2,1)}), bf16[4,256,640]{2,1,0:T(8,128)(2,1)S(1)}, u32[]{:S(2)}, u32[]{:S(2)}) async-start(bf16[4,256,640]{2,1,0:T(8,128)(2,1)} %broadcast_in_dim.25), calls=%async_computation | async-start | bytes 2621440 | tf_op jit(solution)/shard_map/all_to_all | solution.py:36
  169.2 31.6 %all_gather.7.g_ref = bf16[256,1536]{1,0:T(8,128)(2,1)S(1)} all-gather(bf16[16,1536]{1,0:T(8,128)(2,1)} %bitcast.23), channel_id=1, replica_groups=mesh['chain'=4,'zh'=4,'zl'=4,'core'=2,'dec'=4] {'zh','zl'}, dimensions={0}, use_global_device_ids=true | all-gather | bytes 835584 | tf_op jit(solution)/shard_map/all_gather | solution.py:315
  200.7 1.5 reshape.29
  202.3 1.9 collective-permute-start.1
  204.3 4.0 %copy.13 = bf16[4,4,4,640]{1,0,3,2:T(4,128)(2,1)} copy(bf16[4,4,4,640]{3,2,1,0:T(4,128)(2,1)} %reshape.29) | data formatting | bytes 163840 | tf_op jit(solution)/shard_map/optimization_barrier | solution.py:326
  208.4 3.7 %queries.1.q_ref = bf16[1024,640]{1,0:T(8,128)(2,1)S(1)} custom-call(s32[3]{0:T(128)S(1)} %pad_add_fusion.where_ref, bf16[256,1536]{1,0:T(8,128)(2,1)S(1)} %all_gather.7.g_ref, bf16[1536,384]{1,0:T(8,128)(2,1)S(1)} %copy-done, bf16[2,128,512]{2,1,0:T(8,128)(2,1)S(1)} %copy-done.2, bf16[13824,128]{1,0:T(8,128)(2,1)} %collective-permute-done.packed), custom_call_target="tpu_custom_call" | custom-call | flops 738197504 | bytes 6000000 | tf_op jit(solution)/shard_map/queries/pallas_call | solution.py:329
  212.1 11.5 %attend.1 = (bf16[64,3584]{1,0:T(8,128)(2,1)S(1)}, bf16[64,3584]{1,0:T(8,128)(2,1)S(1)}, bf16[64,3584]{1,0:T(8,128)(2,1)S(1)}, bf16[32,3584]{1,0:T(8,128)(2,1)S(1)}, bf16[32,3584]{1,0:T(8,128)(2,1)S(1)}) custom-call(s32[3]{0:T(128)S(1)} %pad_add_fusion.where_ref, bf16[1024,640]{1,0:T(8,128)(2,1)S(1)} %queries.1.q_ref, bf16[1024,640]{1,0:T(8,128)(2,1)S(1)} %bitcast.21, ...), custom_call_target="tpu_custom_call" | custom-call | flops 4294967296 | bytes 9000000 | tf_op jit(solution)/shard_map/attend/pallas_call | solution.py:349
  223.5 2.8 %collective-permute-start.2 = (bf16[64,3584]{1,0:T(8,128)(2,1)S(1)}, bf16[64,3584]{1,0:T(8,128)(2,1)S(1)}, u32[]{:S(2)}, u32[]{:S(2)}) collective-permute-start(bf16[64,3584]{1,0:T(8,128)(2,1)S(1)} %get-tuple-element.25), channel_id=1, source_target_pairs={{0,8},{8,16},{16,24},{24,32},{32,40},{40,48},{48,56},{56,64},{64,7... | collective-permute-start | bytes 1376264 | tf_op jit(solution)/shard_map/ppermute | solution.py:27
  226.4 4.2 %collective-permute-start.3 = (bf16[64,3584]{1,0:T(8,128)(2,1)S(1)}, bf16[64,3584]{1,0:T(8,128)(2,1)S(1)}, u32[]{:S(2)}, u32[]{:S(2)}) collective-permute-start(bf16[64,3584]{1,0:T(8,128)(2,1)S(1)} %get-tuple-element.26), channel_id=1, source_target_pairs={{0,120},{8,0},{16,8},{24,16},{32,24},{40,32},{48,40},{56,48},{64,5... | collective-permute-start | bytes 1376264 | tf_op jit(solution)/shard_map/ppermute | solution.py:27
  230.6 0.7 slice_convert_fusion.2
  231.6 0.6 copy.15
  232.2 1.9 collective-permute-start.4
  234.1 6.0 %collective-permute-start.5 = (bf16[32,3584]{1,0:T(8,128)(2,1)S(1)}, bf16[32,3584]{1,0:T(8,128)(2,1)S(1)}, u32[]{:S(2)}, u32[]{:S(2)}) collective-permute-start(bf16[32,3584]{1,0:T(8,128)(2,1)S(1)} %get-tuple-element.30), channel_id=1, source_target_pairs={{0,112},{8,120},{16,0},{24,8},{32,16},{40,24},{48,32},{56,40},{64,... | collective-permute-start | bytes 688136 | tf_op jit(solution)/shard_map/ppermute | solution.py:27
  240.2 1.1 collective-permute-done.2
  241.2 4.8 %collective-permute-done.3 = bf16[64,3584]{1,0:T(8,128)(2,1)S(1)} collective-permute-done((bf16[64,3584]{1,0:T(8,128)(2,1)S(1)}, bf16[64,3584]{1,0:T(8,128)(2,1)S(1)}, u32[]{:S(2)}, u32[]{:S(2)}) %collective-permute-start.3) | collective-permute-done | bytes 458784 | tf_op jit(solution)/shard_map/ppermute | solution.py:27
  246.1 2.7 collective-permute-start.6
  248.8 1.8 collective-permute-done.5
  250.7 5.5 %collective-permute-start.8 = (bf16[16,1792]{1,0:T(8,128)(2,1)S(1)}, bf16[16,1792]{1,0:T(8,128)(2,1)S(1)}, u32[]{:S(2)}, u32[]{:S(2)}) collective-permute-start(bf16[16,1792]{1,0:T(8,128)(2,1)S(1)} %get-tuple-element.39), channel_id=1, source_target_pairs={{0,96},{8,104},{16,112},{24,120},{32,0},{40,8},{48,16},{56,24},{64... | collective-permute-start | bytes 172040 | tf_op jit(solution)/shard_map/ppermute | solution.py:27
  256.8 4.3 %collective-permute-start.7 = (bf16[16,3584]{1,0:T(8,128)(2,1)S(1)}, bf16[16,3584]{1,0:T(8,128)(2,1)S(1)}, u32[]{:S(2)}, u32[]{:S(2)}) collective-permute-start(bf16[16,3584]{1,0:T(8,128)(2,1)S(1)} %pad_maximum_fusion), channel_id=1, source_target_pairs={{0,32},{8,40},{16,48},{24,56},{32,64},{40,72},{48,80},{56,88},{64,... | collective-permute-start | bytes 344072 | tf_op jit(solution)/shard_map/ppermute | solution.py:27
  261.5 5.1 %collective-permute-start.9 = (bf16[16,3584]{1,0:T(8,128)(2,1)S(1)}, bf16[16,3584]{1,0:T(8,128)(2,1)S(1)}, u32[]{:S(2)}, u32[]{:S(2)}) collective-permute-start(bf16[16,3584]{1,0:T(8,128)(2,1)S(1)} %pad_maximum_fusion.1), channel_id=1, source_target_pairs={{0,96},{8,104},{16,112},{24,120},{32,0},{40,8},{48,16},{56,24},{64... | collective-permute-start | bytes 344072 | tf_op jit(solution)/shard_map/ppermute | solution.py:27
  266.6 0.6 copy.16
  267.2 1.2 collective-permute-done.7
  268.4 7.4 %collective-permute-done.9 = bf16[16,3584]{1,0:T(8,128)(2,1)S(1)} collective-permute-done((bf16[16,3584]{1,0:T(8,128)(2,1)S(1)}, bf16[16,3584]{1,0:T(8,128)(2,1)S(1)}, u32[]{:S(2)}, u32[]{:S(2)}) %collective-permute-start.9) | collective-permute-done | bytes 114720 | tf_op jit(solution)/shard_map/ppermute | solution.py:27
  275.8 0.8 fusion
  (37 shorter events, 2.1 us)
Async XLA Ops:
  2.7 149.4 %copy-start.5 = (s32[1,4]{1,0:T(1,128)S(1)}, s32[1,4]{1,0:T(1,128)}, u32[]{:S(2)}) copy-start(s32[1,4]{1,0:T(1,128)} %owner_ref.1) | copy-start | bytes 52
  2.7 149.4 %copy-start.6 = (s32[1,4]{1,0:T(1,128)S(1)}, s32[1,4]{1,0:T(1,128)}, u32[]{:S(2)}) copy-start(s32[1,4]{1,0:T(1,128)} %slot_ref.1) | copy-start | bytes 52
  112.7 95.6 %collective-permute-start = (bf16[13824,128]{1,0:T(8,128)(2,1)}, bf16[13824,128]{1,0:T(8,128)(2,1)}, u32[]{:S(2)}, u32[]{:S(2)}) collective-permute-start(bf16[13824,128]{1,0:T(8,128)(2,1)} %get-tuple-element.22), channel_id=1, source_target_pairs={{0,4},{4,0},{1,5},{5,1},{2,6},{6,2},{3,7},{7,3},{8,12},{12,8},{9,1... | collective-permute-start | bytes 10616840 | tf_op jit(solution)/shard_map/ppermute | solution.py:31
  152.0 0.7 copy-start.4
  164.5 37.8 %all-to-all-start = ((bf16[4,256,640]{2,1,0:T(8,128)(2,1)}), bf16[4,256,640]{2,1,0:T(8,128)(2,1)S(1)}, u32[]{:S(2)}, u32[]{:S(2)}) async-start(bf16[4,256,640]{2,1,0:T(8,128)(2,1)} %broadcast_in_dim.25), calls=%async_computation | async-start | bytes 2621440 | tf_op jit(solution)/shard_map/all_to_all | solution.py:36
  169.2 39.2 %copy-start = (bf16[1536,384]{1,0:T(8,128)(2,1)S(1)}, bf16[1536,384]{1,0:T(8,128)(2,1)}, u32[]{:S(2)}) copy-start(bf16[1536,384]{1,0:T(8,128)(2,1)} %wq0.1) | copy-start | bytes 3538948
  169.2 39.2 %copy-start.2 = (bf16[2,128,512]{2,1,0:T(8,128)(2,1)S(1)}, bf16[2,128,512]{2,1,0:T(8,128)(2,1)}, u32[]{:S(2)}) copy-start(bf16[2,128,512]{2,1,0:T(8,128)(2,1)} %ak0.1) | copy-start | bytes 786436
  202.3 9.8 %collective-permute-start.1 = (bf16[1024,640]{1,0:T(8,128)(2,1)S(1)}, bf16[1024,640]{1,0:T(8,128)(2,1)}, u32[]{:S(2)}, u32[]{:S(2)}) collective-permute-start(bf16[1024,640]{1,0:T(8,128)(2,1)S(1)} %bitcast.20), channel_id=1, source_target_pairs={{0,4},{4,0},{1,5},{5,1},{2,6},{6,2},{3,7},{7,3},{8,12},{12,8},{9,1... | collective-permute-start | bytes 3932168 | tf_op jit(solution)/shard_map/ppermute | solution.py:31
  208.3 3.7 %copy-start.1 = (bf16[256,3584]{1,0:T(8,128)(2,1)S(1)}, bf16[256,3584]{1,0:T(8,128)(2,1)}, u32[]{:S(2)}) copy-start(bf16[256,3584]{1,0:T(8,128)(2,1)} %op0.1) | copy-start | bytes 5505028
  208.3 3.7 %copy-start.3 = (bf16[2,512,128]{2,1,0:T(8,128)(2,1)S(1)}, bf16[2,512,128]{2,1,0:T(8,128)(2,1)}, u32[]{:S(2)}) copy-start(bf16[2,512,128]{2,1,0:T(8,128)(2,1)} %av0.1) | copy-start | bytes 786436
  212.0 19.3 %copy-start.7 = (bf16[4,4,4,640]{3,2,1,0:T(4,128)(2,1)S(1)}, bf16[4,4,4,640]{3,2,1,0:T(4,128)(2,1)}, u32[]{:S(2)}) copy-start(bf16[4,4,4,640]{3,2,1,0:T(4,128)(2,1)} %reshape.29) | copy-start | bytes 245764
  223.5 17.7 %collective-permute-start.2 = (bf16[64,3584]{1,0:T(8,128)(2,1)S(1)}, bf16[64,3584]{1,0:T(8,128)(2,1)S(1)}, u32[]{:S(2)}, u32[]{:S(2)}) collective-permute-start(bf16[64,3584]{1,0:T(8,128)(2,1)S(1)} %get-tuple-element.25), channel_id=1, source_target_pairs={{0,8},{8,16},{16,24},{24,32},{32,40},{40,48},{48,56},{56,64},{64,7... | collective-permute-start | bytes 1376264 | tf_op jit(solution)/shard_map/ppermute | solution.py:27
  226.4 19.6 %collective-permute-start.3 = (bf16[64,3584]{1,0:T(8,128)(2,1)S(1)}, bf16[64,3584]{1,0:T(8,128)(2,1)S(1)}, u32[]{:S(2)}, u32[]{:S(2)}) collective-permute-start(bf16[64,3584]{1,0:T(8,128)(2,1)S(1)} %get-tuple-element.26), channel_id=1, source_target_pairs={{0,120},{8,0},{16,8},{24,16},{32,24},{40,32},{48,40},{56,48},{64,5... | collective-permute-start | bytes 1376264 | tf_op jit(solution)/shard_map/ppermute | solution.py:27
  232.2 16.6 %collective-permute-start.4 = (bf16[32,3584]{1,0:T(8,128)(2,1)S(1)}, bf16[32,3584]{1,0:T(8,128)(2,1)S(1)}, u32[]{:S(2)}, u32[]{:S(2)}) collective-permute-start(bf16[32,3584]{1,0:T(8,128)(2,1)S(1)} %get-tuple-element.29), channel_id=1, source_target_pairs={{0,16},{8,24},{16,32},{24,40},{32,48},{40,56},{48,64},{56,72},{64,... | collective-permute-start | bytes 688136 | tf_op jit(solution)/shard_map/ppermute | solution.py:27
  234.1 16.5 %collective-permute-start.5 = (bf16[32,3584]{1,0:T(8,128)(2,1)S(1)}, bf16[32,3584]{1,0:T(8,128)(2,1)S(1)}, u32[]{:S(2)}, u32[]{:S(2)}) collective-permute-start(bf16[32,3584]{1,0:T(8,128)(2,1)S(1)} %get-tuple-element.30), channel_id=1, source_target_pairs={{0,112},{8,120},{16,0},{24,8},{32,16},{40,24},{48,32},{56,40},{64,... | collective-permute-start | bytes 688136 | tf_op jit(solution)/shard_map/ppermute | solution.py:27
  246.1 10.6 %collective-permute-start.6 = (bf16[16,1792]{1,0:T(8,128)(2,1)S(1)}, bf16[16,1792]{1,0:T(8,128)(2,1)S(1)}, u32[]{:S(2)}, u32[]{:S(2)}) collective-permute-start(bf16[16,1792]{1,0:T(8,128)(2,1)S(1)} %get-tuple-element.38), channel_id=1, source_target_pairs={{0,32},{8,40},{16,48},{24,56},{32,64},{40,72},{48,80},{56,88},{64,... | collective-permute-start | bytes 172040 | tf_op jit(solution)/shard_map/ppermute | solution.py:27
  250.7 10.7 %collective-permute-start.8 = (bf16[16,1792]{1,0:T(8,128)(2,1)S(1)}, bf16[16,1792]{1,0:T(8,128)(2,1)S(1)}, u32[]{:S(2)}, u32[]{:S(2)}) collective-permute-start(bf16[16,1792]{1,0:T(8,128)(2,1)S(1)} %get-tuple-element.39), channel_id=1, source_target_pairs={{0,96},{8,104},{16,112},{24,120},{32,0},{40,8},{48,16},{56,24},{64... | collective-permute-start | bytes 172040 | tf_op jit(solution)/shard_map/ppermute | solution.py:27
  256.8 11.6 %collective-permute-start.7 = (bf16[16,3584]{1,0:T(8,128)(2,1)S(1)}, bf16[16,3584]{1,0:T(8,128)(2,1)S(1)}, u32[]{:S(2)}, u32[]{:S(2)}) collective-permute-start(bf16[16,3584]{1,0:T(8,128)(2,1)S(1)} %pad_maximum_fusion), channel_id=1, source_target_pairs={{0,32},{8,40},{16,48},{24,56},{32,64},{40,72},{48,80},{56,88},{64,... | collective-permute-start | bytes 344072 | tf_op jit(solution)/shard_map/ppermute | solution.py:27
  261.5 14.3 %collective-permute-start.9 = (bf16[16,3584]{1,0:T(8,128)(2,1)S(1)}, bf16[16,3584]{1,0:T(8,128)(2,1)S(1)}, u32[]{:S(2)}, u32[]{:S(2)}) collective-permute-start(bf16[16,3584]{1,0:T(8,128)(2,1)S(1)} %pad_maximum_fusion.1), channel_id=1, source_target_pairs={{0,96},{8,104},{16,112},{24,120},{32,0},{40,8},{48,16},{56,24},{64... | collective-permute-start | bytes 344072 | tf_op jit(solution)/shard_map/ppermute | solution.py:27

commit v11 on v10

--- a/solution.py
+++ b/solution.py
@@ -87,13 +87,7 @@
 
 
 def key_kernel(base_ref, x_ref, gain_ref, *refs, lat, part, page_len, shapes):
-    ins, out_ref, packed, sems = refs[: len(shapes)], refs[-3], refs[-2], refs[-1]
-    loads = [
-        pltpu.make_async_copy(block_of(ins[w], lead, c), packed.at[pl.ds(at, n), :], sems.at[i])
-        for i, (at, w, lead, c, n) in enumerate(blocks(shapes))
-    ]
-    for load in loads:
-        load.start()
+    ins, out_ref, packed = refs[: len(shapes)], refs[-2], refs[-1]
     x = x_ref[...].astype(F32)
     latent, rot = x[:, :lat], x[:, lat:]
     norm = lax.rsqrt(jnp.mean(latent * latent, -1, keepdims=True) + 1e-06)
@@ -102,8 +96,12 @@
     cosine, sine = rope_factors(base_ref[0] + row // part * page_len + row % part)
     turned = rot * cosine + swap_halves(rot) * sine
     out_ref[:, lat:] = jnp.concatenate([turned, jnp.zeros_like(turned)], -1).astype(BF)
-    for load in loads:
-        load.wait()
+    for at, w, lead, c, n in blocks(shapes):
+        src = ins[w]
+        if len(src.shape) == 3:
+            packed[at : at + n, :] = src[lead, :, c : c + 128]
+        else:
+            packed[at : at + n, :] = src[:, c : c + 128]
 
 
 def weight_loads(own, packed, dst, which, shapes, sems):
@@ -194,42 +192,37 @@
             idx = lax.broadcasted_iota(jnp.int32, (1, n), 1)
             kpos = (idx % qrows) // part * (chips * 2 * part) + idx // qrows * (2 * part) + idx % part
             ok = [kpos + i * part <= qpos for i in (core, 1 - core)]
-        for h in range(heads):
-            q = q_ref[h * rows : (h + 1) * rows, :]
-            for i, k_ref in enumerate((ka_ref, kb_ref)):
-                s = lax.dot_general(q, k_ref[block(back), :], nt, preferred_element_type=F32)
+        for i, k_ref in enumerate((ka_ref, kb_ref)):
+            at = (2 * back + i) * n
+            all_heads = lax.dot_general(
+                q_ref[...], k_ref[block(back), :], nt, preferred_element_type=F32
+            )
+            for h in range(heads):
+                s = all_heads[h * rows : (h + 1) * rows]
                 if back == 0:
                     s = jnp.where(ok[i], s, NEG)
-                at = (2 * back + i) * n
-                s_ref[h, :, at : at + n] = s
+                s_ref[h * rows : (h + 1) * rows, at : at + n] = s
                 top = lanes(s, jnp.maximum)
                 if back or i:
-                    top = jnp.maximum(top, top_ref[h])
-                top_ref[h] = top
+                    top = jnp.maximum(top, top_ref[h * rows : (h + 1) * rows])
+                top_ref[h * rows : (h + 1) * rows] = top
 
     def mix(back):
-        for h in range(heads):
-            m = top_ref[h][:, :1]
-            pv = None
-            for i, k_ref in enumerate((ka_ref, kb_ref)):
-                at = (2 * back + i) * n
-                p = jnp.exp2(s_ref[h, :, at : at + n] * s2 - m)
-                total = lanes(p, jnp.add)
-                if back or i:
-                    total += l_ref[h]
-                l_ref[h] = total
-                part_pv = jnp.dot(
-                    p.astype(BF), k_ref[block(back), :lat], preferred_element_type=F32
-                )
-                pv = part_pv if pv is None else pv + part_pv
-            acc_ref[h] = acc_ref[h] + pv if back else pv
+        m = top_ref[:, :1]
+        for i, k_ref in enumerate((ka_ref, kb_ref)):
+            at = (2 * back + i) * n
+            p = jnp.exp2(s_ref[:, at : at + n] * s2 - m)
+            total = lanes(p, jnp.add)
+            l_ref[...] = total + l_ref[...] if back or i else total
+            pv = jnp.dot(p.astype(BF), k_ref[block(back), :lat], preferred_element_type=F32)
+            acc_ref[...] = acc_ref[...] + pv if back or i else pv
 
     score(0)
     for back in range(1, nch):
         pl.when(chain >= back)(functools.partial(score, back))
-    for h in range(heads):
-        m = jnp.max(top_ref[h], -1, keepdims=True) * s2
-        top_ref[h] = jnp.broadcast_to(m, top_ref.shape[1:])
+    top_ref[...] = jnp.broadcast_to(
+        jnp.max(top_ref[...], -1, keepdims=True) * s2, top_ref.shape
+    )
     mix(0)
     for back in range(1, nch):
         pl.when(chain >= back)(functools.partial(mix, back))
@@ -237,8 +230,9 @@
         load.wait()
     per = heads // 2
     for h in range(heads):
-        total = jnp.sum(l_ref[h], -1, keepdims=True)
-        mixed = (acc_ref[h] / total).astype(BF)
+        at = slice(h * rows, (h + 1) * rows)
+        total = jnp.sum(l_ref[at], -1, keepdims=True)
+        mixed = (acc_ref[at] / total).astype(BF)
         av = av_ref[h // per, h % per]
         ho_ref[:, h * vh : (h + 1) * vh] = jnp.dot(mixed, av, preferred_element_type=F32).astype(BF)
     ho = ho_ref[...]
@@ -289,7 +283,6 @@
     where = jnp.stack([chain, z, core]).astype(jnp.int32)
     weights = (query_up, absorb_key, absorb_value, out_proj)
     shapes = tuple(w.shape for w in weights)
-    count = len(list(blocks(shapes)))
     keys, packed = pl.pallas_call(
         functools.partial(
             key_kernel, lat=lat, part=part, page_len=part * tp_count, shapes=shapes
@@ -298,9 +291,8 @@
             jax.ShapeDtypeStruct((pages * part, kw), BF),
             jax.ShapeDtypeStruct((packed_rows(shapes), 128), BF),
         ),
-        in_specs=[smem, vm, vm] + [hbm] * 4,
-        out_specs=(vm, hbm),
-        scratch_shapes=[pltpu.SemaphoreType.DMA((count,))],
+        in_specs=[smem] + [vm] * 6,
+        out_specs=(vm, vm),
         compiler_params=room(56),
         name="keys",
     )(
@@ -313,17 +305,7 @@
     mine = spread(own, "chain").reshape(nch * rows, kw)
     held = lax.optimization_barrier((query_comp[0], own))[0]
     qg = lax.all_gather(held, Z, axis=0, tiled=True)
-    page = lax.optimization_barrier((keys, own))[0]
-    page = pl.pallas_call(
-        functools.partial(page_kernel, lat=lat, part=part, slots=slots),
-        out_shape=jax.ShapeDtypeStruct((lax.axis_size("dec"),) + keys.shape, BF),
-        in_specs=[smem, smem, vm],
-        out_specs=vm,
-        compiler_params=room(4),
-        name="pages",
-    )(page_owner, page_slot, page)
-    page = lax.all_to_all(page, "dec", 0, 0, tiled=True).reshape(-1, pages, part, kw)
-    qg, mine, page = lax.optimization_barrier((qg, mine, page))
+    qg, mine = lax.optimization_barrier((qg, mine))
     other = swap_core(mine)
 
     q = pl.pallas_call(
@@ -355,10 +337,10 @@
         in_specs=[smem] + [vm] * 3 + [hbm] * 3,
         out_specs=[vm] * 5,
         scratch_shapes=[
-            pltpu.VMEM((heads, rows, nch * block_len), F32),
-            pltpu.VMEM((heads, rows, 128), F32),
-            pltpu.VMEM((heads, rows, 128), F32),
-            pltpu.VMEM((heads, rows, lat), F32),
+            pltpu.VMEM((heads * rows, nch * block_len), F32),
+            pltpu.VMEM((heads * rows, 128), F32),
+            pltpu.VMEM((heads * rows, 128), F32),
+            pltpu.VMEM((heads * rows, lat), F32),
             pltpu.VMEM((rows, heads * vh), BF),
             pltpu.VMEM((2,) + absorb_value.shape, BF),
             pltpu.VMEM((2,) + out_proj.shape, BF),
@@ -388,14 +370,25 @@
     right = shift_z(far[:, cut:], -nzl).astype(F32)
     ahead = near(1, up, down) + up2[qrows:].astype(F32)
     ahead = jnp.concatenate([ahead[:, :cut] + left, ahead[:, cut:]], -1)
-    ahead = shift_z(ahead.astype(BF), nzl)
+    ahead = ahead.astype(BF)
     behind = near(-1, up, down) + down2[:qrows].astype(F32)
     behind = jnp.concatenate([behind[:, :cut], behind[:, cut:] + right], -1)
-    behind = shift_z(behind.astype(BF), -nzl)
+    behind = behind.astype(BF)
     total = near(0, up, down) + up2[:qrows].astype(F32) + down2[qrows:].astype(F32)
-    total = total + ahead.astype(F32) + behind.astype(F32)
+    total = total + shift_z(ahead, nzl).astype(F32) + shift_z(behind, -nzl).astype(F32)
     layer_output = total.astype(BF)[None]
 
+    page = lax.optimization_barrier((keys, ahead, behind))[0]
+    page = pl.pallas_call(
+        functools.partial(page_kernel, lat=lat, part=part, slots=slots),
+        out_shape=jax.ShapeDtypeStruct((lax.axis_size("dec"),) + keys.shape, BF),
+        in_specs=[smem, smem, vm],
+        out_specs=vm,
+        compiler_params=room(4),
+        cost_estimate=pl.CostEstimate(flops=0, bytes_accessed=4000000, transcendentals=0),
+        name="pages",
+    )(page_owner, page_slot, page)
+    page = lax.all_to_all(page, "dec", 0, 0, tiled=True).reshape(-1, pages, part, kw)
     came = page[:, :, 0, lat + rope].reshape(-1).astype(jnp.int32)
     take = (came[None, :] == dec * slots + jnp.arange(slots, dtype=jnp.int32)[:, None]).astype(BF)
     placed = jnp.einsum(

time: 279 us -> 166 us (0.59)
  the two profiles are of different devices: /device:TPU:24 before, /device:TPU:58 now
where the time goes in v11:
time: 166 us; the launch traced here: 165 us
  blocking collectives  67.9 us (41%)
  starting transfers between devices  45.8 us (28%)
  waiting for transfers between devices  25 us (15%)
  Pallas kernels  19.7 us (12%)
  local copies, waits for them, and re-layouts  3.61 us (2%)
  other arithmetic  2.34 us (1%)
    all_gather x1, blocking collectives, local(): own = lax.all_gather(keys, Z, axis=0, tiled=True)  35.4 us
    all_gather x1, blocking collectives, local(): qg = lax.all_gather(held, Z, axis=0, tiled=True)  32.6 us
    ppermute x8, starting transfers between devices, shift_z(): return lax.ppermute(x, Z, [(i, (i + step) % n) for i in range(n)])  32.4 us
    ppermute x8, waiting for transfers between devices, shift_z(): return lax.ppermute(x, Z, [(i, (i + step) % n) for i in range(n)])  24.9 us
    pallas_call x1, Pallas kernels, local(): pl.pallas_call(functools.partial(attend_kernel, rows=rows, lat=lat, scale...  10.4 us
    all_to_all x1, starting transfers between devices, spread(): lax.all_to_all(jnp.broadcast_to(x[None], (n,) + x.shape), axis, 0, 0, til...  4.82 us
    all_to_all x1, starting transfers between devices, local(): lax.all_to_all(page, 'dec', 0, 0, tiled=True).reshape(-1, pages, part, kw)  4.78 us
    pallas_call x1, Pallas kernels, local(): pl.pallas_call(functools.partial(key_kernel, lat=lat, part=part, page_len...  4.44 us
  transfers between devices with their start and end apart: 12, of which 6 were waited for; matrix products, arithmetic and copies ran while one was open for 2% of the time, Pallas kernels for 2%

profile of v11, /device:TPU:58, one launch (start us, length us, event | category | flops | bytes accessed | tf_op | source)
XLA Modules:
  0.0 165.5 jit_solution(1082362590762035244)
XLA Ops:
  0.6 0.7 reshape_squeeze.7
  1.4 1.3 pad_maximum_fusion.2.x_ref
  2.7 4.4 %keys.1 = (bf16[16,640]{1,0:T(8,128)(2,1)}, bf16[13824,128]{1,0:T(8,128)(2,1)}) custom-call(s32[1]{0:T(128)} %bitcast.4.base_ref, bf16[16,576]{1,0:T(8,128)(2,1)} %pad_maximum_fusion.2.x_ref, f32[1,512]{1,0:T(1,128)} %bitcast.23, bf16[1536,384]{1,0:T(8,128)(2,1)} %wq0.1, bf16[2,128,512]{2,1,0:T(8,128)(2,1)} %ak0.1, bf16[2,512,128]{2,1,0:T(8,128)(2,1)} %av0.1, ...), custom_call_target="tpu_custom_call" | custom-call | tf_op jit(solution)/shard_map/keys/pallas_call | solution.py:286
  7.1 1.9 %collective-permute-start = (bf16[13824,128]{1,0:T(8,128)(2,1)}, bf16[13824,128]{1,0:T(8,128)(2,1)}, u32[]{:S(2)}, u32[]{:S(2)}) collective-permute-start(bf16[13824,128]{1,0:T(8,128)(2,1)} %get-tuple-element.20), channel_id=1, source_target_pairs={{0,4},{4,0},{1,5},{5,1},{2,6},{6,2},{3,7},{7,3},{8,12},{12,8},{9,1... | collective-permute-start | bytes 10616840 | tf_op jit(solution)/shard_map/ppermute | solution.py:31
  9.0 35.4 %all_gather.6 = bf16[256,640]{1,0:T(8,128)(2,1)S(1)} all-gather(bf16[16,640]{1,0:T(8,128)(2,1)} %get-tuple-element.30.key_ref), channel_id=1, replica_groups=mesh['chain'=4,'zh'=4,'zl'=4,'core'=2,'dec'=4] {'zh','zl'}, dimensions={0}, use_global_device_ids=true | all-gather | bytes 348160 | tf_op jit(solution)/shard_map/all_gather | solution.py:304
  44.4 1.2 broadcast_in_dim.25
  45.6 4.8 %all-to-all-start = ((bf16[4,256,640]{2,1,0:T(8,128)(2,1)}), bf16[4,256,640]{2,1,0:T(8,128)(2,1)S(1)}, u32[]{:S(2)}, u32[]{:S(2)}) async-start(bf16[4,256,640]{2,1,0:T(8,128)(2,1)} %broadcast_in_dim.25), calls=%async_computation | async-start | bytes 2621440 | tf_op jit(solution)/shard_map/all_to_all | solution.py:36
  50.5 32.6 %all_gather.7.g_ref = bf16[256,1536]{1,0:T(8,128)(2,1)S(1)} all-gather(bf16[16,1536]{1,0:T(8,128)(2,1)} %bitcast.21), channel_id=1, replica_groups=mesh['chain'=4,'zh'=4,'zl'=4,'core'=2,'dec'=4] {'zh','zl'}, dimensions={0}, use_global_device_ids=true | all-gather | bytes 835584 | tf_op jit(solution)/shard_map/all_gather | solution.py:307
  83.0 1.9 %collective-permute-start.1 = (bf16[1024,640]{1,0:T(8,128)(2,1)S(1)}, bf16[1024,640]{1,0:T(8,128)(2,1)S(1)}, u32[]{:S(2)}, u32[]{:S(2)}) collective-permute-start(bf16[1024,640]{1,0:T(8,128)(2,1)S(1)} %bitcast.19), channel_id=1, source_target_pairs={{0,4},{4,0},{1,5},{5,1},{2,6},{6,2},{3,7},{7,3},{8,12},{12,8},{9,1... | collective-permute-start | bytes 3932168 | tf_op jit(solution)/shard_map/ppermute | solution.py:31
  85.1 3.7 %queries.1.q_ref = bf16[1024,640]{1,0:T(8,128)(2,1)S(1)} custom-call(s32[3]{0:T(128)S(1)} %pad_add_fusion.where_ref, bf16[256,1536]{1,0:T(8,128)(2,1)S(1)} %all_gather.7.g_ref, bf16[1536,384]{1,0:T(8,128)(2,1)S(1)} %copy-done, bf16[2,128,512]{2,1,0:T(8,128)(2,1)S(1)} %copy-done.2, bf16[13824,128]{1,0:T(8,128)(2,1)} %collective-permute-done.packed), custom_call_target="tpu_custom_call" | custom-call | flops 738197504 | bytes 6000000 | tf_op jit(solution)/shard_map/queries/pallas_call | solution.py:311
  88.8 10.4 %attend.1 = (bf16[64,3584]{1,0:T(8,128)(2,1)S(1)}, bf16[64,3584]{1,0:T(8,128)(2,1)S(1)}, bf16[64,3584]{1,0:T(8,128)(2,1)S(1)}, bf16[32,3584]{1,0:T(8,128)(2,1)S(1)}, bf16[32,3584]{1,0:T(8,128)(2,1)S(1)}) custom-call(s32[3]{0:T(128)S(1)} %pad_add_fusion.where_ref, bf16[1024,640]{1,0:T(8,128)(2,1)S(1)} %queries.1.q_ref, bf16[1024,640]{1,0:T(8,128)(2,1)S(1)} %bitcast.20, ...), custom_call_target="tpu_custom_call" | custom-call | flops 4294967296 | bytes 9000000 | tf_op jit(solution)/shard_map/attend/pallas_call | solution.py:331
  99.1 1.9 %collective-permute-start.2 = (bf16[64,3584]{1,0:T(8,128)(2,1)S(1)}, bf16[64,3584]{1,0:T(8,128)(2,1)S(1)}, u32[]{:S(2)}, u32[]{:S(2)}) collective-permute-start(bf16[64,3584]{1,0:T(8,128)(2,1)S(1)} %get-tuple-element.23), channel_id=1, source_target_pairs={{0,8},{8,16},{16,24},{24,32},{32,40},{40,48},{48,56},{56,64},{64,7... | collective-permute-start | bytes 1376264 | tf_op jit(solution)/shard_map/ppermute | solution.py:27
  101.1 3.9 %collective-permute-start.3 = (bf16[64,3584]{1,0:T(8,128)(2,1)S(1)}, bf16[64,3584]{1,0:T(8,128)(2,1)S(1)}, u32[]{:S(2)}, u32[]{:S(2)}) collective-permute-start(bf16[64,3584]{1,0:T(8,128)(2,1)S(1)} %get-tuple-element.24), channel_id=1, source_target_pairs={{0,120},{8,0},{16,8},{24,16},{32,24},{40,32},{48,40},{56,48},{64,5... | collective-permute-start | bytes 1376264 | tf_op jit(solution)/shard_map/ppermute | solution.py:27
  105.0 2.2 %collective-permute-start.4 = (bf16[32,3584]{1,0:T(8,128)(2,1)S(1)}, bf16[32,3584]{1,0:T(8,128)(2,1)S(1)}, u32[]{:S(2)}, u32[]{:S(2)}) collective-permute-start(bf16[32,3584]{1,0:T(8,128)(2,1)S(1)} %get-tuple-element.27), channel_id=1, source_target_pairs={{0,16},{8,24},{16,32},{24,40},{32,48},{40,56},{48,64},{56,72},{64,... | collective-permute-start | bytes 688136 | tf_op jit(solution)/shard_map/ppermute | solution.py:27
  107.2 5.8 %collective-permute-start.5 = (bf16[32,3584]{1,0:T(8,128)(2,1)S(1)}, bf16[32,3584]{1,0:T(8,128)(2,1)S(1)}, u32[]{:S(2)}, u32[]{:S(2)}) collective-permute-start(bf16[32,3584]{1,0:T(8,128)(2,1)S(1)} %get-tuple-element.28), channel_id=1, source_target_pairs={{0,112},{8,120},{16,0},{24,8},{32,16},{40,24},{48,32},{56,40},{64,... | collective-permute-start | bytes 688136 | tf_op jit(solution)/shard_map/ppermute | solution.py:27
  113.0 1.4 collective-permute-done.2
  114.4 4.3 %collective-permute-done.3 = bf16[64,3584]{1,0:T(8,128)(2,1)S(1)} collective-permute-done((bf16[64,3584]{1,0:T(8,128)(2,1)S(1)}, bf16[64,3584]{1,0:T(8,128)(2,1)S(1)}, u32[]{:S(2)}, u32[]{:S(2)}) %collective-permute-start.3) | collective-permute-done | bytes 458784 | tf_op jit(solution)/shard_map/ppermute | solution.py:27
  118.8 2.5 %collective-permute-start.6 = (bf16[16,1792]{1,0:T(8,128)(2,1)S(1)}, bf16[16,1792]{1,0:T(8,128)(2,1)S(1)}, u32[]{:S(2)}, u32[]{:S(2)}) collective-permute-start(bf16[16,1792]{1,0:T(8,128)(2,1)S(1)} %get-tuple-element.36), channel_id=1, source_target_pairs={{0,32},{8,40},{16,48},{24,56},{32,64},{40,72},{48,80},{56,88},{64,... | collective-permute-start | bytes 172040 | tf_op jit(solution)/shard_map/ppermute | solution.py:27
  121.3 5.0 %collective-permute-done.4 = bf16[32,3584]{1,0:T(8,128)(2,1)S(1)} collective-permute-done((bf16[32,3584]{1,0:T(8,128)(2,1)S(1)}, bf16[32,3584]{1,0:T(8,128)(2,1)S(1)}, u32[]{:S(2)}, u32[]{:S(2)}) %collective-permute-start.4) | collective-permute-done | bytes 229408 | tf_op jit(solution)/shard_map/ppermute | solution.py:27
  126.5 6.3 %collective-permute-start.8 = (bf16[16,1792]{1,0:T(8,128)(2,1)S(1)}, bf16[16,1792]{1,0:T(8,128)(2,1)S(1)}, u32[]{:S(2)}, u32[]{:S(2)}) collective-permute-start(bf16[16,1792]{1,0:T(8,128)(2,1)S(1)} %get-tuple-element.37), channel_id=1, source_target_pairs={{0,96},{8,104},{16,112},{24,120},{32,0},{40,8},{48,16},{56,24},{64... | collective-permute-start | bytes 172040 | tf_op jit(solution)/shard_map/ppermute | solution.py:27
  132.9 5.9 %collective-permute-done.8 = bf16[16,1792]{1,0:T(8,128)(2,1)S(1)} collective-permute-done((bf16[16,1792]{1,0:T(8,128)(2,1)S(1)}, bf16[16,1792]{1,0:T(8,128)(2,1)S(1)}, u32[]{:S(2)}, u32[]{:S(2)}) %collective-permute-start.8) | collective-permute-done | bytes 57376 | tf_op jit(solution)/shard_map/ppermute | solution.py:27
  138.9 1.2 pages.1
  140.1 4.8 %all-to-all-start.1 = ((bf16[4,16,640]{2,1,0:T(8,128)(2,1)}), bf16[4,16,640]{2,1,0:T(8,128)(2,1)S(1)}, u32[]{:S(2)}, u32[]{:S(2)}) async-start(bf16[4,16,640]{2,1,0:T(8,128)(2,1)} %pages.1), calls=%async_computation.1 | async-start | bytes 163840 | tf_op jit(solution)/shard_map/all_to_all | solution.py:391
  144.8 2.5 %collective-permute-start.7 = (bf16[16,3584]{1,0:T(8,128)(2,1)S(1)}, bf16[16,3584]{1,0:T(8,128)(2,1)S(1)}, u32[]{:S(2)}, u32[]{:S(2)}) collective-permute-start(bf16[16,3584]{1,0:T(8,128)(2,1)S(1)} %pad_maximum_fusion), channel_id=1, source_target_pairs={{0,32},{8,40},{16,48},{24,56},{32,64},{40,72},{48,80},{56,88},{64,... | collective-permute-start | bytes 344072 | tf_op jit(solution)/shard_map/ppermute | solution.py:27
  147.4 7.2 %collective-permute-start.9 = (bf16[16,3584]{1,0:T(8,128)(2,1)S(1)}, bf16[16,3584]{1,0:T(8,128)(2,1)S(1)}, u32[]{:S(2)}, u32[]{:S(2)}) collective-permute-start(bf16[16,3584]{1,0:T(8,128)(2,1)S(1)} %pad_maximum_fusion.1), channel_id=1, source_target_pairs={{0,96},{8,104},{16,112},{24,120},{32,0},{40,8},{48,16},{56,24},{64... | collective-permute-start | bytes 344072 | tf_op jit(solution)/shard_map/ppermute | solution.py:27
  154.7 0.1 copy.17
  155.0 0.2 convolution_convert_fusion
  155.2 0.6 copy.15
  155.8 0.6 copy.16
  156.4 1.9 %collective-permute-done.7 = bf16[16,3584]{1,0:T(8,128)(2,1)S(1)} collective-permute-done((bf16[16,3584]{1,0:T(8,128)(2,1)S(1)}, bf16[16,3584]{1,0:T(8,128)(2,1)S(1)}, u32[]{:S(2)}, u32[]{:S(2)}) %collective-permute-start.7) | collective-permute-done | bytes 114720 | tf_op jit(solution)/shard_map/ppermute | solution.py:27
  158.3 6.4 %collective-permute-done.9 = bf16[16,3584]{1,0:T(8,128)(2,1)S(1)} collective-permute-done((bf16[16,3584]{1,0:T(8,128)(2,1)S(1)}, bf16[16,3584]{1,0:T(8,128)(2,1)S(1)}, u32[]{:S(2)}, u32[]{:S(2)}) %collective-permute-start.9) | collective-permute-done | bytes 114720 | tf_op jit(solution)/shard_map/ppermute | solution.py:27
  164.7 0.8 fusion
  (38 shorter events, 0.6 us)
Async XLA Ops:
  7.1 77.9 %collective-permute-start = (bf16[13824,128]{1,0:T(8,128)(2,1)}, bf16[13824,128]{1,0:T(8,128)(2,1)}, u32[]{:S(2)}, u32[]{:S(2)}) collective-permute-start(bf16[13824,128]{1,0:T(8,128)(2,1)} %get-tuple-element.20), channel_id=1, source_target_pairs={{0,4},{4,0},{1,5},{5,1},{2,6},{6,2},{3,7},{7,3},{8,12},{12,8},{9,1... | collective-permute-start | bytes 10616840 | tf_op jit(solution)/shard_map/ppermute | solution.py:31
  45.6 39.4 %copy-start = (bf16[1536,384]{1,0:T(8,128)(2,1)S(1)}, bf16[1536,384]{1,0:T(8,128)(2,1)}, u32[]{:S(2)}) copy-start(bf16[1536,384]{1,0:T(8,128)(2,1)} %wq0.1) | copy-start | bytes 3538948
  45.6 39.4 %copy-start.2 = (bf16[2,128,512]{2,1,0:T(8,128)(2,1)S(1)}, bf16[2,128,512]{2,1,0:T(8,128)(2,1)}, u32[]{:S(2)}) copy-start(bf16[2,128,512]{2,1,0:T(8,128)(2,1)} %ak0.1) | copy-start | bytes 786436
  45.6 37.4 %all-to-all-start = ((bf16[4,256,640]{2,1,0:T(8,128)(2,1)}), bf16[4,256,640]{2,1,0:T(8,128)(2,1)S(1)}, u32[]{:S(2)}, u32[]{:S(2)}) async-start(bf16[4,256,640]{2,1,0:T(8,128)(2,1)} %broadcast_in_dim.25), calls=%async_computation | async-start | bytes 2621440 | tf_op jit(solution)/shard_map/all_to_all | solution.py:36
  83.0 5.7 %collective-permute-start.1 = (bf16[1024,640]{1,0:T(8,128)(2,1)S(1)}, bf16[1024,640]{1,0:T(8,128)(2,1)S(1)}, u32[]{:S(2)}, u32[]{:S(2)}) collective-permute-start(bf16[1024,640]{1,0:T(8,128)(2,1)S(1)} %bitcast.19), channel_id=1, source_target_pairs={{0,4},{4,0},{1,5},{5,1},{2,6},{6,2},{3,7},{7,3},{8,12},{12,8},{9,1... | collective-permute-start | bytes 3932168 | tf_op jit(solution)/shard_map/ppermute | solution.py:31
  85.0 3.7 %copy-start.1 = (bf16[256,3584]{1,0:T(8,128)(2,1)S(1)}, bf16[256,3584]{1,0:T(8,128)(2,1)}, u32[]{:S(2)}) copy-start(bf16[256,3584]{1,0:T(8,128)(2,1)} %op0.1) | copy-start | bytes 5505028
  85.0 3.7 %copy-start.3 = (bf16[2,512,128]{2,1,0:T(8,128)(2,1)S(1)}, bf16[2,512,128]{2,1,0:T(8,128)(2,1)}, u32[]{:S(2)}) copy-start(bf16[2,512,128]{2,1,0:T(8,128)(2,1)} %av0.1) | copy-start | bytes 786436
  99.1 15.2 %collective-permute-start.2 = (bf16[64,3584]{1,0:T(8,128)(2,1)S(1)}, bf16[64,3584]{1,0:T(8,128)(2,1)S(1)}, u32[]{:S(2)}, u32[]{:S(2)}) collective-permute-start(bf16[64,3584]{1,0:T(8,128)(2,1)S(1)} %get-tuple-element.23), channel_id=1, source_target_pairs={{0,8},{8,16},{16,24},{24,32},{32,40},{40,48},{48,56},{56,64},{64,7... | collective-permute-start | bytes 1376264 | tf_op jit(solution)/shard_map/ppermute | solution.py:27
  101.1 17.6 %collective-permute-start.3 = (bf16[64,3584]{1,0:T(8,128)(2,1)S(1)}, bf16[64,3584]{1,0:T(8,128)(2,1)S(1)}, u32[]{:S(2)}, u32[]{:S(2)}) collective-permute-start(bf16[64,3584]{1,0:T(8,128)(2,1)S(1)} %get-tuple-element.24), channel_id=1, source_target_pairs={{0,120},{8,0},{16,8},{24,16},{32,24},{40,32},{48,40},{56,48},{64,5... | collective-permute-start | bytes 1376264 | tf_op jit(solution)/shard_map/ppermute | solution.py:27
  105.0 21.4 %collective-permute-start.4 = (bf16[32,3584]{1,0:T(8,128)(2,1)S(1)}, bf16[32,3584]{1,0:T(8,128)(2,1)S(1)}, u32[]{:S(2)}, u32[]{:S(2)}) collective-permute-start(bf16[32,3584]{1,0:T(8,128)(2,1)S(1)} %get-tuple-element.27), channel_id=1, source_target_pairs={{0,16},{8,24},{16,32},{24,40},{32,48},{40,56},{48,64},{56,72},{64,... | collective-permute-start | bytes 688136 | tf_op jit(solution)/shard_map/ppermute | solution.py:27
  107.2 19.2 %collective-permute-start.5 = (bf16[32,3584]{1,0:T(8,128)(2,1)S(1)}, bf16[32,3584]{1,0:T(8,128)(2,1)S(1)}, u32[]{:S(2)}, u32[]{:S(2)}) collective-permute-start(bf16[32,3584]{1,0:T(8,128)(2,1)S(1)} %get-tuple-element.28), channel_id=1, source_target_pairs={{0,112},{8,120},{16,0},{24,8},{32,16},{40,24},{48,32},{56,40},{64,... | collective-permute-start | bytes 688136 | tf_op jit(solution)/shard_map/ppermute | solution.py:27
  118.8 20.1 %copy-start.4 = (bf16[16,640]{1,0:T(8,128)(2,1)S(1)}, bf16[16,640]{1,0:T(8,128)(2,1)}, u32[]{:S(2)}) copy-start(bf16[16,640]{1,0:T(8,128)(2,1)} %get-tuple-element.30.key_ref) | copy-start | bytes 61444
  118.8 20.1 %copy-start.5 = (s32[1,4]{1,0:T(1,128)S(1)}, s32[1,4]{1,0:T(1,128)}, u32[]{:S(2)}) copy-start(s32[1,4]{1,0:T(1,128)} %owner_ref.1) | copy-start | bytes 52
  118.8 20.1 %copy-start.6 = (s32[1,4]{1,0:T(1,128)S(1)}, s32[1,4]{1,0:T(1,128)}, u32[]{:S(2)}) copy-start(s32[1,4]{1,0:T(1,128)} %slot_ref.1) | copy-start | bytes 52
  118.8 14.1 %collective-permute-start.6 = (bf16[16,1792]{1,0:T(8,128)(2,1)S(1)}, bf16[16,1792]{1,0:T(8,128)(2,1)S(1)}, u32[]{:S(2)}, u32[]{:S(2)}) collective-permute-start(bf16[16,1792]{1,0:T(8,128)(2,1)S(1)} %get-tuple-element.36), channel_id=1, source_target_pairs={{0,32},{8,40},{16,48},{24,56},{32,64},{40,72},{48,80},{56,88},{64,... | collective-permute-start | bytes 172040 | tf_op jit(solution)/shard_map/ppermute | solution.py:27
  126.5 12.3 %collective-permute-start.8 = (bf16[16,1792]{1,0:T(8,128)(2,1)S(1)}, bf16[16,1792]{1,0:T(8,128)(2,1)S(1)}, u32[]{:S(2)}, u32[]{:S(2)}) collective-permute-start(bf16[16,1792]{1,0:T(8,128)(2,1)S(1)} %get-tuple-element.37), channel_id=1, source_target_pairs={{0,96},{8,104},{16,112},{24,120},{32,0},{40,8},{48,16},{56,24},{64... | collective-permute-start | bytes 172040 | tf_op jit(solution)/shard_map/ppermute | solution.py:27
  140.1 14.5 %all-to-all-start.1 = ((bf16[4,16,640]{2,1,0:T(8,128)(2,1)}), bf16[4,16,640]{2,1,0:T(8,128)(2,1)S(1)}, u32[]{:S(2)}, u32[]{:S(2)}) async-start(bf16[4,16,640]{2,1,0:T(8,128)(2,1)} %pages.1), calls=%async_computation.1 | async-start | bytes 163840 | tf_op jit(solution)/shard_map/all_to_all | solution.py:391
  144.8 13.4 %collective-permute-start.7 = (bf16[16,3584]{1,0:T(8,128)(2,1)S(1)}, bf16[16,3584]{1,0:T(8,128)(2,1)S(1)}, u32[]{:S(2)}, u32[]{:S(2)}) collective-permute-start(bf16[16,3584]{1,0:T(8,128)(2,1)S(1)} %pad_maximum_fusion), channel_id=1, source_target_pairs={{0,32},{8,40},{16,48},{24,56},{32,64},{40,72},{48,80},{56,88},{64,... | collective-permute-start | bytes 344072 | tf_op jit(solution)/shard_map/ppermute | solution.py:27
  147.4 17.4 %collective-permute-start.9 = (bf16[16,3584]{1,0:T(8,128)(2,1)S(1)}, bf16[16,3584]{1,0:T(8,128)(2,1)S(1)}, u32[]{:S(2)}, u32[]{:S(2)}) collective-permute-start(bf16[16,3584]{1,0:T(8,128)(2,1)S(1)} %pad_maximum_fusion.1), channel_id=1, source_target_pairs={{0,96},{8,104},{16,112},{24,120},{32,0},{40,8},{48,16},{56,24},{64... | collective-permute-start | bytes 344072 | tf_op jit(solution)/shard_map/ppermute | solution.py:27

commit v12 on v11

--- a/solution.py
+++ b/solution.py
@@ -164,7 +164,7 @@
 
 def attend_kernel(
     where_ref, q_ref, ka_ref, kb_ref, av0, op0, packed, o0, o1, o2, o3, o4,
-    s_ref, top_ref, l_ref, acc_ref, ho_ref, av_ref, op_ref, sems, *, rows, lat, scale, nch, chips, qrows, part, shapes,
+    acc_ref, ho_ref, av_ref, op_ref, sems, *, rows, lat, scale, nch, chips, qrows, part, shapes,
 ):
     chain, z, core = where_ref[0], where_ref[1], where_ref[2]
     s2 = scale * LOG2E
@@ -176,65 +176,38 @@
     n = ka_ref.shape[0] // nch
     nt = (((1,), (1,)), ((), ()))
 
-    def lanes(x, op):
-        out = x[:, :128]
-        for c in range(128, x.shape[1], 128):
-            out = op(out, x[:, c : c + 128])
-        return out
-
-    def block(back):
-        return pl.ds(pl.multiple_of(jnp.maximum(chain - back, 0) * n, n), n)
-
-    def score(back):
-        if back == 0:
-            idx = lax.broadcasted_iota(jnp.int32, (rows, 1), 0)
-            qpos = query_where(idx, z, core, qrows, chips)
-            idx = lax.broadcasted_iota(jnp.int32, (1, n), 1)
-            kpos = (idx % qrows) // part * (chips * 2 * part) + idx // qrows * (2 * part) + idx % part
-            ok = [kpos + i * part <= qpos for i in (core, 1 - core)]
-        for i, k_ref in enumerate((ka_ref, kb_ref)):
-            at = (2 * back + i) * n
-            all_heads = lax.dot_general(
-                q_ref[...], k_ref[block(back), :], nt, preferred_element_type=F32
-            )
-            for h in range(heads):
-                s = all_heads[h * rows : (h + 1) * rows]
-                if back == 0:
-                    s = jnp.where(ok[i], s, NEG)
-                s_ref[h * rows : (h + 1) * rows, at : at + n] = s
-                top = lanes(s, jnp.maximum)
-                if back or i:
-                    top = jnp.maximum(top, top_ref[h * rows : (h + 1) * rows])
-                top_ref[h * rows : (h + 1) * rows] = top
-
-    def mix(back):
-        m = top_ref[:, :1]
-        for i, k_ref in enumerate((ka_ref, kb_ref)):
-            at = (2 * back + i) * n
-            p = jnp.exp2(s_ref[:, at : at + n] * s2 - m)
-            total = lanes(p, jnp.add)
-            l_ref[...] = total + l_ref[...] if back or i else total
-            pv = jnp.dot(p.astype(BF), k_ref[block(back), :lat], preferred_element_type=F32)
-            acc_ref[...] = acc_ref[...] + pv if back or i else pv
-
-    score(0)
-    for back in range(1, nch):
-        pl.when(chain >= back)(functools.partial(score, back))
-    top_ref[...] = jnp.broadcast_to(
-        jnp.max(top_ref[...], -1, keepdims=True) * s2, top_ref.shape
-    )
-    mix(0)
-    for back in range(1, nch):
-        pl.when(chain >= back)(functools.partial(mix, back))
+    def attend(blocks_seen):
+        count = blocks_seen * n
+        idx = lax.broadcasted_iota(jnp.int32, (rows, 1), 0)
+        qpos = query_where(idx, z, core, qrows, chips)
+        idx = lax.broadcasted_iota(jnp.int32, (1, n), 1)
+        kpos = (idx % qrows) // part * (chips * 2 * part) + idx // qrows * (2 * part) + idx % part
+        ok = [kpos + i * part <= qpos for i in (core, 1 - core)]
+        for h in range(heads):
+            q = q_ref[h * rows : (h + 1) * rows, :]
+            scores = []
+            for i, k_ref in enumerate((ka_ref, kb_ref)):
+                s = lax.dot_general(q, k_ref[:count, :], nt, preferred_element_type=F32)
+                own = jnp.where(ok[i], s[:, count - n :], NEG)
+                scores.append(own if count == n else jnp.concatenate([s[:, : count - n], own], -1))
+            m = jnp.maximum(*[jnp.max(s, -1, keepdims=True) for s in scores]) * s2
+            total, mixed = 0.0, 0.0
+            for s, k_ref in zip(scores, (ka_ref, kb_ref)):
+                p = jnp.exp2(s * s2 - m)
+                total = total + jnp.sum(p, -1, keepdims=True)
+                mixed = mixed + jnp.dot(p.astype(BF), k_ref[:count, :lat], preferred_element_type=F32)
+            acc_ref[h * rows : (h + 1) * rows, :] = (mixed / total).astype(BF)
+
+    for seen in range(1, nch + 1):
+        pl.when(chain == seen - 1)(functools.partial(attend, seen))
     for load in loads:
         load.wait()
     per = heads // 2
     for h in range(heads):
-        at = slice(h * rows, (h + 1) * rows)
-        total = jnp.sum(l_ref[at], -1, keepdims=True)
-        mixed = (acc_ref[at] / total).astype(BF)
         av = av_ref[h // per, h % per]
-        ho_ref[:, h * vh : (h + 1) * vh] = jnp.dot(mixed, av, preferred_element_type=F32).astype(BF)
+        ho_ref[:, h * vh : (h + 1) * vh] = jnp.dot(
+            acc_ref[h * rows : (h + 1) * rows, :], av, preferred_element_type=F32
+        ).astype(BF)
     ho = ho_ref[...]
     k, width = op_ref.shape[1:]
     cut = 512 if width % 512 == 0 else width
@@ -337,10 +310,7 @@
         in_specs=[smem] + [vm] * 3 + [hbm] * 3,
         out_specs=[vm] * 5,
         scratch_shapes=[
-            pltpu.VMEM((heads * rows, nch * block_len), F32),
-            pltpu.VMEM((heads * rows, 128), F32),
-            pltpu.VMEM((heads * rows, 128), F32),
-            pltpu.VMEM((heads * rows, lat), F32),
+            pltpu.VMEM((heads * rows, lat), BF),
             pltpu.VMEM((rows, heads * vh), BF),
             pltpu.VMEM((2,) + absorb_value.shape, BF),
             pltpu.VMEM((2,) + out_proj.shape, BF),
@@ -370,22 +340,22 @@
     right = shift_z(far[:, cut:], -nzl).astype(F32)
     ahead = near(1, up, down) + up2[qrows:].astype(F32)
     ahead = jnp.concatenate([ahead[:, :cut] + left, ahead[:, cut:]], -1)
-    ahead = ahead.astype(BF)
+    ahead = shift_z(ahead.astype(BF), nzl)
     behind = near(-1, up, down) + down2[:qrows].astype(F32)
     behind = jnp.concatenate([behind[:, :cut], behind[:, cut:] + right], -1)
-    behind = behind.astype(BF)
+    behind = shift_z(behind.astype(BF), -nzl)
     total = near(0, up, down) + up2[:qrows].astype(F32) + down2[qrows:].astype(F32)
-    total = total + shift_z(ahead, nzl).astype(F32) + shift_z(behind, -nzl).astype(F32)
+    total = total + ahead.astype(F32) + behind.astype(F32)
     layer_output = total.astype(BF)[None]
 
-    page = lax.optimization_barrier((keys, ahead, behind))[0]
+    page = lax.optimization_barrier((keys, sums[0]))[0]
     page = pl.pallas_call(
         functools.partial(page_kernel, lat=lat, part=part, slots=slots),
         out_shape=jax.ShapeDtypeStruct((lax.axis_size("dec"),) + keys.shape, BF),
         in_specs=[smem, smem, vm],
         out_specs=vm,
         compiler_params=room(4),
-        cost_estimate=pl.CostEstimate(flops=0, bytes_accessed=4000000, transcendentals=0),
+        cost_estimate=pl.CostEstimate(flops=10**10, bytes_accessed=400000, transcendentals=0),
         name="pages",
     )(page_owner, page_slot, page)
     page = lax.all_to_all(page, "dec", 0, 0, tiled=True).reshape(-1, pages, part, kw)

time: 166 us -> 158 us (0.952)
  the two profiles are of different devices: /device:TPU:58 before, /device:TPU:24 now
where the time goes in v12:
time: 158 us; the launch traced here: 157 us
  blocking collectives  68 us (43%)
  starting transfers between devices  46.4 us (29%)
  Pallas kernels  19.6 us (12%)
  waiting for transfers between devices  16.2 us (10%)
  local copies, waits for them, and re-layouts  3.6 us (2%)
  other arithmetic  2.35 us (1%)
    all_gather x1, blocking collectives, local(): own = lax.all_gather(keys, Z, axis=0, tiled=True)  37.4 us
    ppermute x8, starting transfers between devices, shift_z(): return lax.ppermute(x, Z, [(i, (i + step) % n) for i in range(n)])  33.4 us
    all_gather x1, blocking collectives, local(): qg = lax.all_gather(held, Z, axis=0, tiled=True)  30.6 us
    ppermute x8, waiting for transfers between devices, shift_z(): return lax.ppermute(x, Z, [(i, (i + step) % n) for i in range(n)])  16.2 us
    pallas_call x1, Pallas kernels, local(): pl.pallas_call(functools.partial(attend_kernel, rows=rows, lat=lat, scale...  10.4 us
    all_to_all x1, starting transfers between devices, spread(): lax.all_to_all(jnp.broadcast_to(x[None], (n,) + x.shape), axis, 0, 0, til...  4.82 us
    pallas_call x1, Pallas kernels, local(): pl.pallas_call(functools.partial(key_kernel, lat=lat, part=part, page_len...  4.44 us
    all_to_all x1, starting transfers between devices, local(): lax.all_to_all(page, 'dec', 0, 0, tiled=True).reshape(-1, pages, part, kw)  4.31 us
  transfers between devices with their start and end apart: 12, of which 7 were waited for; matrix products, arithmetic and copies ran while one was open for 2% of the time, Pallas kernels for 2%

profile of v12, /device:TPU:24, one launch (start us, length us, event | category | flops | bytes accessed | tf_op | source)
XLA Modules:
  0.0 157.3 jit_solution(16959051859951543432)
XLA Ops:
  0.6 0.7 reshape_squeeze.7
  1.4 1.3 pad_maximum_fusion.2.x_ref
  2.7 4.4 %keys.1 = (bf16[16,640]{1,0:T(8,128)(2,1)}, bf16[13824,128]{1,0:T(8,128)(2,1)}) custom-call(s32[1]{0:T(128)} %bitcast.4.base_ref, bf16[16,576]{1,0:T(8,128)(2,1)} %pad_maximum_fusion.2.x_ref, f32[1,512]{1,0:T(1,128)} %bitcast.23, bf16[1536,384]{1,0:T(8,128)(2,1)} %wq0.1, bf16[2,128,512]{2,1,0:T(8,128)(2,1)} %ak0.1, bf16[2,512,128]{2,1,0:T(8,128)(2,1)} %av0.1, ...), custom_call_target="tpu_custom_call" | custom-call | tf_op jit(solution)/shard_map/keys/pallas_call | solution.py:259
  7.1 1.9 %collective-permute-start = (bf16[13824,128]{1,0:T(8,128)(2,1)}, bf16[13824,128]{1,0:T(8,128)(2,1)}, u32[]{:S(2)}, u32[]{:S(2)}) collective-permute-start(bf16[13824,128]{1,0:T(8,128)(2,1)} %get-tuple-element.20), channel_id=1, source_target_pairs={{0,4},{4,0},{1,5},{5,1},{2,6},{6,2},{3,7},{7,3},{8,12},{12,8},{9,1... | collective-permute-start | bytes 10616840 | tf_op jit(solution)/shard_map/ppermute | solution.py:31
  9.0 37.4 %all_gather.6 = bf16[256,640]{1,0:T(8,128)(2,1)S(1)} all-gather(bf16[16,640]{1,0:T(8,128)(2,1)} %get-tuple-element.30.key_ref), channel_id=1, replica_groups=mesh['chain'=4,'zh'=4,'zl'=4,'core'=2,'dec'=4] {'zh','zl'}, dimensions={0}, use_global_device_ids=true | all-gather | bytes 348160 | tf_op jit(solution)/shard_map/all_gather | solution.py:277
  46.4 1.2 broadcast_in_dim.25
  47.7 4.8 %all-to-all-start = ((bf16[4,256,640]{2,1,0:T(8,128)(2,1)}), bf16[4,256,640]{2,1,0:T(8,128)(2,1)S(1)}, u32[]{:S(2)}, u32[]{:S(2)}) async-start(bf16[4,256,640]{2,1,0:T(8,128)(2,1)} %broadcast_in_dim.25), calls=%async_computation | async-start | bytes 2621440 | tf_op jit(solution)/shard_map/all_to_all | solution.py:36
  52.5 30.6 %all_gather.7.g_ref = bf16[256,1536]{1,0:T(8,128)(2,1)S(1)} all-gather(bf16[16,1536]{1,0:T(8,128)(2,1)} %bitcast.21), channel_id=1, replica_groups=mesh['chain'=4,'zh'=4,'zl'=4,'core'=2,'dec'=4] {'zh','zl'}, dimensions={0}, use_global_device_ids=true | all-gather | bytes 835584 | tf_op jit(solution)/shard_map/all_gather | solution.py:280
  83.1 1.9 %collective-permute-start.1 = (bf16[1024,640]{1,0:T(8,128)(2,1)S(1)}, bf16[1024,640]{1,0:T(8,128)(2,1)}, u32[]{:S(2)}, u32[]{:S(2)}) collective-permute-start(bf16[1024,640]{1,0:T(8,128)(2,1)S(1)} %bitcast.19), channel_id=1, source_target_pairs={{0,4},{4,0},{1,5},{5,1},{2,6},{6,2},{3,7},{7,3},{8,12},{12,8},{9,1... | collective-permute-start | bytes 3932168 | tf_op jit(solution)/shard_map/ppermute | solution.py:31
  85.1 3.7 %queries.1.q_ref = bf16[1024,640]{1,0:T(8,128)(2,1)S(1)} custom-call(s32[3]{0:T(128)S(1)} %pad_add_fusion.where_ref, bf16[256,1536]{1,0:T(8,128)(2,1)S(1)} %all_gather.7.g_ref, bf16[1536,384]{1,0:T(8,128)(2,1)S(1)} %copy-done, bf16[2,128,512]{2,1,0:T(8,128)(2,1)S(1)} %copy-done.2, bf16[13824,128]{1,0:T(8,128)(2,1)} %collective-permute-done.packed), custom_call_target="tpu_custom_call" | custom-call | flops 738197504 | bytes 6000000 | tf_op jit(solution)/shard_map/queries/pallas_call | solution.py:284
  88.8 10.4 %attend.1 = (bf16[64,3584]{1,0:T(8,128)(2,1)S(1)}, bf16[64,3584]{1,0:T(8,128)(2,1)S(1)}, bf16[64,3584]{1,0:T(8,128)(2,1)S(1)}, bf16[32,3584]{1,0:T(8,128)(2,1)S(1)}, bf16[32,3584]{1,0:T(8,128)(2,1)S(1)}) custom-call(s32[3]{0:T(128)S(1)} %pad_add_fusion.where_ref, bf16[1024,640]{1,0:T(8,128)(2,1)S(1)} %queries.1.q_ref, bf16[1024,640]{1,0:T(8,128)(2,1)S(1)} %bitcast.20, ...), custom_call_target="tpu_custom_call" | custom-call | flops 4294967296 | bytes 9000000 | tf_op jit(solution)/shard_map/attend/pallas_call | solution.py:304
  99.2 1.2 pages.1
  100.4 4.3 %all-to-all-start.1 = ((bf16[4,16,640]{2,1,0:T(8,128)(2,1)}), bf16[4,16,640]{2,1,0:T(8,128)(2,1)S(1)}, u32[]{:S(2)}, u32[]{:S(2)}) async-start(bf16[4,16,640]{2,1,0:T(8,128)(2,1)} %pages.1), calls=%async_computation.1 | async-start | bytes 163840 | tf_op jit(solution)/shard_map/all_to_all | solution.py:361
  104.7 3.7 %collective-permute-start.2 = (bf16[64,3584]{1,0:T(8,128)(2,1)S(1)}, bf16[64,3584]{1,0:T(8,128)(2,1)S(1)}, u32[]{:S(2)}, u32[]{:S(2)}) collective-permute-start(bf16[64,3584]{1,0:T(8,128)(2,1)S(1)} %get-tuple-element.23), channel_id=1, source_target_pairs={{0,8},{8,16},{16,24},{24,32},{32,40},{40,48},{48,56},{56,64},{64,7... | collective-permute-start | bytes 1376264 | tf_op jit(solution)/shard_map/ppermute | solution.py:27
  108.5 3.3 %collective-permute-start.3 = (bf16[64,3584]{1,0:T(8,128)(2,1)S(1)}, bf16[64,3584]{1,0:T(8,128)(2,1)S(1)}, u32[]{:S(2)}, u32[]{:S(2)}) collective-permute-start(bf16[64,3584]{1,0:T(8,128)(2,1)S(1)} %get-tuple-element.24), channel_id=1, source_target_pairs={{0,120},{8,0},{16,8},{24,16},{32,24},{40,32},{48,40},{56,48},{64,5... | collective-permute-start | bytes 1376264 | tf_op jit(solution)/shard_map/ppermute | solution.py:27
  111.8 2.0 %collective-permute-start.4 = (bf16[32,3584]{1,0:T(8,128)(2,1)S(1)}, bf16[32,3584]{1,0:T(8,128)(2,1)S(1)}, u32[]{:S(2)}, u32[]{:S(2)}) collective-permute-start(bf16[32,3584]{1,0:T(8,128)(2,1)S(1)} %get-tuple-element.27), channel_id=1, source_target_pairs={{0,16},{8,24},{16,32},{24,40},{32,48},{40,56},{48,64},{56,72},{64,... | collective-permute-start | bytes 688136 | tf_op jit(solution)/shard_map/ppermute | solution.py:27
  113.8 6.0 %collective-permute-start.5 = (bf16[32,3584]{1,0:T(8,128)(2,1)S(1)}, bf16[32,3584]{1,0:T(8,128)(2,1)S(1)}, u32[]{:S(2)}, u32[]{:S(2)}) collective-permute-start(bf16[32,3584]{1,0:T(8,128)(2,1)S(1)} %get-tuple-element.28), channel_id=1, source_target_pairs={{0,112},{8,120},{16,0},{24,8},{32,16},{40,24},{48,32},{56,40},{64,... | collective-permute-start | bytes 688136 | tf_op jit(solution)/shard_map/ppermute | solution.py:27
  120.1 0.2 convolution_convert_fusion
  120.3 0.6 copy.15
  121.0 1.3 collective-permute-done.2
  122.3 2.3 %collective-permute-done.3 = bf16[64,3584]{1,0:T(8,128)(2,1)S(1)} collective-permute-done((bf16[64,3584]{1,0:T(8,128)(2,1)S(1)}, bf16[64,3584]{1,0:T(8,128)(2,1)S(1)}, u32[]{:S(2)}, u32[]{:S(2)}) %collective-permute-start.3) | collective-permute-done | bytes 458784 | tf_op jit(solution)/shard_map/ppermute | solution.py:27
  124.7 3.7 %collective-permute-start.6 = (bf16[16,1792]{1,0:T(8,128)(2,1)S(1)}, bf16[16,1792]{1,0:T(8,128)(2,1)S(1)}, u32[]{:S(2)}, u32[]{:S(2)}) collective-permute-start(bf16[16,1792]{1,0:T(8,128)(2,1)S(1)} %get-tuple-element.36), channel_id=1, source_target_pairs={{0,32},{8,40},{16,48},{24,56},{32,64},{40,72},{48,80},{56,88},{64,... | collective-permute-start | bytes 172040 | tf_op jit(solution)/shard_map/ppermute | solution.py:27
  128.4 2.1 %collective-permute-done.4 = bf16[32,3584]{1,0:T(8,128)(2,1)S(1)} collective-permute-done((bf16[32,3584]{1,0:T(8,128)(2,1)S(1)}, bf16[32,3584]{1,0:T(8,128)(2,1)S(1)}, u32[]{:S(2)}, u32[]{:S(2)}) %collective-permute-start.4) | collective-permute-done | bytes 229408 | tf_op jit(solution)/shard_map/ppermute | solution.py:27
  130.5 1.9 %collective-permute-done.5 = bf16[32,3584]{1,0:T(8,128)(2,1)S(1)} collective-permute-done((bf16[32,3584]{1,0:T(8,128)(2,1)S(1)}, bf16[32,3584]{1,0:T(8,128)(2,1)S(1)}, u32[]{:S(2)}, u32[]{:S(2)}) %collective-permute-start.5) | collective-permute-done | bytes 229408 | tf_op jit(solution)/shard_map/ppermute | solution.py:27
  132.6 5.5 %collective-permute-start.8 = (bf16[16,1792]{1,0:T(8,128)(2,1)S(1)}, bf16[16,1792]{1,0:T(8,128)(2,1)S(1)}, u32[]{:S(2)}, u32[]{:S(2)}) collective-permute-start(bf16[16,1792]{1,0:T(8,128)(2,1)S(1)} %get-tuple-element.37), channel_id=1, source_target_pairs={{0,96},{8,104},{16,112},{24,120},{32,0},{40,8},{48,16},{56,24},{64... | collective-permute-start | bytes 172040 | tf_op jit(solution)/shard_map/ppermute | solution.py:27
  138.1 4.3 %collective-permute-start.7 = (bf16[16,3584]{1,0:T(8,128)(2,1)S(1)}, bf16[16,3584]{1,0:T(8,128)(2,1)S(1)}, u32[]{:S(2)}, u32[]{:S(2)}) collective-permute-start(bf16[16,3584]{1,0:T(8,128)(2,1)S(1)} %pad_maximum_fusion), channel_id=1, source_target_pairs={{0,32},{8,40},{16,48},{24,56},{32,64},{40,72},{48,80},{56,88},{64,... | collective-permute-start | bytes 344072 | tf_op jit(solution)/shard_map/ppermute | solution.py:27
  142.4 0.9 collective-permute-done.8
  143.3 5.0 %collective-permute-start.9 = (bf16[16,3584]{1,0:T(8,128)(2,1)S(1)}, bf16[16,3584]{1,0:T(8,128)(2,1)S(1)}, u32[]{:S(2)}, u32[]{:S(2)}) collective-permute-start(bf16[16,3584]{1,0:T(8,128)(2,1)S(1)} %pad_maximum_fusion.1), channel_id=1, source_target_pairs={{0,96},{8,104},{16,112},{24,120},{32,0},{40,8},{48,16},{56,24},{64... | collective-permute-start | bytes 344072 | tf_op jit(solution)/shard_map/ppermute | solution.py:27
  148.3 0.6 copy.16
  148.9 0.9 collective-permute-done.7
  149.8 6.8 %collective-permute-done.9 = bf16[16,3584]{1,0:T(8,128)(2,1)S(1)} collective-permute-done((bf16[16,3584]{1,0:T(8,128)(2,1)S(1)}, bf16[16,3584]{1,0:T(8,128)(2,1)S(1)}, u32[]{:S(2)}, u32[]{:S(2)}) %collective-permute-start.9) | collective-permute-done | bytes 114720 | tf_op jit(solution)/shard_map/ppermute | solution.py:27
  156.6 0.8 fusion
  (38 shorter events, 0.7 us)
Async XLA Ops:
  7.1 78.0 %collective-permute-start = (bf16[13824,128]{1,0:T(8,128)(2,1)}, bf16[13824,128]{1,0:T(8,128)(2,1)}, u32[]{:S(2)}, u32[]{:S(2)}) collective-permute-start(bf16[13824,128]{1,0:T(8,128)(2,1)} %get-tuple-element.20), channel_id=1, source_target_pairs={{0,4},{4,0},{1,5},{5,1},{2,6},{6,2},{3,7},{7,3},{8,12},{12,8},{9,1... | collective-permute-start | bytes 10616840 | tf_op jit(solution)/shard_map/ppermute | solution.py:31
  47.7 37.4 %copy-start = (bf16[1536,384]{1,0:T(8,128)(2,1)S(1)}, bf16[1536,384]{1,0:T(8,128)(2,1)}, u32[]{:S(2)}) copy-start(bf16[1536,384]{1,0:T(8,128)(2,1)} %wq0.1) | copy-start | bytes 3538948
  47.7 37.4 %copy-start.2 = (bf16[2,128,512]{2,1,0:T(8,128)(2,1)S(1)}, bf16[2,128,512]{2,1,0:T(8,128)(2,1)}, u32[]{:S(2)}) copy-start(bf16[2,128,512]{2,1,0:T(8,128)(2,1)} %ak0.1) | copy-start | bytes 786436
  47.7 35.4 %all-to-all-start = ((bf16[4,256,640]{2,1,0:T(8,128)(2,1)}), bf16[4,256,640]{2,1,0:T(8,128)(2,1)S(1)}, u32[]{:S(2)}, u32[]{:S(2)}) async-start(bf16[4,256,640]{2,1,0:T(8,128)(2,1)} %broadcast_in_dim.25), calls=%async_computation | async-start | bytes 2621440 | tf_op jit(solution)/shard_map/all_to_all | solution.py:36
  83.1 5.7 %collective-permute-start.1 = (bf16[1024,640]{1,0:T(8,128)(2,1)S(1)}, bf16[1024,640]{1,0:T(8,128)(2,1)}, u32[]{:S(2)}, u32[]{:S(2)}) collective-permute-start(bf16[1024,640]{1,0:T(8,128)(2,1)S(1)} %bitcast.19), channel_id=1, source_target_pairs={{0,4},{4,0},{1,5},{5,1},{2,6},{6,2},{3,7},{7,3},{8,12},{12,8},{9,1... | collective-permute-start | bytes 3932168 | tf_op jit(solution)/shard_map/ppermute | solution.py:31
  85.1 3.7 %copy-start.1 = (bf16[256,3584]{1,0:T(8,128)(2,1)S(1)}, bf16[256,3584]{1,0:T(8,128)(2,1)}, u32[]{:S(2)}) copy-start(bf16[256,3584]{1,0:T(8,128)(2,1)} %op0.1) | copy-start | bytes 5505028
  85.1 3.8 %copy-start.3 = (bf16[2,512,128]{2,1,0:T(8,128)(2,1)S(1)}, bf16[2,512,128]{2,1,0:T(8,128)(2,1)}, u32[]{:S(2)}) copy-start(bf16[2,512,128]{2,1,0:T(8,128)(2,1)} %av0.1) | copy-start | bytes 786436
  88.8 10.4 %copy-start.4 = (bf16[16,640]{1,0:T(8,128)(2,1)S(1)}, bf16[16,640]{1,0:T(8,128)(2,1)}, u32[]{:S(2)}) copy-start(bf16[16,640]{1,0:T(8,128)(2,1)} %get-tuple-element.30.key_ref) | copy-start | bytes 61444
  88.8 10.4 %copy-start.5 = (s32[1,4]{1,0:T(1,128)S(1)}, s32[1,4]{1,0:T(1,128)}, u32[]{:S(2)}) copy-start(s32[1,4]{1,0:T(1,128)} %owner_ref.1) | copy-start | bytes 52
  88.8 10.4 %copy-start.6 = (s32[1,4]{1,0:T(1,128)S(1)}, s32[1,4]{1,0:T(1,128)}, u32[]{:S(2)}) copy-start(s32[1,4]{1,0:T(1,128)} %slot_ref.1) | copy-start | bytes 52
  100.4 19.4 %all-to-all-start.1 = ((bf16[4,16,640]{2,1,0:T(8,128)(2,1)}), bf16[4,16,640]{2,1,0:T(8,128)(2,1)S(1)}, u32[]{:S(2)}, u32[]{:S(2)}) async-start(bf16[4,16,640]{2,1,0:T(8,128)(2,1)} %pages.1), calls=%async_computation.1 | async-start | bytes 163840 | tf_op jit(solution)/shard_map/all_to_all | solution.py:361
  104.7 17.6 %collective-permute-start.2 = (bf16[64,3584]{1,0:T(8,128)(2,1)S(1)}, bf16[64,3584]{1,0:T(8,128)(2,1)S(1)}, u32[]{:S(2)}, u32[]{:S(2)}) collective-permute-start(bf16[64,3584]{1,0:T(8,128)(2,1)S(1)} %get-tuple-element.23), channel_id=1, source_target_pairs={{0,8},{8,16},{16,24},{24,32},{32,40},{40,48},{48,56},{56,64},{64,7... | collective-permute-start | bytes 1376264 | tf_op jit(solution)/shard_map/ppermute | solution.py:27
  108.5 16.2 %collective-permute-start.3 = (bf16[64,3584]{1,0:T(8,128)(2,1)S(1)}, bf16[64,3584]{1,0:T(8,128)(2,1)S(1)}, u32[]{:S(2)}, u32[]{:S(2)}) collective-permute-start(bf16[64,3584]{1,0:T(8,128)(2,1)S(1)} %get-tuple-element.24), channel_id=1, source_target_pairs={{0,120},{8,0},{16,8},{24,16},{32,24},{40,32},{48,40},{56,48},{64,5... | collective-permute-start | bytes 1376264 | tf_op jit(solution)/shard_map/ppermute | solution.py:27
  111.8 18.7 %collective-permute-start.4 = (bf16[32,3584]{1,0:T(8,128)(2,1)S(1)}, bf16[32,3584]{1,0:T(8,128)(2,1)S(1)}, u32[]{:S(2)}, u32[]{:S(2)}) collective-permute-start(bf16[32,3584]{1,0:T(8,128)(2,1)S(1)} %get-tuple-element.27), channel_id=1, source_target_pairs={{0,16},{8,24},{16,32},{24,40},{32,48},{40,56},{48,64},{56,72},{64,... | collective-permute-start | bytes 688136 | tf_op jit(solution)/shard_map/ppermute | solution.py:27
  113.8 18.6 %collective-permute-start.5 = (bf16[32,3584]{1,0:T(8,128)(2,1)S(1)}, bf16[32,3584]{1,0:T(8,128)(2,1)S(1)}, u32[]{:S(2)}, u32[]{:S(2)}) collective-permute-start(bf16[32,3584]{1,0:T(8,128)(2,1)S(1)} %get-tuple-element.28), channel_id=1, source_target_pairs={{0,112},{8,120},{16,0},{24,8},{32,16},{40,24},{48,32},{56,40},{64,... | collective-permute-start | bytes 688136 | tf_op jit(solution)/shard_map/ppermute | solution.py:27
  124.7 13.3 %collective-permute-start.6 = (bf16[16,1792]{1,0:T(8,128)(2,1)S(1)}, bf16[16,1792]{1,0:T(8,128)(2,1)S(1)}, u32[]{:S(2)}, u32[]{:S(2)}) collective-permute-start(bf16[16,1792]{1,0:T(8,128)(2,1)S(1)} %get-tuple-element.36), channel_id=1, source_target_pairs={{0,32},{8,40},{16,48},{24,56},{32,64},{40,72},{48,80},{56,88},{64,... | collective-permute-start | bytes 172040 | tf_op jit(solution)/shard_map/ppermute | solution.py:27
  132.6 10.7 %collective-permute-start.8 = (bf16[16,1792]{1,0:T(8,128)(2,1)S(1)}, bf16[16,1792]{1,0:T(8,128)(2,1)S(1)}, u32[]{:S(2)}, u32[]{:S(2)}) collective-permute-start(bf16[16,1792]{1,0:T(8,128)(2,1)S(1)} %get-tuple-element.37), channel_id=1, source_target_pairs={{0,96},{8,104},{16,112},{24,120},{32,0},{40,8},{48,16},{56,24},{64... | collective-permute-start | bytes 172040 | tf_op jit(solution)/shard_map/ppermute | solution.py:27
  138.1 11.7 %collective-permute-start.7 = (bf16[16,3584]{1,0:T(8,128)(2,1)S(1)}, bf16[16,3584]{1,0:T(8,128)(2,1)S(1)}, u32[]{:S(2)}, u32[]{:S(2)}) collective-permute-start(bf16[16,3584]{1,0:T(8,128)(2,1)S(1)} %pad_maximum_fusion), channel_id=1, source_target_pairs={{0,32},{8,40},{16,48},{24,56},{32,64},{40,72},{48,80},{56,88},{64,... | collective-permute-start | bytes 344072 | tf_op jit(solution)/shard_map/ppermute | solution.py:27
  143.3 13.3 %collective-permute-start.9 = (bf16[16,3584]{1,0:T(8,128)(2,1)S(1)}, bf16[16,3584]{1,0:T(8,128)(2,1)S(1)}, u32[]{:S(2)}, u32[]{:S(2)}) collective-permute-start(bf16[16,3584]{1,0:T(8,128)(2,1)S(1)} %pad_maximum_fusion.1), channel_id=1, source_target_pairs={{0,96},{8,104},{16,112},{24,120},{32,0},{40,8},{48,16},{56,24},{64... | collective-permute-start | bytes 344072 | tf_op jit(solution)/shard_map/ppermute | solution.py:27

commit v13 on v12

--- a/solution.py
+++ b/solution.py
@@ -53,20 +53,6 @@
     return jnp.cos(angle), jnp.where(lane < width // 2, -sine, sine)
 
 
-def page_kernel(owner_ref, slot_ref, key_ref, out_ref, *, lat, part, slots):
-    tail = key_ref[:, lat:].astype(F32)
-    row = lax.broadcasted_iota(jnp.int32, tail.shape, 0)
-    lane = lax.broadcasted_iota(jnp.int32, tail.shape, 1)
-    code = jnp.zeros(tail.shape, F32)
-    for p in range(tail.shape[0] // part):
-        here = (owner_ref[0, p] * slots + slot_ref[0, p]).astype(F32)
-        code = jnp.where(row // part == p, here, code)
-    tail = jnp.where(lane < tail.shape[1] // 2, tail, code).astype(BF)
-    for i in range(out_ref.shape[0]):
-        out_ref[i, :, :lat] = key_ref[:, :lat]
-        out_ref[i, :, lat:] = tail
-
-
 def blocks(shapes):
     at = 0
     for w, shape in enumerate(shapes):
@@ -86,16 +72,28 @@
     return ref.at[:, pl.ds(c, 128)]
 
 
-def key_kernel(base_ref, x_ref, gain_ref, *refs, lat, part, page_len, shapes):
-    ins, out_ref, packed = refs[: len(shapes)], refs[-2], refs[-1]
-    x = x_ref[...].astype(F32)
-    latent, rot = x[:, :lat], x[:, lat:]
+def key_kernel(
+    where_ref, owner_ref, slot_ref, lat_ref, rope_ref, gain_ref, *refs, slots, page_len, shapes
+):
+    ins, out_ref, page_ref, packed = refs[: len(shapes)], refs[-3], refs[-2], refs[-1]
+    pages, part, lat = lat_ref.shape[1:]
+    latent = jnp.concatenate([lat_ref[0, p].astype(F32) for p in range(pages)], 0)
+    rot = jnp.concatenate([rope_ref[0, p].astype(F32) for p in range(pages)], 0)
     norm = lax.rsqrt(jnp.mean(latent * latent, -1, keepdims=True) + 1e-06)
-    out_ref[:, :lat] = (latent * norm * gain_ref[...]).astype(BF)
+    normed = (latent * norm * gain_ref[...]).astype(BF)
     row = lax.broadcasted_iota(jnp.int32, rot.shape, 0)
-    cosine, sine = rope_factors(base_ref[0] + row // part * page_len + row % part)
+    cosine, sine = rope_factors(where_ref[0] + row // part * page_len + row % part)
     turned = rot * cosine + swap_halves(rot) * sine
+    code = jnp.zeros_like(turned)
+    for p in range(pages):
+        here = (owner_ref[0, p] * slots + slot_ref[0, p]).astype(F32)
+        code = jnp.where(row // part == p, here, code)
+    out_ref[:, :lat] = normed
     out_ref[:, lat:] = jnp.concatenate([turned, jnp.zeros_like(turned)], -1).astype(BF)
+    tail = jnp.concatenate([turned, code], -1).astype(BF)
+    for i in range(page_ref.shape[0]):
+        page_ref[i, :, :lat] = normed
+        page_ref[i, :, lat:] = tail
     for at, w, lead, c, n in blocks(shapes):
         src = ins[w]
         if len(src.shape) == 3:
@@ -143,9 +141,9 @@
     place = chain * (chips * 2 * qrows) + query_where(idx, z, core, qrows, chips)
     cosine, sine = rope_factors(place)
     head = 0
-    for load in loads:
-        load.wait()
     for side in range(2):
+        for load in loads[2:] if side else loads[:2]:
+            load.wait()
         ak = ak_ref.at[side]
         q = jnp.dot(x, wq_ref[side], preferred_element_type=F32).astype(BF)
         for h in range(ak.shape[0]):
@@ -246,9 +244,6 @@
     def room(mib):
         return pltpu.CompilerParams(vmem_limit_bytes=mib * 1024 * 1024)
 
-    raw = jnp.concatenate(
-        [latent_rows[0].reshape(pages * part, lat), rope_keys[0].reshape(pages * part, rope)], -1
-    )
     rows = qrows * nzh * nzl
     kw = lat + 2 * rope
     heads = 2 * heads_here
@@ -256,21 +251,20 @@
     where = jnp.stack([chain, z, core]).astype(jnp.int32)
     weights = (query_up, absorb_key, absorb_value, out_proj)
     shapes = tuple(w.shape for w in weights)
-    keys, packed = pl.pallas_call(
-        functools.partial(
-            key_kernel, lat=lat, part=part, page_len=part * tp_count, shapes=shapes
-        ),
+    keys, page, packed = pl.pallas_call(
+        functools.partial(key_kernel, slots=slots, page_len=part * tp_count, shapes=shapes),
         out_shape=(
             jax.ShapeDtypeStruct((pages * part, kw), BF),
+            jax.ShapeDtypeStruct((lax.axis_size("dec"), pages * part, kw), BF),
             jax.ShapeDtypeStruct((packed_rows(shapes), 128), BF),
         ),
-        in_specs=[smem] + [vm] * 6,
-        out_specs=(vm, vm),
+        in_specs=[smem] * 3 + [vm] * 7,
+        out_specs=(vm, vm, vm),
         compiler_params=room(56),
         name="keys",
     )(
-        (chain * block_len + tp_index * part).astype(jnp.int32)[None], raw, latent_gain[None],
-        *weights,
+        (chain * block_len + tp_index * part).astype(jnp.int32)[None], page_owner, page_slot,
+        latent_rows, rope_keys, latent_gain[None], *weights,
     )
     packed = swap_core(packed)
 
@@ -336,28 +330,18 @@
 
     far = near(2, up, down).astype(BF)
     far, up, down = lax.optimization_barrier((far, up, down))
-    left = shift_z(far[:, :cut], nzl).astype(F32)
-    right = shift_z(far[:, cut:], -nzl).astype(F32)
+    left, right = lax.optimization_barrier((shift_z(far[:, :cut], nzl), shift_z(far[:, cut:], -nzl)))
     ahead = near(1, up, down) + up2[qrows:].astype(F32)
-    ahead = jnp.concatenate([ahead[:, :cut] + left, ahead[:, cut:]], -1)
+    ahead = jnp.concatenate([ahead[:, :cut] + left.astype(F32), ahead[:, cut:]], -1)
     ahead = shift_z(ahead.astype(BF), nzl)
     behind = near(-1, up, down) + down2[:qrows].astype(F32)
-    behind = jnp.concatenate([behind[:, :cut], behind[:, cut:] + right], -1)
+    behind = jnp.concatenate([behind[:, :cut], behind[:, cut:] + right.astype(F32)], -1)
     behind = shift_z(behind.astype(BF), -nzl)
     total = near(0, up, down) + up2[:qrows].astype(F32) + down2[qrows:].astype(F32)
     total = total + ahead.astype(F32) + behind.astype(F32)
     layer_output = total.astype(BF)[None]
 
-    page = lax.optimization_barrier((keys, sums[0]))[0]
-    page = pl.pallas_call(
-        functools.partial(page_kernel, lat=lat, part=part, slots=slots),
-        out_shape=jax.ShapeDtypeStruct((lax.axis_size("dec"),) + keys.shape, BF),
-        in_specs=[smem, smem, vm],
-        out_specs=vm,
-        compiler_params=room(4),
-        cost_estimate=pl.CostEstimate(flops=10**10, bytes_accessed=400000, transcendentals=0),
-        name="pages",
-    )(page_owner, page_slot, page)
+    page = lax.optimization_barrier((page, ahead))[0]
     page = lax.all_to_all(page, "dec", 0, 0, tiled=True).reshape(-1, pages, part, kw)
     came = page[:, :, 0, lat + rope].reshape(-1).astype(jnp.int32)
     take = (came[None, :] == dec * slots + jnp.arange(slots, dtype=jnp.int32)[:, None]).astype(BF)

time: 158 us -> 156 us (0.987)
  Pallas kernels: 19.6 us -> 17.6 us
    all_to_all x1, waiting for transfers between devices: 0.01 us -> 4.67 us  [local(): lax.all_to_all(page, 'dec', 0, 0, tiled=True).reshape(-1, pages, part, kw)]
    ppermute x8, waiting for transfers between devices: 16.2 us -> 13 us  [shift_z(): return lax.ppermute(x, Z, [(i, (i + step) % n) for i in range(n)])]
    pallas_call x2 -> x1, Pallas kernels: 5.63 us -> 4.47 us  [local(): pl.pallas_call(functools.partial(key_kernel, slots=slots, page_len=part *...]
  transfers between devices with their start and end apart: 12 -> 12, of which waited for: 7 -> 7; matrix products, arithmetic and copies ran while one was open for 2% -> 1% of each run, Pallas kernels for 2% -> 2%
where the time goes in v13:
time: 156 us
  blocking collectives  68 us (44%)
  starting transfers between devices  47.4 us (30%)
  waiting for transfers between devices  17.7 us (11%)
  Pallas kernels  17.6 us (11%)
  local copies, waits for them, and re-layouts  2.85 us (2%)
    all_gather x1, blocking collectives, local(): own = lax.all_gather(keys, Z, axis=0, tiled=True)  37.4 us
    ppermute x8, starting transfers between devices, shift_z(): return lax.ppermute(x, Z, [(i, (i + step) % n) for i in range(n)])  34.5 us
    all_gather x1, blocking collectives, local(): qg = lax.all_gather(held, Z, axis=0, tiled=True)  30.6 us
    ppermute x8, waiting for transfers between devices, shift_z(): return lax.ppermute(x, Z, [(i, (i + step) % n) for i in range(n)])  13 us
    pallas_call x1, Pallas kernels, local(): pl.pallas_call(functools.partial(attend_kernel, rows=rows, lat=lat, scale...  9.8 us
    all_to_all x1, starting transfers between devices, spread(): lax.all_to_all(jnp.broadcast_to(x[None], (n,) + x.shape), axis, 0, 0, til...  4.82 us
    all_to_all x1, waiting for transfers between devices, local(): lax.all_to_all(page, 'dec', 0, 0, tiled=True).reshape(-1, pages, part, kw)  4.67 us
    pallas_call x1, Pallas kernels, local(): pl.pallas_call(functools.partial(key_kernel, slots=slots, page_len=part *...  4.47 us
  transfers between devices with their start and end apart: 12, of which 7 were waited for; matrix products, arithmetic and copies ran while one was open for 1% of the time, Pallas kernels for 2%

profile of v13, /device:TPU:24, one launch (start us, length us, event | category | flops | bytes accessed | tf_op | source)
XLA Modules:
  0.0 155.6 jit_solution(12431597652302975752)
XLA Ops:
  0.6 4.5 %keys.1 = (bf16[16,640]{1,0:T(8,128)(2,1)}, bf16[4,16,640]{2,1,0:T(8,128)(2,1)}, bf16[13824,128]{1,0:T(8,128)(2,1)}) custom-call(s32[1]{0:T(128)} %bitcast.4.where_ref, s32[1,4]{1,0:T(1,128)} %owner_ref.1, s32[1,4]{1,0:T(1,128)} %slot_ref.1, bf16[1,4,4,512]{3,2,1,0:T(4,128)(2,1)} %lat_ref.1, bf16[1,4,4,64]{3,2,1,0:T(4,128)(2,1)} %rope_ref.1, ...), custom_call_target="tpu_custom_call" | custom-call | tf_op jit(solution)/shard_map/keys/pallas_call | solution.py:254
  5.1 1.9 %collective-permute-start = (bf16[13824,128]{1,0:T(8,128)(2,1)}, bf16[13824,128]{1,0:T(8,128)(2,1)}, u32[]{:S(2)}, u32[]{:S(2)}) collective-permute-start(bf16[13824,128]{1,0:T(8,128)(2,1)} %get-tuple-element.23), channel_id=1, source_target_pairs={{0,4},{4,0},{1,5},{5,1},{2,6},{6,2},{3,7},{7,3},{8,12},{12,8},{9,1... | collective-permute-start | bytes 10616840 | tf_op jit(solution)/shard_map/ppermute | solution.py:31
  7.0 37.4 %all_gather.6 = bf16[256,640]{1,0:T(8,128)(2,1)S(1)} all-gather(bf16[16,640]{1,0:T(8,128)(2,1)} %get-tuple-element.20), channel_id=1, replica_groups=mesh['chain'=4,'zh'=4,'zl'=4,'core'=2,'dec'=4] {'zh','zl'}, dimensions={0}, use_global_device_ids=true | all-gather | bytes 348160 | tf_op jit(solution)/shard_map/all_gather | solution.py:271
  44.4 1.2 broadcast_in_dim.25
  45.7 4.8 %all-to-all-start = ((bf16[4,256,640]{2,1,0:T(8,128)(2,1)}), bf16[4,256,640]{2,1,0:T(8,128)(2,1)S(1)}, u32[]{:S(2)}, u32[]{:S(2)}) async-start(bf16[4,256,640]{2,1,0:T(8,128)(2,1)} %broadcast_in_dim.25), calls=%async_computation | async-start | bytes 2621440 | tf_op jit(solution)/shard_map/all_to_all | solution.py:36
  50.5 30.6 %all_gather.7.g_ref = bf16[256,1536]{1,0:T(8,128)(2,1)S(1)} all-gather(bf16[16,1536]{1,0:T(8,128)(2,1)} %bitcast.20), channel_id=1, replica_groups=mesh['chain'=4,'zh'=4,'zl'=4,'core'=2,'dec'=4] {'zh','zl'}, dimensions={0}, use_global_device_ids=true | all-gather | bytes 835584 | tf_op jit(solution)/shard_map/all_gather | solution.py:274
  81.1 1.9 %collective-permute-start.1 = (bf16[1024,640]{1,0:T(8,128)(2,1)S(1)}, bf16[1024,640]{1,0:T(8,128)(2,1)S(1)}, u32[]{:S(2)}, u32[]{:S(2)}) collective-permute-start(bf16[1024,640]{1,0:T(8,128)(2,1)S(1)} %bitcast.18), channel_id=1, source_target_pairs={{0,4},{4,0},{1,5},{5,1},{2,6},{6,2},{3,7},{7,3},{8,12},{12,8},{9,1... | collective-permute-start | bytes 3932168 | tf_op jit(solution)/shard_map/ppermute | solution.py:31
  83.1 3.3 %queries.1.q_ref = bf16[1024,640]{1,0:T(8,128)(2,1)S(1)} custom-call(s32[3]{0:T(128)S(1)} %pad_add_fusion.where_ref, bf16[256,1536]{1,0:T(8,128)(2,1)S(1)} %all_gather.7.g_ref, bf16[1536,384]{1,0:T(8,128)(2,1)S(1)} %copy-done, bf16[2,128,512]{2,1,0:T(8,128)(2,1)S(1)} %copy-done.2, bf16[13824,128]{1,0:T(8,128)(2,1)} %collective-permute-done.packed), custom_call_target="tpu_custom_call" | custom-call | flops 738197504 | bytes 6000000 | tf_op jit(solution)/shard_map/queries/pallas_call | solution.py:278
  86.4 9.8 %attend.1 = (bf16[64,3584]{1,0:T(8,128)(2,1)S(1)}, bf16[64,3584]{1,0:T(8,128)(2,1)S(1)}, bf16[64,3584]{1,0:T(8,128)(2,1)S(1)}, bf16[32,3584]{1,0:T(8,128)(2,1)S(1)}, bf16[32,3584]{1,0:T(8,128)(2,1)S(1)}) custom-call(s32[3]{0:T(128)S(1)} %pad_add_fusion.where_ref, bf16[1024,640]{1,0:T(8,128)(2,1)S(1)} %queries.1.q_ref, bf16[1024,640]{1,0:T(8,128)(2,1)S(1)} %bitcast.19, ...), custom_call_target="tpu_custom_call" | custom-call | flops 4294967296 | bytes 9000000 | tf_op jit(solution)/shard_map/attend/pallas_call | solution.py:298
  96.2 3.8 %collective-permute-start.2 = (bf16[64,3584]{1,0:T(8,128)(2,1)S(1)}, bf16[64,3584]{1,0:T(8,128)(2,1)S(1)}, u32[]{:S(2)}, u32[]{:S(2)}) collective-permute-start(bf16[64,3584]{1,0:T(8,128)(2,1)S(1)} %get-tuple-element.26), channel_id=1, source_target_pairs={{0,8},{8,16},{16,24},{24,32},{32,40},{40,48},{48,56},{56,64},{64,7... | collective-permute-start | bytes 1376264 | tf_op jit(solution)/shard_map/ppermute | solution.py:27
  100.0 3.3 %collective-permute-start.3 = (bf16[64,3584]{1,0:T(8,128)(2,1)S(1)}, bf16[64,3584]{1,0:T(8,128)(2,1)S(1)}, u32[]{:S(2)}, u32[]{:S(2)}) collective-permute-start(bf16[64,3584]{1,0:T(8,128)(2,1)S(1)} %get-tuple-element.27), channel_id=1, source_target_pairs={{0,120},{8,0},{16,8},{24,16},{32,24},{40,32},{48,40},{56,48},{64,5... | collective-permute-start | bytes 1376264 | tf_op jit(solution)/shard_map/ppermute | solution.py:27
  103.3 2.0 %collective-permute-start.4 = (bf16[32,3584]{1,0:T(8,128)(2,1)S(1)}, bf16[32,3584]{1,0:T(8,128)(2,1)S(1)}, u32[]{:S(2)}, u32[]{:S(2)}) collective-permute-start(bf16[32,3584]{1,0:T(8,128)(2,1)S(1)} %get-tuple-element.30), channel_id=1, source_target_pairs={{0,16},{8,24},{16,32},{24,40},{32,48},{40,56},{48,64},{56,72},{64,... | collective-permute-start | bytes 688136 | tf_op jit(solution)/shard_map/ppermute | solution.py:27
  105.3 6.0 %collective-permute-start.5 = (bf16[32,3584]{1,0:T(8,128)(2,1)S(1)}, bf16[32,3584]{1,0:T(8,128)(2,1)S(1)}, u32[]{:S(2)}, u32[]{:S(2)}) collective-permute-start(bf16[32,3584]{1,0:T(8,128)(2,1)S(1)} %get-tuple-element.31), channel_id=1, source_target_pairs={{0,112},{8,120},{16,0},{24,8},{32,16},{40,24},{48,32},{56,40},{64,... | collective-permute-start | bytes 688136 | tf_op jit(solution)/shard_map/ppermute | solution.py:27
  111.3 2.4 %collective-permute-done.2 = bf16[64,3584]{1,0:T(8,128)(2,1)S(1)} collective-permute-done((bf16[64,3584]{1,0:T(8,128)(2,1)S(1)}, bf16[64,3584]{1,0:T(8,128)(2,1)S(1)}, u32[]{:S(2)}, u32[]{:S(2)}) %collective-permute-start.2) | collective-permute-done | bytes 458784 | tf_op jit(solution)/shard_map/ppermute | solution.py:27
  113.7 1.8 %collective-permute-done.3 = bf16[64,3584]{1,0:T(8,128)(2,1)S(1)} collective-permute-done((bf16[64,3584]{1,0:T(8,128)(2,1)S(1)}, bf16[64,3584]{1,0:T(8,128)(2,1)S(1)}, u32[]{:S(2)}, u32[]{:S(2)}) %collective-permute-start.3) | collective-permute-done | bytes 458784 | tf_op jit(solution)/shard_map/ppermute | solution.py:27
  115.5 4.0 %collective-permute-start.6 = (bf16[16,1792]{1,0:T(8,128)(2,1)S(1)}, bf16[16,1792]{1,0:T(8,128)(2,1)S(1)}, u32[]{:S(2)}, u32[]{:S(2)}) collective-permute-start(bf16[16,1792]{1,0:T(8,128)(2,1)S(1)} %get-tuple-element.43), channel_id=1, source_target_pairs={{0,32},{8,40},{16,48},{24,56},{32,64},{40,72},{48,80},{56,88},{64,... | collective-permute-start | bytes 172040 | tf_op jit(solution)/shard_map/ppermute | solution.py:27
  119.5 5.8 %collective-permute-start.7 = (bf16[16,1792]{1,0:T(8,128)(2,1)S(1)}, bf16[16,1792]{1,0:T(8,128)(2,1)S(1)}, u32[]{:S(2)}, u32[]{:S(2)}) collective-permute-start(bf16[16,1792]{1,0:T(8,128)(2,1)S(1)} %get-tuple-element.42), channel_id=1, source_target_pairs={{0,96},{8,104},{16,112},{24,120},{32,0},{40,8},{48,16},{56,24},{64... | collective-permute-start | bytes 172040 | tf_op jit(solution)/shard_map/ppermute | solution.py:27
  125.3 0.1 convert_add_fusion.1
  125.5 2.6 %collective-permute-done.6 = bf16[16,1792]{1,0:T(8,128)(2,1)S(1)} collective-permute-done((bf16[16,1792]{1,0:T(8,128)(2,1)S(1)}, bf16[16,1792]{1,0:T(8,128)(2,1)S(1)}, u32[]{:S(2)}, u32[]{:S(2)}) %collective-permute-start.6) | collective-permute-done | bytes 57376 | tf_op jit(solution)/shard_map/ppermute | solution.py:27
  128.0 2.1 %collective-permute-done.7 = bf16[16,1792]{1,0:T(8,128)(2,1)S(1)} collective-permute-done((bf16[16,1792]{1,0:T(8,128)(2,1)S(1)}, bf16[16,1792]{1,0:T(8,128)(2,1)S(1)}, u32[]{:S(2)}, u32[]{:S(2)}) %collective-permute-start.7) | collective-permute-done | bytes 57376 | tf_op jit(solution)/shard_map/ppermute | solution.py:27
  130.2 6.2 %collective-permute-start.8 = (bf16[16,3584]{1,0:T(8,128)(2,1)S(1)}, bf16[16,3584]{1,0:T(8,128)(2,1)S(1)}, u32[]{:S(2)}, u32[]{:S(2)}) collective-permute-start(bf16[16,3584]{1,0:T(8,128)(2,1)S(1)} %pad_maximum_fusion), channel_id=1, source_target_pairs={{0,32},{8,40},{16,48},{24,56},{32,64},{40,72},{48,80},{56,88},{64,... | collective-permute-start | bytes 344072 | tf_op jit(solution)/shard_map/ppermute | solution.py:27
  136.5 3.5 %collective-permute-start.9 = (bf16[16,3584]{1,0:T(8,128)(2,1)S(1)}, bf16[16,3584]{1,0:T(8,128)(2,1)S(1)}, u32[]{:S(2)}, u32[]{:S(2)}) collective-permute-start(bf16[16,3584]{1,0:T(8,128)(2,1)S(1)} %pad_maximum_fusion.1), channel_id=1, source_target_pairs={{0,96},{8,104},{16,112},{24,120},{32,0},{40,8},{48,16},{56,24},{64... | collective-permute-start | bytes 344072 | tf_op jit(solution)/shard_map/ppermute | solution.py:27
  140.0 3.8 %collective-permute-done.8 = bf16[16,3584]{1,0:T(8,128)(2,1)S(1)} collective-permute-done((bf16[16,3584]{1,0:T(8,128)(2,1)S(1)}, bf16[16,3584]{1,0:T(8,128)(2,1)S(1)}, u32[]{:S(2)}, u32[]{:S(2)}) %collective-permute-start.8) | collective-permute-done | bytes 114720 | tf_op jit(solution)/shard_map/ppermute | solution.py:27
  143.8 4.2 %all-to-all-start.1 = ((bf16[4,16,640]{2,1,0:T(8,128)(2,1)}), bf16[4,16,640]{2,1,0:T(8,128)(2,1)S(1)}, u32[]{:S(2)}, u32[]{:S(2)}) async-start(bf16[4,16,640]{2,1,0:T(8,128)(2,1)} %get-tuple-element.36), calls=%async_computation.1 | async-start | bytes 163840 | tf_op jit(solution)/shard_map/all_to_all | solution.py:345
  148.1 0.3 collective-permute-done.9
  148.3 0.8 fusion
  149.1 4.7 %all-to-all-done.1 = bf16[4,16,640]{2,1,0:T(8,128)(2,1)S(1)} async-done(((bf16[4,16,640]{2,1,0:T(8,128)(2,1)}), bf16[4,16,640]{2,1,0:T(8,128)(2,1)S(1)}, u32[]{:S(2)}, u32[]{:S(2)}) %all-to-all-start.1) | async-done | bytes 81952 | tf_op jit(solution)/shard_map/all_to_all | solution.py:345
  153.9 0.1 copy.17
  154.0 0.1 reshape.27
  154.1 0.2 convolution_convert_fusion
  154.3 0.6 copy.15
  155.0 0.6 copy.16
  (29 shorter events, 0.4 us)
Async XLA Ops:
  5.1 78.0 %collective-permute-start = (bf16[13824,128]{1,0:T(8,128)(2,1)}, bf16[13824,128]{1,0:T(8,128)(2,1)}, u32[]{:S(2)}, u32[]{:S(2)}) collective-permute-start(bf16[13824,128]{1,0:T(8,128)(2,1)} %get-tuple-element.23), channel_id=1, source_target_pairs={{0,4},{4,0},{1,5},{5,1},{2,6},{6,2},{3,7},{7,3},{8,12},{12,8},{9,1... | collective-permute-start | bytes 10616840 | tf_op jit(solution)/shard_map/ppermute | solution.py:31
  45.7 37.4 %copy-start = (bf16[1536,384]{1,0:T(8,128)(2,1)S(1)}, bf16[1536,384]{1,0:T(8,128)(2,1)}, u32[]{:S(2)}) copy-start(bf16[1536,384]{1,0:T(8,128)(2,1)} %wq0.1) | copy-start | bytes 3538948
  45.7 37.4 %copy-start.2 = (bf16[2,128,512]{2,1,0:T(8,128)(2,1)S(1)}, bf16[2,128,512]{2,1,0:T(8,128)(2,1)}, u32[]{:S(2)}) copy-start(bf16[2,128,512]{2,1,0:T(8,128)(2,1)} %ak0.1) | copy-start | bytes 786436
  45.7 35.4 %all-to-all-start = ((bf16[4,256,640]{2,1,0:T(8,128)(2,1)}), bf16[4,256,640]{2,1,0:T(8,128)(2,1)S(1)}, u32[]{:S(2)}, u32[]{:S(2)}) async-start(bf16[4,256,640]{2,1,0:T(8,128)(2,1)} %broadcast_in_dim.25), calls=%async_computation | async-start | bytes 2621440 | tf_op jit(solution)/shard_map/all_to_all | solution.py:36
  81.1 5.3 %collective-permute-start.1 = (bf16[1024,640]{1,0:T(8,128)(2,1)S(1)}, bf16[1024,640]{1,0:T(8,128)(2,1)S(1)}, u32[]{:S(2)}, u32[]{:S(2)}) collective-permute-start(bf16[1024,640]{1,0:T(8,128)(2,1)S(1)} %bitcast.18), channel_id=1, source_target_pairs={{0,4},{4,0},{1,5},{5,1},{2,6},{6,2},{3,7},{7,3},{8,12},{12,8},{9,1... | collective-permute-start | bytes 3932168 | tf_op jit(solution)/shard_map/ppermute | solution.py:31
  83.1 3.4 %copy-start.1 = (bf16[256,3584]{1,0:T(8,128)(2,1)S(1)}, bf16[256,3584]{1,0:T(8,128)(2,1)}, u32[]{:S(2)}) copy-start(bf16[256,3584]{1,0:T(8,128)(2,1)} %op0.1) | copy-start | bytes 5505028
  83.1 3.4 %copy-start.3 = (bf16[2,512,128]{2,1,0:T(8,128)(2,1)S(1)}, bf16[2,512,128]{2,1,0:T(8,128)(2,1)}, u32[]{:S(2)}) copy-start(bf16[2,512,128]{2,1,0:T(8,128)(2,1)} %av0.1) | copy-start | bytes 786436
  96.2 17.5 %collective-permute-start.2 = (bf16[64,3584]{1,0:T(8,128)(2,1)S(1)}, bf16[64,3584]{1,0:T(8,128)(2,1)S(1)}, u32[]{:S(2)}, u32[]{:S(2)}) collective-permute-start(bf16[64,3584]{1,0:T(8,128)(2,1)S(1)} %get-tuple-element.26), channel_id=1, source_target_pairs={{0,8},{8,16},{16,24},{24,32},{32,40},{40,48},{48,56},{56,64},{64,7... | collective-permute-start | bytes 1376264 | tf_op jit(solution)/shard_map/ppermute | solution.py:27
  100.0 15.5 %collective-permute-start.3 = (bf16[64,3584]{1,0:T(8,128)(2,1)S(1)}, bf16[64,3584]{1,0:T(8,128)(2,1)S(1)}, u32[]{:S(2)}, u32[]{:S(2)}) collective-permute-start(bf16[64,3584]{1,0:T(8,128)(2,1)S(1)} %get-tuple-element.27), channel_id=1, source_target_pairs={{0,120},{8,0},{16,8},{24,16},{32,24},{40,32},{48,40},{56,48},{64,5... | collective-permute-start | bytes 1376264 | tf_op jit(solution)/shard_map/ppermute | solution.py:27
  103.3 22.0 %collective-permute-start.4 = (bf16[32,3584]{1,0:T(8,128)(2,1)S(1)}, bf16[32,3584]{1,0:T(8,128)(2,1)S(1)}, u32[]{:S(2)}, u32[]{:S(2)}) collective-permute-start(bf16[32,3584]{1,0:T(8,128)(2,1)S(1)} %get-tuple-element.30), channel_id=1, source_target_pairs={{0,16},{8,24},{16,32},{24,40},{32,48},{40,56},{48,64},{56,72},{64,... | collective-permute-start | bytes 688136 | tf_op jit(solution)/shard_map/ppermute | solution.py:27
  105.3 20.0 %collective-permute-start.5 = (bf16[32,3584]{1,0:T(8,128)(2,1)S(1)}, bf16[32,3584]{1,0:T(8,128)(2,1)S(1)}, u32[]{:S(2)}, u32[]{:S(2)}) collective-permute-start(bf16[32,3584]{1,0:T(8,128)(2,1)S(1)} %get-tuple-element.31), channel_id=1, source_target_pairs={{0,112},{8,120},{16,0},{24,8},{32,16},{40,24},{48,32},{56,40},{64,... | collective-permute-start | bytes 688136 | tf_op jit(solution)/shard_map/ppermute | solution.py:27
  115.5 12.5 %collective-permute-start.6 = (bf16[16,1792]{1,0:T(8,128)(2,1)S(1)}, bf16[16,1792]{1,0:T(8,128)(2,1)S(1)}, u32[]{:S(2)}, u32[]{:S(2)}) collective-permute-start(bf16[16,1792]{1,0:T(8,128)(2,1)S(1)} %get-tuple-element.43), channel_id=1, source_target_pairs={{0,32},{8,40},{16,48},{24,56},{32,64},{40,72},{48,80},{56,88},{64,... | collective-permute-start | bytes 172040 | tf_op jit(solution)/shard_map/ppermute | solution.py:27
  119.5 10.6 %collective-permute-start.7 = (bf16[16,1792]{1,0:T(8,128)(2,1)S(1)}, bf16[16,1792]{1,0:T(8,128)(2,1)S(1)}, u32[]{:S(2)}, u32[]{:S(2)}) collective-permute-start(bf16[16,1792]{1,0:T(8,128)(2,1)S(1)} %get-tuple-element.42), channel_id=1, source_target_pairs={{0,96},{8,104},{16,112},{24,120},{32,0},{40,8},{48,16},{56,24},{64... | collective-permute-start | bytes 172040 | tf_op jit(solution)/shard_map/ppermute | solution.py:27
  130.2 13.6 %collective-permute-start.8 = (bf16[16,3584]{1,0:T(8,128)(2,1)S(1)}, bf16[16,3584]{1,0:T(8,128)(2,1)S(1)}, u32[]{:S(2)}, u32[]{:S(2)}) collective-permute-start(bf16[16,3584]{1,0:T(8,128)(2,1)S(1)} %pad_maximum_fusion), channel_id=1, source_target_pairs={{0,32},{8,40},{16,48},{24,56},{32,64},{40,72},{48,80},{56,88},{64,... | collective-permute-start | bytes 344072 | tf_op jit(solution)/shard_map/ppermute | solution.py:27
  136.5 11.8 %collective-permute-start.9 = (bf16[16,3584]{1,0:T(8,128)(2,1)S(1)}, bf16[16,3584]{1,0:T(8,128)(2,1)S(1)}, u32[]{:S(2)}, u32[]{:S(2)}) collective-permute-start(bf16[16,3584]{1,0:T(8,128)(2,1)S(1)} %pad_maximum_fusion.1), channel_id=1, source_target_pairs={{0,96},{8,104},{16,112},{24,120},{32,0},{40,8},{48,16},{56,24},{64... | collective-permute-start | bytes 344072 | tf_op jit(solution)/shard_map/ppermute | solution.py:27
  143.8 9.9 %all-to-all-start.1 = ((bf16[4,16,640]{2,1,0:T(8,128)(2,1)}), bf16[4,16,640]{2,1,0:T(8,128)(2,1)S(1)}, u32[]{:S(2)}, u32[]{:S(2)}) async-start(bf16[4,16,640]{2,1,0:T(8,128)(2,1)} %get-tuple-element.36), calls=%async_computation.1 | async-start | bytes 163840 | tf_op jit(solution)/shard_map/all_to_all | solution.py:345

commit v14 on v13

--- a/solution.py
+++ b/solution.py
@@ -341,7 +341,7 @@
     total = total + ahead.astype(F32) + behind.astype(F32)
     layer_output = total.astype(BF)[None]
 
-    page = lax.optimization_barrier((page, ahead))[0]
+    page = lax.optimization_barrier((page, down2))[0]
     page = lax.all_to_all(page, "dec", 0, 0, tiled=True).reshape(-1, pages, part, kw)
     came = page[:, :, 0, lat + rope].reshape(-1).astype(jnp.int32)
     take = (came[None, :] == dec * slots + jnp.arange(slots, dtype=jnp.int32)[:, None]).astype(BF)

time: 156 us -> 160 us (1.026); the launches traced: 156 us -> 158 us
  waiting for transfers between devices: 17.7 us -> 21.6 us
  starting transfers between devices: 47.4 us -> 45.8 us
    ppermute x8, waiting for transfers between devices: 13 us -> 18.9 us  [shift_z(): return lax.ppermute(x, Z, [(i, (i + step) % n) for i in range(n)])]
    all_to_all x1, waiting for transfers between devices: 4.67 us -> 2.64 us  [local(): lax.all_to_all(page, 'dec', 0, 0, tiled=True).reshape(-1, pages, part, kw)]
    ppermute x8, starting transfers between devices: 34.5 us -> 32.9 us  [shift_z(): return lax.ppermute(x, Z, [(i, (i + step) % n) for i in range(n)])]
  transfers between devices with their start and end apart: 12 -> 12, of which waited for: 7 -> 7; matrix products, arithmetic and copies ran while one was open for 1% -> 2% of each run, Pallas kernels for 2% -> 2%
where the time goes in v14:
time: 160 us; the launch traced here: 158 us
  blocking collectives  68 us (42%)
  starting transfers between devices  45.8 us (29%)
  waiting for transfers between devices  21.6 us (14%)
  Pallas kernels  17.6 us (11%)
  local copies, waits for them, and re-layouts  2.85 us (2%)
    all_gather x1, blocking collectives, local(): own = lax.all_gather(keys, Z, axis=0, tiled=True)  37.4 us
    ppermute x8, starting transfers between devices, shift_z(): return lax.ppermute(x, Z, [(i, (i + step) % n) for i in range(n)])  32.9 us
    all_gather x1, blocking collectives, local(): qg = lax.all_gather(held, Z, axis=0, tiled=True)  30.6 us
    ppermute x8, waiting for transfers between devices, shift_z(): return lax.ppermute(x, Z, [(i, (i + step) % n) for i in range(n)])  18.9 us
    pallas_call x1, Pallas kernels, local(): pl.pallas_call(functools.partial(attend_kernel, rows=rows, lat=lat, scale...  9.8 us
    all_to_all x1, starting transfers between devices, spread(): lax.all_to_all(jnp.broadcast_to(x[None], (n,) + x.shape), axis, 0, 0, til...  4.82 us
    pallas_call x1, Pallas kernels, local(): pl.pallas_call(functools.partial(key_kernel, slots=slots, page_len=part *...  4.47 us
    all_to_all x1, starting transfers between devices, local(): lax.all_to_all(page, 'dec', 0, 0, tiled=True).reshape(-1, pages, part, kw)  4.3 us
  transfers between devices with their start and end apart: 12, of which 7 were waited for; matrix products, arithmetic and copies ran while one was open for 2% of the time, Pallas kernels for 2%

profile of v14, /device:TPU:24, one launch (start us, length us, event | category | flops | bytes accessed | tf_op | source)
XLA Modules:
  0.0 157.9 jit_solution(13949273645080347347)
XLA Ops:
  0.6 4.5 %keys.1 = (bf16[16,640]{1,0:T(8,128)(2,1)}, bf16[4,16,640]{2,1,0:T(8,128)(2,1)}, bf16[13824,128]{1,0:T(8,128)(2,1)}) custom-call(s32[1]{0:T(128)} %bitcast.4.where_ref, s32[1,4]{1,0:T(1,128)} %owner_ref.1, s32[1,4]{1,0:T(1,128)} %slot_ref.1, bf16[1,4,4,512]{3,2,1,0:T(4,128)(2,1)} %lat_ref.1, bf16[1,4,4,64]{3,2,1,0:T(4,128)(2,1)} %rope_ref.1, ...), custom_call_target="tpu_custom_call" | custom-call | tf_op jit(solution)/shard_map/keys/pallas_call | solution.py:254
  5.1 1.9 %collective-permute-start = (bf16[13824,128]{1,0:T(8,128)(2,1)}, bf16[13824,128]{1,0:T(8,128)(2,1)}, u32[]{:S(2)}, u32[]{:S(2)}) collective-permute-start(bf16[13824,128]{1,0:T(8,128)(2,1)} %get-tuple-element.23), channel_id=1, source_target_pairs={{0,4},{4,0},{1,5},{5,1},{2,6},{6,2},{3,7},{7,3},{8,12},{12,8},{9,1... | collective-permute-start | bytes 10616840 | tf_op jit(solution)/shard_map/ppermute | solution.py:31
  7.0 37.4 %all_gather.6 = bf16[256,640]{1,0:T(8,128)(2,1)S(1)} all-gather(bf16[16,640]{1,0:T(8,128)(2,1)} %get-tuple-element.20), channel_id=1, replica_groups=mesh['chain'=4,'zh'=4,'zl'=4,'core'=2,'dec'=4] {'zh','zl'}, dimensions={0}, use_global_device_ids=true | all-gather | bytes 348160 | tf_op jit(solution)/shard_map/all_gather | solution.py:271
  44.4 1.2 broadcast_in_dim.25
  45.7 4.8 %all-to-all-start = ((bf16[4,256,640]{2,1,0:T(8,128)(2,1)}), bf16[4,256,640]{2,1,0:T(8,128)(2,1)S(1)}, u32[]{:S(2)}, u32[]{:S(2)}) async-start(bf16[4,256,640]{2,1,0:T(8,128)(2,1)} %broadcast_in_dim.25), calls=%async_computation | async-start | bytes 2621440 | tf_op jit(solution)/shard_map/all_to_all | solution.py:36
  50.5 30.6 %all_gather.7.g_ref = bf16[256,1536]{1,0:T(8,128)(2,1)S(1)} all-gather(bf16[16,1536]{1,0:T(8,128)(2,1)} %bitcast.20), channel_id=1, replica_groups=mesh['chain'=4,'zh'=4,'zl'=4,'core'=2,'dec'=4] {'zh','zl'}, dimensions={0}, use_global_device_ids=true | all-gather | bytes 835584 | tf_op jit(solution)/shard_map/all_gather | solution.py:274
  81.1 1.9 %collective-permute-start.1 = (bf16[1024,640]{1,0:T(8,128)(2,1)S(1)}, bf16[1024,640]{1,0:T(8,128)(2,1)S(1)}, u32[]{:S(2)}, u32[]{:S(2)}) collective-permute-start(bf16[1024,640]{1,0:T(8,128)(2,1)S(1)} %bitcast.18), channel_id=1, source_target_pairs={{0,4},{4,0},{1,5},{5,1},{2,6},{6,2},{3,7},{7,3},{8,12},{12,8},{9,1... | collective-permute-start | bytes 3932168 | tf_op jit(solution)/shard_map/ppermute | solution.py:31
  83.1 3.3 %queries.1.q_ref = bf16[1024,640]{1,0:T(8,128)(2,1)S(1)} custom-call(s32[3]{0:T(128)S(1)} %pad_add_fusion.where_ref, bf16[256,1536]{1,0:T(8,128)(2,1)S(1)} %all_gather.7.g_ref, bf16[1536,384]{1,0:T(8,128)(2,1)S(1)} %copy-done, bf16[2,128,512]{2,1,0:T(8,128)(2,1)S(1)} %copy-done.2, bf16[13824,128]{1,0:T(8,128)(2,1)} %collective-permute-done.packed), custom_call_target="tpu_custom_call" | custom-call | flops 738197504 | bytes 6000000 | tf_op jit(solution)/shard_map/queries/pallas_call | solution.py:278
  86.4 9.8 %attend.1 = (bf16[64,3584]{1,0:T(8,128)(2,1)S(1)}, bf16[64,3584]{1,0:T(8,128)(2,1)S(1)}, bf16[64,3584]{1,0:T(8,128)(2,1)S(1)}, bf16[32,3584]{1,0:T(8,128)(2,1)S(1)}, bf16[32,3584]{1,0:T(8,128)(2,1)S(1)}) custom-call(s32[3]{0:T(128)S(1)} %pad_add_fusion.where_ref, bf16[1024,640]{1,0:T(8,128)(2,1)S(1)} %queries.1.q_ref, bf16[1024,640]{1,0:T(8,128)(2,1)S(1)} %bitcast.19, ...), custom_call_target="tpu_custom_call" | custom-call | flops 4294967296 | bytes 9000000 | tf_op jit(solution)/shard_map/attend/pallas_call | solution.py:298
  96.2 3.3 %collective-permute-start.5 = (bf16[32,3584]{1,0:T(8,128)(2,1)S(1)}, bf16[32,3584]{1,0:T(8,128)(2,1)S(1)}, u32[]{:S(2)}, u32[]{:S(2)}) collective-permute-start(bf16[32,3584]{1,0:T(8,128)(2,1)S(1)} %get-tuple-element.31), channel_id=1, source_target_pairs={{0,112},{8,120},{16,0},{24,8},{32,16},{40,24},{48,32},{56,40},{64,... | collective-permute-start | bytes 688136 | tf_op jit(solution)/shard_map/ppermute | solution.py:27
  99.5 3.9 %collective-permute-start.2 = (bf16[64,3584]{1,0:T(8,128)(2,1)S(1)}, bf16[64,3584]{1,0:T(8,128)(2,1)S(1)}, u32[]{:S(2)}, u32[]{:S(2)}) collective-permute-start(bf16[64,3584]{1,0:T(8,128)(2,1)S(1)} %get-tuple-element.26), channel_id=1, source_target_pairs={{0,8},{8,16},{16,24},{24,32},{32,40},{40,48},{48,56},{56,64},{64,7... | collective-permute-start | bytes 1376264 | tf_op jit(solution)/shard_map/ppermute | solution.py:27
  103.4 3.2 %collective-permute-start.3 = (bf16[64,3584]{1,0:T(8,128)(2,1)S(1)}, bf16[64,3584]{1,0:T(8,128)(2,1)S(1)}, u32[]{:S(2)}, u32[]{:S(2)}) collective-permute-start(bf16[64,3584]{1,0:T(8,128)(2,1)S(1)} %get-tuple-element.27), channel_id=1, source_target_pairs={{0,120},{8,0},{16,8},{24,16},{32,24},{40,32},{48,40},{56,48},{64,5... | collective-permute-start | bytes 1376264 | tf_op jit(solution)/shard_map/ppermute | solution.py:27
  106.6 2.3 %collective-permute-done.5 = bf16[32,3584]{1,0:T(8,128)(2,1)S(1)} collective-permute-done((bf16[32,3584]{1,0:T(8,128)(2,1)S(1)}, bf16[32,3584]{1,0:T(8,128)(2,1)S(1)}, u32[]{:S(2)}, u32[]{:S(2)}) %collective-permute-start.5) | collective-permute-done | bytes 229408 | tf_op jit(solution)/shard_map/ppermute | solution.py:27
  109.0 4.3 %all-to-all-start.1 = ((bf16[4,16,640]{2,1,0:T(8,128)(2,1)}), bf16[4,16,640]{2,1,0:T(8,128)(2,1)S(1)}, u32[]{:S(2)}, u32[]{:S(2)}) async-start(bf16[4,16,640]{2,1,0:T(8,128)(2,1)} %get-tuple-element.36), calls=%async_computation.1 | async-start | bytes 163840 | tf_op jit(solution)/shard_map/all_to_all | solution.py:345
  113.3 3.1 %collective-permute-start.4 = (bf16[32,3584]{1,0:T(8,128)(2,1)S(1)}, bf16[32,3584]{1,0:T(8,128)(2,1)S(1)}, u32[]{:S(2)}, u32[]{:S(2)}) collective-permute-start(bf16[32,3584]{1,0:T(8,128)(2,1)S(1)} %get-tuple-element.30), channel_id=1, source_target_pairs={{0,16},{8,24},{16,32},{24,40},{32,48},{40,56},{48,64},{56,72},{64,... | collective-permute-start | bytes 688136 | tf_op jit(solution)/shard_map/ppermute | solution.py:27
  116.3 2.6 %all-to-all-done.1 = bf16[4,16,640]{2,1,0:T(8,128)(2,1)S(1)} async-done(((bf16[4,16,640]{2,1,0:T(8,128)(2,1)}), bf16[4,16,640]{2,1,0:T(8,128)(2,1)S(1)}, u32[]{:S(2)}, u32[]{:S(2)}) %all-to-all-start.1) | async-done | bytes 81952 | tf_op jit(solution)/shard_map/all_to_all | solution.py:345
  119.1 0.1 copy.17
  119.2 0.1 reshape.27
  119.3 0.2 convolution_convert_fusion
  119.5 0.6 copy.15
  120.2 1.6 %collective-permute-done.3 = bf16[64,3584]{1,0:T(8,128)(2,1)S(1)} collective-permute-done((bf16[64,3584]{1,0:T(8,128)(2,1)S(1)}, bf16[64,3584]{1,0:T(8,128)(2,1)S(1)}, u32[]{:S(2)}, u32[]{:S(2)}) %collective-permute-start.3) | collective-permute-done | bytes 458784 | tf_op jit(solution)/shard_map/ppermute | solution.py:27
  121.9 4.3 %collective-permute-start.6 = (bf16[16,1792]{1,0:T(8,128)(2,1)S(1)}, bf16[16,1792]{1,0:T(8,128)(2,1)S(1)}, u32[]{:S(2)}, u32[]{:S(2)}) collective-permute-start(bf16[16,1792]{1,0:T(8,128)(2,1)S(1)} %get-tuple-element.43), channel_id=1, source_target_pairs={{0,32},{8,40},{16,48},{24,56},{32,64},{40,72},{48,80},{56,88},{64,... | collective-permute-start | bytes 172040 | tf_op jit(solution)/shard_map/ppermute | solution.py:27
  126.2 5.4 %collective-permute-start.7 = (bf16[16,1792]{1,0:T(8,128)(2,1)S(1)}, bf16[16,1792]{1,0:T(8,128)(2,1)S(1)}, u32[]{:S(2)}, u32[]{:S(2)}) collective-permute-start(bf16[16,1792]{1,0:T(8,128)(2,1)S(1)} %get-tuple-element.42), channel_id=1, source_target_pairs={{0,96},{8,104},{16,112},{24,120},{32,0},{40,8},{48,16},{56,24},{64... | collective-permute-start | bytes 172040 | tf_op jit(solution)/shard_map/ppermute | solution.py:27
  131.7 0.1 convert_add_fusion.1
  131.8 0.5 collective-permute-done.6
  132.3 5.3 %collective-permute-done.7 = bf16[16,1792]{1,0:T(8,128)(2,1)S(1)} collective-permute-done((bf16[16,1792]{1,0:T(8,128)(2,1)S(1)}, bf16[16,1792]{1,0:T(8,128)(2,1)S(1)}, u32[]{:S(2)}, u32[]{:S(2)}) %collective-permute-start.7) | collective-permute-done | bytes 57376 | tf_op jit(solution)/shard_map/ppermute | solution.py:27
  137.6 5.9 %collective-permute-start.8 = (bf16[16,3584]{1,0:T(8,128)(2,1)S(1)}, bf16[16,3584]{1,0:T(8,128)(2,1)S(1)}, u32[]{:S(2)}, u32[]{:S(2)}) collective-permute-start(bf16[16,3584]{1,0:T(8,128)(2,1)S(1)} %pad_maximum_fusion), channel_id=1, source_target_pairs={{0,32},{8,40},{16,48},{24,56},{32,64},{40,72},{48,80},{56,88},{64,... | collective-permute-start | bytes 344072 | tf_op jit(solution)/shard_map/ppermute | solution.py:27
  143.6 3.8 %collective-permute-start.9 = (bf16[16,3584]{1,0:T(8,128)(2,1)S(1)}, bf16[16,3584]{1,0:T(8,128)(2,1)S(1)}, u32[]{:S(2)}, u32[]{:S(2)}) collective-permute-start(bf16[16,3584]{1,0:T(8,128)(2,1)S(1)} %pad_maximum_fusion.1), channel_id=1, source_target_pairs={{0,96},{8,104},{16,112},{24,120},{32,0},{40,8},{48,16},{56,24},{64... | collective-permute-start | bytes 344072 | tf_op jit(solution)/shard_map/ppermute | solution.py:27
  147.4 0.6 copy.16
  148.0 2.6 %collective-permute-done.8 = bf16[16,3584]{1,0:T(8,128)(2,1)S(1)} collective-permute-done((bf16[16,3584]{1,0:T(8,128)(2,1)S(1)}, bf16[16,3584]{1,0:T(8,128)(2,1)S(1)}, u32[]{:S(2)}, u32[]{:S(2)}) %collective-permute-start.8) | collective-permute-done | bytes 114720 | tf_op jit(solution)/shard_map/ppermute | solution.py:27
  150.7 6.5 %collective-permute-done.9 = bf16[16,3584]{1,0:T(8,128)(2,1)S(1)} collective-permute-done((bf16[16,3584]{1,0:T(8,128)(2,1)S(1)}, bf16[16,3584]{1,0:T(8,128)(2,1)S(1)}, u32[]{:S(2)}, u32[]{:S(2)}) %collective-permute-start.9) | collective-permute-done | bytes 114720 | tf_op jit(solution)/shard_map/ppermute | solution.py:27
  157.2 0.8 fusion
  (29 shorter events, 0.4 us)
Async XLA Ops:
  5.1 78.0 %collective-permute-start = (bf16[13824,128]{1,0:T(8,128)(2,1)}, bf16[13824,128]{1,0:T(8,128)(2,1)}, u32[]{:S(2)}, u32[]{:S(2)}) collective-permute-start(bf16[13824,128]{1,0:T(8,128)(2,1)} %get-tuple-element.23), channel_id=1, source_target_pairs={{0,4},{4,0},{1,5},{5,1},{2,6},{6,2},{3,7},{7,3},{8,12},{12,8},{9,1... | collective-permute-start | bytes 10616840 | tf_op jit(solution)/shard_map/ppermute | solution.py:31
  45.7 37.4 %copy-start = (bf16[1536,384]{1,0:T(8,128)(2,1)S(1)}, bf16[1536,384]{1,0:T(8,128)(2,1)}, u32[]{:S(2)}) copy-start(bf16[1536,384]{1,0:T(8,128)(2,1)} %wq0.1) | copy-start | bytes 3538948
  45.7 37.4 %copy-start.2 = (bf16[2,128,512]{2,1,0:T(8,128)(2,1)S(1)}, bf16[2,128,512]{2,1,0:T(8,128)(2,1)}, u32[]{:S(2)}) copy-start(bf16[2,128,512]{2,1,0:T(8,128)(2,1)} %ak0.1) | copy-start | bytes 786436
  45.7 35.4 %all-to-all-start = ((bf16[4,256,640]{2,1,0:T(8,128)(2,1)}), bf16[4,256,640]{2,1,0:T(8,128)(2,1)S(1)}, u32[]{:S(2)}, u32[]{:S(2)}) async-start(bf16[4,256,640]{2,1,0:T(8,128)(2,1)} %broadcast_in_dim.25), calls=%async_computation | async-start | bytes 2621440 | tf_op jit(solution)/shard_map/all_to_all | solution.py:36
  81.1 5.3 %collective-permute-start.1 = (bf16[1024,640]{1,0:T(8,128)(2,1)S(1)}, bf16[1024,640]{1,0:T(8,128)(2,1)S(1)}, u32[]{:S(2)}, u32[]{:S(2)}) collective-permute-start(bf16[1024,640]{1,0:T(8,128)(2,1)S(1)} %bitcast.18), channel_id=1, source_target_pairs={{0,4},{4,0},{1,5},{5,1},{2,6},{6,2},{3,7},{7,3},{8,12},{12,8},{9,1... | collective-permute-start | bytes 3932168 | tf_op jit(solution)/shard_map/ppermute | solution.py:31
  83.1 3.4 %copy-start.1 = (bf16[256,3584]{1,0:T(8,128)(2,1)S(1)}, bf16[256,3584]{1,0:T(8,128)(2,1)}, u32[]{:S(2)}) copy-start(bf16[256,3584]{1,0:T(8,128)(2,1)} %op0.1) | copy-start | bytes 5505028
  83.1 3.4 %copy-start.3 = (bf16[2,512,128]{2,1,0:T(8,128)(2,1)S(1)}, bf16[2,512,128]{2,1,0:T(8,128)(2,1)}, u32[]{:S(2)}) copy-start(bf16[2,512,128]{2,1,0:T(8,128)(2,1)} %av0.1) | copy-start | bytes 786436
  96.2 12.7 %collective-permute-start.5 = (bf16[32,3584]{1,0:T(8,128)(2,1)S(1)}, bf16[32,3584]{1,0:T(8,128)(2,1)S(1)}, u32[]{:S(2)}, u32[]{:S(2)}) collective-permute-start(bf16[32,3584]{1,0:T(8,128)(2,1)S(1)} %get-tuple-element.31), channel_id=1, source_target_pairs={{0,112},{8,120},{16,0},{24,8},{32,16},{40,24},{48,32},{56,40},{64,... | collective-permute-start | bytes 688136 | tf_op jit(solution)/shard_map/ppermute | solution.py:27
  99.5 20.6 %collective-permute-start.2 = (bf16[64,3584]{1,0:T(8,128)(2,1)S(1)}, bf16[64,3584]{1,0:T(8,128)(2,1)S(1)}, u32[]{:S(2)}, u32[]{:S(2)}) collective-permute-start(bf16[64,3584]{1,0:T(8,128)(2,1)S(1)} %get-tuple-element.26), channel_id=1, source_target_pairs={{0,8},{8,16},{16,24},{24,32},{32,40},{40,48},{48,56},{56,64},{64,7... | collective-permute-start | bytes 1376264 | tf_op jit(solution)/shard_map/ppermute | solution.py:27
  103.4 18.4 %collective-permute-start.3 = (bf16[64,3584]{1,0:T(8,128)(2,1)S(1)}, bf16[64,3584]{1,0:T(8,128)(2,1)S(1)}, u32[]{:S(2)}, u32[]{:S(2)}) collective-permute-start(bf16[64,3584]{1,0:T(8,128)(2,1)S(1)} %get-tuple-element.27), channel_id=1, source_target_pairs={{0,120},{8,0},{16,8},{24,16},{32,24},{40,32},{48,40},{56,48},{64,5... | collective-permute-start | bytes 1376264 | tf_op jit(solution)/shard_map/ppermute | solution.py:27
  109.0 10.0 %all-to-all-start.1 = ((bf16[4,16,640]{2,1,0:T(8,128)(2,1)}), bf16[4,16,640]{2,1,0:T(8,128)(2,1)S(1)}, u32[]{:S(2)}, u32[]{:S(2)}) async-start(bf16[4,16,640]{2,1,0:T(8,128)(2,1)} %get-tuple-element.36), calls=%async_computation.1 | async-start | bytes 163840 | tf_op jit(solution)/shard_map/all_to_all | solution.py:345
  113.3 18.4 %collective-permute-start.4 = (bf16[32,3584]{1,0:T(8,128)(2,1)S(1)}, bf16[32,3584]{1,0:T(8,128)(2,1)S(1)}, u32[]{:S(2)}, u32[]{:S(2)}) collective-permute-start(bf16[32,3584]{1,0:T(8,128)(2,1)S(1)} %get-tuple-element.30), channel_id=1, source_target_pairs={{0,16},{8,24},{16,32},{24,40},{32,48},{40,56},{48,64},{56,72},{64,... | collective-permute-start | bytes 688136 | tf_op jit(solution)/shard_map/ppermute | solution.py:27
  121.9 10.4 %collective-permute-start.6 = (bf16[16,1792]{1,0:T(8,128)(2,1)S(1)}, bf16[16,1792]{1,0:T(8,128)(2,1)S(1)}, u32[]{:S(2)}, u32[]{:S(2)}) collective-permute-start(bf16[16,1792]{1,0:T(8,128)(2,1)S(1)} %get-tuple-element.43), channel_id=1, source_target_pairs={{0,32},{8,40},{16,48},{24,56},{32,64},{40,72},{48,80},{56,88},{64,... | collective-permute-start | bytes 172040 | tf_op jit(solution)/shard_map/ppermute | solution.py:27
  126.2 11.4 %collective-permute-start.7 = (bf16[16,1792]{1,0:T(8,128)(2,1)S(1)}, bf16[16,1792]{1,0:T(8,128)(2,1)S(1)}, u32[]{:S(2)}, u32[]{:S(2)}) collective-permute-start(bf16[16,1792]{1,0:T(8,128)(2,1)S(1)} %get-tuple-element.42), channel_id=1, source_target_pairs={{0,96},{8,104},{16,112},{24,120},{32,0},{40,8},{48,16},{56,24},{64... | collective-permute-start | bytes 172040 | tf_op jit(solution)/shard_map/ppermute | solution.py:27
  137.6 13.0 %collective-permute-start.8 = (bf16[16,3584]{1,0:T(8,128)(2,1)S(1)}, bf16[16,3584]{1,0:T(8,128)(2,1)S(1)}, u32[]{:S(2)}, u32[]{:S(2)}) collective-permute-start(bf16[16,3584]{1,0:T(8,128)(2,1)S(1)} %pad_maximum_fusion), channel_id=1, source_target_pairs={{0,32},{8,40},{16,48},{24,56},{32,64},{40,72},{48,80},{56,88},{64,... | collective-permute-start | bytes 344072 | tf_op jit(solution)/shard_map/ppermute | solution.py:27
  143.6 13.6 %collective-permute-start.9 = (bf16[16,3584]{1,0:T(8,128)(2,1)S(1)}, bf16[16,3584]{1,0:T(8,128)(2,1)S(1)}, u32[]{:S(2)}, u32[]{:S(2)}) collective-permute-start(bf16[16,3584]{1,0:T(8,128)(2,1)S(1)} %pad_maximum_fusion.1), channel_id=1, source_target_pairs={{0,96},{8,104},{16,112},{24,120},{32,0},{40,8},{48,16},{56,24},{64... | collective-permute-start | bytes 344072 | tf_op jit(solution)/shard_map/ppermute | solution.py:27

commit v15 on v14

--- a/solution.py
+++ b/solution.py
@@ -185,15 +185,22 @@
             q = q_ref[h * rows : (h + 1) * rows, :]
             scores = []
             for i, k_ref in enumerate((ka_ref, kb_ref)):
-                s = lax.dot_general(q, k_ref[:count, :], nt, preferred_element_type=F32)
-                own = jnp.where(ok[i], s[:, count - n :], NEG)
-                scores.append(own if count == n else jnp.concatenate([s[:, : count - n], own], -1))
-            m = jnp.maximum(*[jnp.max(s, -1, keepdims=True) for s in scores]) * s2
+                for part_keys in (slice(0, count - n), slice(count - n, count)):
+                    if part_keys.start == part_keys.stop:
+                        continue
+                    s = lax.dot_general(q, k_ref[part_keys, :], nt, preferred_element_type=F32)
+                    if part_keys.stop == count:
+                        s = jnp.where(ok[i], s, NEG)
+                    scores.append((s, k_ref, part_keys))
+            m = functools.reduce(jnp.maximum, [jnp.max(s, -1, keepdims=True) for s, _, _ in scores])
+            m = m * s2
             total, mixed = 0.0, 0.0
-            for s, k_ref in zip(scores, (ka_ref, kb_ref)):
+            for s, k_ref, part_keys in scores:
                 p = jnp.exp2(s * s2 - m)
                 total = total + jnp.sum(p, -1, keepdims=True)
-                mixed = mixed + jnp.dot(p.astype(BF), k_ref[:count, :lat], preferred_element_type=F32)
+                mixed = mixed + jnp.dot(
+                    p.astype(BF), k_ref[part_keys, :lat], preferred_element_type=F32
+                )
             acc_ref[h * rows : (h + 1) * rows, :] = (mixed / total).astype(BF)
 
     for seen in range(1, nch + 1):
@@ -330,7 +337,8 @@
 
     far = near(2, up, down).astype(BF)
     far, up, down = lax.optimization_barrier((far, up, down))
-    left, right = lax.optimization_barrier((shift_z(far[:, :cut], nzl), shift_z(far[:, cut:], -nzl)))
+    first = shift_z(far[:, :cut], nzl)
+    left, right = lax.optimization_barrier((first, shift_z(far[:, cut:], -nzl)))
     ahead = near(1, up, down) + up2[qrows:].astype(F32)
     ahead = jnp.concatenate([ahead[:, :cut] + left.astype(F32), ahead[:, cut:]], -1)
     ahead = shift_z(ahead.astype(BF), nzl)
@@ -341,7 +349,7 @@
     total = total + ahead.astype(F32) + behind.astype(F32)
     layer_output = total.astype(BF)[None]
 
-    page = lax.optimization_barrier((page, down2))[0]
+    page = lax.optimization_barrier((page, first))[0]
     page = lax.all_to_all(page, "dec", 0, 0, tiled=True).reshape(-1, pages, part, kw)
     came = page[:, :, 0, lat + rope].reshape(-1).astype(jnp.int32)
     take = (came[None, :] == dec * slots + jnp.arange(slots, dtype=jnp.int32)[:, None]).astype(BF)

time: 160 us -> 153 us (0.956); the launches traced: 158 us -> 153 us
  waiting for transfers between devices: 21.6 us -> 14.8 us
  starting transfers between devices: 45.8 us -> 47.4 us
    ppermute x8, waiting for transfers between devices: 18.9 us -> 14.7 us  [shift_z(): return lax.ppermute(x, Z, [(i, (i + step) % n) for i in range(n)])]
    all_to_all x1, waiting for transfers between devices: 2.64 us -> 0.01 us  [local(): lax.all_to_all(page, 'dec', 0, 0, tiled=True).reshape(-1, pages, part, kw)]
    ppermute x8, starting transfers between devices: 32.9 us -> 34.5 us  [shift_z(): return lax.ppermute(x, Z, [(i, (i + step) % n) for i in range(n)])]
  transfers between devices with their start and end apart: 12 -> 12, of which waited for: 7 -> 5; matrix products, arithmetic and copies ran while one was open for 2% -> 2% of each run, Pallas kernels for 2% -> 2%
where the time goes in v15:
time: 153 us
  blocking collectives  68 us (44%)
  starting transfers between devices  47.4 us (31%)
  Pallas kernels  17.4 us (11%)
  waiting for transfers between devices  14.8 us (10%)
  local copies, waits for them, and re-layouts  2.85 us (2%)
    all_gather x1, blocking collectives, local(): own = lax.all_gather(keys, Z, axis=0, tiled=True)  37.4 us
    ppermute x8, starting transfers between devices, shift_z(): return lax.ppermute(x, Z, [(i, (i + step) % n) for i in range(n)])  34.5 us
    all_gather x1, blocking collectives, local(): qg = lax.all_gather(held, Z, axis=0, tiled=True)  30.6 us
    ppermute x8, waiting for transfers between devices, shift_z(): return lax.ppermute(x, Z, [(i, (i + step) % n) for i in range(n)])  14.7 us
    pallas_call x1, Pallas kernels, local(): pl.pallas_call(functools.partial(attend_kernel, rows=rows, lat=lat, scale...  9.65 us
    all_to_all x1, starting transfers between devices, spread(): lax.all_to_all(jnp.broadcast_to(x[None], (n,) + x.shape), axis, 0, 0, til...  4.82 us
    pallas_call x1, Pallas kernels, local(): pl.pallas_call(functools.partial(key_kernel, slots=slots, page_len=part *...  4.47 us
    all_to_all x1, starting transfers between devices, local(): lax.all_to_all(page, 'dec', 0, 0, tiled=True).reshape(-1, pages, part, kw)  4.28 us
  transfers between devices with their start and end apart: 12, of which 5 were waited for; matrix products, arithmetic and copies ran while one was open for 2% of the time, Pallas kernels for 2%

profile of v15, /device:TPU:24, one launch (start us, length us, event | category | flops | bytes accessed | tf_op | source)
XLA Modules:
  0.0 152.6 jit_solution(9510740420288516846)
XLA Ops:
  0.6 4.5 %keys.1 = (bf16[16,640]{1,0:T(8,128)(2,1)}, bf16[4,16,640]{2,1,0:T(8,128)(2,1)}, bf16[13824,128]{1,0:T(8,128)(2,1)}) custom-call(s32[1]{0:T(128)} %bitcast.4.where_ref, s32[1,4]{1,0:T(1,128)} %owner_ref.1, s32[1,4]{1,0:T(1,128)} %slot_ref.1, bf16[1,4,4,512]{3,2,1,0:T(4,128)(2,1)} %lat_ref.1, bf16[1,4,4,64]{3,2,1,0:T(4,128)(2,1)} %rope_ref.1, ...), custom_call_target="tpu_custom_call" | custom-call | tf_op jit(solution)/shard_map/keys/pallas_call | solution.py:261
  5.1 1.9 %collective-permute-start = (bf16[13824,128]{1,0:T(8,128)(2,1)}, bf16[13824,128]{1,0:T(8,128)(2,1)}, u32[]{:S(2)}, u32[]{:S(2)}) collective-permute-start(bf16[13824,128]{1,0:T(8,128)(2,1)} %get-tuple-element.23), channel_id=1, source_target_pairs={{0,4},{4,0},{1,5},{5,1},{2,6},{6,2},{3,7},{7,3},{8,12},{12,8},{9,1... | collective-permute-start | bytes 10616840 | tf_op jit(solution)/shard_map/ppermute | solution.py:31
  7.0 37.4 %all_gather.6 = bf16[256,640]{1,0:T(8,128)(2,1)S(1)} all-gather(bf16[16,640]{1,0:T(8,128)(2,1)} %get-tuple-element.20), channel_id=1, replica_groups=mesh['chain'=4,'zh'=4,'zl'=4,'core'=2,'dec'=4] {'zh','zl'}, dimensions={0}, use_global_device_ids=true | all-gather | bytes 348160 | tf_op jit(solution)/shard_map/all_gather | solution.py:278
  44.4 1.2 broadcast_in_dim.25
  45.7 4.8 %all-to-all-start = ((bf16[4,256,640]{2,1,0:T(8,128)(2,1)}), bf16[4,256,640]{2,1,0:T(8,128)(2,1)S(1)}, u32[]{:S(2)}, u32[]{:S(2)}) async-start(bf16[4,256,640]{2,1,0:T(8,128)(2,1)} %broadcast_in_dim.25), calls=%async_computation | async-start | bytes 2621440 | tf_op jit(solution)/shard_map/all_to_all | solution.py:36
  50.5 30.6 %all_gather.7.g_ref = bf16[256,1536]{1,0:T(8,128)(2,1)S(1)} all-gather(bf16[16,1536]{1,0:T(8,128)(2,1)} %bitcast.20), channel_id=1, replica_groups=mesh['chain'=4,'zh'=4,'zl'=4,'core'=2,'dec'=4] {'zh','zl'}, dimensions={0}, use_global_device_ids=true | all-gather | bytes 835584 | tf_op jit(solution)/shard_map/all_gather | solution.py:281
  81.1 1.9 %collective-permute-start.1 = (bf16[1024,640]{1,0:T(8,128)(2,1)S(1)}, bf16[1024,640]{1,0:T(8,128)(2,1)S(1)}, u32[]{:S(2)}, u32[]{:S(2)}) collective-permute-start(bf16[1024,640]{1,0:T(8,128)(2,1)S(1)} %bitcast.18), channel_id=1, source_target_pairs={{0,4},{4,0},{1,5},{5,1},{2,6},{6,2},{3,7},{7,3},{8,12},{12,8},{9,1... | collective-permute-start | bytes 3932168 | tf_op jit(solution)/shard_map/ppermute | solution.py:31
  83.0 0.1 pad_add_fusion.where_ref
  83.1 3.3 %queries.1.q_ref = bf16[1024,640]{1,0:T(8,128)(2,1)S(1)} custom-call(s32[3]{0:T(128)S(1)} %pad_add_fusion.where_ref, bf16[256,1536]{1,0:T(8,128)(2,1)S(1)} %all_gather.7.g_ref, bf16[1536,384]{1,0:T(8,128)(2,1)S(1)} %copy-done, bf16[2,128,512]{2,1,0:T(8,128)(2,1)S(1)} %copy-done.2, bf16[13824,128]{1,0:T(8,128)(2,1)} %collective-permute-done.packed), custom_call_target="tpu_custom_call" | custom-call | flops 738197504 | bytes 6000000 | tf_op jit(solution)/shard_map/queries/pallas_call | solution.py:285
  86.4 9.6 %attend.1 = (bf16[64,3584]{1,0:T(8,128)(2,1)S(1)}, bf16[64,3584]{1,0:T(8,128)(2,1)S(1)}, bf16[64,3584]{1,0:T(8,128)(2,1)S(1)}, bf16[32,3584]{1,0:T(8,128)(2,1)S(1)}, bf16[32,3584]{1,0:T(8,128)(2,1)S(1)}) custom-call(s32[3]{0:T(128)S(1)} %pad_add_fusion.where_ref, bf16[1024,640]{1,0:T(8,128)(2,1)S(1)} %queries.1.q_ref, bf16[1024,640]{1,0:T(8,128)(2,1)S(1)} %bitcast.19, ...), custom_call_target="tpu_custom_call" | custom-call | flops 4294967296 | bytes 9000000 | tf_op jit(solution)/shard_map/attend/pallas_call | solution.py:305
  96.1 3.8 %collective-permute-start.2 = (bf16[64,3584]{1,0:T(8,128)(2,1)S(1)}, bf16[64,3584]{1,0:T(8,128)(2,1)S(1)}, u32[]{:S(2)}, u32[]{:S(2)}) collective-permute-start(bf16[64,3584]{1,0:T(8,128)(2,1)S(1)} %get-tuple-element.26), channel_id=1, source_target_pairs={{0,8},{8,16},{16,24},{24,32},{32,40},{40,48},{48,56},{56,64},{64,7... | collective-permute-start | bytes 1376264 | tf_op jit(solution)/shard_map/ppermute | solution.py:27
  99.9 3.3 %collective-permute-start.3 = (bf16[64,3584]{1,0:T(8,128)(2,1)S(1)}, bf16[64,3584]{1,0:T(8,128)(2,1)S(1)}, u32[]{:S(2)}, u32[]{:S(2)}) collective-permute-start(bf16[64,3584]{1,0:T(8,128)(2,1)S(1)} %get-tuple-element.27), channel_id=1, source_target_pairs={{0,120},{8,0},{16,8},{24,16},{32,24},{40,32},{48,40},{56,48},{64,5... | collective-permute-start | bytes 1376264 | tf_op jit(solution)/shard_map/ppermute | solution.py:27
  103.2 2.0 %collective-permute-start.4 = (bf16[32,3584]{1,0:T(8,128)(2,1)S(1)}, bf16[32,3584]{1,0:T(8,128)(2,1)S(1)}, u32[]{:S(2)}, u32[]{:S(2)}) collective-permute-start(bf16[32,3584]{1,0:T(8,128)(2,1)S(1)} %get-tuple-element.30), channel_id=1, source_target_pairs={{0,16},{8,24},{16,32},{24,40},{32,48},{40,56},{48,64},{56,72},{64,... | collective-permute-start | bytes 688136 | tf_op jit(solution)/shard_map/ppermute | solution.py:27
  105.2 5.9 %collective-permute-start.5 = (bf16[32,3584]{1,0:T(8,128)(2,1)S(1)}, bf16[32,3584]{1,0:T(8,128)(2,1)S(1)}, u32[]{:S(2)}, u32[]{:S(2)}) collective-permute-start(bf16[32,3584]{1,0:T(8,128)(2,1)S(1)} %get-tuple-element.31), channel_id=1, source_target_pairs={{0,112},{8,120},{16,0},{24,8},{32,16},{40,24},{48,32},{56,40},{64,... | collective-permute-start | bytes 688136 | tf_op jit(solution)/shard_map/ppermute | solution.py:27
  111.1 2.4 %collective-permute-done.2 = bf16[64,3584]{1,0:T(8,128)(2,1)S(1)} collective-permute-done((bf16[64,3584]{1,0:T(8,128)(2,1)S(1)}, bf16[64,3584]{1,0:T(8,128)(2,1)S(1)}, u32[]{:S(2)}, u32[]{:S(2)}) %collective-permute-start.2) | collective-permute-done | bytes 458784 | tf_op jit(solution)/shard_map/ppermute | solution.py:27
  113.5 1.8 %collective-permute-done.3 = bf16[64,3584]{1,0:T(8,128)(2,1)S(1)} collective-permute-done((bf16[64,3584]{1,0:T(8,128)(2,1)S(1)}, bf16[64,3584]{1,0:T(8,128)(2,1)S(1)}, u32[]{:S(2)}, u32[]{:S(2)}) %collective-permute-start.3) | collective-permute-done | bytes 458784 | tf_op jit(solution)/shard_map/ppermute | solution.py:27
  115.4 4.0 %collective-permute-start.6 = (bf16[16,1792]{1,0:T(8,128)(2,1)S(1)}, bf16[16,1792]{1,0:T(8,128)(2,1)S(1)}, u32[]{:S(2)}, u32[]{:S(2)}) collective-permute-start(bf16[16,1792]{1,0:T(8,128)(2,1)S(1)} %get-tuple-element.43), channel_id=1, source_target_pairs={{0,32},{8,40},{16,48},{24,56},{32,64},{40,72},{48,80},{56,88},{64,... | collective-permute-start | bytes 172040 | tf_op jit(solution)/shard_map/ppermute | solution.py:27
  119.4 5.7 %collective-permute-start.7 = (bf16[16,1792]{1,0:T(8,128)(2,1)S(1)}, bf16[16,1792]{1,0:T(8,128)(2,1)S(1)}, u32[]{:S(2)}, u32[]{:S(2)}) collective-permute-start(bf16[16,1792]{1,0:T(8,128)(2,1)S(1)} %get-tuple-element.42), channel_id=1, source_target_pairs={{0,96},{8,104},{16,112},{24,120},{32,0},{40,8},{48,16},{56,24},{64... | collective-permute-start | bytes 172040 | tf_op jit(solution)/shard_map/ppermute | solution.py:27
  125.2 0.1 convert_add_fusion.1
  125.4 2.6 %collective-permute-done.6 = bf16[16,1792]{1,0:T(8,128)(2,1)S(1)} collective-permute-done((bf16[16,1792]{1,0:T(8,128)(2,1)S(1)}, bf16[16,1792]{1,0:T(8,128)(2,1)S(1)}, u32[]{:S(2)}, u32[]{:S(2)}) %collective-permute-start.6) | collective-permute-done | bytes 57376 | tf_op jit(solution)/shard_map/ppermute | solution.py:27
  127.9 4.3 %all-to-all-start.1 = ((bf16[4,16,640]{2,1,0:T(8,128)(2,1)}), bf16[4,16,640]{2,1,0:T(8,128)(2,1)S(1)}, u32[]{:S(2)}, u32[]{:S(2)}) async-start(bf16[4,16,640]{2,1,0:T(8,128)(2,1)} %get-tuple-element.36), calls=%async_computation.1 | async-start | bytes 163840 | tf_op jit(solution)/shard_map/all_to_all | solution.py:353
  132.2 4.1 %collective-permute-start.8 = (bf16[16,3584]{1,0:T(8,128)(2,1)S(1)}, bf16[16,3584]{1,0:T(8,128)(2,1)S(1)}, u32[]{:S(2)}, u32[]{:S(2)}) collective-permute-start(bf16[16,3584]{1,0:T(8,128)(2,1)S(1)} %pad_maximum_fusion), channel_id=1, source_target_pairs={{0,32},{8,40},{16,48},{24,56},{32,64},{40,72},{48,80},{56,88},{64,... | collective-permute-start | bytes 344072 | tf_op jit(solution)/shard_map/ppermute | solution.py:27
  136.4 5.7 %collective-permute-start.9 = (bf16[16,3584]{1,0:T(8,128)(2,1)S(1)}, bf16[16,3584]{1,0:T(8,128)(2,1)S(1)}, u32[]{:S(2)}, u32[]{:S(2)}) collective-permute-start(bf16[16,3584]{1,0:T(8,128)(2,1)S(1)} %pad_maximum_fusion.1), channel_id=1, source_target_pairs={{0,96},{8,104},{16,112},{24,120},{32,0},{40,8},{48,16},{56,24},{64... | collective-permute-start | bytes 344072 | tf_op jit(solution)/shard_map/ppermute | solution.py:27
  142.1 0.1 slice.112
  142.2 0.1 copy.17
  142.3 0.1 reshape.27
  142.4 0.2 convolution_convert_fusion
  142.6 0.6 copy.15
  143.3 0.6 copy.16
  143.9 2.7 %collective-permute-done.8 = bf16[16,3584]{1,0:T(8,128)(2,1)S(1)} collective-permute-done((bf16[16,3584]{1,0:T(8,128)(2,1)S(1)}, bf16[16,3584]{1,0:T(8,128)(2,1)S(1)}, u32[]{:S(2)}, u32[]{:S(2)}) %collective-permute-start.8) | collective-permute-done | bytes 114720 | tf_op jit(solution)/shard_map/ppermute | solution.py:27
  146.6 5.3 %collective-permute-done.9 = bf16[16,3584]{1,0:T(8,128)(2,1)S(1)} collective-permute-done((bf16[16,3584]{1,0:T(8,128)(2,1)S(1)}, bf16[16,3584]{1,0:T(8,128)(2,1)S(1)}, u32[]{:S(2)}, u32[]{:S(2)}) %collective-permute-start.9) | collective-permute-done | bytes 114720 | tf_op jit(solution)/shard_map/ppermute | solution.py:27
  151.8 0.8 fusion
  (29 shorter events, 0.2 us)
Async XLA Ops:
  5.1 78.0 %collective-permute-start = (bf16[13824,128]{1,0:T(8,128)(2,1)}, bf16[13824,128]{1,0:T(8,128)(2,1)}, u32[]{:S(2)}, u32[]{:S(2)}) collective-permute-start(bf16[13824,128]{1,0:T(8,128)(2,1)} %get-tuple-element.23), channel_id=1, source_target_pairs={{0,4},{4,0},{1,5},{5,1},{2,6},{6,2},{3,7},{7,3},{8,12},{12,8},{9,1... | collective-permute-start | bytes 10616840 | tf_op jit(solution)/shard_map/ppermute | solution.py:31
  45.7 37.4 %copy-start = (bf16[1536,384]{1,0:T(8,128)(2,1)S(1)}, bf16[1536,384]{1,0:T(8,128)(2,1)}, u32[]{:S(2)}) copy-start(bf16[1536,384]{1,0:T(8,128)(2,1)} %wq0.1) | copy-start | bytes 3538948
  45.7 37.4 %copy-start.2 = (bf16[2,128,512]{2,1,0:T(8,128)(2,1)S(1)}, bf16[2,128,512]{2,1,0:T(8,128)(2,1)}, u32[]{:S(2)}) copy-start(bf16[2,128,512]{2,1,0:T(8,128)(2,1)} %ak0.1) | copy-start | bytes 786436
  45.7 35.4 %all-to-all-start = ((bf16[4,256,640]{2,1,0:T(8,128)(2,1)}), bf16[4,256,640]{2,1,0:T(8,128)(2,1)S(1)}, u32[]{:S(2)}, u32[]{:S(2)}) async-start(bf16[4,256,640]{2,1,0:T(8,128)(2,1)} %broadcast_in_dim.25), calls=%async_computation | async-start | bytes 2621440 | tf_op jit(solution)/shard_map/all_to_all | solution.py:36
  81.1 5.3 %collective-permute-start.1 = (bf16[1024,640]{1,0:T(8,128)(2,1)S(1)}, bf16[1024,640]{1,0:T(8,128)(2,1)S(1)}, u32[]{:S(2)}, u32[]{:S(2)}) collective-permute-start(bf16[1024,640]{1,0:T(8,128)(2,1)S(1)} %bitcast.18), channel_id=1, source_target_pairs={{0,4},{4,0},{1,5},{5,1},{2,6},{6,2},{3,7},{7,3},{8,12},{12,8},{9,1... | collective-permute-start | bytes 3932168 | tf_op jit(solution)/shard_map/ppermute | solution.py:31
  83.1 3.4 %copy-start.1 = (bf16[256,3584]{1,0:T(8,128)(2,1)S(1)}, bf16[256,3584]{1,0:T(8,128)(2,1)}, u32[]{:S(2)}) copy-start(bf16[256,3584]{1,0:T(8,128)(2,1)} %op0.1) | copy-start | bytes 5505028
  83.1 3.4 %copy-start.3 = (bf16[2,512,128]{2,1,0:T(8,128)(2,1)S(1)}, bf16[2,512,128]{2,1,0:T(8,128)(2,1)}, u32[]{:S(2)}) copy-start(bf16[2,512,128]{2,1,0:T(8,128)(2,1)} %av0.1) | copy-start | bytes 786436
  96.1 17.5 %collective-permute-start.2 = (bf16[64,3584]{1,0:T(8,128)(2,1)S(1)}, bf16[64,3584]{1,0:T(8,128)(2,1)S(1)}, u32[]{:S(2)}, u32[]{:S(2)}) collective-permute-start(bf16[64,3584]{1,0:T(8,128)(2,1)S(1)} %get-tuple-element.26), channel_id=1, source_target_pairs={{0,8},{8,16},{16,24},{24,32},{32,40},{40,48},{48,56},{56,64},{64,7... | collective-permute-start | bytes 1376264 | tf_op jit(solution)/shard_map/ppermute | solution.py:27
  99.9 15.5 %collective-permute-start.3 = (bf16[64,3584]{1,0:T(8,128)(2,1)S(1)}, bf16[64,3584]{1,0:T(8,128)(2,1)S(1)}, u32[]{:S(2)}, u32[]{:S(2)}) collective-permute-start(bf16[64,3584]{1,0:T(8,128)(2,1)S(1)} %get-tuple-element.27), channel_id=1, source_target_pairs={{0,120},{8,0},{16,8},{24,16},{32,24},{40,32},{48,40},{56,48},{64,5... | collective-permute-start | bytes 1376264 | tf_op jit(solution)/shard_map/ppermute | solution.py:27
  103.2 22.0 %collective-permute-start.4 = (bf16[32,3584]{1,0:T(8,128)(2,1)S(1)}, bf16[32,3584]{1,0:T(8,128)(2,1)S(1)}, u32[]{:S(2)}, u32[]{:S(2)}) collective-permute-start(bf16[32,3584]{1,0:T(8,128)(2,1)S(1)} %get-tuple-element.30), channel_id=1, source_target_pairs={{0,16},{8,24},{16,32},{24,40},{32,48},{40,56},{48,64},{56,72},{64,... | collective-permute-start | bytes 688136 | tf_op jit(solution)/shard_map/ppermute | solution.py:27
  105.2 20.0 %collective-permute-start.5 = (bf16[32,3584]{1,0:T(8,128)(2,1)S(1)}, bf16[32,3584]{1,0:T(8,128)(2,1)S(1)}, u32[]{:S(2)}, u32[]{:S(2)}) collective-permute-start(bf16[32,3584]{1,0:T(8,128)(2,1)S(1)} %get-tuple-element.31), channel_id=1, source_target_pairs={{0,112},{8,120},{16,0},{24,8},{32,16},{40,24},{48,32},{56,40},{64,... | collective-permute-start | bytes 688136 | tf_op jit(solution)/shard_map/ppermute | solution.py:27
  115.4 12.5 %collective-permute-start.6 = (bf16[16,1792]{1,0:T(8,128)(2,1)S(1)}, bf16[16,1792]{1,0:T(8,128)(2,1)S(1)}, u32[]{:S(2)}, u32[]{:S(2)}) collective-permute-start(bf16[16,1792]{1,0:T(8,128)(2,1)S(1)} %get-tuple-element.43), channel_id=1, source_target_pairs={{0,32},{8,40},{16,48},{24,56},{32,64},{40,72},{48,80},{56,88},{64,... | collective-permute-start | bytes 172040 | tf_op jit(solution)/shard_map/ppermute | solution.py:27
  119.4 12.8 %collective-permute-start.7 = (bf16[16,1792]{1,0:T(8,128)(2,1)S(1)}, bf16[16,1792]{1,0:T(8,128)(2,1)S(1)}, u32[]{:S(2)}, u32[]{:S(2)}) collective-permute-start(bf16[16,1792]{1,0:T(8,128)(2,1)S(1)} %get-tuple-element.42), channel_id=1, source_target_pairs={{0,96},{8,104},{16,112},{24,120},{32,0},{40,8},{48,16},{56,24},{64... | collective-permute-start | bytes 172040 | tf_op jit(solution)/shard_map/ppermute | solution.py:27
  127.9 14.1 %all-to-all-start.1 = ((bf16[4,16,640]{2,1,0:T(8,128)(2,1)}), bf16[4,16,640]{2,1,0:T(8,128)(2,1)S(1)}, u32[]{:S(2)}, u32[]{:S(2)}) async-start(bf16[4,16,640]{2,1,0:T(8,128)(2,1)} %get-tuple-element.36), calls=%async_computation.1 | async-start | bytes 163840 | tf_op jit(solution)/shard_map/all_to_all | solution.py:353
  132.2 14.3 %collective-permute-start.8 = (bf16[16,3584]{1,0:T(8,128)(2,1)S(1)}, bf16[16,3584]{1,0:T(8,128)(2,1)S(1)}, u32[]{:S(2)}, u32[]{:S(2)}) collective-permute-start(bf16[16,3584]{1,0:T(8,128)(2,1)S(1)} %pad_maximum_fusion), channel_id=1, source_target_pairs={{0,32},{8,40},{16,48},{24,56},{32,64},{40,72},{48,80},{56,88},{64,... | collective-permute-start | bytes 344072 | tf_op jit(solution)/shard_map/ppermute | solution.py:27
  136.4 15.5 %collective-permute-start.9 = (bf16[16,3584]{1,0:T(8,128)(2,1)S(1)}, bf16[16,3584]{1,0:T(8,128)(2,1)S(1)}, u32[]{:S(2)}, u32[]{:S(2)}) collective-permute-start(bf16[16,3584]{1,0:T(8,128)(2,1)S(1)} %pad_maximum_fusion.1), channel_id=1, source_target_pairs={{0,96},{8,104},{16,112},{24,120},{32,0},{40,8},{48,16},{56,24},{64... | collective-permute-start | bytes 344072 | tf_op jit(solution)/shard_map/ppermute | solution.py:27

commit v16 on v15

--- a/solution.py
+++ b/solution.py
@@ -176,13 +176,13 @@
 
     def attend(blocks_seen):
         count = blocks_seen * n
-        idx = lax.broadcasted_iota(jnp.int32, (rows, 1), 0)
+        idx = lax.broadcasted_iota(jnp.int32, (2 * rows, 1), 0) % rows
         qpos = query_where(idx, z, core, qrows, chips)
         idx = lax.broadcasted_iota(jnp.int32, (1, n), 1)
         kpos = (idx % qrows) // part * (chips * 2 * part) + idx // qrows * (2 * part) + idx % part
         ok = [kpos + i * part <= qpos for i in (core, 1 - core)]
-        for h in range(heads):
-            q = q_ref[h * rows : (h + 1) * rows, :]
+        for h in range(0, heads, 2):
+            q = q_ref[h * rows : (h + 2) * rows, :]
             scores = []
             for i, k_ref in enumerate((ka_ref, kb_ref)):
                 for part_keys in (slice(0, count - n), slice(count - n, count)):
@@ -201,7 +201,7 @@
                 mixed = mixed + jnp.dot(
                     p.astype(BF), k_ref[part_keys, :lat], preferred_element_type=F32
                 )
-            acc_ref[h * rows : (h + 1) * rows, :] = (mixed / total).astype(BF)
+            acc_ref[h * rows : (h + 2) * rows, :] = (mixed / total).astype(BF)
 
     for seen in range(1, nch + 1):
         pl.when(chain == seen - 1)(functools.partial(attend, seen))

time: 153 us -> 153 us (level)
  no operation moved by 1% of the time
where the time goes in v16:
time: 153 us; the launch traced here: 152 us
  blocking collectives  68 us (44%)
  starting transfers between devices  47.4 us (31%)
  Pallas kernels  16.9 us (11%)
  waiting for transfers between devices  14.7 us (10%)
  local copies, waits for them, and re-layouts  2.85 us (2%)
    all_gather x1, blocking collectives, local(): own = lax.all_gather(keys, Z, axis=0, tiled=True)  37.4 us
    ppermute x8, starting transfers between devices, shift_z(): return lax.ppermute(x, Z, [(i, (i + step) % n) for i in range(n)])  34.5 us
    all_gather x1, blocking collectives, local(): qg = lax.all_gather(held, Z, axis=0, tiled=True)  30.6 us
    ppermute x8, waiting for transfers between devices, shift_z(): return lax.ppermute(x, Z, [(i, (i + step) % n) for i in range(n)])  14.6 us
    pallas_call x1, Pallas kernels, local(): pl.pallas_call(functools.partial(attend_kernel, rows=rows, lat=lat, scale...  9.09 us
    all_to_all x1, starting transfers between devices, spread(): lax.all_to_all(jnp.broadcast_to(x[None], (n,) + x.shape), axis, 0, 0, til...  4.82 us
    pallas_call x1, Pallas kernels, local(): pl.pallas_call(functools.partial(key_kernel, slots=slots, page_len=part *...  4.47 us
    all_to_all x1, starting transfers between devices, local(): lax.all_to_all(page, 'dec', 0, 0, tiled=True).reshape(-1, pages, part, kw)  4.3 us
  transfers between devices with their start and end apart: 12, of which 5 were waited for; matrix products, arithmetic and copies ran while one was open for 2% of the time, Pallas kernels for 2%

profile of v16, /device:TPU:24, one launch (start us, length us, event | category | flops | bytes accessed | tf_op | source)
XLA Modules:
  0.0 152.0 jit_solution(17492481789758239844)
XLA Ops:
  0.6 4.5 %keys.1 = (bf16[16,640]{1,0:T(8,128)(2,1)}, bf16[4,16,640]{2,1,0:T(8,128)(2,1)}, bf16[13824,128]{1,0:T(8,128)(2,1)}) custom-call(s32[1]{0:T(128)} %bitcast.4.where_ref, s32[1,4]{1,0:T(1,128)} %owner_ref.1, s32[1,4]{1,0:T(1,128)} %slot_ref.1, bf16[1,4,4,512]{3,2,1,0:T(4,128)(2,1)} %lat_ref.1, bf16[1,4,4,64]{3,2,1,0:T(4,128)(2,1)} %rope_ref.1, ...), custom_call_target="tpu_custom_call" | custom-call | tf_op jit(solution)/shard_map/keys/pallas_call | solution.py:261
  5.1 1.9 %collective-permute-start = (bf16[13824,128]{1,0:T(8,128)(2,1)}, bf16[13824,128]{1,0:T(8,128)(2,1)}, u32[]{:S(2)}, u32[]{:S(2)}) collective-permute-start(bf16[13824,128]{1,0:T(8,128)(2,1)} %get-tuple-element.23), channel_id=1, source_target_pairs={{0,4},{4,0},{1,5},{5,1},{2,6},{6,2},{3,7},{7,3},{8,12},{12,8},{9,1... | collective-permute-start | bytes 10616840 | tf_op jit(solution)/shard_map/ppermute | solution.py:31
  7.0 37.4 %all_gather.6 = bf16[256,640]{1,0:T(8,128)(2,1)S(1)} all-gather(bf16[16,640]{1,0:T(8,128)(2,1)} %get-tuple-element.20), channel_id=1, replica_groups=mesh['chain'=4,'zh'=4,'zl'=4,'core'=2,'dec'=4] {'zh','zl'}, dimensions={0}, use_global_device_ids=true | all-gather | bytes 348160 | tf_op jit(solution)/shard_map/all_gather | solution.py:278
  44.4 1.2 broadcast_in_dim.25
  45.7 4.8 %all-to-all-start = ((bf16[4,256,640]{2,1,0:T(8,128)(2,1)}), bf16[4,256,640]{2,1,0:T(8,128)(2,1)S(1)}, u32[]{:S(2)}, u32[]{:S(2)}) async-start(bf16[4,256,640]{2,1,0:T(8,128)(2,1)} %broadcast_in_dim.25), calls=%async_computation | async-start | bytes 2621440 | tf_op jit(solution)/shard_map/all_to_all | solution.py:36
  50.5 30.6 %all_gather.7.g_ref = bf16[256,1536]{1,0:T(8,128)(2,1)S(1)} all-gather(bf16[16,1536]{1,0:T(8,128)(2,1)} %bitcast.20), channel_id=1, replica_groups=mesh['chain'=4,'zh'=4,'zl'=4,'core'=2,'dec'=4] {'zh','zl'}, dimensions={0}, use_global_device_ids=true | all-gather | bytes 835584 | tf_op jit(solution)/shard_map/all_gather | solution.py:281
  81.1 1.9 %collective-permute-start.1 = (bf16[1024,640]{1,0:T(8,128)(2,1)S(1)}, bf16[1024,640]{1,0:T(8,128)(2,1)S(1)}, u32[]{:S(2)}, u32[]{:S(2)}) collective-permute-start(bf16[1024,640]{1,0:T(8,128)(2,1)S(1)} %bitcast.18), channel_id=1, source_target_pairs={{0,4},{4,0},{1,5},{5,1},{2,6},{6,2},{3,7},{7,3},{8,12},{12,8},{9,1... | collective-permute-start | bytes 3932168 | tf_op jit(solution)/shard_map/ppermute | solution.py:31
  83.0 0.1 pad_add_fusion.where_ref
  83.1 3.3 %queries.1.q_ref = bf16[1024,640]{1,0:T(8,128)(2,1)S(1)} custom-call(s32[3]{0:T(128)S(1)} %pad_add_fusion.where_ref, bf16[256,1536]{1,0:T(8,128)(2,1)S(1)} %all_gather.7.g_ref, bf16[1536,384]{1,0:T(8,128)(2,1)S(1)} %copy-done, bf16[2,128,512]{2,1,0:T(8,128)(2,1)S(1)} %copy-done.2, bf16[13824,128]{1,0:T(8,128)(2,1)} %collective-permute-done.packed), custom_call_target="tpu_custom_call" | custom-call | flops 738197504 | bytes 6000000 | tf_op jit(solution)/shard_map/queries/pallas_call | solution.py:285
  86.4 9.1 %attend.1 = (bf16[64,3584]{1,0:T(8,128)(2,1)S(1)}, bf16[64,3584]{1,0:T(8,128)(2,1)S(1)}, bf16[64,3584]{1,0:T(8,128)(2,1)S(1)}, bf16[32,3584]{1,0:T(8,128)(2,1)S(1)}, bf16[32,3584]{1,0:T(8,128)(2,1)S(1)}) custom-call(s32[3]{0:T(128)S(1)} %pad_add_fusion.where_ref, bf16[1024,640]{1,0:T(8,128)(2,1)S(1)} %queries.1.q_ref, bf16[1024,640]{1,0:T(8,128)(2,1)S(1)} %bitcast.19, ...), custom_call_target="tpu_custom_call" | custom-call | flops 4294967296 | bytes 9000000 | tf_op jit(solution)/shard_map/attend/pallas_call | solution.py:305
  95.5 3.8 %collective-permute-start.2 = (bf16[64,3584]{1,0:T(8,128)(2,1)S(1)}, bf16[64,3584]{1,0:T(8,128)(2,1)S(1)}, u32[]{:S(2)}, u32[]{:S(2)}) collective-permute-start(bf16[64,3584]{1,0:T(8,128)(2,1)S(1)} %get-tuple-element.26), channel_id=1, source_target_pairs={{0,8},{8,16},{16,24},{24,32},{32,40},{40,48},{48,56},{56,64},{64,7... | collective-permute-start | bytes 1376264 | tf_op jit(solution)/shard_map/ppermute | solution.py:27
  99.3 3.3 %collective-permute-start.3 = (bf16[64,3584]{1,0:T(8,128)(2,1)S(1)}, bf16[64,3584]{1,0:T(8,128)(2,1)S(1)}, u32[]{:S(2)}, u32[]{:S(2)}) collective-permute-start(bf16[64,3584]{1,0:T(8,128)(2,1)S(1)} %get-tuple-element.27), channel_id=1, source_target_pairs={{0,120},{8,0},{16,8},{24,16},{32,24},{40,32},{48,40},{56,48},{64,5... | collective-permute-start | bytes 1376264 | tf_op jit(solution)/shard_map/ppermute | solution.py:27
  102.6 2.0 %collective-permute-start.4 = (bf16[32,3584]{1,0:T(8,128)(2,1)S(1)}, bf16[32,3584]{1,0:T(8,128)(2,1)S(1)}, u32[]{:S(2)}, u32[]{:S(2)}) collective-permute-start(bf16[32,3584]{1,0:T(8,128)(2,1)S(1)} %get-tuple-element.30), channel_id=1, source_target_pairs={{0,16},{8,24},{16,32},{24,40},{32,48},{40,56},{48,64},{56,72},{64,... | collective-permute-start | bytes 688136 | tf_op jit(solution)/shard_map/ppermute | solution.py:27
  104.6 5.9 %collective-permute-start.5 = (bf16[32,3584]{1,0:T(8,128)(2,1)S(1)}, bf16[32,3584]{1,0:T(8,128)(2,1)S(1)}, u32[]{:S(2)}, u32[]{:S(2)}) collective-permute-start(bf16[32,3584]{1,0:T(8,128)(2,1)S(1)} %get-tuple-element.31), channel_id=1, source_target_pairs={{0,112},{8,120},{16,0},{24,8},{32,16},{40,24},{48,32},{56,40},{64,... | collective-permute-start | bytes 688136 | tf_op jit(solution)/shard_map/ppermute | solution.py:27
  110.6 2.4 %collective-permute-done.2 = bf16[64,3584]{1,0:T(8,128)(2,1)S(1)} collective-permute-done((bf16[64,3584]{1,0:T(8,128)(2,1)S(1)}, bf16[64,3584]{1,0:T(8,128)(2,1)S(1)}, u32[]{:S(2)}, u32[]{:S(2)}) %collective-permute-start.2) | collective-permute-done | bytes 458784 | tf_op jit(solution)/shard_map/ppermute | solution.py:27
  113.0 1.8 %collective-permute-done.3 = bf16[64,3584]{1,0:T(8,128)(2,1)S(1)} collective-permute-done((bf16[64,3584]{1,0:T(8,128)(2,1)S(1)}, bf16[64,3584]{1,0:T(8,128)(2,1)S(1)}, u32[]{:S(2)}, u32[]{:S(2)}) %collective-permute-start.3) | collective-permute-done | bytes 458784 | tf_op jit(solution)/shard_map/ppermute | solution.py:27
  114.9 4.0 %collective-permute-start.6 = (bf16[16,1792]{1,0:T(8,128)(2,1)S(1)}, bf16[16,1792]{1,0:T(8,128)(2,1)S(1)}, u32[]{:S(2)}, u32[]{:S(2)}) collective-permute-start(bf16[16,1792]{1,0:T(8,128)(2,1)S(1)} %get-tuple-element.43), channel_id=1, source_target_pairs={{0,32},{8,40},{16,48},{24,56},{32,64},{40,72},{48,80},{56,88},{64,... | collective-permute-start | bytes 172040 | tf_op jit(solution)/shard_map/ppermute | solution.py:27
  118.8 5.8 %collective-permute-start.7 = (bf16[16,1792]{1,0:T(8,128)(2,1)S(1)}, bf16[16,1792]{1,0:T(8,128)(2,1)S(1)}, u32[]{:S(2)}, u32[]{:S(2)}) collective-permute-start(bf16[16,1792]{1,0:T(8,128)(2,1)S(1)} %get-tuple-element.42), channel_id=1, source_target_pairs={{0,96},{8,104},{16,112},{24,120},{32,0},{40,8},{48,16},{56,24},{64... | collective-permute-start | bytes 172040 | tf_op jit(solution)/shard_map/ppermute | solution.py:27
  124.6 0.1 convert_add_fusion.1
  124.8 2.6 %collective-permute-done.6 = bf16[16,1792]{1,0:T(8,128)(2,1)S(1)} collective-permute-done((bf16[16,1792]{1,0:T(8,128)(2,1)S(1)}, bf16[16,1792]{1,0:T(8,128)(2,1)S(1)}, u32[]{:S(2)}, u32[]{:S(2)}) %collective-permute-start.6) | collective-permute-done | bytes 57376 | tf_op jit(solution)/shard_map/ppermute | solution.py:27
  127.4 4.3 %all-to-all-start.1 = ((bf16[4,16,640]{2,1,0:T(8,128)(2,1)}), bf16[4,16,640]{2,1,0:T(8,128)(2,1)S(1)}, u32[]{:S(2)}, u32[]{:S(2)}) async-start(bf16[4,16,640]{2,1,0:T(8,128)(2,1)} %get-tuple-element.36), calls=%async_computation.1 | async-start | bytes 163840 | tf_op jit(solution)/shard_map/all_to_all | solution.py:353
  131.7 4.1 %collective-permute-start.8 = (bf16[16,3584]{1,0:T(8,128)(2,1)S(1)}, bf16[16,3584]{1,0:T(8,128)(2,1)S(1)}, u32[]{:S(2)}, u32[]{:S(2)}) collective-permute-start(bf16[16,3584]{1,0:T(8,128)(2,1)S(1)} %pad_maximum_fusion), channel_id=1, source_target_pairs={{0,32},{8,40},{16,48},{24,56},{32,64},{40,72},{48,80},{56,88},{64,... | collective-permute-start | bytes 344072 | tf_op jit(solution)/shard_map/ppermute | solution.py:27
  135.8 5.7 %collective-permute-start.9 = (bf16[16,3584]{1,0:T(8,128)(2,1)S(1)}, bf16[16,3584]{1,0:T(8,128)(2,1)S(1)}, u32[]{:S(2)}, u32[]{:S(2)}) collective-permute-start(bf16[16,3584]{1,0:T(8,128)(2,1)S(1)} %pad_maximum_fusion.1), channel_id=1, source_target_pairs={{0,96},{8,104},{16,112},{24,120},{32,0},{40,8},{48,16},{56,24},{64... | collective-permute-start | bytes 344072 | tf_op jit(solution)/shard_map/ppermute | solution.py:27
  141.5 0.1 slice.112
  141.6 0.1 copy.17
  141.8 0.1 reshape.27
  141.9 0.2 convolution_convert_fusion
  142.1 0.6 copy.15
  142.7 0.6 copy.16
  143.3 2.7 %collective-permute-done.8 = bf16[16,3584]{1,0:T(8,128)(2,1)S(1)} collective-permute-done((bf16[16,3584]{1,0:T(8,128)(2,1)S(1)}, bf16[16,3584]{1,0:T(8,128)(2,1)S(1)}, u32[]{:S(2)}, u32[]{:S(2)}) %collective-permute-start.8) | collective-permute-done | bytes 114720 | tf_op jit(solution)/shard_map/ppermute | solution.py:27
  146.0 5.2 %collective-permute-done.9 = bf16[16,3584]{1,0:T(8,128)(2,1)S(1)} collective-permute-done((bf16[16,3584]{1,0:T(8,128)(2,1)S(1)}, bf16[16,3584]{1,0:T(8,128)(2,1)S(1)}, u32[]{:S(2)}, u32[]{:S(2)}) %collective-permute-start.9) | collective-permute-done | bytes 114720 | tf_op jit(solution)/shard_map/ppermute | solution.py:27
  151.2 0.8 fusion
  (29 shorter events, 0.2 us)
Async XLA Ops:
  5.1 78.0 %collective-permute-start = (bf16[13824,128]{1,0:T(8,128)(2,1)}, bf16[13824,128]{1,0:T(8,128)(2,1)}, u32[]{:S(2)}, u32[]{:S(2)}) collective-permute-start(bf16[13824,128]{1,0:T(8,128)(2,1)} %get-tuple-element.23), channel_id=1, source_target_pairs={{0,4},{4,0},{1,5},{5,1},{2,6},{6,2},{3,7},{7,3},{8,12},{12,8},{9,1... | collective-permute-start | bytes 10616840 | tf_op jit(solution)/shard_map/ppermute | solution.py:31
  45.7 37.4 %copy-start = (bf16[1536,384]{1,0:T(8,128)(2,1)S(1)}, bf16[1536,384]{1,0:T(8,128)(2,1)}, u32[]{:S(2)}) copy-start(bf16[1536,384]{1,0:T(8,128)(2,1)} %wq0.1) | copy-start | bytes 3538948
  45.7 37.4 %copy-start.2 = (bf16[2,128,512]{2,1,0:T(8,128)(2,1)S(1)}, bf16[2,128,512]{2,1,0:T(8,128)(2,1)}, u32[]{:S(2)}) copy-start(bf16[2,128,512]{2,1,0:T(8,128)(2,1)} %ak0.1) | copy-start | bytes 786436
  45.7 35.4 %all-to-all-start = ((bf16[4,256,640]{2,1,0:T(8,128)(2,1)}), bf16[4,256,640]{2,1,0:T(8,128)(2,1)S(1)}, u32[]{:S(2)}, u32[]{:S(2)}) async-start(bf16[4,256,640]{2,1,0:T(8,128)(2,1)} %broadcast_in_dim.25), calls=%async_computation | async-start | bytes 2621440 | tf_op jit(solution)/shard_map/all_to_all | solution.py:36
  81.1 5.3 %collective-permute-start.1 = (bf16[1024,640]{1,0:T(8,128)(2,1)S(1)}, bf16[1024,640]{1,0:T(8,128)(2,1)S(1)}, u32[]{:S(2)}, u32[]{:S(2)}) collective-permute-start(bf16[1024,640]{1,0:T(8,128)(2,1)S(1)} %bitcast.18), channel_id=1, source_target_pairs={{0,4},{4,0},{1,5},{5,1},{2,6},{6,2},{3,7},{7,3},{8,12},{12,8},{9,1... | collective-permute-start | bytes 3932168 | tf_op jit(solution)/shard_map/ppermute | solution.py:31
  83.1 3.4 %copy-start.1 = (bf16[256,3584]{1,0:T(8,128)(2,1)S(1)}, bf16[256,3584]{1,0:T(8,128)(2,1)}, u32[]{:S(2)}) copy-start(bf16[256,3584]{1,0:T(8,128)(2,1)} %op0.1) | copy-start | bytes 5505028
  83.1 3.4 %copy-start.3 = (bf16[2,512,128]{2,1,0:T(8,128)(2,1)S(1)}, bf16[2,512,128]{2,1,0:T(8,128)(2,1)}, u32[]{:S(2)}) copy-start(bf16[2,512,128]{2,1,0:T(8,128)(2,1)} %av0.1) | copy-start | bytes 786436
  95.5 17.5 %collective-permute-start.2 = (bf16[64,3584]{1,0:T(8,128)(2,1)S(1)}, bf16[64,3584]{1,0:T(8,128)(2,1)S(1)}, u32[]{:S(2)}, u32[]{:S(2)}) collective-permute-start(bf16[64,3584]{1,0:T(8,128)(2,1)S(1)} %get-tuple-element.26), channel_id=1, source_target_pairs={{0,8},{8,16},{16,24},{24,32},{32,40},{40,48},{48,56},{56,64},{64,7... | collective-permute-start | bytes 1376264 | tf_op jit(solution)/shard_map/ppermute | solution.py:27
  99.3 15.5 %collective-permute-start.3 = (bf16[64,3584]{1,0:T(8,128)(2,1)S(1)}, bf16[64,3584]{1,0:T(8,128)(2,1)S(1)}, u32[]{:S(2)}, u32[]{:S(2)}) collective-permute-start(bf16[64,3584]{1,0:T(8,128)(2,1)S(1)} %get-tuple-element.27), channel_id=1, source_target_pairs={{0,120},{8,0},{16,8},{24,16},{32,24},{40,32},{48,40},{56,48},{64,5... | collective-permute-start | bytes 1376264 | tf_op jit(solution)/shard_map/ppermute | solution.py:27
  102.6 22.0 %collective-permute-start.4 = (bf16[32,3584]{1,0:T(8,128)(2,1)S(1)}, bf16[32,3584]{1,0:T(8,128)(2,1)S(1)}, u32[]{:S(2)}, u32[]{:S(2)}) collective-permute-start(bf16[32,3584]{1,0:T(8,128)(2,1)S(1)} %get-tuple-element.30), channel_id=1, source_target_pairs={{0,16},{8,24},{16,32},{24,40},{32,48},{40,56},{48,64},{56,72},{64,... | collective-permute-start | bytes 688136 | tf_op jit(solution)/shard_map/ppermute | solution.py:27
  104.6 20.0 %collective-permute-start.5 = (bf16[32,3584]{1,0:T(8,128)(2,1)S(1)}, bf16[32,3584]{1,0:T(8,128)(2,1)S(1)}, u32[]{:S(2)}, u32[]{:S(2)}) collective-permute-start(bf16[32,3584]{1,0:T(8,128)(2,1)S(1)} %get-tuple-element.31), channel_id=1, source_target_pairs={{0,112},{8,120},{16,0},{24,8},{32,16},{40,24},{48,32},{56,40},{64,... | collective-permute-start | bytes 688136 | tf_op jit(solution)/shard_map/ppermute | solution.py:27
  114.9 12.5 %collective-permute-start.6 = (bf16[16,1792]{1,0:T(8,128)(2,1)S(1)}, bf16[16,1792]{1,0:T(8,128)(2,1)S(1)}, u32[]{:S(2)}, u32[]{:S(2)}) collective-permute-start(bf16[16,1792]{1,0:T(8,128)(2,1)S(1)} %get-tuple-element.43), channel_id=1, source_target_pairs={{0,32},{8,40},{16,48},{24,56},{32,64},{40,72},{48,80},{56,88},{64,... | collective-permute-start | bytes 172040 | tf_op jit(solution)/shard_map/ppermute | solution.py:27
  118.8 12.8 %collective-permute-start.7 = (bf16[16,1792]{1,0:T(8,128)(2,1)S(1)}, bf16[16,1792]{1,0:T(8,128)(2,1)S(1)}, u32[]{:S(2)}, u32[]{:S(2)}) collective-permute-start(bf16[16,1792]{1,0:T(8,128)(2,1)S(1)} %get-tuple-element.42), channel_id=1, source_target_pairs={{0,96},{8,104},{16,112},{24,120},{32,0},{40,8},{48,16},{56,24},{64... | collective-permute-start | bytes 172040 | tf_op jit(solution)/shard_map/ppermute | solution.py:27
  127.4 14.2 %all-to-all-start.1 = ((bf16[4,16,640]{2,1,0:T(8,128)(2,1)}), bf16[4,16,640]{2,1,0:T(8,128)(2,1)S(1)}, u32[]{:S(2)}, u32[]{:S(2)}) async-start(bf16[4,16,640]{2,1,0:T(8,128)(2,1)} %get-tuple-element.36), calls=%async_computation.1 | async-start | bytes 163840 | tf_op jit(solution)/shard_map/all_to_all | solution.py:353
  131.7 14.3 %collective-permute-start.8 = (bf16[16,3584]{1,0:T(8,128)(2,1)S(1)}, bf16[16,3584]{1,0:T(8,128)(2,1)S(1)}, u32[]{:S(2)}, u32[]{:S(2)}) collective-permute-start(bf16[16,3584]{1,0:T(8,128)(2,1)S(1)} %pad_maximum_fusion), channel_id=1, source_target_pairs={{0,32},{8,40},{16,48},{24,56},{32,64},{40,72},{48,80},{56,88},{64,... | collective-permute-start | bytes 344072 | tf_op jit(solution)/shard_map/ppermute | solution.py:27
  135.8 15.4 %collective-permute-start.9 = (bf16[16,3584]{1,0:T(8,128)(2,1)S(1)}, bf16[16,3584]{1,0:T(8,128)(2,1)S(1)}, u32[]{:S(2)}, u32[]{:S(2)}) collective-permute-start(bf16[16,3584]{1,0:T(8,128)(2,1)S(1)} %pad_maximum_fusion.1), channel_id=1, source_target_pairs={{0,96},{8,104},{16,112},{24,120},{32,0},{40,8},{48,16},{56,24},{64... | collective-permute-start | bytes 344072 | tf_op jit(solution)/shard_map/ppermute | solution.py:27
